TPU v7x, 128 devices: a whole 4x4x4 slice. The times are simulated.
128 devices in a mesh: grp: 8 (over x, core), tp: 16 (over z, y).
Axes of the slice: x: 4, y: 4, z: 4, core: 2. Of those that a mesh axis runs over, the one named last changes fastest.
Arguments:
- image: bfloat16 [4096, 2432], P('grp'), may hold values from -6 to 6
- prompt_encoder_rows: bfloat16 [2560, 4096], P(('grp', 'tp')), may hold values from -6 to 6
- prompt_row_request: int32 [2560, 1], P(('grp', 'tp')), may hold values from 0 to 15; in each aligned block of 20 rows (0 to 19, 20 to 39, ...) at most 2 rows name the same one
- request_adapter: int32 [16], P('grp'), may hold values from 0 to 31
- modulation: float32 [16, 2, 6, 2432], P('grp'), may hold values from -3 to 3
- query_key_gain: float32 [2, 2, 64], replicated, may hold values from 0.25 to 1.75
- prompt_embed_weight: bfloat16 [4096, 2432], P('tp'), may hold values from -0.09375 to 0.09375
- image_query_key_value: bfloat16 [2432, 3, 2048], P(None, None, 'tp'), may hold values from -0.125 to 0.125
- prompt_query_key_value: bfloat16 [2432, 3, 2048], P(None, None, 'tp'), may hold values from -0.125 to 0.125
- image_out_weight: bfloat16 [2048, 2432], P('tp'), may hold values from -0.125 to 0.125
- prompt_out_weight: bfloat16 [2048, 2432], P('tp'), may hold values from -0.125 to 0.125
- feed_in_weight: bfloat16 [2, 2432, 9728], P(None, None, 'tp'), may hold values from -0.125 to 0.125
- feed_out_weight: bfloat16 [2, 9728, 2432], P(None, 'tp'), may hold values from -0.0625 to 0.0625
- adapter_down: bfloat16 [32, 2432, 192], P(None, 'tp'), may hold values from -0.125 to 0.125
- adapter_up: bfloat16 [32, 3, 64, 2048], P(None, None, None, 'tp'), may hold values from -0.75 to 0.75
Outputs:
- image_out: bfloat16 [4096, 2432], P(('grp', 'tp'))
- prompt_out: bfloat16 [4096, 2432], P(('grp', 'tp'))
Inputs may be any that keep to these rules, and one draw needn't show every extreme that they name: `prompt_row_request`: among the rows of one encoder device (20 aligned rows) no request is named more than 2 times, a bound that some block reaches.
All inputs are finite; a program needn't handle non-finite values.
Results may differ from a plain program's by a relative error of at most 0.024.
Values may be sent and summed in bfloat16 or wider, within the bound.
No kernel may reach another device: no remote copies, remote signals or barrier semaphores. Data moves between devices by JAX's collectives and lax.ppermute only.
A program may use at most 128 MiB of HBM per device.

v0:
```python
import functools

import jax
import jax.numpy as jnp
from jax import lax
from jax.experimental import pallas as pl
from jax.experimental.pallas import tpu as pltpu
from jax.sharding import PartitionSpec as P

HEAD_DIM = 64
CAP = 2
EPSILON = 1e-06
ADAPTER_SCALE = 0.5
SIDE = 4
POOL = 20
F32 = jnp.float32
BF16 = jnp.bfloat16


def torus_shift(values, stage, step):
    pairs = []
    for grp in range(8):
        for tp in range(16):
            z, y = divmod(tp, SIDE)
            if (grp + stage) % 2 == 0:
                y = (y + step) % SIDE
            else:
                z = (z + step) % SIDE
            pairs.append((grp * 16 + tp, grp * 16 + z * SIDE + y))
    return lax.ppermute(values, ("grp", "tp"), pairs)


def spread(rows, stage):
    return [
        rows,
        torus_shift(rows, stage, -1),
        torus_shift(rows, stage, 2),
        torus_shift(rows, stage, 1),
    ]


def exchange(parts, stage):
    return [
        parts[0],
        torus_shift(parts[3], stage, -1),
        torus_shift(parts[2], stage, 2),
        torus_shift(parts[1], stage, 1),
    ]


def run(kernel, outs, args, smem=0, scratch=(), flops=0, limit=32, after=()):
    specs = [pl.BlockSpec(memory_space=pltpu.SMEM)] * smem
    specs += [pl.BlockSpec(memory_space=pltpu.VMEM)] * (len(args) - smem)
    specs += [pl.BlockSpec(memory_space=pl.ANY)] * len(after)
    count = len(args)
    single = not isinstance(outs, list)
    shapes = [outs] if single else outs
    moved = sum(a.size * a.dtype.itemsize for a in args)
    moved += sum(s.size * s.dtype.itemsize for s in shapes)

    def body(*refs):
        kernel(*refs[:count], *refs[count + len(after) :])

    result = pl.pallas_call(
        body,
        out_shape=shapes,
        in_specs=specs,
        out_specs=[pl.BlockSpec(memory_space=pltpu.VMEM)] * len(shapes),
        scratch_shapes=list(scratch),
        compiler_params=pltpu.CompilerParams(vmem_limit_bytes=limit << 20),
        cost_estimate=pl.CostEstimate(flops=flops, bytes_accessed=moved, transcendentals=0),
    )(*args, *after)
    return result[0] if single else result


def like(shape, dtype=BF16):
    return jax.ShapeDtypeStruct(shape, dtype)


def normed(values):
    centred = values - jnp.mean(values, -1, keepdims=True)
    return centred * lax.rsqrt(jnp.mean(centred * centred, -1, keepdims=True) + EPSILON)


def low_half(shape):
    return lax.broadcasted_iota(jnp.int32, shape, len(shape) - 1) < HEAD_DIM


def head_norm(values, gains):
    first = low_half(values.shape)
    squares = values * values
    head0 = jnp.sum(jnp.where(first, squares, 0.0), -1, keepdims=True)
    head1 = jnp.sum(jnp.where(first, 0.0, squares), -1, keepdims=True)
    scale = jnp.where(
        first,
        lax.rsqrt(head0 * (1.0 / HEAD_DIM) + EPSILON),
        lax.rsqrt(head1 * (1.0 / HEAD_DIM) + EPSILON),
    )
    return values * scale * gains


def pack_kernel(rows_ref, line_ref, out_ref, held, wide):
    wide[...] = jnp.full(wide.shape, -1, jnp.int32)
    wide[0:1, 0:POOL] = line_ref[...]
    line = wide[0:1, :]
    first = lax.broadcasted_iota(jnp.int32, (POOL, 256), 0)
    second = lax.broadcasted_iota(jnp.int32, (POOL, 256), 1)
    column = jnp.sum(jnp.where(first == second, line, 0), 1, keepdims=True)
    rank = jnp.sum(jnp.where((column == line) & (first < second), 1, 0), 0, keepdims=True)
    held[...] = jnp.zeros_like(held)
    held[POOL : POOL + 1, :] = (line * CAP + rank).astype(F32)
    for block in range(16):
        held[0:POOL, :] = rows_ref[:, block * 256 : (block + 1) * 256].astype(F32)
        out_ref[block] = held[...].astype(BF16)


def embed_kernel(places_ref, arrived_ref, weight_ref, out0, out1, out2, out3, label_ref, held):
    for far, out in enumerate((out0, out1, out2, out3)):
        for near in range(SIDE):
            place = far * SIDE + near
            block = arrived_ref[places_ref[place]].astype(F32)
            held[near * POOL : (near + 1) * POOL, :] = block[0:POOL]
            label_ref[place : place + 1, :] = block[POOL : POOL + 1]
        out[...] = jnp.dot(
            held[...].astype(BF16), weight_ref[...], preferred_element_type=F32
        ).astype(BF16)


def middle_kernel(in0, in1, in2, in3, out0, out1, out2, out3, held):
    held[...] = total_of((in0, in1, in2, in3))
    part = out0.shape[0]
    for place, out in enumerate((out0, out1, out2, out3)):
        out[...] = held[place * part : (place + 1) * part, :].astype(BF16)


def both_middle_kernel(*refs):
    held = refs[12]
    held[...] = total_of(refs[4:8])
    total = total_of(refs[0:4])
    for place, out in enumerate(refs[8:12]):
        out[0:32, :] = total[place * 32 : (place + 1) * 32].astype(BF16)
        out[32 : 32 + POOL, :] = held[place * POOL : (place + 1) * POOL, :].astype(BF16)


def join_kernel(start, in0, in1, in2, in3, out_ref, held):
    part = out_ref.shape[0] // SIDE
    for place, piece in enumerate((in0, in1, in2, in3)):
        held[place * part : (place + 1) * part, :] = piece[start : start + part, :].astype(F32)
    out_ref[...] = held[...].astype(BF16)


def repeat_mod_kernel(mod_ref, out_ref):
    out_ref[...] = jnp.zeros_like(out_ref)
    for own in range(2):
        for place in range(6):
            line = mod_ref[own, place, 1:2, :]
            for group in range(8):
                out_ref[group, own, place : place + 1, :] = line


def row_mod_kernel(index_ref, mod_ref, out_ref):
    for row in range(POOL):
        values = mod_ref[index_ref[row]]
        for place in range(6):
            out_ref[place, row : row + 1, :] = values[place : place + 1]


def total_of(parts):
    return functools.reduce(jnp.add, [part[...].astype(F32) for part in parts])


def embed_norm_kernel(in0, in1, in2, in3, mod_ref, embedded_ref, out_ref):
    embedded = total_of((in0, in1, in2, in3)).astype(BF16)
    embedded_ref[...] = embedded
    out_ref[...] = (normed(embedded.astype(F32)) * (1.0 + mod_ref[1]) + mod_ref[0]).astype(BF16)


def both_norm_kernel(
    image_ref, embedded_ref, in0, in1, in2, in3, img_mod_ref, txt_mod_ref,
    img_ref, txt_ref, out_ref,
):
    projected = total_of((in0, in1, in2, in3))
    gate, shift, scale = img_mod_ref[2:3, :], img_mod_ref[3:4, :], img_mod_ref[4:5, :]
    mixed = (image_ref[...].astype(F32) + gate * projected[0:32]).astype(BF16)
    img_ref[...] = mixed
    out_ref[0:32, :] = (normed(mixed.astype(F32)) * (1.0 + scale) + shift).astype(BF16)
    mixed = (embedded_ref[...].astype(F32) + txt_mod_ref[2] * projected[32:]).astype(BF16)
    txt_ref[...] = mixed
    hidden = normed(mixed.astype(F32)) * (1.0 + txt_mod_ref[4]) + txt_mod_ref[3]
    out_ref[32 : 32 + POOL, :] = hidden.astype(BF16)


def one_hot(slot_ref, count):
    line = slot_ref[...]
    shape = (count, line.shape[1])
    return jnp.where(lax.broadcasted_iota(jnp.int32, shape, 0) == line, 1.0, 0.0)


def with_keep(values, keep):
    first = low_half(values.shape)
    return jnp.where(first, values, keep), jnp.where(first, keep, values)


def project(rows, weight_ref):
    both = jnp.concatenate([weight_ref[0], weight_ref[1]], -1)
    first = jnp.dot(rows, both, preferred_element_type=F32)
    return first, jnp.dot(rows, weight_ref[2], preferred_element_type=F32)


def txt_qkv_kernel(in0, in1, in2, in3, weight_ref, gain_ref, slot_ref, out_ref, held, rows_ref):
    part = in0.shape[0]
    for place, piece in enumerate((in0, in1, in2, in3)):
        rows_ref[place * part : (place + 1) * part, :] = piece[...]
    projected, values = project(rows_ref[...], weight_ref)
    held[:, 0:128] = head_norm(projected[:, 0:128], gain_ref[0:1, :]).astype(BF16)
    held[:, 128:256] = head_norm(projected[:, 128:256], gain_ref[1:2, :]).astype(BF16)
    held[:, 256:384] = values.astype(BF16)
    hot = one_hot(slot_ref, 512)
    keep = jnp.sum(hot, -1, keepdims=True)
    slots = jnp.dot(hot.astype(BF16), held[...], preferred_element_type=F32)
    val0, val1 = with_keep(slots[:, 256:384], keep)
    out_ref[:, 0:256] = slots[:, 0:256].astype(BF16)
    out_ref[:, 256:384] = val0.astype(BF16)
    out_ref[:, 384:512] = val1.astype(BF16)


def img_project_kernel(image_ref, mod_ref, weight_ref, out_ref, projected_ref):
    rows = image_ref[...].astype(F32)
    modded = (normed(rows) * (1.0 + mod_ref[0, 1, 0:1, :]) + mod_ref[0, 0, 0:1, :]).astype(BF16)
    out_ref[...] = modded
    projected, values = project(modded, weight_ref)
    projected_ref[:, 0:256] = projected
    projected_ref[:, 256:384] = values


def low_part_kernel(adapter_ref, tp_ref, mod_ref, down_ref, out_ref, wide):
    depth = down_ref.shape[1]
    wide[...] = jnp.zeros_like(wide)
    start = pl.multiple_of(tp_ref[0] * depth, 8)
    wide[pl.ds(start, depth), :] = down_ref[0].astype(F32)
    low = jnp.dot(mod_ref[...], wide[...].astype(BF16), preferred_element_type=F32)
    for block in range(8):
        out_ref[block] = low[block * 32 : (block + 1) * 32].astype(BF16)


def low_sum_kernel(part_ref, out_ref):
    total = part_ref[0].astype(F32)
    for block in range(1, 16):
        total = total + part_ref[block].astype(F32)
    for block in range(16):
        out_ref[block] = total.astype(BF16)


def img_adapt_kernel(adapter_ref, low_ref, projected_ref, up_ref, gain_ref, out_ref, lift):
    lift[...] = jnp.zeros_like(lift)
    for part in range(3):
        lift[part * 64 : (part + 1) * 64, part * 128 : (part + 1) * 128] = up_ref[0, part]
    projected = projected_ref[...] + ADAPTER_SCALE * jnp.dot(
        low_ref[...], lift[...], preferred_element_type=F32
    )
    out_ref[:, 0:128] = head_norm(projected[:, 0:128], gain_ref[0:1, :]).astype(BF16)
    out_ref[:, 128:256] = head_norm(projected[:, 128:256], gain_ref[1:2, :]).astype(BF16)
    val0, val1 = with_keep(projected[:, 256:384], 1.0)
    out_ref[:, 256:384] = val0.astype(BF16)
    out_ref[:, 384:512] = val1.astype(BF16)


def attend(queries, tokens):
    scaled = queries.astype(F32) * HEAD_DIM ** (-0.5)
    first = low_half(scaled.shape)
    keys = tokens[:, 128:256]
    results = []
    for head in range(2):
        own = jnp.where(first if head == 0 else ~first, scaled, 0.0).astype(BF16)
        scores = lax.dot_general(
            own, keys, (((1,), (1,)), ((), ())), preferred_element_type=F32
        )
        weights = jnp.exp(scores).astype(BF16)
        summed = jnp.dot(
            weights, tokens[:, 256 + head * 128 : 384 + head * 128], preferred_element_type=F32
        )
        results.append(summed / pltpu.roll(summed, HEAD_DIM, 1))
    return jnp.where(first, results[0], results[1]).astype(BF16)


def img_attend_kernel(
    places_ref, img_ref, slot_ref, weight_ref,
    out0, out1, out2, out3, token_ref, tokens, held, ranked,
):
    for own in range(2):
        tokens[own, 0:256, :] = img_ref[own * 256 : (own + 1) * 256, :]
        for source in range(8):
            start = 256 + source * 32
            tokens[own, start : start + 32, :] = slot_ref[source, own * 32 : (own + 1) * 32, :]
    token_ref[...] = tokens[...]
    for own in range(2):
        held[own * 256 : (own + 1) * 256, :] = attend(tokens[own, 0:256, 0:128], tokens[own])
    for place in range(16):
        start = pl.multiple_of(places_ref[place] * 32, 32)
        ranked[place * 32 : (place + 1) * 32, :] = held[pl.ds(start, 32), :]
    result = jnp.dot(ranked[...], weight_ref[...], preferred_element_type=F32)
    for place, out in enumerate((out0, out1, out2, out3)):
        out[...] = result[place * 128 : (place + 1) * 128].astype(BF16)


def txt_attend_kernel(token_ref, out_ref):
    for own in range(2):
        attended = attend(token_ref[own, 256:512, 0:128], token_ref[own])
        for source in range(8):
            start = source * 32
            out_ref[source, own * 32 : (own + 1) * 32, :] = attended[start : start + 32]


def txt_project_kernel(att_ref, slot_ref, weight_ref, out0, out1, out2, out3):
    hot = one_hot(slot_ref, 512).astype(BF16)
    rows = lax.dot_general(
        hot, att_ref[...], (((0,), (0,)), ((), ())), preferred_element_type=F32
    ).astype(BF16)
    part = out0.shape[0]
    result = jnp.dot(rows, weight_ref[...], preferred_element_type=F32)
    for place, out in enumerate((out0, out1, out2, out3)):
        out[...] = result[place * part : (place + 1) * part].astype(BF16)


def feed_kernel(in0, in1, in2, in3, win_ref, wout_ref, out0, out1, out2, out3, rows_ref):
    part = in0.shape[0]
    for place, piece in enumerate((in0, in1, in2, in3)):
        rows_ref[place * part : (place + 1) * part, :] = piece[...]
    hidden = lax.dot_general(
        rows_ref[...], win_ref[0], (((1,), (1,)), ((), ())), preferred_element_type=F32
    )
    hidden = jax.nn.gelu(hidden, approximate=True).astype(BF16)
    result = jnp.dot(hidden, wout_ref[0], preferred_element_type=F32)
    for place, out in enumerate((out0, out1, out2, out3)):
        out[...] = result[place * part : (place + 1) * part].astype(BF16)


def both_final_kernel(
    img_ref, txt_ref, in0, in1, in2, in3, img_mod_ref, txt_mod_ref, slot_ref, out_ref, placed_ref
):
    total = total_of((in0, in1, in2, in3))
    out_ref[...] = (img_ref[...].astype(F32) + img_mod_ref[5:6, :] * total[0:32]).astype(BF16)
    rows = txt_ref[...].astype(F32) + txt_mod_ref[5] * total[32:]
    hot = one_hot(slot_ref, 32).astype(BF16)
    placed_ref[...] = jnp.dot(hot, rows.astype(BF16), preferred_element_type=F32).astype(BF16)


def middle(parts, after=()):
    rows, width = parts[0].shape
    return run(
        middle_kernel,
        [like((rows // SIDE, width))] * SIDE,
        parts,
        scratch=[pltpu.VMEM((rows, width), F32)],
        after=after,
    )


def both_middle(img_parts, txt_parts):
    rows, width = txt_parts[0].shape
    return run(
        both_middle_kernel,
        [like((32 + POOL, width))] * SIDE,
        (*img_parts, *txt_parts),
        scratch=[pltpu.VMEM((rows, width), F32)],
    )


def join(parts, start, count, after=()):
    width = parts[0].shape[1]
    return run(
        functools.partial(join_kernel, start),
        like((SIDE * count, width)),
        parts,
        scratch=[pltpu.VMEM((SIDE * count, width), F32)],
        after=after,
    )


def feed(parts, weight_in, weight_out, stream):
    rows, width = parts[0].shape
    hidden = weight_in.shape[1]
    plain = pl.BlockSpec((rows, width), lambda i: (0, 0))
    return pl.pallas_call(
        feed_kernel,
        grid=(1,),
        out_shape=[like((rows, width))] * SIDE,
        in_specs=[plain] * SIDE
        + [
            pl.BlockSpec((1, hidden, width), lambda i: (stream, 0, 0)),
            pl.BlockSpec((1, hidden, width), lambda i: (stream, 0, 0)),
        ],
        out_specs=[plain] * SIDE,
        scratch_shapes=[pltpu.VMEM((rows * SIDE, width), BF16)],
        compiler_params=pltpu.CompilerParams(vmem_limit_bytes=40 << 20),
        cost_estimate=pl.CostEstimate(
            flops=rows * SIDE * width * hidden * 4,
            bytes_accessed=width * hidden * 4 + rows * width * 16,
            transcendentals=rows * SIDE * hidden,
        ),
    )(*parts, weight_in, weight_out)


def shards(
    image,
    prompt_encoder_rows,
    prompt_row_request,
    request_adapter,
    modulation,
    query_key_gain,
    prompt_embed_weight,
    image_query_key_value,
    prompt_query_key_value,
    image_out_weight,
    prompt_out_weight,
    feed_in_weight,
    feed_out_weight,
    adapter_down,
    adapter_up,
):
    grp = lax.axis_index("grp")
    tp = lax.axis_index("tp")
    chip, core = grp // 2, grp % 2
    z, y = tp // SIDE, tp % SIDE
    width = image.shape[1]

    steps = jnp.arange(16)
    far, near = steps // SIDE, steps % SIDE
    places = jnp.where(
        core == 0,
        ((z + far) % SIDE) * SIDE + (y + near) % SIDE,
        ((z + near) % SIDE) * SIDE + (y + far) % SIDE,
    ).astype(jnp.int32)
    gains = jnp.concatenate([query_key_gain, query_key_gain], -1)

    request = prompt_row_request[:, 0]
    outgoing = run(
        pack_kernel,
        like((16, 32, 256)),
        (prompt_encoder_rows, prompt_row_request.reshape(1, POOL)),
        scratch=[pltpu.VMEM((32, 256), F32), pltpu.VMEM((8, 256), jnp.int32)],
    )
    arrived = lax.all_to_all(outgoing, "tp", 0, 0, tiled=True)
    blocks = 4
    block = image.shape[0] // blocks
    img_mod, img_projected = pl.pallas_call(
        img_project_kernel,
        grid=(blocks,),
        out_shape=[like(image.shape), like((image.shape[0], 384), F32)],
        in_specs=[
            pl.BlockSpec((block, width), lambda i: (i, 0)),
            pl.BlockSpec((1, 6, 2, width), lambda i: (i // 2, 0, 0, 0)),
            pl.BlockSpec((3, width, 128), lambda i: (0, 0, 0)),
        ],
        out_specs=[
            pl.BlockSpec((block, width), lambda i: (i, 0)),
            pl.BlockSpec((block, 384), lambda i: (i, 0)),
        ],
        compiler_params=pltpu.CompilerParams(vmem_limit_bytes=32 << 20),
        cost_estimate=pl.CostEstimate(
            flops=512 * width * 384 * 2, bytes_accessed=7 << 20, transcendentals=0
        ),
    )(image, modulation.transpose(0, 2, 1, 3), image_query_key_value.transpose(1, 0, 2))
    half = image.shape[0] // 2
    low_part = pl.pallas_call(
        low_part_kernel,
        grid_spec=pltpu.PrefetchScalarGridSpec(
            num_scalar_prefetch=2,
            grid=(2,),
            in_specs=[
                pl.BlockSpec((half, width), lambda i, *_: (i, 0)),
                pl.BlockSpec((1, *adapter_down.shape[1:]), lambda i, ids, _: (ids[i], 0, 0)),
            ],
            out_specs=pl.BlockSpec((8, 32, 192), lambda i, *_: (i, 0, 0)),
            scratch_shapes=[pltpu.VMEM((width, 192), F32)],
        ),
        out_shape=like((16, 32, 192)),
        compiler_params=pltpu.CompilerParams(vmem_limit_bytes=32 << 20),
        cost_estimate=pl.CostEstimate(
            flops=512 * width * 192 * 2, bytes_accessed=3 << 20, transcendentals=0
        ),
    )(request_adapter, tp.reshape(1).astype(jnp.int32), img_mod, adapter_down)
    low_sum = run(
        low_sum_kernel,
        like((16, 32, 192)),
        (lax.all_to_all(low_part, "tp", 0, 0, tiled=True),),
    )
    low = lax.all_to_all(low_sum, "tp", 0, 0, tiled=True).reshape(2 * half, 192)

    mod_all = run(
        repeat_mod_kernel, like((8, 2, 8, width), F32), (modulation.transpose(0, 2, 1, 3),)
    )
    mod_all = lax.all_to_all(mod_all, "grp", 0, 0, tiled=True).reshape(16, 8, width)
    row_mod = run(row_mod_kernel, like((6, POOL, width), F32), (request, mod_all), smem=1)

    *embed_parts, labels = run(
        embed_kernel,
        [like((SIDE * POOL, width))] * SIDE + [like((16, 256), F32)],
        (places, arrived, prompt_embed_weight),
        smem=1,
        scratch=[pltpu.VMEM((SIDE * POOL, 256), F32)],
        flops=320 * 256 * width * 2,
        after=(img_projected,),
    )
    embed_sums = exchange(middle(exchange(embed_parts, 1), after=(low_part,)), 0)
    embedded, txt_mod = run(
        embed_norm_kernel,
        [like((POOL, width))] * 2,
        (*embed_sums, row_mod),
        after=(low_sum,),
    )
    txt_mods = spread(join(spread(txt_mod, 0), 0, POOL), 1)

    target = labels[:, :POOL].astype(jnp.int32)
    slots_all = target // 4 * 64 + target // 2 % 2 * 32 + target % 2
    slots_all = (slots_all + 2 * steps[:, None]).reshape(1, 16 * POOL).astype(jnp.int32)
    earlier = (request[:, None] == request[None, :]) & (
        jnp.arange(POOL)[None, :] < jnp.arange(POOL)[:, None]
    )
    ranked = jnp.sum(earlier.astype(jnp.int32), 1)
    slots_own = (request * CAP + ranked).reshape(1, POOL).astype(jnp.int32)

    img_parts = pl.pallas_call(
        img_adapt_kernel,
        grid_spec=pltpu.PrefetchScalarGridSpec(
            num_scalar_prefetch=1,
            grid=(2,),
            in_specs=[
                pl.BlockSpec((half, 192), lambda i, _: (i, 0)),
                pl.BlockSpec((half, 384), lambda i, _: (i, 0)),
                pl.BlockSpec((1, 3, 64, 128), lambda i, ids: (ids[i], 0, 0, 0)),
                pl.BlockSpec((2, 128), lambda i, _: (0, 0)),
            ],
            out_specs=pl.BlockSpec((half, 512), lambda i, _: (i, 0)),
            scratch_shapes=[pltpu.VMEM((192, 384), BF16)],
        ),
        out_shape=like((image.shape[0], 512)),
        cost_estimate=pl.CostEstimate(
            flops=512 * 384 * 192 * 2, bytes_accessed=2 << 20, transcendentals=0
        ),
    )(request_adapter, low, img_projected, adapter_up, gains[0])

    slot_parts = run(
        txt_qkv_kernel,
        like((512, 512)),
        (*txt_mods, prompt_query_key_value.transpose(1, 0, 2), gains[1], slots_all),
        scratch=[pltpu.VMEM((16 * POOL, 384), BF16), pltpu.VMEM((16 * POOL, width), BF16)],
        flops=320 * width * 384 * 2,
        after=(img_parts,),
    )
    slot_parts = lax.all_to_all(slot_parts.reshape(8, 64, 512), "grp", 0, 0, tiled=True)

    *img_terms, tokens = run(
        img_attend_kernel,
        [like((128, width))] * SIDE + [like((2, 512, 512))],
        (places, img_parts, slot_parts, image_out_weight),
        smem=1,
        scratch=[
            pltpu.VMEM((2, 512, 512), BF16),
            pltpu.VMEM((512, 128), BF16),
            pltpu.VMEM((512, 128), BF16),
        ],
        flops=1 << 30,
    )
    img_sums = exchange(img_terms, 1)
    att_parts = run(txt_attend_kernel, like((8, 64, 128)), (tokens,), flops=1 << 29)
    att_parts = lax.all_to_all(att_parts, "grp", 0, 0, tiled=True).reshape(512, 128)
    txt_terms = run(
        txt_project_kernel,
        [like((SIDE * POOL, width))] * SIDE,
        (att_parts, slots_all, prompt_out_weight),
        flops=320 * 128 * width * 2,
        after=(img_sums[1], img_sums[3]),
    )
    txt_sums = exchange(txt_terms, 1)

    own_mod = lax.dynamic_index_in_dim(modulation[:, 0], tp // 8, 0, keepdims=False)
    own_image = lax.dynamic_slice_in_dim(image, tp * 32, 32, 0)
    sums = exchange(both_middle(img_sums, txt_sums), 0)
    mixed_img, mixed_txt, norm_rows = run(
        both_norm_kernel,
        [like((32, width)), like((POOL, width)), like((32 + POOL, width))],
        (own_image, embedded, *sums, own_mod, row_mod),
    )
    near_rows = spread(norm_rows, 0)
    img_rows = spread(join(near_rows, 0, 32), 1)
    txt_rows = spread(join(near_rows, 32, POOL, after=(img_rows[1], img_rows[3])), 1)
    weight_in = feed_in_weight.transpose(0, 2, 1)
    img_terms = feed(img_rows, weight_in, feed_out_weight, 0)
    txt_terms = feed(txt_rows, weight_in, feed_out_weight, 1)
    sums = exchange(both_middle(exchange(img_terms, 1), exchange(txt_terms, 1)), 0)
    image_out, placed = run(
        both_final_kernel,
        [like((32, width))] * 2,
        (mixed_img, mixed_txt, *sums, own_mod, row_mod, slots_own),
    )

    placed = lax.all_to_all(placed.reshape(8, 4, width), "grp", 0, 0, tiled=True)
    prompt_out = placed.reshape(32, width)

    return (image_out, prompt_out)


def solution(mesh):
    placed = (
        P("grp", None),
        P(("grp", "tp"), None),
        P(("grp", "tp"), None),
        P("grp"),
        P("grp", None, None, None),
        P(),
        P("tp", None),
        P(None, None, "tp"),
        P(None, None, "tp"),
        P("tp", None),
        P("tp", None),
        P(None, None, "tp"),
        P(None, "tp", None),
        P(None, "tp", None),
        P(None, None, None, "tp"),
    )
    return jax.shard_map(
        shards,
        mesh=mesh,
        in_specs=placed,
        out_specs=(P(("grp", "tp"), None), P(("grp", "tp"), None)),
        check_vma=False,
    )
```

profile of v0, /device:TPU:1, one launch (start us, length us, event | category | flops | bytes accessed | tf_op | source)
XLA Modules:
  0.0 301.4 jit_solution(16018775237142609910)
XLA Ops:
  0.6 1.7 copy-done.1
  2.3 1.5 copy-done.9
  4.8 3.5 %shard_map.159 = (bf16[512,2432]{1,0:T(8,128)(2,1)S(1)}, f32[512,384]{1,0:T(8,128)S(1)}) custom-call(bf16[512,2432]{1,0:T(8,128)(2,1)S(1)} %copy-done.1, f32[2,6,2,2432]{3,2,1,0:T(2,128)S(1)} %bitcast.29, bf16[3,2432,128]{2,1,0:T(8,128)(2,1)S(1)} %bitcast.27), custom_call_target="tpu_custom_call" | custom-call | flops 956301312 | bytes 7340032 | tf_op jit(solution)/shard_map/pallas_call | solution.py:446
  8.3 2.6 shard_map.161.refs_4_
  11.0 8.6 %all-to-all-start.2 = ((bf16[16,32,192]{2,1,0:T(8,128)(2,1)}), bf16[16,32,192]{2,1,0:T(8,128)(2,1)S(1)}, u32[]{:S(2)}, u32[]{:S(2)}) async-start(bf16[16,32,192]{2,1,0:T(8,128)(2,1)} %shard_map.161.refs_4_), calls=%async_computation.2 | async-start | bytes 524288 | tf_op jit(solution)/shard_map/all_to_all | solution.py:486
  20.5 6.6 %all-to-all-done.2.refs_0_ = bf16[16,32,192]{2,1,0:T(8,128)(2,1)S(1)} async-done(((bf16[16,32,192]{2,1,0:T(8,128)(2,1)}), bf16[16,32,192]{2,1,0:T(8,128)(2,1)S(1)}, u32[]{:S(2)}, u32[]{:S(2)}) %all-to-all-start.2) | async-done | bytes 196640 | tf_op jit(solution)/shard_map/all_to_all | solution.py:486
  27.1 3.5 %all-to-all-start = ((bf16[16,32,256]{2,1,0:T(8,128)(2,1)}), bf16[16,32,256]{2,1,0:T(8,128)(2,1)S(1)}, u32[]{:S(2)}, u32[]{:S(2)}) async-start(bf16[16,32,256]{2,1,0:T(8,128)(2,1)} %shard_map.158), calls=%async_computation | async-start | bytes 524288 | tf_op jit(solution)/shard_map/all_to_all | solution.py:443
  30.7 1.3 shard_map.163
  32.0 6.2 %all-to-all-done.refs_1_ = bf16[16,32,256]{2,1,0:T(8,128)(2,1)S(1)} async-done(((bf16[16,32,256]{2,1,0:T(8,128)(2,1)}), bf16[16,32,256]{2,1,0:T(8,128)(2,1)S(1)}, u32[]{:S(2)}, u32[]{:S(2)}) %all-to-all-start) | async-done | bytes 262176 | tf_op jit(solution)/shard_map/all_to_all | solution.py:443
  38.2 7.5 %all-to-all-start.1 = ((f32[8,2,8,2432]{3,2,1,0:T(8,128)}), f32[8,2,8,2432]{3,2,1,0:T(8,128)S(1)}, u32[]{:S(2)}, u32[]{:S(2)}) async-start(f32[8,2,8,2432]{3,2,1,0:T(8,128)} %shard_map.163), calls=%async_computation.1 | async-start | bytes 2490368 | tf_op jit(solution)/shard_map/all_to_all | solution.py:493
  45.8 1.3 copy-done.13
  47.0 1.4 shard_map.160
  49.0 1.6 collective-permute-start.1
  50.6 4.8 %collective-permute-done.refs_1_ = bf16[80,2432]{1,0:T(8,128)(2,1)S(1)} collective-permute-done((bf16[80,2432]{1,0:T(8,128)(2,1)S(1)}, bf16[80,2432]{1,0:T(8,128)(2,1)S(1)}, u32[]{:S(2)}, u32[]{:S(2)}) %collective-permute-start) | collective-permute-done | bytes 389152 | tf_op jit(solution)/shard_map/ppermute | solution.py:30
  55.4 2.0 collective-permute-done.1.refs_2_
  57.4 4.1 %collective-permute-done.2.refs_3_ = bf16[80,2432]{1,0:T(8,128)(2,1)S(1)} collective-permute-done((bf16[80,2432]{1,0:T(8,128)(2,1)S(1)}, bf16[80,2432]{1,0:T(8,128)(2,1)S(1)}, u32[]{:S(2)}, u32[]{:S(2)}) %collective-permute-start.2) | collective-permute-done | bytes 389152 | tf_op jit(solution)/shard_map/ppermute | solution.py:30
  61.5 1.0 shard_map.162
  63.3 1.2 collective-permute-start.4
  66.4 2.4 collective-permute-done.4.refs_2_
  68.9 1.5 collective-permute-done.5.refs_3_
  70.4 1.3 shard_map.166
  72.3 1.5 collective-permute-start.7
  73.8 1.8 collective-permute-start.6
  75.6 2.8 collective-permute-done.8.refs_3_
  80.1 1.2 collective-permute-start.10
  81.3 1.9 collective-permute-start.9
  83.9 5.4 %all-to-all-start.3 = ((bf16[16,32,192]{2,1,0:T(8,128)(2,1)}), bf16[16,32,192]{2,1,0:T(8,128)(2,1)}, u32[]{:S(2)}, u32[]{:S(2)}) async-start(bf16[16,32,192]{2,1,0:T(8,128)(2,1)} %shard_map.165.refs_5_), calls=%async_computation.3 | async-start | bytes 524288 | tf_op jit(solution)/shard_map/all_to_all | solution.py:488
  89.5 7.8 %all-to-all-done.3 = bf16[16,32,192]{2,1,0:T(8,128)(2,1)} async-done(((bf16[16,32,192]{2,1,0:T(8,128)(2,1)}), bf16[16,32,192]{2,1,0:T(8,128)(2,1)}, u32[]{:S(2)}, u32[]{:S(2)}) %all-to-all-start.3) | async-done | bytes 196640 | tf_op jit(solution)/shard_map/all_to_all | solution.py:488
  97.3 3.2 %shard_map.167.refs_7_.refs_1_ = bf16[512,512]{1,0:T(8,128)(2,1)} custom-call(s32[2]{0:T(128)} %adapter_ref.3, bf16[512,192]{1,0:T(8,128)(2,1)} %bitcast.6.low_ref, f32[512,384]{1,0:T(8,128)} %copy-done, bf16[32,3,64,128]{3,2,1,0:T(8,128)(2,1)} %up_ref.1, f32[2,128]{1,0:T(2,128)} %get-tuple-element.89.gain_ref), custom_call_target="tpu_custom_call" | custom-call | flops 75497472 | bytes 2097152 | tf_op jit(solution)/shard_map/pallas_call | solution.py:523
  101.6 3.1 %shard_map.169 = bf16[512,512]{1,0:T(8,128)(2,1)S(1)} custom-call(bf16[80,2432]{1,0:T(8,128)(2,1)} %shard_map.168.refs_0_, bf16[80,2432]{1,0:T(8,128)(2,1)} %collective-permute-done.9.refs_1_, bf16[80,2432]{1,0:T(8,128)(2,1)} %collective-permute-done.10.refs_2_, bf16[80,2432]{1,0:T(8,128)(2,1)} %collective-permute-done.11.refs_3_, ...), custom_call_target="tpu_custom_call" | custom-call | flops 597688320 | bytes 3950848 | tf_op jit(solution)/shard_map/pallas_call | solution.py:64
  104.7 19.4 %all_to_all.35.refs_2_ = bf16[8,64,512]{2,1,0:T(8,128)(2,1)S(1)} all-to-all(bf16[8,64,512]{2,1,0:T(8,128)(2,1)S(1)} %bitcast.26), channel_id=1, replica_groups=mesh['grp'=8,'tp'=16] {'grp'}, dimensions={0} | all-to-all | bytes 1048576 | tf_op jit(solution)/shard_map/all_to_all | solution.py:551
  124.1 3.3 %shard_map.170 = (bf16[128,2432]{1,0:T(8,128)(2,1)S(1)}, bf16[128,2432]{1,0:T(8,128)(2,1)S(1)}, bf16[128,2432]{1,0:T(8,128)(2,1)}, bf16[128,2432]{1,0:T(8,128)(2,1)S(1)}, bf16[2,512,512]{2,1,0:T(8,128)(2,1)S(1)}) custom-call(s32[16]{0:T(128)S(1)} %broadcast_select_fusion.refs_0_, bf16[512,512]{1,0:T(8,128)(2,1)S(1)} %copy-done.8, ...), custom_call_target="tpu_custom_call" | custom-call | flops 1073741824 | bytes 5210176 | tf_op jit(solution)/shard_map/pallas_call | solution.py:64
  130.4 1.1 shard_map.171
  131.5 9.8 %all_to_all.36 = bf16[8,64,128]{2,1,0:T(8,128)(2,1)S(1)} all-to-all(bf16[8,64,128]{2,1,0:T(8,128)(2,1)S(1)} %shard_map.171), channel_id=1, replica_groups=mesh['grp'=8,'tp'=16] {'grp'}, dimensions={0} | all-to-all | bytes 262144 | tf_op jit(solution)/shard_map/all_to_all | solution.py:567
  141.4 4.7 %collective-permute-done.14.refs_4_.refs_3_ = bf16[128,2432]{1,0:T(8,128)(2,1)S(1)} collective-permute-done((bf16[128,2432]{1,0:T(8,128)(2,1)S(1)}, bf16[128,2432]{1,0:T(8,128)(2,1)S(1)}, u32[]{:S(2)}, u32[]{:S(2)}) %collective-permute-start.14) | collective-permute-done | bytes 622624 | tf_op jit(solution)/shard_map/ppermute | solution.py:30
  146.1 1.9 shard_map.172
  150.0 1.1 collective-permute-start.17
  151.2 5.6 %collective-permute-done.15.refs_5_ = bf16[80,2432]{1,0:T(8,128)(2,1)} collective-permute-done((bf16[80,2432]{1,0:T(8,128)(2,1)}, bf16[80,2432]{1,0:T(8,128)(2,1)}, u32[]{:S(2)}, u32[]{:S(2)}) %collective-permute-start.15) | collective-permute-done | bytes 389152 | tf_op jit(solution)/shard_map/ppermute | solution.py:30
  156.8 1.6 collective-permute-done.16.refs_6_
  158.3 4.1 %collective-permute-done.17.refs_7_ = bf16[80,2432]{1,0:T(8,128)(2,1)} collective-permute-done((bf16[80,2432]{1,0:T(8,128)(2,1)}, bf16[80,2432]{1,0:T(8,128)(2,1)}, u32[]{:S(2)}, u32[]{:S(2)}) %collective-permute-start.17) | collective-permute-done | bytes 389152 | tf_op jit(solution)/shard_map/ppermute | solution.py:30
  162.5 1.1 copy-done.4
  163.5 1.1 copy-done.6
  164.6 1.1 copy-done.16
  166.7 2.5 shard_map.173
  169.2 2.4 collective-permute-start.18
  173.2 4.7 %collective-permute-done.18.refs_3_ = bf16[52,2432]{1,0:T(8,128)(2,1)S(1)} collective-permute-done((bf16[52,2432]{1,0:T(8,128)(2,1)S(1)}, bf16[52,2432]{1,0:T(8,128)(2,1)S(1)}, u32[]{:S(2)}, u32[]{:S(2)}) %collective-permute-start.18) | collective-permute-done | bytes 252960 | tf_op jit(solution)/shard_map/ppermute | solution.py:30
  178.6 2.8 collective-permute-done.20.refs_5_
  182.0 1.8 collective-permute-start.22
  184.7 7.1 %collective-permute-done.23.refs_3_ = bf16[52,2432]{1,0:T(8,128)(2,1)S(1)} collective-permute-done((bf16[52,2432]{1,0:T(8,128)(2,1)S(1)}, bf16[52,2432]{1,0:T(8,128)(2,1)S(1)}, u32[]{:S(2)}, u32[]{:S(2)}) %collective-permute-start.23) | collective-permute-done | bytes 252960 | tf_op jit(solution)/shard_map/ppermute | solution.py:30
  192.5 2.7 collective-permute-start.24
  195.2 14.7 %collective-permute-done.26.in3.refs_5_ = bf16[128,2432]{1,0:T(8,128)(2,1)S(1)} collective-permute-done((bf16[128,2432]{1,0:T(8,128)(2,1)S(1)}, bf16[128,2432]{1,0:T(8,128)(2,1)S(1)}, u32[]{:S(2)}, u32[]{:S(2)}) %collective-permute-start.26) | collective-permute-done | bytes 622624 | tf_op jit(solution)/shard_map/ppermute | solution.py:30
  210.3 6.8 %shard_map.176 = (bf16[128,2432]{1,0:T(8,128)(2,1)S(1)}, bf16[128,2432]{1,0:T(8,128)(2,1)S(1)}, bf16[128,2432]{1,0:T(8,128)(2,1)S(1)}, bf16[128,2432]{1,0:T(8,128)(2,1)S(1)}) custom-call(bf16[128,2432]{1,0:T(8,128)(2,1)S(1)} %shard_map.175.in0, bf16[128,2432]{1,0:T(8,128)(2,1)S(1)} %collective-permute-done.24.in1.refs_4_, ...), custom_call_target="tpu_custom_call" | custom-call | flops 3028287488 | bytes 10895360 | tf_op jit(solution)/shard_map/pallas_call | solution.py:384
  217.1 2.9 collective-permute-start.27
  221.0 2.0 collective-permute-start.28
  223.9 4.3 %collective-permute-done.31.in2 = bf16[80,2432]{1,0:T(8,128)(2,1)S(1)} collective-permute-done((bf16[80,2432]{1,0:T(8,128)(2,1)S(1)}, bf16[80,2432]{1,0:T(8,128)(2,1)S(1)}, u32[]{:S(2)}, u32[]{:S(2)}) %collective-permute-start.31) | collective-permute-done | bytes 389152 | tf_op jit(solution)/shard_map/ppermute | solution.py:30
  228.2 14.0 %collective-permute-done.30.in1 = bf16[80,2432]{1,0:T(8,128)(2,1)S(1)} collective-permute-done((bf16[80,2432]{1,0:T(8,128)(2,1)S(1)}, bf16[80,2432]{1,0:T(8,128)(2,1)S(1)}, u32[]{:S(2)}, u32[]{:S(2)}) %collective-permute-start.30) | collective-permute-done | bytes 389152 | tf_op jit(solution)/shard_map/ppermute | solution.py:30
  242.2 5.0 %shard_map.178 = (bf16[80,2432]{1,0:T(8,128)(2,1)S(1)}, bf16[80,2432]{1,0:T(8,128)(2,1)S(1)}, bf16[80,2432]{1,0:T(8,128)(2,1)S(1)}, bf16[80,2432]{1,0:T(8,128)(2,1)S(1)}) custom-call(bf16[80,2432]{1,0:T(8,128)(2,1)S(1)} %shard_map.177.in0, bf16[80,2432]{1,0:T(8,128)(2,1)S(1)} %collective-permute-done.30.in1, ...), custom_call_target="tpu_custom_call" | custom-call | flops 1892679680 | bytes 9027584 | tf_op jit(solution)/shard_map/pallas_call | solution.py:384
  247.3 3.5 %collective-permute-start.33 = (bf16[80,2432]{1,0:T(8,128)(2,1)S(1)}, bf16[80,2432]{1,0:T(8,128)(2,1)S(1)}, u32[]{:S(2)}, u32[]{:S(2)}) collective-permute-start(bf16[80,2432]{1,0:T(8,128)(2,1)S(1)} %get-tuple-element.79), channel_id=1, source_target_pairs={{0,12},{1,13},{2,14},{3,15},{4,0},{5,1},{6,2},{7,3},{8,4},{9,5},{1... | collective-permute-start | bytes 1167368 | tf_op jit(solution)/shard_map/ppermute | solution.py:30
  251.4 8.2 %collective-permute-done.33.refs_5_ = bf16[80,2432]{1,0:T(8,128)(2,1)S(1)} collective-permute-done((bf16[80,2432]{1,0:T(8,128)(2,1)S(1)}, bf16[80,2432]{1,0:T(8,128)(2,1)S(1)}, u32[]{:S(2)}, u32[]{:S(2)}) %collective-permute-start.33) | collective-permute-done | bytes 389152 | tf_op jit(solution)/shard_map/ppermute | solution.py:30
  259.6 3.1 %collective-permute-done.35.refs_7_ = bf16[80,2432]{1,0:T(8,128)(2,1)S(1)} collective-permute-done((bf16[80,2432]{1,0:T(8,128)(2,1)S(1)}, bf16[80,2432]{1,0:T(8,128)(2,1)S(1)}, u32[]{:S(2)}, u32[]{:S(2)}) %collective-permute-start.35) | collective-permute-done | bytes 389152 | tf_op jit(solution)/shard_map/ppermute | solution.py:30
  263.7 2.1 collective-permute-start.36
  266.6 8.5 %collective-permute-done.36.refs_3_ = bf16[52,2432]{1,0:T(8,128)(2,1)S(1)} collective-permute-done((bf16[52,2432]{1,0:T(8,128)(2,1)S(1)}, bf16[52,2432]{1,0:T(8,128)(2,1)S(1)}, u32[]{:S(2)}, u32[]{:S(2)}) %collective-permute-start.36) | collective-permute-done | bytes 252960 | tf_op jit(solution)/shard_map/ppermute | solution.py:30
  275.6 2.9 collective-permute-done.38.refs_5_
  279.6 21.1 %all_to_all.37 = bf16[8,4,2432]{2,1,0:T(4,128)(2,1)S(1)} all-to-all(bf16[8,4,2432]{2,1,0:T(4,128)(2,1)S(1)} %reshape.64), channel_id=1, replica_groups=mesh['grp'=8,'tp'=16] {'grp'}, dimensions={0} | all-to-all | bytes 311296 | tf_op jit(solution)/shard_map/all_to_all | solution.py:598
  (118 shorter events, 26.7 us)
Async XLA Ops:
  0.6 1.7 copy-start.1
  2.3 1.5 copy-start.9
  4.8 3.5 %copy-start.2 = (bf16[32,152,192]{2,1,0:T(8,128)(2,1)S(1)}, bf16[32,152,192]{2,1,0:T(8,128)(2,1)}, u32[]{:S(2)}) copy-start(bf16[32,152,192]{2,1,0:T(8,128)(2,1)} %down_ref.1) | copy-start | bytes 5603332
  4.8 3.5 %copy-start.22 = (s32[2]{0:T(128)S(1)}, s32[2]{0:T(128)}, u32[]{:S(2)}) copy-start(s32[2]{0:T(128)} %adapter_ref.3) | copy-start | bytes 28
  8.3 37.4 %copy-start = (f32[512,384]{1,0:T(8,128)}, f32[512,384]{1,0:T(8,128)S(1)}, u32[]{:S(2)}) copy-start(f32[512,384]{1,0:T(8,128)S(1)} %get-tuple-element.45.refs_3_.projected_ref) | copy-start | bytes 2359300
  8.3 11.3 %copy-start.19 = (bf16[20,4096]{1,0:T(8,128)(2,1)S(1)}, bf16[20,4096]{1,0:T(8,128)(2,1)}, u32[]{:S(2)}) copy-start(bf16[20,4096]{1,0:T(8,128)(2,1)} %refs_0_.1) | copy-start | bytes 491524
  8.3 11.3 %copy-start.23 = (s32[20,1]{0,1:T(1,128)S(1)}, s32[20,1]{0,1:T(1,128)}, u32[]{:S(2)}) copy-start(s32[20,1]{0,1:T(1,128)} %param.17) | copy-start | bytes 244
  8.3 22.3 %copy-start.12 = (f32[2,2,6,2432]{3,1,2,0:T(2,128)S(1)}, f32[2,2,6,2432]{3,1,2,0:T(2,128)}, u32[]{:S(2)}) copy-start(f32[2,2,6,2432]{3,1,2,0:T(2,128)} %param.19) | copy-start | bytes 700420
  11.0 16.1 %all-to-all-start.2 = ((bf16[16,32,192]{2,1,0:T(8,128)(2,1)}), bf16[16,32,192]{2,1,0:T(8,128)(2,1)S(1)}, u32[]{:S(2)}, u32[]{:S(2)}) async-start(bf16[16,32,192]{2,1,0:T(8,128)(2,1)} %shard_map.161.refs_4_), calls=%async_computation.2 | async-start | bytes 524288 | tf_op jit(solution)/shard_map/all_to_all | solution.py:486
  27.1 11.0 %all-to-all-start = ((bf16[16,32,256]{2,1,0:T(8,128)(2,1)}), bf16[16,32,256]{2,1,0:T(8,128)(2,1)S(1)}, u32[]{:S(2)}, u32[]{:S(2)}) async-start(bf16[16,32,256]{2,1,0:T(8,128)(2,1)} %shard_map.158), calls=%async_computation | async-start | bytes 524288 | tf_op jit(solution)/shard_map/all_to_all | solution.py:443
  38.2 27.2 %all-to-all-start.1 = ((f32[8,2,8,2432]{3,2,1,0:T(8,128)}), f32[8,2,8,2432]{3,2,1,0:T(8,128)S(1)}, u32[]{:S(2)}, u32[]{:S(2)}) async-start(f32[8,2,8,2432]{3,2,1,0:T(8,128)} %shard_map.163), calls=%async_computation.1 | async-start | bytes 2490368 | tf_op jit(solution)/shard_map/all_to_all | solution.py:493
  45.7 1.3 copy-start.13
  48.5 6.9 %collective-permute-start = (bf16[80,2432]{1,0:T(8,128)(2,1)S(1)}, bf16[80,2432]{1,0:T(8,128)(2,1)S(1)}, u32[]{:S(2)}, u32[]{:S(2)}) collective-permute-start(bf16[80,2432]{1,0:T(8,128)(2,1)S(1)} %get-tuple-element.47), channel_id=1, source_target_pairs={{0,12},{1,13},{2,14},{3,15},{4,0},{5,1},{6,2},{7,3},{8,4},{9,5},{1... | collective-permute-start | bytes 1167368 | tf_op jit(solution)/shard_map/ppermute | solution.py:30
  49.0 8.4 %collective-permute-start.1 = (bf16[80,2432]{1,0:T(8,128)(2,1)S(1)}, bf16[80,2432]{1,0:T(8,128)(2,1)S(1)}, u32[]{:S(2)}, u32[]{:S(2)}) collective-permute-start(bf16[80,2432]{1,0:T(8,128)(2,1)S(1)} %get-tuple-element.48), channel_id=1, source_target_pairs={{0,8},{1,9},{2,10},{3,11},{4,12},{5,13},{6,14},{7,15},{8,0},{9,1},... | collective-permute-start | bytes 1167368 | tf_op jit(solution)/shard_map/ppermute | solution.py:30
  50.6 10.9 %collective-permute-start.2 = (bf16[80,2432]{1,0:T(8,128)(2,1)S(1)}, bf16[80,2432]{1,0:T(8,128)(2,1)S(1)}, u32[]{:S(2)}, u32[]{:S(2)}) collective-permute-start(bf16[80,2432]{1,0:T(8,128)(2,1)S(1)} %get-tuple-element.49), channel_id=1, source_target_pairs={{0,4},{1,5},{2,6},{3,7},{4,8},{5,9},{6,10},{7,11},{8,12},{9,13},{1... | collective-permute-start | bytes 1167368 | tf_op jit(solution)/shard_map/ppermute | solution.py:30
  62.6 3.9 %collective-permute-start.3 = (bf16[20,2432]{1,0:T(8,128)(2,1)}, bf16[20,2432]{1,0:T(8,128)(2,1)S(1)}, u32[]{:S(2)}, u32[]{:S(2)}) collective-permute-start(bf16[20,2432]{1,0:T(8,128)(2,1)} %get-tuple-element.52), channel_id=1, source_target_pairs={{0,3},{1,0},{2,1},{3,2},{4,7},{5,4},{6,5},{7,6},{8,11},{9,8},{10,9... | collective-permute-start | bytes 291848 | tf_op jit(solution)/shard_map/ppermute | solution.py:30
  63.3 5.5 %collective-permute-start.4 = (bf16[20,2432]{1,0:T(8,128)(2,1)}, bf16[20,2432]{1,0:T(8,128)(2,1)}, u32[]{:S(2)}, u32[]{:S(2)}) collective-permute-start(bf16[20,2432]{1,0:T(8,128)(2,1)} %get-tuple-element.53), channel_id=1, source_target_pairs={{0,2},{1,3},{2,0},{3,1},{4,6},{5,7},{6,4},{7,5},{8,10},{9,11},{10,... | collective-permute-start | bytes 291848 | tf_op jit(solution)/shard_map/ppermute | solution.py:30
  64.6 5.8 %collective-permute-start.5 = (bf16[20,2432]{1,0:T(8,128)(2,1)}, bf16[20,2432]{1,0:T(8,128)(2,1)}, u32[]{:S(2)}, u32[]{:S(2)}) collective-permute-start(bf16[20,2432]{1,0:T(8,128)(2,1)} %get-tuple-element.54), channel_id=1, source_target_pairs={{0,1},{1,2},{2,3},{3,0},{4,5},{5,6},{6,7},{7,4},{8,9},{9,10},{10,1... | collective-permute-start | bytes 291848 | tf_op jit(solution)/shard_map/ppermute | solution.py:30
  66.3 17.0 %copy-start.25 = (f32[2,2,64]{2,1,0:T(2,128)S(1)}, f32[2,2,64]{2,1,0:T(2,128)}, u32[]{:S(2)}) copy-start(f32[2,2,64]{2,1,0:T(2,128)} %param.20) | copy-start | bytes 3076
  72.3 6.1 %collective-permute-start.8 = (bf16[20,2432]{1,0:T(8,128)(2,1)S(1)}, bf16[20,2432]{1,0:T(8,128)(2,1)S(1)}, u32[]{:S(2)}, u32[]{:S(2)}) collective-permute-start(bf16[20,2432]{1,0:T(8,128)(2,1)S(1)} %get-tuple-element.56.refs_0_), channel_id=1, source_target_pairs={{0,1},{1,2},{2,3},{3,0},{4,5},{5,6},{6,7},{7,4},{8,9},{9,10},{10,1... | collective-permute-start | bytes 291848 | tf_op jit(solution)/shard_map/ppermute | solution.py:30
  72.3 6.1 %collective-permute-start.7 = (bf16[20,2432]{1,0:T(8,128)(2,1)S(1)}, bf16[20,2432]{1,0:T(8,128)(2,1)S(1)}, u32[]{:S(2)}, u32[]{:S(2)}) collective-permute-start(bf16[20,2432]{1,0:T(8,128)(2,1)S(1)} %get-tuple-element.56.refs_0_), channel_id=1, source_target_pairs={{0,2},{1,3},{2,0},{3,1},{4,6},{5,7},{6,4},{7,5},{8,10},{9,11},{10,... | collective-permute-start | bytes 291848 | tf_op jit(solution)/shard_map/ppermute | solution.py:30
  73.8 5.5 %collective-permute-start.6 = (bf16[20,2432]{1,0:T(8,128)(2,1)S(1)}, bf16[20,2432]{1,0:T(8,128)(2,1)S(1)}, u32[]{:S(2)}, u32[]{:S(2)}) collective-permute-start(bf16[20,2432]{1,0:T(8,128)(2,1)S(1)} %get-tuple-element.56.refs_0_), channel_id=1, source_target_pairs={{0,3},{1,0},{2,1},{3,2},{4,7},{5,4},{6,5},{7,6},{8,11},{9,8},{10,9... | collective-permute-start | bytes 291848 | tf_op jit(solution)/shard_map/ppermute | solution.py:30
  80.1 20.4 %copy-start.10 = (bf16[2432,3,128]{2,0,1:T(8,128)(2,1)S(1)}, bf16[2432,3,128]{2,0,1:T(8,128)(2,1)}, u32[]{:S(2)}) copy-start(bf16[2432,3,128]{2,0,1:T(8,128)(2,1)} %param.23) | copy-start | bytes 5603332
  80.1 20.4 %collective-permute-start.11 = (bf16[80,2432]{1,0:T(8,128)(2,1)}, bf16[80,2432]{1,0:T(8,128)(2,1)}, u32[]{:S(2)}, u32[]{:S(2)}) collective-permute-start(bf16[80,2432]{1,0:T(8,128)(2,1)} %shard_map.168.refs_0_), channel_id=1, source_target_pairs={{0,4},{1,5},{2,6},{3,7},{4,8},{5,9},{6,10},{7,11},{8,12},{9,13},{1... | collective-permute-start | bytes 1167368 | tf_op jit(solution)/shard_map/ppermute | solution.py:30
  80.1 20.4 %collective-permute-start.10 = (bf16[80,2432]{1,0:T(8,128)(2,1)}, bf16[80,2432]{1,0:T(8,128)(2,1)}, u32[]{:S(2)}, u32[]{:S(2)}) collective-permute-start(bf16[80,2432]{1,0:T(8,128)(2,1)} %shard_map.168.refs_0_), channel_id=1, source_target_pairs={{0,8},{1,9},{2,10},{3,11},{4,12},{5,13},{6,14},{7,15},{8,0},{9,1},... | collective-permute-start | bytes 1167368 | tf_op jit(solution)/shard_map/ppermute | solution.py:30
  81.3 19.2 %collective-permute-start.9 = (bf16[80,2432]{1,0:T(8,128)(2,1)}, bf16[80,2432]{1,0:T(8,128)(2,1)}, u32[]{:S(2)}, u32[]{:S(2)}) collective-permute-start(bf16[80,2432]{1,0:T(8,128)(2,1)} %shard_map.168.refs_0_), channel_id=1, source_target_pairs={{0,12},{1,13},{2,14},{3,15},{4,0},{5,1},{6,2},{7,3},{8,4},{9,5},{1... | collective-permute-start | bytes 1167368 | tf_op jit(solution)/shard_map/ppermute | solution.py:30
  83.9 13.3 %all-to-all-start.3 = ((bf16[16,32,192]{2,1,0:T(8,128)(2,1)}), bf16[16,32,192]{2,1,0:T(8,128)(2,1)}, u32[]{:S(2)}, u32[]{:S(2)}) async-start(bf16[16,32,192]{2,1,0:T(8,128)(2,1)} %shard_map.165.refs_5_), calls=%async_computation.3 | async-start | bytes 524288 | tf_op jit(solution)/shard_map/all_to_all | solution.py:488
  101.6 22.5 %copy-start.8 = (bf16[512,512]{1,0:T(8,128)(2,1)S(1)}, bf16[512,512]{1,0:T(8,128)(2,1)}, u32[]{:S(2)}) copy-start(bf16[512,512]{1,0:T(8,128)(2,1)} %shard_map.167.refs_7_.refs_1_) | copy-start | bytes 1572868
  101.6 22.5 %copy-start.24 = (bf16[128,2432]{1,0:T(8,128)(2,1)S(1)}, bf16[128,2432]{1,0:T(8,128)(2,1)}, u32[]{:S(2)}) copy-start(bf16[128,2432]{1,0:T(8,128)(2,1)} %refs_3_.1) | copy-start | bytes 1867780
  128.2 17.9 %copy-start.14 = (bf16[128,2432]{1,0:T(8,128)(2,1)S(1)}, bf16[128,2432]{1,0:T(8,128)(2,1)}, u32[]{:S(2)}) copy-start(bf16[128,2432]{1,0:T(8,128)(2,1)} %refs_2_.3) | copy-start | bytes 1867780
  128.2 13.1 %collective-permute-start.12 = (bf16[128,2432]{1,0:T(8,128)(2,1)S(1)}, bf16[128,2432]{1,0:T(8,128)(2,1)S(1)}, u32[]{:S(2)}, u32[]{:S(2)}) collective-permute-start(bf16[128,2432]{1,0:T(8,128)(2,1)S(1)} %get-tuple-element.59), channel_id=1, source_target_pairs={{0,12},{1,13},{2,14},{3,15},{4,0},{5,1},{6,2},{7,3},{8,4},{9,5},{1... | collective-permute-start | bytes 1867784 | tf_op jit(solution)/shard_map/ppermute | solution.py:30
  128.7 17.4 %collective-permute-start.14 = (bf16[128,2432]{1,0:T(8,128)(2,1)S(1)}, bf16[128,2432]{1,0:T(8,128)(2,1)S(1)}, u32[]{:S(2)}, u32[]{:S(2)}) collective-permute-start(bf16[128,2432]{1,0:T(8,128)(2,1)S(1)} %get-tuple-element.61), channel_id=1, source_target_pairs={{0,4},{1,5},{2,6},{3,7},{4,8},{5,9},{6,10},{7,11},{8,12},{9,13},{1... | collective-permute-start | bytes 1867784 | tf_op jit(solution)/shard_map/ppermute | solution.py:30
  129.7 21.5 %collective-permute-start.13 = (bf16[128,2432]{1,0:T(8,128)(2,1)}, bf16[128,2432]{1,0:T(8,128)(2,1)}, u32[]{:S(2)}, u32[]{:S(2)}) collective-permute-start(bf16[128,2432]{1,0:T(8,128)(2,1)} %get-tuple-element.60), channel_id=1, source_target_pairs={{0,8},{1,9},{2,10},{3,11},{4,12},{5,13},{6,14},{7,15},{8,0},{9,1},... | collective-permute-start | bytes 1867784 | tf_op jit(solution)/shard_map/ppermute | solution.py:30
  130.4 79.9 %slice-start = ((s8[5914624]{0:T(1024)(128)(4,1)}), s8[1720320]{0:T(1024)(128)(4,1)S(1)}, s32[]{:S(2)}) async-start(s8[5914624]{0:T(1024)(128)(4,1)} %bitcast.21), calls=%async_computation.7 | async-start | bytes 3440640
  146.1 1.9 copy-start.5
  149.6 7.2 %collective-permute-start.15 = (bf16[80,2432]{1,0:T(8,128)(2,1)}, bf16[80,2432]{1,0:T(8,128)(2,1)}, u32[]{:S(2)}, u32[]{:S(2)}) collective-permute-start(bf16[80,2432]{1,0:T(8,128)(2,1)} %get-tuple-element.64), channel_id=1, source_target_pairs={{0,12},{1,13},{2,14},{3,15},{4,0},{5,1},{6,2},{7,3},{8,4},{9,5},{1... | collective-permute-start | bytes 1167368 | tf_op jit(solution)/shard_map/ppermute | solution.py:30
  149.6 8.7 %collective-permute-start.16 = (bf16[80,2432]{1,0:T(8,128)(2,1)}, bf16[80,2432]{1,0:T(8,128)(2,1)}, u32[]{:S(2)}, u32[]{:S(2)}) collective-permute-start(bf16[80,2432]{1,0:T(8,128)(2,1)} %get-tuple-element.65), channel_id=1, source_target_pairs={{0,8},{1,9},{2,10},{3,11},{4,12},{5,13},{6,14},{7,15},{8,0},{9,1},... | collective-permute-start | bytes 1167368 | tf_op jit(solution)/shard_map/ppermute | solution.py:30
  150.0 12.5 %collective-permute-start.17 = (bf16[80,2432]{1,0:T(8,128)(2,1)}, bf16[80,2432]{1,0:T(8,128)(2,1)}, u32[]{:S(2)}, u32[]{:S(2)}) collective-permute-start(bf16[80,2432]{1,0:T(8,128)(2,1)} %get-tuple-element.66), channel_id=1, source_target_pairs={{0,4},{1,5},{2,6},{3,7},{4,8},{5,9},{6,10},{7,11},{8,12},{9,13},{1... | collective-permute-start | bytes 1167368 | tf_op jit(solution)/shard_map/ppermute | solution.py:30
  162.5 1.1 copy-start.4
  163.5 1.1 copy-start.6
  164.6 1.1 copy-start.16
  166.7 14.7 %copy-start.21 = (bf16[20,2432]{1,0:T(8,128)(2,1)S(1)}, bf16[20,2432]{1,0:T(8,128)(2,1)}, u32[]{:S(2)}) copy-start(bf16[20,2432]{1,0:T(8,128)(2,1)} %copy-done.20) | copy-start | bytes 291844
  166.7 43.6 %slice-start.1 = ((s8[5914624]{0:T(1024)(128)(4,1)}), s8[4194304]{0:T(1024)(128)(4,1)S(1)}, s32[]{:S(2)}) async-start(s8[5914624]{0:T(1024)(128)(4,1)} %bitcast.21), calls=%async_computation.8 | async-start | bytes 8388608
  169.2 8.7 %collective-permute-start.18 = (bf16[52,2432]{1,0:T(8,128)(2,1)S(1)}, bf16[52,2432]{1,0:T(8,128)(2,1)S(1)}, u32[]{:S(2)}, u32[]{:S(2)}) collective-permute-start(bf16[52,2432]{1,0:T(8,128)(2,1)S(1)} %get-tuple-element.68), channel_id=1, source_target_pairs={{0,3},{1,0},{2,1},{3,2},{4,7},{5,4},{6,5},{7,6},{8,11},{9,8},{10,9... | collective-permute-start | bytes 758792 | tf_op jit(solution)/shard_map/ppermute | solution.py:30
  171.6 6.9 %collective-permute-start.19 = (bf16[52,2432]{1,0:T(8,128)(2,1)S(1)}, bf16[52,2432]{1,0:T(8,128)(2,1)S(1)}, u32[]{:S(2)}, u32[]{:S(2)}) collective-permute-start(bf16[52,2432]{1,0:T(8,128)(2,1)S(1)} %get-tuple-element.69), channel_id=1, source_target_pairs={{0,2},{1,3},{2,0},{3,1},{4,6},{5,7},{6,4},{7,5},{8,10},{9,11},{10,... | collective-permute-start | bytes 758792 | tf_op jit(solution)/shard_map/ppermute | solution.py:30
  171.6 9.8 %collective-permute-start.20 = (bf16[52,2432]{1,0:T(8,128)(2,1)S(1)}, bf16[52,2432]{1,0:T(8,128)(2,1)S(1)}, u32[]{:S(2)}, u32[]{:S(2)}) collective-permute-start(bf16[52,2432]{1,0:T(8,128)(2,1)S(1)} %get-tuple-element.70), channel_id=1, source_target_pairs={{0,1},{1,2},{2,3},{3,0},{4,5},{5,6},{6,7},{7,4},{8,9},{9,10},{10,1... | collective-permute-start | bytes 758792 | tf_op jit(solution)/shard_map/ppermute | solution.py:30
  181.9 9.8 %collective-permute-start.23 = (bf16[52,2432]{1,0:T(8,128)(2,1)S(1)}, bf16[52,2432]{1,0:T(8,128)(2,1)S(1)}, u32[]{:S(2)}, u32[]{:S(2)}) collective-permute-start(bf16[52,2432]{1,0:T(8,128)(2,1)S(1)} %get-tuple-element.73.refs_0_), channel_id=1, source_target_pairs={{0,1},{1,2},{2,3},{3,0},{4,5},{5,6},{6,7},{7,4},{8,9},{9,10},{10,1... | collective-permute-start | bytes 758792 | tf_op jit(solution)/shard_map/ppermute | solution.py:30
  182.0 9.7 %collective-permute-start.22 = (bf16[52,2432]{1,0:T(8,128)(2,1)S(1)}, bf16[52,2432]{1,0:T(8,128)(2,1)S(1)}, u32[]{:S(2)}, u32[]{:S(2)}) collective-permute-start(bf16[52,2432]{1,0:T(8,128)(2,1)S(1)} %get-tuple-element.73.refs_0_), channel_id=1, source_target_pairs={{0,2},{1,3},{2,0},{3,1},{4,6},{5,7},{6,4},{7,5},{8,10},{9,11},{10,... | collective-permute-start | bytes 758792 | tf_op jit(solution)/shard_map/ppermute | solution.py:30
  183.8 8.6 %collective-permute-start.21 = (bf16[52,2432]{1,0:T(8,128)(2,1)S(1)}, bf16[52,2432]{1,0:T(8,128)(2,1)S(1)}, u32[]{:S(2)}, u32[]{:S(2)}) collective-permute-start(bf16[52,2432]{1,0:T(8,128)(2,1)S(1)} %get-tuple-element.73.refs_0_), channel_id=1, source_target_pairs={{0,3},{1,0},{2,1},{3,2},{4,7},{5,4},{6,5},{7,6},{8,11},{9,8},{10,9... | collective-permute-start | bytes 758792 | tf_op jit(solution)/shard_map/ppermute | solution.py:30
  192.4 17.5 %collective-permute-start.26 = (bf16[128,2432]{1,0:T(8,128)(2,1)S(1)}, bf16[128,2432]{1,0:T(8,128)(2,1)S(1)}, u32[]{:S(2)}, u32[]{:S(2)}) collective-permute-start(bf16[128,2432]{1,0:T(8,128)(2,1)S(1)} %shard_map.175.in0), channel_id=1, source_target_pairs={{0,4},{1,5},{2,6},{3,7},{4,8},{5,9},{6,10},{7,11},{8,12},{9,13},{1... | collective-permute-start | bytes 1867784 | tf_op jit(solution)/shard_map/ppermute | solution.py:30
  192.5 17.4 %collective-permute-start.24 = (bf16[128,2432]{1,0:T(8,128)(2,1)S(1)}, bf16[128,2432]{1,0:T(8,128)(2,1)S(1)}, u32[]{:S(2)}, u32[]{:S(2)}) collective-permute-start(bf16[128,2432]{1,0:T(8,128)(2,1)S(1)} %shard_map.175.in0), channel_id=1, source_target_pairs={{0,12},{1,13},{2,14},{3,15},{4,0},{5,1},{6,2},{7,3},{8,4},{9,5},{1... | collective-permute-start | bytes 1867784 | tf_op jit(solution)/shard_map/ppermute | solution.py:30
  195.2 15.1 %collective-permute-start.25 = (bf16[128,2432]{1,0:T(8,128)(2,1)S(1)}, bf16[128,2432]{1,0:T(8,128)(2,1)S(1)}, u32[]{:S(2)}, u32[]{:S(2)}) collective-permute-start(bf16[128,2432]{1,0:T(8,128)(2,1)S(1)} %shard_map.175.in0), channel_id=1, source_target_pairs={{0,8},{1,9},{2,10},{3,11},{4,12},{5,13},{6,14},{7,15},{8,0},{9,1},... | collective-permute-start | bytes 1867784 | tf_op jit(solution)/shard_map/ppermute | solution.py:30
  210.0 13.0 %collective-permute-start.32 = (bf16[80,2432]{1,0:T(8,128)(2,1)S(1)}, bf16[80,2432]{1,0:T(8,128)(2,1)S(1)}, u32[]{:S(2)}, u32[]{:S(2)}) collective-permute-start(bf16[80,2432]{1,0:T(8,128)(2,1)S(1)} %shard_map.177.in0), channel_id=1, source_target_pairs={{0,4},{1,5},{2,6},{3,7},{4,8},{5,9},{6,10},{7,11},{8,12},{9,13},{1... | collective-permute-start | bytes 1167368 | tf_op jit(solution)/shard_map/ppermute | solution.py:30
  217.1 33.6 %collective-permute-start.27 = (bf16[128,2432]{1,0:T(8,128)(2,1)S(1)}, bf16[128,2432]{1,0:T(8,128)(2,1)S(1)}, u32[]{:S(2)}, u32[]{:S(2)}) collective-permute-start(bf16[128,2432]{1,0:T(8,128)(2,1)S(1)} %get-tuple-element.75), channel_id=1, source_target_pairs={{0,12},{1,13},{2,14},{3,15},{4,0},{5,1},{6,2},{7,3},{8,4},{9,5},{1... | collective-permute-start | bytes 1867784 | tf_op jit(solution)/shard_map/ppermute | solution.py:30
  220.0 8.2 %collective-permute-start.31 = (bf16[80,2432]{1,0:T(8,128)(2,1)S(1)}, bf16[80,2432]{1,0:T(8,128)(2,1)S(1)}, u32[]{:S(2)}, u32[]{:S(2)}) collective-permute-start(bf16[80,2432]{1,0:T(8,128)(2,1)S(1)} %shard_map.177.in0), channel_id=1, source_target_pairs={{0,8},{1,9},{2,10},{3,11},{4,12},{5,13},{6,14},{7,15},{8,0},{9,1},... | collective-permute-start | bytes 1167368 | tf_op jit(solution)/shard_map/ppermute | solution.py:30
  220.0 22.2 %collective-permute-start.30 = (bf16[80,2432]{1,0:T(8,128)(2,1)S(1)}, bf16[80,2432]{1,0:T(8,128)(2,1)S(1)}, u32[]{:S(2)}, u32[]{:S(2)}) collective-permute-start(bf16[80,2432]{1,0:T(8,128)(2,1)S(1)} %shard_map.177.in0), channel_id=1, source_target_pairs={{0,12},{1,13},{2,14},{3,15},{4,0},{5,1},{6,2},{7,3},{8,4},{9,5},{1... | collective-permute-start | bytes 1167368 | tf_op jit(solution)/shard_map/ppermute | solution.py:30
  221.0 30.4 %collective-permute-start.28 = (bf16[128,2432]{1,0:T(8,128)(2,1)S(1)}, bf16[128,2432]{1,0:T(8,128)(2,1)S(1)}, u32[]{:S(2)}, u32[]{:S(2)}) collective-permute-start(bf16[128,2432]{1,0:T(8,128)(2,1)S(1)} %get-tuple-element.76), channel_id=1, source_target_pairs={{0,8},{1,9},{2,10},{3,11},{4,12},{5,13},{6,14},{7,15},{8,0},{9,1},... | collective-permute-start | bytes 1867784 | tf_op jit(solution)/shard_map/ppermute | solution.py:30
  223.0 28.4 %collective-permute-start.29 = (bf16[128,2432]{1,0:T(8,128)(2,1)S(1)}, bf16[128,2432]{1,0:T(8,128)(2,1)S(1)}, u32[]{:S(2)}, u32[]{:S(2)}) collective-permute-start(bf16[128,2432]{1,0:T(8,128)(2,1)S(1)} %get-tuple-element.77), channel_id=1, source_target_pairs={{0,4},{1,5},{2,6},{3,7},{4,8},{5,9},{6,10},{7,11},{8,12},{9,13},{1... | collective-permute-start | bytes 1867784 | tf_op jit(solution)/shard_map/ppermute | solution.py:30
  247.3 12.3 %collective-permute-start.33 = (bf16[80,2432]{1,0:T(8,128)(2,1)S(1)}, bf16[80,2432]{1,0:T(8,128)(2,1)S(1)}, u32[]{:S(2)}, u32[]{:S(2)}) collective-permute-start(bf16[80,2432]{1,0:T(8,128)(2,1)S(1)} %get-tuple-element.79), channel_id=1, source_target_pairs={{0,12},{1,13},{2,14},{3,15},{4,0},{5,1},{6,2},{7,3},{8,4},{9,5},{1... | collective-permute-start | bytes 1167368 | tf_op jit(solution)/shard_map/ppermute | solution.py:30
  250.7 8.8 %collective-permute-start.34 = (bf16[80,2432]{1,0:T(8,128)(2,1)S(1)}, bf16[80,2432]{1,0:T(8,128)(2,1)S(1)}, u32[]{:S(2)}, u32[]{:S(2)}) collective-permute-start(bf16[80,2432]{1,0:T(8,128)(2,1)S(1)} %get-tuple-element.80), channel_id=1, source_target_pairs={{0,8},{1,9},{2,10},{3,11},{4,12},{5,13},{6,14},{7,15},{8,0},{9,1},... | collective-permute-start | bytes 1167368 | tf_op jit(solution)/shard_map/ppermute | solution.py:30
  250.7 12.0 %collective-permute-start.35 = (bf16[80,2432]{1,0:T(8,128)(2,1)S(1)}, bf16[80,2432]{1,0:T(8,128)(2,1)S(1)}, u32[]{:S(2)}, u32[]{:S(2)}) collective-permute-start(bf16[80,2432]{1,0:T(8,128)(2,1)S(1)} %get-tuple-element.81), channel_id=1, source_target_pairs={{0,4},{1,5},{2,6},{3,7},{4,8},{5,9},{6,10},{7,11},{8,12},{9,13},{1... | collective-permute-start | bytes 1167368 | tf_op jit(solution)/shard_map/ppermute | solution.py:30
  263.7 11.4 %collective-permute-start.36 = (bf16[52,2432]{1,0:T(8,128)(2,1)S(1)}, bf16[52,2432]{1,0:T(8,128)(2,1)S(1)}, u32[]{:S(2)}, u32[]{:S(2)}) collective-permute-start(bf16[52,2432]{1,0:T(8,128)(2,1)S(1)} %get-tuple-element.83), channel_id=1, source_target_pairs={{0,3},{1,0},{2,1},{3,2},{4,7},{5,4},{6,5},{7,6},{8,11},{9,8},{10,9... | collective-permute-start | bytes 758792 | tf_op jit(solution)/shard_map/ppermute | solution.py:30
  265.8 9.8 %collective-permute-start.37 = (bf16[52,2432]{1,0:T(8,128)(2,1)S(1)}, bf16[52,2432]{1,0:T(8,128)(2,1)S(1)}, u32[]{:S(2)}, u32[]{:S(2)}) collective-permute-start(bf16[52,2432]{1,0:T(8,128)(2,1)S(1)} %get-tuple-element.84), channel_id=1, source_target_pairs={{0,2},{1,3},{2,0},{3,1},{4,6},{5,7},{6,4},{7,5},{8,10},{9,11},{10,... | collective-permute-start | bytes 758792 | tf_op jit(solution)/shard_map/ppermute | solution.py:30
  265.8 12.7 %collective-permute-start.38 = (bf16[52,2432]{1,0:T(8,128)(2,1)S(1)}, bf16[52,2432]{1,0:T(8,128)(2,1)S(1)}, u32[]{:S(2)}, u32[]{:S(2)}) collective-permute-start(bf16[52,2432]{1,0:T(8,128)(2,1)S(1)} %get-tuple-element.85), channel_id=1, source_target_pairs={{0,1},{1,2},{2,3},{3,0},{4,5},{5,6},{6,7},{7,4},{8,9},{9,10},{10,1... | collective-permute-start | bytes 758792 | tf_op jit(solution)/shard_map/ppermute | solution.py:30
  (7 other events, 6.0 us)
where the time goes:
time: 302 us; the launch traced here: 301 us
  waiting for transfers between devices  127 us (42%)
  starting transfers between devices  61.8 us (20%)
  blocking collectives  50.4 us (17%)
  Pallas kernels  44.2 us (15%)
  local copies, waits for them, and re-layouts  15.7 us (5%)
    ppermute x39, waiting for transfers between devices, torus_shift(): return lax.ppermute(values, ('grp', 'tp'), pairs)  107 us
    ppermute x39, starting transfers between devices, torus_shift(): return lax.ppermute(values, ('grp', 'tp'), pairs)  36.7 us
    pallas_call x18, Pallas kernels, run(): pl.pallas_call(body, out_shape=shapes, in_specs=specs, out_specs=[pl.Bloc...  23 us
    all_to_all x1, blocking collectives, shards(): lax.all_to_all(placed.reshape(8, 4, width), 'grp', 0, 0, tiled=True)  21.1 us
    all_to_all x1, blocking collectives, shards(): lax.all_to_all(slot_parts.reshape(8, 64, 512), 'grp', 0, 0, tiled=True)  19.4 us
    unnamed x57, local copies, waits for them, and re-layouts  13.8 us
    pallas_call x2, Pallas kernels, feed(): pl.pallas_call(feed_kernel, grid=(1,), out_shape=[like((rows, width))] *...  11.8 us
    all_to_all x1, blocking collectives, shards(): lax.all_to_all(att_parts, 'grp', 0, 0, tiled=True).reshape(512, 128)  9.85 us
  transfers between devices with their start and end apart: 43, of which 28 were waited for; matrix products, arithmetic and copies ran while one was open for 1% of the time, Pallas kernels for 8%

commit v1 on v0

--- a/solution.py
+++ b/solution.py
@@ -48,7 +48,7 @@
     ]
 
 
-def run(kernel, outs, args, smem=0, scratch=(), flops=0, limit=32, after=()):
+def run(kernel, outs, args, smem=0, scratch=(), flops=0, limit=16, after=()):
     specs = [pl.BlockSpec(memory_space=pltpu.SMEM)] * smem
     specs += [pl.BlockSpec(memory_space=pltpu.VMEM)] * (len(args) - smem)
     specs += [pl.BlockSpec(memory_space=pl.ANY)] * len(after)
@@ -224,7 +224,7 @@
     out_ref[:, 384:512] = val1.astype(BF16)
 
 
-def img_project_kernel(image_ref, mod_ref, weight_ref, out_ref, projected_ref):
+def img_project_kernel(image_ref, mod_ref, weight_ref, _, out_ref, projected_ref):
     rows = image_ref[...].astype(F32)
     modded = (normed(rows) * (1.0 + mod_ref[0, 1, 0:1, :]) + mod_ref[0, 0, 0:1, :]).astype(BF16)
     out_ref[...] = modded
@@ -233,7 +233,7 @@
     projected_ref[:, 256:384] = values
 
 
-def low_part_kernel(adapter_ref, tp_ref, mod_ref, down_ref, out_ref, wide):
+def low_part_kernel(adapter_ref, tp_ref, mod_ref, down_ref, _, out_ref, wide):
     depth = down_ref.shape[1]
     wide[...] = jnp.zeros_like(wide)
     start = pl.multiple_of(tp_ref[0] * depth, 8)
@@ -392,7 +392,7 @@
         ],
         out_specs=[plain] * SIDE,
         scratch_shapes=[pltpu.VMEM((rows * SIDE, width), BF16)],
-        compiler_params=pltpu.CompilerParams(vmem_limit_bytes=40 << 20),
+        compiler_params=pltpu.CompilerParams(vmem_limit_bytes=32 << 20),
         cost_estimate=pl.CostEstimate(
             flops=rows * SIDE * width * hidden * 4,
             bytes_accessed=width * hidden * 4 + rows * width * 16,
@@ -451,16 +451,31 @@
             pl.BlockSpec((block, width), lambda i: (i, 0)),
             pl.BlockSpec((1, 6, 2, width), lambda i: (i // 2, 0, 0, 0)),
             pl.BlockSpec((3, width, 128), lambda i: (0, 0, 0)),
+            pl.BlockSpec(memory_space=pl.ANY),
         ],
         out_specs=[
             pl.BlockSpec((block, width), lambda i: (i, 0)),
             pl.BlockSpec((block, 384), lambda i: (i, 0)),
         ],
-        compiler_params=pltpu.CompilerParams(vmem_limit_bytes=32 << 20),
+        compiler_params=pltpu.CompilerParams(vmem_limit_bytes=24 << 20),
         cost_estimate=pl.CostEstimate(
             flops=512 * width * 384 * 2, bytes_accessed=7 << 20, transcendentals=0
         ),
-    )(image, modulation.transpose(0, 2, 1, 3), image_query_key_value.transpose(1, 0, 2))
+    )(
+        image,
+        modulation.transpose(0, 2, 1, 3),
+        image_query_key_value.transpose(1, 0, 2),
+        outgoing,
+    )
+    *embed_parts, labels = run(
+        embed_kernel,
+        [like((SIDE * POOL, width))] * SIDE + [like((16, 256), F32)],
+        (places, arrived, prompt_embed_weight),
+        smem=1,
+        scratch=[pltpu.VMEM((SIDE * POOL, 256), F32)],
+        flops=320 * 256 * width * 2,
+        after=(img_projected,),
+    )
     half = image.shape[0] // 2
     low_part = pl.pallas_call(
         low_part_kernel,
@@ -470,16 +485,17 @@
             in_specs=[
                 pl.BlockSpec((half, width), lambda i, *_: (i, 0)),
                 pl.BlockSpec((1, *adapter_down.shape[1:]), lambda i, ids, _: (ids[i], 0, 0)),
+                pl.BlockSpec(memory_space=pl.ANY),
             ],
             out_specs=pl.BlockSpec((8, 32, 192), lambda i, *_: (i, 0, 0)),
             scratch_shapes=[pltpu.VMEM((width, 192), F32)],
         ),
         out_shape=like((16, 32, 192)),
-        compiler_params=pltpu.CompilerParams(vmem_limit_bytes=32 << 20),
+        compiler_params=pltpu.CompilerParams(vmem_limit_bytes=24 << 20),
         cost_estimate=pl.CostEstimate(
             flops=512 * width * 192 * 2, bytes_accessed=3 << 20, transcendentals=0
         ),
-    )(request_adapter, tp.reshape(1).astype(jnp.int32), img_mod, adapter_down)
+    )(request_adapter, tp.reshape(1).astype(jnp.int32), img_mod, adapter_down, embed_parts[0])
     low_sum = run(
         low_sum_kernel,
         like((16, 32, 192)),
@@ -488,20 +504,12 @@
     low = lax.all_to_all(low_sum, "tp", 0, 0, tiled=True).reshape(2 * half, 192)
 
     mod_all = run(
-        repeat_mod_kernel, like((8, 2, 8, width), F32), (modulation.transpose(0, 2, 1, 3),)
+        repeat_mod_kernel, like((8, 2, 8, width), F32), (modulation.transpose(0, 2, 1, 3),),
+        after=(embed_parts[0],),
     )
     mod_all = lax.all_to_all(mod_all, "grp", 0, 0, tiled=True).reshape(16, 8, width)
     row_mod = run(row_mod_kernel, like((6, POOL, width), F32), (request, mod_all), smem=1)
 
-    *embed_parts, labels = run(
-        embed_kernel,
-        [like((SIDE * POOL, width))] * SIDE + [like((16, 256), F32)],
-        (places, arrived, prompt_embed_weight),
-        smem=1,
-        scratch=[pltpu.VMEM((SIDE * POOL, 256), F32)],
-        flops=320 * 256 * width * 2,
-        after=(img_projected,),
-    )
     embed_sums = exchange(middle(exchange(embed_parts, 1), after=(low_part,)), 0)
     embedded, txt_mod = run(
         embed_norm_kernel,
@@ -509,7 +517,7 @@
         (*embed_sums, row_mod),
         after=(low_sum,),
     )
-    txt_mods = spread(join(spread(txt_mod, 0), 0, POOL), 1)
+    txt_mods = spread(join(spread(txt_mod, 0), 0, POOL, after=(low,)), 1)
 
     target = labels[:, :POOL].astype(jnp.int32)
     slots_all = target // 4 * 64 + target // 2 % 2 * 32 + target % 2
@@ -570,7 +578,7 @@
         [like((SIDE * POOL, width))] * SIDE,
         (att_parts, slots_all, prompt_out_weight),
         flops=320 * 128 * width * 2,
-        after=(img_sums[1], img_sums[3]),
+        after=(img_sums[1],),
     )
     txt_sums = exchange(txt_terms, 1)
 
@@ -583,8 +591,8 @@
         (own_image, embedded, *sums, own_mod, row_mod),
     )
     near_rows = spread(norm_rows, 0)
-    img_rows = spread(join(near_rows, 0, 32), 1)
-    txt_rows = spread(join(near_rows, 32, POOL, after=(img_rows[1], img_rows[3])), 1)
+    txt_rows = spread(join(near_rows, 32, POOL), 1)
+    img_rows = spread(join(near_rows, 0, 32, after=(txt_rows[1],)), 1)
     weight_in = feed_in_weight.transpose(0, 2, 1)
     img_terms = feed(img_rows, weight_in, feed_out_weight, 0)
     txt_terms = feed(txt_rows, weight_in, feed_out_weight, 1)

time: 302 us -> 297 us (0.983)
  local copies, waits for them, and re-layouts: 15.7 us -> 29.8 us
  waiting for transfers between devices: 127 us -> 115 us
  Pallas kernels: 44.2 us -> 40.6 us
    unnamed x57 -> x71, local copies, waits for them, and re-layouts: 13.8 us -> 26.4 us
    all_to_all x1, waiting for transfers between devices: 7.75 us -> 0.01 us  [shards(): low = lax.all_to_all(low_sum, 'tp', 0, 0, tiled=True).reshape(2 * half, 192)]
    all_to_all x1, waiting for transfers between devices: 6.16 us -> 0.01 us  [shards(): arrived = lax.all_to_all(outgoing, 'tp', 0, 0, tiled=True)]
    all_to_all x1, starting transfers between devices: 3.53 us -> 8.6 us  [shards(): arrived = lax.all_to_all(outgoing, 'tp', 0, 0, tiled=True)]
    pallas_call x2, Pallas kernels: 11.8 us -> 8.14 us  [feed(): pl.pallas_call(feed_kernel, grid=(1,), out_shape=[like((rows, width))] *...]
  transfers between devices with their start and end apart: 43 -> 43, of which waited for: 28 -> 27; matrix products, arithmetic and copies ran while one was open for 1% -> 1% of each run, Pallas kernels for 8% -> 8%
where the time goes in v1:
time: 297 us; the launch traced here: 296 us
  waiting for transfers between devices  115 us (39%)
  starting transfers between devices  61.6 us (21%)
  blocking collectives  47.6 us (16%)
  Pallas kernels  40.6 us (14%)
  local copies, waits for them, and re-layouts  29.8 us (10%)
    ppermute x39, waiting for transfers between devices, torus_shift(): return lax.ppermute(values, ('grp', 'tp'), pairs)  108 us
    ppermute x39, starting transfers between devices, torus_shift(): return lax.ppermute(values, ('grp', 'tp'), pairs)  34 us
    unnamed x71, local copies, waits for them, and re-layouts  26.4 us
    pallas_call x18, Pallas kernels, run(): pl.pallas_call(body, out_shape=shapes, in_specs=specs, out_specs=[pl.Bloc...  23.1 us
    all_to_all x1, blocking collectives, shards(): lax.all_to_all(placed.reshape(8, 4, width), 'grp', 0, 0, tiled=True)  19.3 us
    all_to_all x1, blocking collectives, shards(): lax.all_to_all(slot_parts.reshape(8, 64, 512), 'grp', 0, 0, tiled=True)  18.4 us
    all_to_all x1, blocking collectives, shards(): lax.all_to_all(att_parts, 'grp', 0, 0, tiled=True).reshape(512, 128)  9.9 us
    all_to_all x1, starting transfers between devices, shards(): arrived = lax.all_to_all(outgoing, 'tp', 0, 0, tiled=True)  8.6 us
  transfers between devices with their start and end apart: 43, of which 27 were waited for; matrix products, arithmetic and copies ran while one was open for 1% of the time, Pallas kernels for 8%

profile of v1, /device:TPU:1, one launch (start us, length us, event | category | flops | bytes accessed | tf_op | source)
XLA Modules:
  0.0 296.2 jit_solution(4969157603273065422)
XLA Ops:
  3.1 8.6 %all-to-all-start = ((bf16[16,32,256]{2,1,0:T(8,128)(2,1)}), bf16[16,32,256]{2,1,0:T(8,128)(2,1)S(1)}, u32[]{:S(2)}, u32[]{:S(2)}) async-start(bf16[16,32,256]{2,1,0:T(8,128)(2,1)} %shard_map.158._), calls=%async_computation | async-start | bytes 524288 | tf_op jit(solution)/shard_map/all_to_all | solution.py:443
  11.8 1.7 copy-done.3
  13.5 1.5 copy-done.12
  15.9 3.5 %shard_map.159 = (bf16[512,2432]{1,0:T(8,128)(2,1)S(1)}, f32[512,384]{1,0:T(8,128)S(1)}) custom-call(bf16[512,2432]{1,0:T(8,128)(2,1)S(1)} %copy-done.3, f32[2,6,2,2432]{3,2,1,0:T(2,128)S(1)} %bitcast.31, bf16[3,2432,128]{2,1,0:T(8,128)(2,1)S(1)} %bitcast.29, bf16[16,32,256]{2,1,0:T(8,128)(2,1)} %shard_map.158._), custom_call_target="tpu_custom_call" | custom-call | flops 956301312 | bytes 7340032 | tf_op jit(solution)/shard_map/pallas_call | solution.py:446
  19.4 1.4 copy-done.7
  20.9 2.2 shard_map.160
  23.8 1.7 copy-done.6
  25.5 1.7 copy-done.8
  27.2 2.6 shard_map.161.refs_4_
  29.9 6.6 %all-to-all-start.2 = ((bf16[16,32,192]{2,1,0:T(8,128)(2,1)}), bf16[16,32,192]{2,1,0:T(8,128)(2,1)S(1)}, u32[]{:S(2)}, u32[]{:S(2)}) async-start(bf16[16,32,192]{2,1,0:T(8,128)(2,1)} %shard_map.161.refs_4_), calls=%async_computation.2 | async-start | bytes 524288 | tf_op jit(solution)/shard_map/all_to_all | solution.py:502
  36.5 1.3 shard_map.163
  37.9 6.2 %all-to-all-done.2.refs_0_ = bf16[16,32,192]{2,1,0:T(8,128)(2,1)S(1)} async-done(((bf16[16,32,192]{2,1,0:T(8,128)(2,1)}), bf16[16,32,192]{2,1,0:T(8,128)(2,1)S(1)}, u32[]{:S(2)}, u32[]{:S(2)}) %all-to-all-start.2) | async-done | bytes 196640 | tf_op jit(solution)/shard_map/all_to_all | solution.py:502
  44.0 7.0 %all-to-all-start.1 = ((f32[8,2,8,2432]{3,2,1,0:T(8,128)}), f32[8,2,8,2432]{3,2,1,0:T(8,128)S(1)}, u32[]{:S(2)}, u32[]{:S(2)}) async-start(f32[8,2,8,2432]{3,2,1,0:T(8,128)} %shard_map.163), calls=%async_computation.1 | async-start | bytes 2490368 | tf_op jit(solution)/shard_map/all_to_all | solution.py:510
  51.5 1.6 collective-permute-start.1
  53.1 5.0 %collective-permute-done.refs_1_ = bf16[80,2432]{1,0:T(8,128)(2,1)S(1)} collective-permute-done((bf16[80,2432]{1,0:T(8,128)(2,1)}, bf16[80,2432]{1,0:T(8,128)(2,1)S(1)}, u32[]{:S(2)}, u32[]{:S(2)}) %collective-permute-start) | collective-permute-done | bytes 389152 | tf_op jit(solution)/shard_map/ppermute | solution.py:30
  58.1 2.0 collective-permute-done.1.refs_2_
  60.1 4.1 %collective-permute-done.2.refs_3_ = bf16[80,2432]{1,0:T(8,128)(2,1)S(1)} collective-permute-done((bf16[80,2432]{1,0:T(8,128)(2,1)}, bf16[80,2432]{1,0:T(8,128)(2,1)S(1)}, u32[]{:S(2)}, u32[]{:S(2)}) %collective-permute-start.2) | collective-permute-done | bytes 389152 | tf_op jit(solution)/shard_map/ppermute | solution.py:30
  68.2 5.4 %all-to-all-start.3 = ((bf16[16,32,192]{2,1,0:T(8,128)(2,1)}), bf16[16,32,192]{2,1,0:T(8,128)(2,1)S(1)}, u32[]{:S(2)}, u32[]{:S(2)}) async-start(bf16[16,32,192]{2,1,0:T(8,128)(2,1)} %shard_map.165.refs_5_), calls=%async_computation.3 | async-start | bytes 524288 | tf_op jit(solution)/shard_map/all_to_all | solution.py:504
  77.1 1.3 shard_map.166
  78.3 2.6 collective-permute-start.6
  82.1 1.9 collective-permute-done.6.refs_1_
  84.0 2.3 collective-permute-done.7.refs_2_
  86.3 1.1 collective-permute-done.8.refs_3_
  87.5 2.7 collective-permute-start.9
  91.9 3.3 %shard_map.167.refs_7_.refs_1_ = bf16[512,512]{1,0:T(8,128)(2,1)} custom-call(s32[2]{0:T(128)} %adapter_ref.3, bf16[512,192]{1,0:T(8,128)(2,1)} %bitcast.27, f32[512,384]{1,0:T(8,128)} %copy-done.2, bf16[32,3,64,128]{3,2,1,0:T(8,128)(2,1)} %up_ref.1, f32[2,128]{1,0:T(2,128)} %get-tuple-element.89.gain_ref), custom_call_target="tpu_custom_call" | custom-call | flops 75497472 | bytes 2097152 | tf_op jit(solution)/shard_map/pallas_call | solution.py:531
  95.2 3.8 %collective-permute-done.9.refs_1_ = bf16[80,2432]{1,0:T(8,128)(2,1)S(1)} collective-permute-done((bf16[80,2432]{1,0:T(8,128)(2,1)S(1)}, bf16[80,2432]{1,0:T(8,128)(2,1)S(1)}, u32[]{:S(2)}, u32[]{:S(2)}) %collective-permute-start.9) | collective-permute-done | bytes 389152 | tf_op jit(solution)/shard_map/ppermute | solution.py:30
  99.0 3.8 %collective-permute-done.11.refs_3_ = bf16[80,2432]{1,0:T(8,128)(2,1)} collective-permute-done((bf16[80,2432]{1,0:T(8,128)(2,1)S(1)}, bf16[80,2432]{1,0:T(8,128)(2,1)}, u32[]{:S(2)}, u32[]{:S(2)}) %collective-permute-start.11) | collective-permute-done | bytes 389152 | tf_op jit(solution)/shard_map/ppermute | solution.py:30
  102.8 1.0 copy-done.10
  103.9 1.5 copy-done.13
  105.4 2.7 shard_map.169
  108.1 18.4 %all_to_all.35.refs_2_ = bf16[8,64,512]{2,1,0:T(8,128)(2,1)S(1)} all-to-all(bf16[8,64,512]{2,1,0:T(8,128)(2,1)S(1)} %bitcast.28), channel_id=1, replica_groups=mesh['grp'=8,'tp'=16] {'grp'}, dimensions={0} | all-to-all | bytes 1048576 | tf_op jit(solution)/shard_map/all_to_all | solution.py:559
  126.6 3.5 %shard_map.170 = (bf16[128,2432]{1,0:T(8,128)(2,1)S(1)}, bf16[128,2432]{1,0:T(8,128)(2,1)}, bf16[128,2432]{1,0:T(8,128)(2,1)}, bf16[128,2432]{1,0:T(8,128)(2,1)S(1)}, bf16[2,512,512]{2,1,0:T(8,128)(2,1)S(1)}) custom-call(s32[16]{0:T(128)S(1)} %broadcast_select_fusion.refs_0_, bf16[512,512]{1,0:T(8,128)(2,1)S(1)} %copy-done.11, ...), custom_call_target="tpu_custom_call" | custom-call | flops 1073741824 | bytes 5210176 | tf_op jit(solution)/shard_map/pallas_call | solution.py:64
  131.5 1.1 shard_map.171
  132.7 9.9 %all_to_all.36 = bf16[8,64,128]{2,1,0:T(8,128)(2,1)S(1)} all-to-all(bf16[8,64,128]{2,1,0:T(8,128)(2,1)S(1)} %shard_map.171), channel_id=1, replica_groups=mesh['grp'=8,'tp'=16] {'grp'}, dimensions={0} | all-to-all | bytes 262144 | tf_op jit(solution)/shard_map/all_to_all | solution.py:575
  142.6 1.9 shard_map.172
  149.9 3.3 %collective-permute-done.15.refs_5_ = bf16[80,2432]{1,0:T(8,128)(2,1)} collective-permute-done((bf16[80,2432]{1,0:T(8,128)(2,1)}, bf16[80,2432]{1,0:T(8,128)(2,1)}, u32[]{:S(2)}, u32[]{:S(2)}) %collective-permute-start.15) | collective-permute-done | bytes 389152 | tf_op jit(solution)/shard_map/ppermute | solution.py:30
  153.3 2.1 collective-permute-done.16.refs_6_
  155.3 4.1 %collective-permute-done.17.refs_7_ = bf16[80,2432]{1,0:T(8,128)(2,1)} collective-permute-done((bf16[80,2432]{1,0:T(8,128)(2,1)}, bf16[80,2432]{1,0:T(8,128)(2,1)}, u32[]{:S(2)}, u32[]{:S(2)}) %collective-permute-start.17) | collective-permute-done | bytes 389152 | tf_op jit(solution)/shard_map/ppermute | solution.py:30
  159.4 1.1 copy-done.5
  160.5 1.1 copy-done.19
  162.6 2.7 shard_map.173
  165.3 2.0 collective-permute-start.18
  169.9 3.8 %collective-permute-done.18.refs_3_ = bf16[52,2432]{1,0:T(8,128)(2,1)S(1)} collective-permute-done((bf16[52,2432]{1,0:T(8,128)(2,1)S(1)}, bf16[52,2432]{1,0:T(8,128)(2,1)S(1)}, u32[]{:S(2)}, u32[]{:S(2)}) %collective-permute-start.18) | collective-permute-done | bytes 252960 | tf_op jit(solution)/shard_map/ppermute | solution.py:30
  174.5 2.9 collective-permute-done.20.refs_5_
  179.7 3.6 %collective-permute-done.21.refs_1_ = bf16[52,2432]{1,0:T(8,128)(2,1)S(1)} collective-permute-done((bf16[52,2432]{1,0:T(8,128)(2,1)S(1)}, bf16[52,2432]{1,0:T(8,128)(2,1)S(1)}, u32[]{:S(2)}, u32[]{:S(2)}) %collective-permute-start.21) | collective-permute-done | bytes 252960 | tf_op jit(solution)/shard_map/ppermute | solution.py:30
  183.3 1.9 collective-permute-done.22.refs_2_
  185.2 3.1 %collective-permute-done.23.refs_3_ = bf16[52,2432]{1,0:T(8,128)(2,1)S(1)} collective-permute-done((bf16[52,2432]{1,0:T(8,128)(2,1)S(1)}, bf16[52,2432]{1,0:T(8,128)(2,1)S(1)}, u32[]{:S(2)}, u32[]{:S(2)}) %collective-permute-start.23) | collective-permute-done | bytes 252960 | tf_op jit(solution)/shard_map/ppermute | solution.py:30
  188.5 6.6 %collective-permute-done.24.refs_4_.in1 = bf16[80,2432]{1,0:T(8,128)(2,1)S(1)} collective-permute-done((bf16[80,2432]{1,0:T(8,128)(2,1)S(1)}, bf16[80,2432]{1,0:T(8,128)(2,1)S(1)}, u32[]{:S(2)}, u32[]{:S(2)}) %collective-permute-start.24) | collective-permute-done | bytes 389152 | tf_op jit(solution)/shard_map/ppermute | solution.py:30
  195.1 1.3 collective-permute-start.25
  197.1 3.1 %collective-permute-start.31 = (bf16[80,2432]{1,0:T(8,128)(2,1)S(1)}, bf16[80,2432]{1,0:T(8,128)(2,1)S(1)}, u32[]{:S(2)}, u32[]{:S(2)}) collective-permute-start(bf16[80,2432]{1,0:T(8,128)(2,1)S(1)} %shard_map.175.in0), channel_id=1, source_target_pairs={{0,8},{1,9},{2,10},{3,11},{4,12},{5,13},{6,14},{7,15},{8,0},{9,1},... | collective-permute-start | bytes 1167368 | tf_op jit(solution)/shard_map/ppermute | solution.py:30
  200.3 17.8 %collective-permute-done.31.in2 = bf16[80,2432]{1,0:T(8,128)(2,1)S(1)} collective-permute-done((bf16[80,2432]{1,0:T(8,128)(2,1)S(1)}, bf16[80,2432]{1,0:T(8,128)(2,1)S(1)}, u32[]{:S(2)}, u32[]{:S(2)}) %collective-permute-start.31) | collective-permute-done | bytes 389152 | tf_op jit(solution)/shard_map/ppermute | solution.py:30
  218.0 4.1 %collective-permute-done.32.in3 = bf16[80,2432]{1,0:T(8,128)(2,1)S(1)} collective-permute-done((bf16[80,2432]{1,0:T(8,128)(2,1)S(1)}, bf16[80,2432]{1,0:T(8,128)(2,1)S(1)}, u32[]{:S(2)}, u32[]{:S(2)}) %collective-permute-start.32) | collective-permute-done | bytes 389152 | tf_op jit(solution)/shard_map/ppermute | solution.py:30
  222.2 2.7 copy-done
  224.8 3.2 %shard_map.178 = (bf16[80,2432]{1,0:T(8,128)(2,1)S(1)}, bf16[80,2432]{1,0:T(8,128)(2,1)S(1)}, bf16[80,2432]{1,0:T(8,128)(2,1)S(1)}, bf16[80,2432]{1,0:T(8,128)(2,1)S(1)}) custom-call(bf16[80,2432]{1,0:T(8,128)(2,1)S(1)} %shard_map.175.in0, bf16[80,2432]{1,0:T(8,128)(2,1)S(1)} %collective-permute-done.24.refs_4_.in1, ...), custom_call_target="tpu_custom_call" | custom-call | flops 1892679680 | bytes 9027584 | tf_op jit(solution)/shard_map/pallas_call | solution.py:384
  228.7 2.7 copy-done.1
  231.4 4.9 %shard_map.177 = (bf16[128,2432]{1,0:T(8,128)(2,1)S(1)}, bf16[128,2432]{1,0:T(8,128)(2,1)S(1)}, bf16[128,2432]{1,0:T(8,128)(2,1)S(1)}, bf16[128,2432]{1,0:T(8,128)(2,1)S(1)}) custom-call(bf16[128,2432]{1,0:T(8,128)(2,1)S(1)} %shard_map.176.in0, bf16[128,2432]{1,0:T(8,128)(2,1)S(1)} %collective-permute-done.25.in1, ...), custom_call_target="tpu_custom_call" | custom-call | flops 3028287488 | bytes 10895360 | tf_op jit(solution)/shard_map/pallas_call | solution.py:384
  236.4 2.7 collective-permute-start.29
  239.1 2.3 collective-permute-start.34
  242.3 15.7 %collective-permute-done.34.refs_6_ = bf16[80,2432]{1,0:T(8,128)(2,1)S(1)} collective-permute-done((bf16[80,2432]{1,0:T(8,128)(2,1)S(1)}, bf16[80,2432]{1,0:T(8,128)(2,1)S(1)}, u32[]{:S(2)}, u32[]{:S(2)}) %collective-permute-start.34) | collective-permute-done | bytes 389152 | tf_op jit(solution)/shard_map/ppermute | solution.py:30
  258.1 4.3 %collective-permute-done.35.refs_7_ = bf16[80,2432]{1,0:T(8,128)(2,1)S(1)} collective-permute-done((bf16[80,2432]{1,0:T(8,128)(2,1)S(1)}, bf16[80,2432]{1,0:T(8,128)(2,1)S(1)}, u32[]{:S(2)}, u32[]{:S(2)}) %collective-permute-start.35) | collective-permute-done | bytes 389152 | tf_op jit(solution)/shard_map/ppermute | solution.py:30
  265.4 3.7 %collective-permute-done.36.refs_3_ = bf16[52,2432]{1,0:T(8,128)(2,1)S(1)} collective-permute-done((bf16[52,2432]{1,0:T(8,128)(2,1)S(1)}, bf16[52,2432]{1,0:T(8,128)(2,1)S(1)}, u32[]{:S(2)}, u32[]{:S(2)}) %collective-permute-start.36) | collective-permute-done | bytes 252960 | tf_op jit(solution)/shard_map/ppermute | solution.py:30
  269.1 3.4 %collective-permute-done.37.refs_4_ = bf16[52,2432]{1,0:T(8,128)(2,1)S(1)} collective-permute-done((bf16[52,2432]{1,0:T(8,128)(2,1)S(1)}, bf16[52,2432]{1,0:T(8,128)(2,1)S(1)}, u32[]{:S(2)}, u32[]{:S(2)}) %collective-permute-start.37) | collective-permute-done | bytes 252960 | tf_op jit(solution)/shard_map/ppermute | solution.py:30
  272.5 2.7 collective-permute-done.38.refs_5_
  276.2 19.3 %all_to_all.37 = bf16[8,4,2432]{2,1,0:T(4,128)(2,1)S(1)} all-to-all(bf16[8,4,2432]{2,1,0:T(4,128)(2,1)S(1)} %reshape.64), channel_id=1, replica_groups=mesh['grp'=8,'tp'=16] {'grp'}, dimensions={0} | all-to-all | bytes 311296 | tf_op jit(solution)/shard_map/all_to_all | solution.py:606
  (132 shorter events, 35.9 us)
Async XLA Ops:
  3.1 17.7 %all-to-all-start = ((bf16[16,32,256]{2,1,0:T(8,128)(2,1)}), bf16[16,32,256]{2,1,0:T(8,128)(2,1)S(1)}, u32[]{:S(2)}, u32[]{:S(2)}) async-start(bf16[16,32,256]{2,1,0:T(8,128)(2,1)} %shard_map.158._), calls=%async_computation | async-start | bytes 524288 | tf_op jit(solution)/shard_map/all_to_all | solution.py:443
  11.8 1.7 copy-start.3
  13.5 1.5 copy-start.12
  15.9 4.9 %copy-start.16 = (bf16[256,2432]{1,0:T(8,128)(2,1)S(1)}, bf16[256,2432]{1,0:T(8,128)(2,1)}, u32[]{:S(2)}) copy-start(bf16[256,2432]{1,0:T(8,128)(2,1)} %refs_2_.2) | copy-start | bytes 3735556
  20.8 9.0 %copy-start.2 = (f32[512,384]{1,0:T(8,128)}, f32[512,384]{1,0:T(8,128)S(1)}, u32[]{:S(2)}) copy-start(f32[512,384]{1,0:T(8,128)S(1)} %get-tuple-element.45.refs_3_.projected_ref) | copy-start | bytes 2359300
  20.8 3.0 %copy-start.29 = (s32[2]{0:T(128)S(1)}, s32[2]{0:T(128)}, u32[]{:S(2)}) copy-start(s32[2]{0:T(128)} %adapter_ref.3) | copy-start | bytes 28
  23.8 1.7 copy-start.6
  25.5 1.7 copy-start.8
  27.2 9.3 %copy-start.15 = (f32[2,2,6,2432]{3,1,2,0:T(2,128)S(1)}, f32[2,2,6,2432]{3,1,2,0:T(2,128)}, u32[]{:S(2)}) copy-start(f32[2,2,6,2432]{3,1,2,0:T(2,128)} %param.19) | copy-start | bytes 700420
  29.9 14.2 %all-to-all-start.2 = ((bf16[16,32,192]{2,1,0:T(8,128)(2,1)}), bf16[16,32,192]{2,1,0:T(8,128)(2,1)S(1)}, u32[]{:S(2)}, u32[]{:S(2)}) async-start(bf16[16,32,192]{2,1,0:T(8,128)(2,1)} %shard_map.161.refs_4_), calls=%async_computation.2 | async-start | bytes 524288 | tf_op jit(solution)/shard_map/all_to_all | solution.py:502
  44.0 24.2 %all-to-all-start.1 = ((f32[8,2,8,2432]{3,2,1,0:T(8,128)}), f32[8,2,8,2432]{3,2,1,0:T(8,128)S(1)}, u32[]{:S(2)}, u32[]{:S(2)}) async-start(f32[8,2,8,2432]{3,2,1,0:T(8,128)} %shard_map.163), calls=%async_computation.1 | async-start | bytes 2490368 | tf_op jit(solution)/shard_map/all_to_all | solution.py:510
  51.0 22.7 %copy-start.28 = (s32[20,1]{0,1:T(1,128)S(1)}, s32[20,1]{0,1:T(1,128)}, u32[]{:S(2)}) copy-start(s32[20,1]{0,1:T(1,128)} %param.17) | copy-start | bytes 244
  51.0 7.1 %collective-permute-start = (bf16[80,2432]{1,0:T(8,128)(2,1)}, bf16[80,2432]{1,0:T(8,128)(2,1)S(1)}, u32[]{:S(2)}, u32[]{:S(2)}) collective-permute-start(bf16[80,2432]{1,0:T(8,128)(2,1)} %get-tuple-element.47), channel_id=1, source_target_pairs={{0,12},{1,13},{2,14},{3,15},{4,0},{5,1},{6,2},{7,3},{8,4},{9,5},{1... | collective-permute-start | bytes 1167368 | tf_op jit(solution)/shard_map/ppermute | solution.py:30
  51.5 8.6 %collective-permute-start.1 = (bf16[80,2432]{1,0:T(8,128)(2,1)}, bf16[80,2432]{1,0:T(8,128)(2,1)S(1)}, u32[]{:S(2)}, u32[]{:S(2)}) collective-permute-start(bf16[80,2432]{1,0:T(8,128)(2,1)} %get-tuple-element.48), channel_id=1, source_target_pairs={{0,8},{1,9},{2,10},{3,11},{4,12},{5,13},{6,14},{7,15},{8,0},{9,1},... | collective-permute-start | bytes 1167368 | tf_op jit(solution)/shard_map/ppermute | solution.py:30
  53.1 11.2 %collective-permute-start.2 = (bf16[80,2432]{1,0:T(8,128)(2,1)}, bf16[80,2432]{1,0:T(8,128)(2,1)S(1)}, u32[]{:S(2)}, u32[]{:S(2)}) collective-permute-start(bf16[80,2432]{1,0:T(8,128)(2,1)} %copy-done.31), channel_id=1, source_target_pairs={{0,4},{1,5},{2,6},{3,7},{4,8},{5,9},{6,10},{7,11},{8,12},{9,13},{1... | collective-permute-start | bytes 1167368 | tf_op jit(solution)/shard_map/ppermute | solution.py:30
  65.3 10.0 %copy-start.23 = (bf16[20,2432]{1,0:T(8,128)(2,1)}, bf16[20,2432]{1,0:T(8,128)(2,1)S(1)}, u32[]{:S(2)}) copy-start(bf16[20,2432]{1,0:T(8,128)(2,1)S(1)} %get-tuple-element.51.refs_0_) | copy-start | bytes 291844
  65.3 9.3 %collective-permute-start.3 = (bf16[20,2432]{1,0:T(8,128)(2,1)}, bf16[20,2432]{1,0:T(8,128)(2,1)S(1)}, u32[]{:S(2)}, u32[]{:S(2)}) collective-permute-start(bf16[20,2432]{1,0:T(8,128)(2,1)} %get-tuple-element.52), channel_id=1, source_target_pairs={{0,3},{1,0},{2,1},{3,2},{4,7},{5,4},{6,5},{7,6},{8,11},{9,8},{10,9... | collective-permute-start | bytes 291848 | tf_op jit(solution)/shard_map/ppermute | solution.py:30
  66.1 9.2 %collective-permute-start.4 = (bf16[20,2432]{1,0:T(8,128)(2,1)}, bf16[20,2432]{1,0:T(8,128)(2,1)}, u32[]{:S(2)}, u32[]{:S(2)}) collective-permute-start(bf16[20,2432]{1,0:T(8,128)(2,1)} %get-tuple-element.53), channel_id=1, source_target_pairs={{0,2},{1,3},{2,0},{3,1},{4,6},{5,7},{6,4},{7,5},{8,10},{9,11},{10,... | collective-permute-start | bytes 291848 | tf_op jit(solution)/shard_map/ppermute | solution.py:30
  67.0 8.3 %collective-permute-start.5 = (bf16[20,2432]{1,0:T(8,128)(2,1)}, bf16[20,2432]{1,0:T(8,128)(2,1)}, u32[]{:S(2)}, u32[]{:S(2)}) collective-permute-start(bf16[20,2432]{1,0:T(8,128)(2,1)} %get-tuple-element.54), channel_id=1, source_target_pairs={{0,1},{1,2},{2,3},{3,0},{4,5},{5,6},{6,7},{7,4},{8,9},{9,10},{10,1... | collective-permute-start | bytes 291848 | tf_op jit(solution)/shard_map/ppermute | solution.py:30
  68.2 13.9 %all-to-all-start.3 = ((bf16[16,32,192]{2,1,0:T(8,128)(2,1)}), bf16[16,32,192]{2,1,0:T(8,128)(2,1)S(1)}, u32[]{:S(2)}, u32[]{:S(2)}) async-start(bf16[16,32,192]{2,1,0:T(8,128)(2,1)} %shard_map.165.refs_5_), calls=%async_computation.3 | async-start | bytes 524288 | tf_op jit(solution)/shard_map/all_to_all | solution.py:504
  73.7 17.4 %copy-start.32 = (f32[2,2,64]{2,1,0:T(2,128)S(1)}, f32[2,2,64]{2,1,0:T(2,128)}, u32[]{:S(2)}) copy-start(f32[2,2,64]{2,1,0:T(2,128)} %param.20) | copy-start | bytes 3076
  78.3 5.7 %collective-permute-start.6 = (bf16[20,2432]{1,0:T(8,128)(2,1)S(1)}, bf16[20,2432]{1,0:T(8,128)(2,1)S(1)}, u32[]{:S(2)}, u32[]{:S(2)}) collective-permute-start(bf16[20,2432]{1,0:T(8,128)(2,1)S(1)} %get-tuple-element.56.refs_0_), channel_id=1, source_target_pairs={{0,3},{1,0},{2,1},{3,2},{4,7},{5,4},{6,5},{7,6},{8,11},{9,8},{10,9... | collective-permute-start | bytes 291848 | tf_op jit(solution)/shard_map/ppermute | solution.py:30
  81.0 5.3 %collective-permute-start.7 = (bf16[20,2432]{1,0:T(8,128)(2,1)S(1)}, bf16[20,2432]{1,0:T(8,128)(2,1)S(1)}, u32[]{:S(2)}, u32[]{:S(2)}) collective-permute-start(bf16[20,2432]{1,0:T(8,128)(2,1)S(1)} %get-tuple-element.56.refs_0_), channel_id=1, source_target_pairs={{0,2},{1,3},{2,0},{3,1},{4,6},{5,7},{6,4},{7,5},{8,10},{9,11},{10,... | collective-permute-start | bytes 291848 | tf_op jit(solution)/shard_map/ppermute | solution.py:30
  81.6 5.8 %collective-permute-start.8 = (bf16[20,2432]{1,0:T(8,128)(2,1)S(1)}, bf16[20,2432]{1,0:T(8,128)(2,1)S(1)}, u32[]{:S(2)}, u32[]{:S(2)}) collective-permute-start(bf16[20,2432]{1,0:T(8,128)(2,1)S(1)} %get-tuple-element.56.refs_0_), channel_id=1, source_target_pairs={{0,1},{1,2},{2,3},{3,0},{4,5},{5,6},{6,7},{7,4},{8,9},{9,10},{10,1... | collective-permute-start | bytes 291848 | tf_op jit(solution)/shard_map/ppermute | solution.py:30
  82.1 9.8 %copy-start.9 = (bf16[16,32,192]{2,1,0:T(8,128)(2,1)}, bf16[16,32,192]{2,1,0:T(8,128)(2,1)S(1)}, u32[]{:S(2)}) copy-start(bf16[16,32,192]{2,1,0:T(8,128)(2,1)S(1)} %all-to-all-done.3) | copy-start | bytes 589828
  87.5 11.5 %collective-permute-start.9 = (bf16[80,2432]{1,0:T(8,128)(2,1)S(1)}, bf16[80,2432]{1,0:T(8,128)(2,1)S(1)}, u32[]{:S(2)}, u32[]{:S(2)}) collective-permute-start(bf16[80,2432]{1,0:T(8,128)(2,1)S(1)} %shard_map.168.refs_0_), channel_id=1, source_target_pairs={{0,12},{1,13},{2,14},{3,15},{4,0},{5,1},{6,2},{7,3},{8,4},{9,5},{1... | collective-permute-start | bytes 1167368 | tf_op jit(solution)/shard_map/ppermute | solution.py:30
  90.2 8.8 %collective-permute-start.10 = (bf16[80,2432]{1,0:T(8,128)(2,1)S(1)}, bf16[80,2432]{1,0:T(8,128)(2,1)S(1)}, u32[]{:S(2)}, u32[]{:S(2)}) collective-permute-start(bf16[80,2432]{1,0:T(8,128)(2,1)S(1)} %shard_map.168.refs_0_), channel_id=1, source_target_pairs={{0,8},{1,9},{2,10},{3,11},{4,12},{5,13},{6,14},{7,15},{8,0},{9,1},... | collective-permute-start | bytes 1167368 | tf_op jit(solution)/shard_map/ppermute | solution.py:30
  90.5 12.3 %collective-permute-start.11 = (bf16[80,2432]{1,0:T(8,128)(2,1)S(1)}, bf16[80,2432]{1,0:T(8,128)(2,1)}, u32[]{:S(2)}, u32[]{:S(2)}) collective-permute-start(bf16[80,2432]{1,0:T(8,128)(2,1)S(1)} %shard_map.168.refs_0_), channel_id=1, source_target_pairs={{0,4},{1,5},{2,6},{3,7},{4,8},{5,9},{6,10},{7,11},{8,12},{9,13},{1... | collective-permute-start | bytes 1167368 | tf_op jit(solution)/shard_map/ppermute | solution.py:30
  103.9 1.5 copy-start.13
  105.4 21.2 %copy-start.11 = (bf16[512,512]{1,0:T(8,128)(2,1)S(1)}, bf16[512,512]{1,0:T(8,128)(2,1)}, u32[]{:S(2)}) copy-start(bf16[512,512]{1,0:T(8,128)(2,1)} %shard_map.167.refs_7_.refs_1_) | copy-start | bytes 1572868
  105.4 21.2 %copy-start.30 = (bf16[128,2432]{1,0:T(8,128)(2,1)S(1)}, bf16[128,2432]{1,0:T(8,128)(2,1)}, u32[]{:S(2)}) copy-start(bf16[128,2432]{1,0:T(8,128)(2,1)} %refs_3_.1) | copy-start | bytes 1867780
  130.0 12.5 %copy-start.18 = (bf16[128,2432]{1,0:T(8,128)(2,1)}, bf16[128,2432]{1,0:T(8,128)(2,1)S(1)}, u32[]{:S(2)}) copy-start(bf16[128,2432]{1,0:T(8,128)(2,1)S(1)} %get-tuple-element.58.refs_0_) | copy-start | bytes 1867780
  130.0 12.5 %copy-start.17 = (bf16[128,2432]{1,0:T(8,128)(2,1)S(1)}, bf16[128,2432]{1,0:T(8,128)(2,1)}, u32[]{:S(2)}) copy-start(bf16[128,2432]{1,0:T(8,128)(2,1)} %refs_2_.3) | copy-start | bytes 1867780
  130.0 12.5 %collective-permute-start.12 = (bf16[128,2432]{1,0:T(8,128)(2,1)S(1)}, bf16[128,2432]{1,0:T(8,128)(2,1)S(1)}, u32[]{:S(2)}, u32[]{:S(2)}) collective-permute-start(bf16[128,2432]{1,0:T(8,128)(2,1)S(1)} %get-tuple-element.59), channel_id=1, source_target_pairs={{0,12},{1,13},{2,14},{3,15},{4,0},{5,1},{6,2},{7,3},{8,4},{9,5},{1... | collective-permute-start | bytes 1867784 | tf_op jit(solution)/shard_map/ppermute | solution.py:30
  130.3 19.6 %collective-permute-start.13 = (bf16[128,2432]{1,0:T(8,128)(2,1)}, bf16[128,2432]{1,0:T(8,128)(2,1)}, u32[]{:S(2)}, u32[]{:S(2)}) collective-permute-start(bf16[128,2432]{1,0:T(8,128)(2,1)} %get-tuple-element.60), channel_id=1, source_target_pairs={{0,8},{1,9},{2,10},{3,11},{4,12},{5,13},{6,14},{7,15},{8,0},{9,1},... | collective-permute-start | bytes 1867784 | tf_op jit(solution)/shard_map/ppermute | solution.py:30
  130.9 19.0 %collective-permute-start.14 = (bf16[128,2432]{1,0:T(8,128)(2,1)}, bf16[128,2432]{1,0:T(8,128)(2,1)}, u32[]{:S(2)}, u32[]{:S(2)}) collective-permute-start(bf16[128,2432]{1,0:T(8,128)(2,1)} %get-tuple-element.61), channel_id=1, source_target_pairs={{0,4},{1,5},{2,6},{3,7},{4,8},{5,9},{6,10},{7,11},{8,12},{9,13},{1... | collective-permute-start | bytes 1867784 | tf_op jit(solution)/shard_map/ppermute | solution.py:30
  131.5 90.7 %slice-start = ((s8[5914624]{0:T(1024)(128)(4,1)}), s8[1720320]{0:T(1024)(128)(4,1)S(1)}, s32[]{:S(2)}) async-start(s8[5914624]{0:T(1024)(128)(4,1)} %bitcast.21), calls=%async_computation.7 | async-start | bytes 3440640
  146.1 7.2 %collective-permute-start.15 = (bf16[80,2432]{1,0:T(8,128)(2,1)}, bf16[80,2432]{1,0:T(8,128)(2,1)}, u32[]{:S(2)}, u32[]{:S(2)}) collective-permute-start(bf16[80,2432]{1,0:T(8,128)(2,1)} %get-tuple-element.64), channel_id=1, source_target_pairs={{0,12},{1,13},{2,14},{3,15},{4,0},{5,1},{6,2},{7,3},{8,4},{9,5},{1... | collective-permute-start | bytes 1167368 | tf_op jit(solution)/shard_map/ppermute | solution.py:30
  146.6 8.7 %collective-permute-start.16 = (bf16[80,2432]{1,0:T(8,128)(2,1)}, bf16[80,2432]{1,0:T(8,128)(2,1)}, u32[]{:S(2)}, u32[]{:S(2)}) collective-permute-start(bf16[80,2432]{1,0:T(8,128)(2,1)} %get-tuple-element.65), channel_id=1, source_target_pairs={{0,8},{1,9},{2,10},{3,11},{4,12},{5,13},{6,14},{7,15},{8,0},{9,1},... | collective-permute-start | bytes 1167368 | tf_op jit(solution)/shard_map/ppermute | solution.py:30
  147.5 12.0 %collective-permute-start.17 = (bf16[80,2432]{1,0:T(8,128)(2,1)}, bf16[80,2432]{1,0:T(8,128)(2,1)}, u32[]{:S(2)}, u32[]{:S(2)}) collective-permute-start(bf16[80,2432]{1,0:T(8,128)(2,1)} %get-tuple-element.66), channel_id=1, source_target_pairs={{0,4},{1,5},{2,6},{3,7},{4,8},{5,9},{6,10},{7,11},{8,12},{9,13},{1... | collective-permute-start | bytes 1167368 | tf_op jit(solution)/shard_map/ppermute | solution.py:30
  162.6 59.6 %slice-start.1 = ((s8[5914624]{0:T(1024)(128)(4,1)}), s8[4194304]{0:T(1024)(128)(4,1)S(1)}, s32[]{:S(2)}) async-start(s8[5914624]{0:T(1024)(128)(4,1)} %bitcast.21), calls=%async_computation.8 | async-start | bytes 8388608
  165.3 8.3 %collective-permute-start.18 = (bf16[52,2432]{1,0:T(8,128)(2,1)S(1)}, bf16[52,2432]{1,0:T(8,128)(2,1)S(1)}, u32[]{:S(2)}, u32[]{:S(2)}) collective-permute-start(bf16[52,2432]{1,0:T(8,128)(2,1)S(1)} %get-tuple-element.68), channel_id=1, source_target_pairs={{0,3},{1,0},{2,1},{3,2},{4,7},{5,4},{6,5},{7,6},{8,11},{9,8},{10,9... | collective-permute-start | bytes 758792 | tf_op jit(solution)/shard_map/ppermute | solution.py:30
  167.3 7.2 %collective-permute-start.19 = (bf16[52,2432]{1,0:T(8,128)(2,1)S(1)}, bf16[52,2432]{1,0:T(8,128)(2,1)S(1)}, u32[]{:S(2)}, u32[]{:S(2)}) collective-permute-start(bf16[52,2432]{1,0:T(8,128)(2,1)S(1)} %get-tuple-element.69), channel_id=1, source_target_pairs={{0,2},{1,3},{2,0},{3,1},{4,6},{5,7},{6,4},{7,5},{8,10},{9,11},{10,... | collective-permute-start | bytes 758792 | tf_op jit(solution)/shard_map/ppermute | solution.py:30
  168.2 9.2 %collective-permute-start.20 = (bf16[52,2432]{1,0:T(8,128)(2,1)S(1)}, bf16[52,2432]{1,0:T(8,128)(2,1)S(1)}, u32[]{:S(2)}, u32[]{:S(2)}) collective-permute-start(bf16[52,2432]{1,0:T(8,128)(2,1)S(1)} %get-tuple-element.70), channel_id=1, source_target_pairs={{0,1},{1,2},{2,3},{3,0},{4,5},{5,6},{6,7},{7,4},{8,9},{9,10},{10,1... | collective-permute-start | bytes 758792 | tf_op jit(solution)/shard_map/ppermute | solution.py:30
  177.9 5.4 %collective-permute-start.21 = (bf16[52,2432]{1,0:T(8,128)(2,1)S(1)}, bf16[52,2432]{1,0:T(8,128)(2,1)S(1)}, u32[]{:S(2)}, u32[]{:S(2)}) collective-permute-start(bf16[52,2432]{1,0:T(8,128)(2,1)S(1)} %get-tuple-element.73.refs_0_), channel_id=1, source_target_pairs={{0,3},{1,0},{2,1},{3,2},{4,7},{5,4},{6,5},{7,6},{8,11},{9,8},{10,9... | collective-permute-start | bytes 758792 | tf_op jit(solution)/shard_map/ppermute | solution.py:30
  178.3 6.9 %collective-permute-start.22 = (bf16[52,2432]{1,0:T(8,128)(2,1)S(1)}, bf16[52,2432]{1,0:T(8,128)(2,1)S(1)}, u32[]{:S(2)}, u32[]{:S(2)}) collective-permute-start(bf16[52,2432]{1,0:T(8,128)(2,1)S(1)} %get-tuple-element.73.refs_0_), channel_id=1, source_target_pairs={{0,2},{1,3},{2,0},{3,1},{4,6},{5,7},{6,4},{7,5},{8,10},{9,11},{10,... | collective-permute-start | bytes 758792 | tf_op jit(solution)/shard_map/ppermute | solution.py:30
  179.2 9.2 %collective-permute-start.23 = (bf16[52,2432]{1,0:T(8,128)(2,1)S(1)}, bf16[52,2432]{1,0:T(8,128)(2,1)S(1)}, u32[]{:S(2)}, u32[]{:S(2)}) collective-permute-start(bf16[52,2432]{1,0:T(8,128)(2,1)S(1)} %get-tuple-element.73.refs_0_), channel_id=1, source_target_pairs={{0,1},{1,2},{2,3},{3,0},{4,5},{5,6},{6,7},{7,4},{8,9},{9,10},{10,1... | collective-permute-start | bytes 758792 | tf_op jit(solution)/shard_map/ppermute | solution.py:30
  188.4 6.7 %collective-permute-start.24 = (bf16[80,2432]{1,0:T(8,128)(2,1)S(1)}, bf16[80,2432]{1,0:T(8,128)(2,1)S(1)}, u32[]{:S(2)}, u32[]{:S(2)}) collective-permute-start(bf16[80,2432]{1,0:T(8,128)(2,1)S(1)} %shard_map.175.in0), channel_id=1, source_target_pairs={{0,12},{1,13},{2,14},{3,15},{4,0},{5,1},{6,2},{7,3},{8,4},{9,5},{1... | collective-permute-start | bytes 1167368 | tf_op jit(solution)/shard_map/ppermute | solution.py:30
  195.1 33.5 %collective-permute-start.25 = (bf16[128,2432]{1,0:T(8,128)(2,1)S(1)}, bf16[128,2432]{1,0:T(8,128)(2,1)S(1)}, u32[]{:S(2)}, u32[]{:S(2)}) collective-permute-start(bf16[128,2432]{1,0:T(8,128)(2,1)S(1)} %shard_map.176.in0), channel_id=1, source_target_pairs={{0,12},{1,13},{2,14},{3,15},{4,0},{5,1},{6,2},{7,3},{8,4},{9,5},{1... | collective-permute-start | bytes 1867784 | tf_op jit(solution)/shard_map/ppermute | solution.py:30
  196.4 32.2 %collective-permute-start.26 = (bf16[128,2432]{1,0:T(8,128)(2,1)S(1)}, bf16[128,2432]{1,0:T(8,128)(2,1)S(1)}, u32[]{:S(2)}, u32[]{:S(2)}) collective-permute-start(bf16[128,2432]{1,0:T(8,128)(2,1)S(1)} %shard_map.176.in0), channel_id=1, source_target_pairs={{0,8},{1,9},{2,10},{3,11},{4,12},{5,13},{6,14},{7,15},{8,0},{9,1},... | collective-permute-start | bytes 1867784 | tf_op jit(solution)/shard_map/ppermute | solution.py:30
  196.6 32.1 %collective-permute-start.27 = (bf16[128,2432]{1,0:T(8,128)(2,1)S(1)}, bf16[128,2432]{1,0:T(8,128)(2,1)S(1)}, u32[]{:S(2)}, u32[]{:S(2)}) collective-permute-start(bf16[128,2432]{1,0:T(8,128)(2,1)S(1)} %shard_map.176.in0), channel_id=1, source_target_pairs={{0,4},{1,5},{2,6},{3,7},{4,8},{5,9},{6,10},{7,11},{8,12},{9,13},{1... | collective-permute-start | bytes 1867784 | tf_op jit(solution)/shard_map/ppermute | solution.py:30
  197.1 20.9 %collective-permute-start.31 = (bf16[80,2432]{1,0:T(8,128)(2,1)S(1)}, bf16[80,2432]{1,0:T(8,128)(2,1)S(1)}, u32[]{:S(2)}, u32[]{:S(2)}) collective-permute-start(bf16[80,2432]{1,0:T(8,128)(2,1)S(1)} %shard_map.175.in0), channel_id=1, source_target_pairs={{0,8},{1,9},{2,10},{3,11},{4,12},{5,13},{6,14},{7,15},{8,0},{9,1},... | collective-permute-start | bytes 1167368 | tf_op jit(solution)/shard_map/ppermute | solution.py:30
  200.2 21.9 %collective-permute-start.32 = (bf16[80,2432]{1,0:T(8,128)(2,1)S(1)}, bf16[80,2432]{1,0:T(8,128)(2,1)S(1)}, u32[]{:S(2)}, u32[]{:S(2)}) collective-permute-start(bf16[80,2432]{1,0:T(8,128)(2,1)S(1)} %shard_map.175.in0), channel_id=1, source_target_pairs={{0,4},{1,5},{2,6},{3,7},{4,8},{5,9},{6,10},{7,11},{8,12},{9,13},{1... | collective-permute-start | bytes 1167368 | tf_op jit(solution)/shard_map/ppermute | solution.py:30
  222.2 2.7 copy-start
  228.0 13.4 %collective-permute-start.33 = (bf16[80,2432]{1,0:T(8,128)(2,1)S(1)}, bf16[80,2432]{1,0:T(8,128)(2,1)S(1)}, u32[]{:S(2)}, u32[]{:S(2)}) collective-permute-start(bf16[80,2432]{1,0:T(8,128)(2,1)S(1)} %get-tuple-element.79), channel_id=1, source_target_pairs={{0,12},{1,13},{2,14},{3,15},{4,0},{5,1},{6,2},{7,3},{8,4},{9,5},{1... | collective-permute-start | bytes 1167368 | tf_op jit(solution)/shard_map/ppermute | solution.py:30
  228.7 2.7 copy-start.1
  236.3 26.1 %collective-permute-start.28 = (bf16[128,2432]{1,0:T(8,128)(2,1)S(1)}, bf16[128,2432]{1,0:T(8,128)(2,1)S(1)}, u32[]{:S(2)}, u32[]{:S(2)}) collective-permute-start(bf16[128,2432]{1,0:T(8,128)(2,1)S(1)} %get-tuple-element.75), channel_id=1, source_target_pairs={{0,12},{1,13},{2,14},{3,15},{4,0},{5,1},{6,2},{7,3},{8,4},{9,5},{1... | collective-permute-start | bytes 1867784 | tf_op jit(solution)/shard_map/ppermute | solution.py:30
  236.4 26.0 %collective-permute-start.29 = (bf16[128,2432]{1,0:T(8,128)(2,1)S(1)}, bf16[128,2432]{1,0:T(8,128)(2,1)S(1)}, u32[]{:S(2)}, u32[]{:S(2)}) collective-permute-start(bf16[128,2432]{1,0:T(8,128)(2,1)S(1)} %get-tuple-element.76), channel_id=1, source_target_pairs={{0,8},{1,9},{2,10},{3,11},{4,12},{5,13},{6,14},{7,15},{8,0},{9,1},... | collective-permute-start | bytes 1867784 | tf_op jit(solution)/shard_map/ppermute | solution.py:30
  239.1 23.3 %collective-permute-start.30 = (bf16[128,2432]{1,0:T(8,128)(2,1)S(1)}, bf16[128,2432]{1,0:T(8,128)(2,1)S(1)}, u32[]{:S(2)}, u32[]{:S(2)}) collective-permute-start(bf16[128,2432]{1,0:T(8,128)(2,1)S(1)} %get-tuple-element.77), channel_id=1, source_target_pairs={{0,4},{1,5},{2,6},{3,7},{4,8},{5,9},{6,10},{7,11},{8,12},{9,13},{1... | collective-permute-start | bytes 1867784 | tf_op jit(solution)/shard_map/ppermute | solution.py:30
  239.1 19.0 %collective-permute-start.34 = (bf16[80,2432]{1,0:T(8,128)(2,1)S(1)}, bf16[80,2432]{1,0:T(8,128)(2,1)S(1)}, u32[]{:S(2)}, u32[]{:S(2)}) collective-permute-start(bf16[80,2432]{1,0:T(8,128)(2,1)S(1)} %get-tuple-element.80), channel_id=1, source_target_pairs={{0,8},{1,9},{2,10},{3,11},{4,12},{5,13},{6,14},{7,15},{8,0},{9,1},... | collective-permute-start | bytes 1167368 | tf_op jit(solution)/shard_map/ppermute | solution.py:30
  241.4 20.9 %collective-permute-start.35 = (bf16[80,2432]{1,0:T(8,128)(2,1)S(1)}, bf16[80,2432]{1,0:T(8,128)(2,1)S(1)}, u32[]{:S(2)}, u32[]{:S(2)}) collective-permute-start(bf16[80,2432]{1,0:T(8,128)(2,1)S(1)} %get-tuple-element.81), channel_id=1, source_target_pairs={{0,4},{1,5},{2,6},{3,7},{4,8},{5,9},{6,10},{7,11},{8,12},{9,13},{1... | collective-permute-start | bytes 1167368 | tf_op jit(solution)/shard_map/ppermute | solution.py:30
  263.4 5.7 %collective-permute-start.36 = (bf16[52,2432]{1,0:T(8,128)(2,1)S(1)}, bf16[52,2432]{1,0:T(8,128)(2,1)S(1)}, u32[]{:S(2)}, u32[]{:S(2)}) collective-permute-start(bf16[52,2432]{1,0:T(8,128)(2,1)S(1)} %get-tuple-element.83), channel_id=1, source_target_pairs={{0,3},{1,0},{2,1},{3,2},{4,7},{5,4},{6,5},{7,6},{8,11},{9,8},{10,9... | collective-permute-start | bytes 758792 | tf_op jit(solution)/shard_map/ppermute | solution.py:30
  264.0 8.4 %collective-permute-start.37 = (bf16[52,2432]{1,0:T(8,128)(2,1)S(1)}, bf16[52,2432]{1,0:T(8,128)(2,1)S(1)}, u32[]{:S(2)}, u32[]{:S(2)}) collective-permute-start(bf16[52,2432]{1,0:T(8,128)(2,1)S(1)} %get-tuple-element.84), channel_id=1, source_target_pairs={{0,2},{1,3},{2,0},{3,1},{4,6},{5,7},{6,4},{7,5},{8,10},{9,11},{10,... | collective-permute-start | bytes 758792 | tf_op jit(solution)/shard_map/ppermute | solution.py:30
  264.6 10.6 %collective-permute-start.38 = (bf16[52,2432]{1,0:T(8,128)(2,1)S(1)}, bf16[52,2432]{1,0:T(8,128)(2,1)S(1)}, u32[]{:S(2)}, u32[]{:S(2)}) collective-permute-start(bf16[52,2432]{1,0:T(8,128)(2,1)S(1)} %get-tuple-element.85), channel_id=1, source_target_pairs={{0,1},{1,2},{2,3},{3,0},{4,5},{5,6},{6,7},{7,4},{8,9},{9,10},{10,1... | collective-permute-start | bytes 758792 | tf_op jit(solution)/shard_map/ppermute | solution.py:30
  (14 other events, 12.9 us)

commit v2 on v1

--- a/solution.py
+++ b/solution.py
@@ -13,6 +13,8 @@
 ADAPTER_SCALE = 0.5
 SIDE = 4
 POOL = 20
+WIDTH = 2432
+EXTRA = 512
 F32 = jnp.float32
 BF16 = jnp.bfloat16
 
@@ -114,39 +116,73 @@
         out_ref[block] = held[...].astype(BF16)
 
 
-def embed_kernel(places_ref, arrived_ref, weight_ref, out0, out1, out2, out3, label_ref, held):
+def embed_kernel(
+    places_ref, arrived_ref, weight_ref, low_ref, out0, out1, out2, out3, label_ref, held
+):
     for far, out in enumerate((out0, out1, out2, out3)):
         for near in range(SIDE):
             place = far * SIDE + near
             block = arrived_ref[places_ref[place]].astype(F32)
             held[near * POOL : (near + 1) * POOL, :] = block[0:POOL]
             label_ref[place : place + 1, :] = block[POOL : POOL + 1]
-        out[...] = jnp.dot(
+        out[:, 0:WIDTH] = jnp.dot(
             held[...].astype(BF16), weight_ref[...], preferred_element_type=F32
         ).astype(BF16)
+        out[:, WIDTH:] = jnp.zeros((SIDE * POOL, EXTRA), BF16)
+        for near in range(SIDE):
+            left = WIDTH + near // 2 * 256
+            top = near % 2 * 32
+            out[top : top + 32, left : left + 192] = low_ref[places_ref[far * SIDE + near]]
 
 
 def middle_kernel(in0, in1, in2, in3, out0, out1, out2, out3, held):
     held[...] = total_of((in0, in1, in2, in3))
-    part = out0.shape[0]
-    for place, out in enumerate((out0, out1, out2, out3)):
-        out[...] = held[place * part : (place + 1) * part, :].astype(BF16)
+    for near, out in enumerate((out0, out1, out2, out3)):
+        out[:, 0:WIDTH] = held[near * POOL : (near + 1) * POOL, 0:WIDTH].astype(BF16)
+        left = WIDTH + near // 2 * 256
+        for half in range(2):
+            top = near % 2 * 32 + half * 16
+            out[0:16, WIDTH + half * 256 : WIDTH + half * 256 + 256] = held[
+                top : top + 16, left : left + 256
+            ].astype(BF16)
+        out[16:POOL, WIDTH:] = jnp.zeros((POOL - 16, EXTRA), BF16)
 
 
 def both_middle_kernel(*refs):
-    held = refs[12]
-    held[...] = total_of(refs[4:8])
-    total = total_of(refs[0:4])
-    for place, out in enumerate(refs[8:12]):
-        out[0:32, :] = total[place * 32 : (place + 1) * 32].astype(BF16)
-        out[32 : 32 + POOL, :] = held[place * POOL : (place + 1) * POOL, :].astype(BF16)
-
-
-def join_kernel(start, in0, in1, in2, in3, out_ref, held):
-    part = out_ref.shape[0] // SIDE
+    inputs, outs = refs[0:8], refs[8:12]
+    img, txt, held, sems = refs[12:16]
+    copies = []
+    for place in range(8):
+        target = img.at[place] if place < SIDE else txt.at[place - SIDE]
+        copies.append(pltpu.make_async_copy(inputs[place], target, sems.at[place]))
+    for copy in copies:
+        copy.start()
+    for copy in copies[0:SIDE]:
+        copy.wait()
+    for near, out in enumerate(outs):
+        rows = slice(near * 32, (near + 1) * 32)
+        total = img[0, rows, :].astype(F32) + img[1, rows, :].astype(F32)
+        total = total + (img[2, rows, :].astype(F32) + img[3, rows, :].astype(F32))
+        out[0:32, :] = total.astype(BF16)
+    for copy in copies[SIDE:]:
+        copy.wait()
+    total = txt[0].astype(F32) + txt[1].astype(F32)
+    held[...] = total + (txt[2].astype(F32) + txt[3].astype(F32))
+    for near, out in enumerate(outs):
+        out[32 : 32 + POOL, :] = held[near * POOL : (near + 1) * POOL, :].astype(BF16)
+
+
+def join_kernel(in0, in1, in2, in3, out_ref, held):
     for place, piece in enumerate((in0, in1, in2, in3)):
-        held[place * part : (place + 1) * part, :] = piece[start : start + part, :].astype(F32)
+        held[place * POOL : (place + 1) * POOL, :] = piece[...].astype(F32)
     out_ref[...] = held[...].astype(BF16)
+
+
+def both_join_kernel(in0, in1, in2, in3, out_ref, held):
+    for place, piece in enumerate((in0, in1, in2, in3)):
+        out_ref[place * 32 : (place + 1) * 32, :] = piece[0:32, :]
+        held[place * POOL : (place + 1) * POOL, :] = piece[32:, :].astype(F32)
+    out_ref[128:, :] = held[...].astype(BF16)
 
 
 def repeat_mod_kernel(mod_ref, out_ref):
@@ -170,9 +206,12 @@
 
 
 def embed_norm_kernel(in0, in1, in2, in3, mod_ref, embedded_ref, out_ref):
-    embedded = total_of((in0, in1, in2, in3)).astype(BF16)
+    total = total_of((in0, in1, in2, in3))
+    embedded = total[:, 0:WIDTH].astype(BF16)
     embedded_ref[...] = embedded
-    out_ref[...] = (normed(embedded.astype(F32)) * (1.0 + mod_ref[1]) + mod_ref[0]).astype(BF16)
+    modded = normed(embedded.astype(F32)) * (1.0 + mod_ref[1]) + mod_ref[0]
+    out_ref[:, 0:WIDTH] = modded.astype(BF16)
+    out_ref[:, WIDTH:] = total[:, WIDTH:].astype(BF16)
 
 
 def both_norm_kernel(
@@ -210,7 +249,7 @@
 def txt_qkv_kernel(in0, in1, in2, in3, weight_ref, gain_ref, slot_ref, out_ref, held, rows_ref):
     part = in0.shape[0]
     for place, piece in enumerate((in0, in1, in2, in3)):
-        rows_ref[place * part : (place + 1) * part, :] = piece[...]
+        rows_ref[place * part : (place + 1) * part, :] = piece[:, 0:WIDTH]
     projected, values = project(rows_ref[...], weight_ref)
     held[:, 0:128] = head_norm(projected[:, 0:128], gain_ref[0:1, :]).astype(BF16)
     held[:, 128:256] = head_norm(projected[:, 128:256], gain_ref[1:2, :]).astype(BF16)
@@ -233,7 +272,7 @@
     projected_ref[:, 256:384] = values
 
 
-def low_part_kernel(adapter_ref, tp_ref, mod_ref, down_ref, _, out_ref, wide):
+def low_part_kernel(adapter_ref, tp_ref, mod_ref, down_ref, out_ref, wide):
     depth = down_ref.shape[1]
     wide[...] = jnp.zeros_like(wide)
     start = pl.multiple_of(tp_ref[0] * depth, 8)
@@ -243,26 +282,30 @@
         out_ref[block] = low[block * 32 : (block + 1) * 32].astype(BF16)
 
 
-def low_sum_kernel(part_ref, out_ref):
-    total = part_ref[0].astype(F32)
-    for block in range(1, 16):
-        total = total + part_ref[block].astype(F32)
-    for block in range(16):
-        out_ref[block] = total.astype(BF16)
-
-
-def img_adapt_kernel(adapter_ref, low_ref, projected_ref, up_ref, gain_ref, out_ref, lift):
-    lift[...] = jnp.zeros_like(lift)
-    for part in range(3):
-        lift[part * 64 : (part + 1) * 64, part * 128 : (part + 1) * 128] = up_ref[0, part]
-    projected = projected_ref[...] + ADAPTER_SCALE * jnp.dot(
-        low_ref[...], lift[...], preferred_element_type=F32
-    )
-    out_ref[:, 0:128] = head_norm(projected[:, 0:128], gain_ref[0:1, :]).astype(BF16)
-    out_ref[:, 128:256] = head_norm(projected[:, 128:256], gain_ref[1:2, :]).astype(BF16)
-    val0, val1 = with_keep(projected[:, 256:384], 1.0)
-    out_ref[:, 256:384] = val0.astype(BF16)
-    out_ref[:, 384:512] = val1.astype(BF16)
+def img_adapt_kernel(
+    places_ref, in0, in1, in2, in3, projected_ref, up0_ref, up1_ref, gain_ref,
+    out_ref, low, lift,
+):
+    for far, piece in enumerate((in0, in1, in2, in3)):
+        wide = piece[:, WIDTH:].astype(F32)
+        for near in range(SIDE):
+            rows = wide[near * POOL : near * POOL + 16]
+            start = pl.multiple_of(places_ref[far * SIDE + near] * 32, 32)
+            low[pl.ds(start, 16), :] = rows[:, 0:192]
+            low[pl.ds(start + 16, 16), :] = rows[:, 256:448]
+    for own, up_ref in enumerate((up0_ref, up1_ref)):
+        lift[...] = jnp.zeros_like(lift)
+        for part in range(3):
+            lift[part * 64 : (part + 1) * 64, part * 128 : (part + 1) * 128] = up_ref[0, part]
+        rows = slice(own * 256, (own + 1) * 256)
+        projected = projected_ref[rows, :] + ADAPTER_SCALE * jnp.dot(
+            low[rows, :].astype(BF16), lift[...], preferred_element_type=F32
+        )
+        out_ref[rows, 0:128] = head_norm(projected[:, 0:128], gain_ref[0:1, :]).astype(BF16)
+        out_ref[rows, 128:256] = head_norm(projected[:, 128:256], gain_ref[1:2, :]).astype(BF16)
+        val0, val1 = with_keep(projected[:, 256:384], 1.0)
+        out_ref[rows, 256:384] = val0.astype(BF16)
+        out_ref[rows, 384:512] = val1.astype(BF16)
 
 
 def attend(queries, tokens):
@@ -322,10 +365,12 @@
         out[...] = result[place * part : (place + 1) * part].astype(BF16)
 
 
-def feed_kernel(in0, in1, in2, in3, win_ref, wout_ref, out0, out1, out2, out3, rows_ref):
-    part = in0.shape[0]
+def feed_kernel(
+    start, in0, in1, in2, in3, win_ref, wout_ref, _, out0, out1, out2, out3, rows_ref
+):
+    part = out0.shape[0]
     for place, piece in enumerate((in0, in1, in2, in3)):
-        rows_ref[place * part : (place + 1) * part, :] = piece[...]
+        rows_ref[place * part : (place + 1) * part, :] = piece[start : start + part, :]
     hidden = lax.dot_general(
         rows_ref[...], win_ref[0], (((1,), (1,)), ((), ())), preferred_element_type=F32
     )
@@ -345,60 +390,67 @@
     placed_ref[...] = jnp.dot(hot, rows.astype(BF16), preferred_element_type=F32).astype(BF16)
 
 
-def middle(parts, after=()):
+def middle(parts):
     rows, width = parts[0].shape
     return run(
         middle_kernel,
         [like((rows // SIDE, width))] * SIDE,
         parts,
         scratch=[pltpu.VMEM((rows, width), F32)],
-        after=after,
     )
 
 
 def both_middle(img_parts, txt_parts):
+    parts = (*img_parts, *txt_parts)
     rows, width = txt_parts[0].shape
-    return run(
+    return pl.pallas_call(
         both_middle_kernel,
-        [like((32 + POOL, width))] * SIDE,
-        (*img_parts, *txt_parts),
-        scratch=[pltpu.VMEM((rows, width), F32)],
-    )
-
-
-def join(parts, start, count, after=()):
+        out_shape=[like((32 + POOL, width))] * SIDE,
+        in_specs=[pl.BlockSpec(memory_space=pl.ANY)] * len(parts),
+        out_specs=[pl.BlockSpec(memory_space=pltpu.VMEM)] * SIDE,
+        scratch_shapes=[
+            pltpu.VMEM((SIDE, *img_parts[0].shape), BF16),
+            pltpu.VMEM((SIDE, rows, width), BF16),
+            pltpu.VMEM((rows, width), F32),
+            pltpu.SemaphoreType.DMA((8,)),
+        ],
+        compiler_params=pltpu.CompilerParams(vmem_limit_bytes=16 << 20),
+        cost_estimate=pl.CostEstimate(flops=0, bytes_accessed=6 << 20, transcendentals=0),
+    )(*parts)
+
+
+def join(kernel, parts):
     width = parts[0].shape[1]
     return run(
-        functools.partial(join_kernel, start),
-        like((SIDE * count, width)),
+        kernel,
+        like((SIDE * parts[0].shape[0], width)),
         parts,
-        scratch=[pltpu.VMEM((SIDE * count, width), F32)],
-        after=after,
-    )
-
-
-def feed(parts, weight_in, weight_out, stream):
-    rows, width = parts[0].shape
+        scratch=[pltpu.VMEM((SIDE * POOL, width), F32)],
+    )
+
+
+def feed(parts, start, rows, weight_in, weight_out, stream, after):
+    count, width = parts[0].shape
     hidden = weight_in.shape[1]
-    plain = pl.BlockSpec((rows, width), lambda i: (0, 0))
     return pl.pallas_call(
-        feed_kernel,
+        functools.partial(feed_kernel, start),
         grid=(1,),
         out_shape=[like((rows, width))] * SIDE,
-        in_specs=[plain] * SIDE
+        in_specs=[pl.BlockSpec((count, width), lambda i: (0, 0))] * SIDE
         + [
             pl.BlockSpec((1, hidden, width), lambda i: (stream, 0, 0)),
             pl.BlockSpec((1, hidden, width), lambda i: (stream, 0, 0)),
+            pl.BlockSpec(memory_space=pl.ANY),
         ],
-        out_specs=[plain] * SIDE,
+        out_specs=[pl.BlockSpec((rows, width), lambda i: (0, 0))] * SIDE,
         scratch_shapes=[pltpu.VMEM((rows * SIDE, width), BF16)],
-        compiler_params=pltpu.CompilerParams(vmem_limit_bytes=32 << 20),
+        compiler_params=pltpu.CompilerParams(vmem_limit_bytes=36 << 20),
         cost_estimate=pl.CostEstimate(
             flops=rows * SIDE * width * hidden * 4,
             bytes_accessed=width * hidden * 4 + rows * width * 16,
             transcendentals=rows * SIDE * hidden,
         ),
-    )(*parts, weight_in, weight_out)
+    )(*parts, weight_in, weight_out, after)
 
 
 def shards(
@@ -467,15 +519,6 @@
         image_query_key_value.transpose(1, 0, 2),
         outgoing,
     )
-    *embed_parts, labels = run(
-        embed_kernel,
-        [like((SIDE * POOL, width))] * SIDE + [like((16, 256), F32)],
-        (places, arrived, prompt_embed_weight),
-        smem=1,
-        scratch=[pltpu.VMEM((SIDE * POOL, 256), F32)],
-        flops=320 * 256 * width * 2,
-        after=(img_projected,),
-    )
     half = image.shape[0] // 2
     low_part = pl.pallas_call(
         low_part_kernel,
@@ -485,7 +528,6 @@
             in_specs=[
                 pl.BlockSpec((half, width), lambda i, *_: (i, 0)),
                 pl.BlockSpec((1, *adapter_down.shape[1:]), lambda i, ids, _: (ids[i], 0, 0)),
-                pl.BlockSpec(memory_space=pl.ANY),
             ],
             out_specs=pl.BlockSpec((8, 32, 192), lambda i, *_: (i, 0, 0)),
             scratch_shapes=[pltpu.VMEM((width, 192), F32)],
@@ -495,14 +537,15 @@
         cost_estimate=pl.CostEstimate(
             flops=512 * width * 192 * 2, bytes_accessed=3 << 20, transcendentals=0
         ),
-    )(request_adapter, tp.reshape(1).astype(jnp.int32), img_mod, adapter_down, embed_parts[0])
-    low_sum = run(
-        low_sum_kernel,
-        like((16, 32, 192)),
-        (lax.all_to_all(low_part, "tp", 0, 0, tiled=True),),
-    )
-    low = lax.all_to_all(low_sum, "tp", 0, 0, tiled=True).reshape(2 * half, 192)
-
+    )(request_adapter, tp.reshape(1).astype(jnp.int32), img_mod, adapter_down)
+    *embed_parts, labels = run(
+        embed_kernel,
+        [like((SIDE * POOL, width + EXTRA))] * SIDE + [like((16, 256), F32)],
+        (places, arrived, prompt_embed_weight, low_part),
+        smem=1,
+        scratch=[pltpu.VMEM((SIDE * POOL, 256), F32)],
+        flops=320 * 256 * width * 2,
+    )
     mod_all = run(
         repeat_mod_kernel, like((8, 2, 8, width), F32), (modulation.transpose(0, 2, 1, 3),),
         after=(embed_parts[0],),
@@ -510,14 +553,13 @@
     mod_all = lax.all_to_all(mod_all, "grp", 0, 0, tiled=True).reshape(16, 8, width)
     row_mod = run(row_mod_kernel, like((6, POOL, width), F32), (request, mod_all), smem=1)
 
-    embed_sums = exchange(middle(exchange(embed_parts, 1), after=(low_part,)), 0)
+    embed_sums = exchange(middle(exchange(embed_parts, 1)), 0)
     embedded, txt_mod = run(
         embed_norm_kernel,
-        [like((POOL, width))] * 2,
+        [like((POOL, width)), like((POOL, width + EXTRA))],
         (*embed_sums, row_mod),
-        after=(low_sum,),
-    )
-    txt_mods = spread(join(spread(txt_mod, 0), 0, POOL, after=(low,)), 1)
+    )
+    txt_mods = spread(join(join_kernel, spread(txt_mod, 0)), 1)
 
     target = labels[:, :POOL].astype(jnp.int32)
     slots_all = target // 4 * 64 + target // 2 % 2 * 32 + target % 2
@@ -528,25 +570,28 @@
     ranked = jnp.sum(earlier.astype(jnp.int32), 1)
     slots_own = (request * CAP + ranked).reshape(1, POOL).astype(jnp.int32)
 
+    up_specs = [
+        pl.BlockSpec((1, 3, 64, 128), lambda i, ids, _: (ids[0], 0, 0, 0)),
+        pl.BlockSpec((1, 3, 64, 128), lambda i, ids, _: (ids[1], 0, 0, 0)),
+    ]
     img_parts = pl.pallas_call(
-        img_adapt_kernel,
+        lambda ids_ref, *refs: img_adapt_kernel(*refs),
         grid_spec=pltpu.PrefetchScalarGridSpec(
-            num_scalar_prefetch=1,
-            grid=(2,),
-            in_specs=[
-                pl.BlockSpec((half, 192), lambda i, _: (i, 0)),
-                pl.BlockSpec((half, 384), lambda i, _: (i, 0)),
-                pl.BlockSpec((1, 3, 64, 128), lambda i, ids: (ids[i], 0, 0, 0)),
-                pl.BlockSpec((2, 128), lambda i, _: (0, 0)),
-            ],
-            out_specs=pl.BlockSpec((half, 512), lambda i, _: (i, 0)),
-            scratch_shapes=[pltpu.VMEM((192, 384), BF16)],
+            num_scalar_prefetch=2,
+            grid=(1,),
+            in_specs=[pl.BlockSpec(txt_mods[0].shape, lambda i, *_: (0, 0))] * SIDE
+            + [pl.BlockSpec(img_projected.shape, lambda i, *_: (0, 0))]
+            + up_specs
+            + [pl.BlockSpec((2, 128), lambda i, *_: (0, 0))],
+            out_specs=pl.BlockSpec((2 * half, 512), lambda i, *_: (0, 0)),
+            scratch_shapes=[pltpu.VMEM((2 * half, 192), F32), pltpu.VMEM((192, 384), BF16)],
         ),
-        out_shape=like((image.shape[0], 512)),
+        out_shape=like((2 * half, 512)),
+        compiler_params=pltpu.CompilerParams(vmem_limit_bytes=24 << 20),
         cost_estimate=pl.CostEstimate(
-            flops=512 * 384 * 192 * 2, bytes_accessed=2 << 20, transcendentals=0
+            flops=512 * 384 * 192 * 2, bytes_accessed=4 << 20, transcendentals=0
         ),
-    )(request_adapter, low, img_projected, adapter_up, gains[0])
+    )(request_adapter, places, *txt_mods, img_projected, adapter_up, adapter_up, gains[0])
 
     slot_parts = run(
         txt_qkv_kernel,
@@ -554,7 +599,6 @@
         (*txt_mods, prompt_query_key_value.transpose(1, 0, 2), gains[1], slots_all),
         scratch=[pltpu.VMEM((16 * POOL, 384), BF16), pltpu.VMEM((16 * POOL, width), BF16)],
         flops=320 * width * 384 * 2,
-        after=(img_parts,),
     )
     slot_parts = lax.all_to_all(slot_parts.reshape(8, 64, 512), "grp", 0, 0, tiled=True)
 
@@ -590,12 +634,12 @@
         [like((32, width)), like((POOL, width)), like((32 + POOL, width))],
         (own_image, embedded, *sums, own_mod, row_mod),
     )
-    near_rows = spread(norm_rows, 0)
-    txt_rows = spread(join(near_rows, 32, POOL), 1)
-    img_rows = spread(join(near_rows, 0, 32, after=(txt_rows[1],)), 1)
+    rows = spread(join(both_join_kernel, spread(norm_rows, 0)), 1)
     weight_in = feed_in_weight.transpose(0, 2, 1)
-    img_terms = feed(img_rows, weight_in, feed_out_weight, 0)
-    txt_terms = feed(txt_rows, weight_in, feed_out_weight, 1)
+    img_terms = feed(rows, 0, 128, weight_in, feed_out_weight, 0, rows[1])
+    txt_terms = feed(
+        rows, 128, SIDE * POOL, weight_in, feed_out_weight, 1, img_terms[0]
+    )
     sums = exchange(both_middle(exchange(img_terms, 1), exchange(txt_terms, 1)), 0)
     image_out, placed = run(
         both_final_kernel,

time: 297 us -> 273 us (0.919)
  blocking collectives: 47.6 us -> 24.4 us
  starting transfers between devices: 61.6 us -> 54.6 us
  waiting for transfers between devices: 115 us -> 121 us
  Pallas kernels: 40.6 us -> 37.5 us
    all_to_all x1 -> x0, blocking collectives: 18.4 us -> none  [shards(): lax.all_to_all(slot_parts.reshape(8, 64, 512), 'grp', 0, 0, tiled=True)]
    ppermute x39 -> x36, waiting for transfers between devices: 108 us -> 118 us  [torus_shift(): return lax.ppermute(values, ('grp', 'tp'), pairs)]
    pallas_call x18 -> x14, Pallas kernels: 23.1 us -> 18 us  [run(): pl.pallas_call(body, out_shape=shapes, in_specs=specs, out_specs=[pl.Bloc...]
    unnamed x71 -> x85, local copies, waits for them, and re-layouts: 26.4 us -> 30.9 us
    all_to_all x1, blocking collectives: 19.3 us -> 14.9 us  [shards(): lax.all_to_all(placed.reshape(8, 4, width), 'grp', 0, 0, tiled=True)]
    all_to_all x2 -> x1, waiting for transfers between devices: 6.19 us -> 3.45 us  [shards(): lax.all_to_all(slot_parts.reshape(8, 64, 512), 'grp', 0, 0, tiled=True)]
    ppermute x39 -> x36, starting transfers between devices: 34 us -> 31.3 us  [torus_shift(): return lax.ppermute(values, ('grp', 'tp'), pairs)]
    all_to_all x2 -> x1, starting transfers between devices: 12.1 us -> 9.34 us  [shards(): lax.all_to_all(slot_parts.reshape(8, 64, 512), 'grp', 0, 0, tiled=True)]
  transfers between devices with their start and end apart: 43 -> 39, of which waited for: 27 -> 30; matrix products, arithmetic and copies ran while one was open for 1% -> 1% of each run, Pallas kernels for 8% -> 4%
where the time goes in v2:
time: 273 us; the launch traced here: 272 us
  waiting for transfers between devices  121 us (44%)
  starting transfers between devices  54.6 us (20%)
  Pallas kernels  37.5 us (14%)
  local copies, waits for them, and re-layouts  32.7 us (12%)
  blocking collectives  24.4 us (9%)
    ppermute x36, waiting for transfers between devices, torus_shift(): return lax.ppermute(values, ('grp', 'tp'), pairs)  118 us
    ppermute x36, starting transfers between devices, torus_shift(): return lax.ppermute(values, ('grp', 'tp'), pairs)  31.3 us
    unnamed x85, local copies, waits for them, and re-layouts  30.9 us
    pallas_call x14, Pallas kernels, run(): pl.pallas_call(body, out_shape=shapes, in_specs=specs, out_specs=[pl.Bloc...  18 us
    all_to_all x1, blocking collectives, shards(): lax.all_to_all(placed.reshape(8, 4, width), 'grp', 0, 0, tiled=True)  14.9 us
    all_to_all x1, blocking collectives, shards(): lax.all_to_all(att_parts, 'grp', 0, 0, tiled=True).reshape(512, 128)  9.44 us
    all_to_all x1, starting transfers between devices, shards(): lax.all_to_all(slot_parts.reshape(8, 64, 512), 'grp', 0, 0, tiled=True)  9.34 us
    all_to_all x1, starting transfers between devices, shards(): arrived = lax.all_to_all(outgoing, 'tp', 0, 0, tiled=True)  8.6 us
  transfers between devices with their start and end apart: 39, of which 30 were waited for; matrix products, arithmetic and copies ran while one was open for 1% of the time, Pallas kernels for 4%

profile of v2, /device:TPU:1, one launch (start us, length us, event | category | flops | bytes accessed | tf_op | source)
XLA Modules:
  0.0 271.6 jit_solution(17622529510609749889)
XLA Ops:
  3.1 8.6 %all-to-all-start = ((bf16[16,32,256]{2,1,0:T(8,128)(2,1)}), bf16[16,32,256]{2,1,0:T(8,128)(2,1)S(1)}, u32[]{:S(2)}, u32[]{:S(2)}) async-start(bf16[16,32,256]{2,1,0:T(8,128)(2,1)} %shard_map.158._), calls=%async_computation | async-start | bytes 524288 | tf_op jit(solution)/shard_map/all_to_all | solution.py:495
  11.8 1.7 copy-done.5
  13.5 1.5 copy-done.15
  15.9 3.5 %shard_map.159 = (bf16[512,2432]{1,0:T(8,128)(2,1)S(1)}, f32[512,384]{1,0:T(8,128)S(1)}) custom-call(bf16[512,2432]{1,0:T(8,128)(2,1)S(1)} %copy-done.5, f32[2,6,2,2432]{3,2,1,0:T(2,128)S(1)} %bitcast.27, bf16[3,2432,128]{2,1,0:T(8,128)(2,1)S(1)} %bitcast.25, bf16[16,32,256]{2,1,0:T(8,128)(2,1)} %shard_map.158._), custom_call_target="tpu_custom_call" | custom-call | flops 956301312 | bytes 7340032 | tf_op jit(solution)/shard_map/pallas_call | solution.py:498
  20.3 2.0 shard_map.160.refs_3_
  22.3 1.3 copy-done.20
  23.7 2.2 shard_map.161
  26.6 1.3 shard_map.163
  28.0 5.4 %all-to-all-start.1 = ((f32[8,2,8,2432]{3,2,1,0:T(8,128)}), f32[8,2,8,2432]{3,2,1,0:T(8,128)S(1)}, u32[]{:S(2)}, u32[]{:S(2)}) async-start(f32[8,2,8,2432]{3,2,1,0:T(8,128)} %shard_map.163), calls=%async_computation.1 | async-start | bytes 2490368 | tf_op jit(solution)/shard_map/all_to_all | solution.py:553
  33.4 2.8 %collective-permute-start = (bf16[80,2944]{1,0:T(8,128)(2,1)}, bf16[80,2944]{1,0:T(8,128)(2,1)S(1)}, u32[]{:S(2)}, u32[]{:S(2)}) collective-permute-start(bf16[80,2944]{1,0:T(8,128)(2,1)} %get-tuple-element.47), channel_id=1, source_target_pairs={{0,12},{1,13},{2,14},{3,15},{4,0},{5,1},{6,2},{7,3},{8,4},{9,5},{1... | collective-permute-start | bytes 1413128 | tf_op jit(solution)/shard_map/ppermute | solution.py:32
  37.4 9.8 %collective-permute-done.refs_1_ = bf16[80,2944]{1,0:T(8,128)(2,1)S(1)} collective-permute-done((bf16[80,2944]{1,0:T(8,128)(2,1)}, bf16[80,2944]{1,0:T(8,128)(2,1)S(1)}, u32[]{:S(2)}, u32[]{:S(2)}) %collective-permute-start) | collective-permute-done | bytes 471072 | tf_op jit(solution)/shard_map/ppermute | solution.py:32
  47.1 3.6 %collective-permute-done.2.refs_3_ = bf16[80,2944]{1,0:T(8,128)(2,1)S(1)} collective-permute-done((bf16[80,2944]{1,0:T(8,128)(2,1)}, bf16[80,2944]{1,0:T(8,128)(2,1)S(1)}, u32[]{:S(2)}, u32[]{:S(2)}) %collective-permute-start.2) | collective-permute-done | bytes 471072 | tf_op jit(solution)/shard_map/ppermute | solution.py:32
  50.7 1.1 shard_map.162
  51.9 2.4 collective-permute-start.3
  56.4 1.8 collective-permute-done.3.refs_1_
  58.1 1.9 collective-permute-done.4.refs_2_
  60.0 1.7 collective-permute-done.5.refs_3_
  64.1 2.5 collective-permute-done.6.refs_1_
  66.6 1.9 collective-permute-done.7.refs_2_
  68.5 1.7 collective-permute-done.8.refs_3_
  72.9 5.3 %collective-permute-done.9.refs_2_.refs_1_ = bf16[80,2944]{1,0:T(8,128)(2,1)S(1)} collective-permute-done((bf16[80,2944]{1,0:T(8,128)(2,1)S(1)}, bf16[80,2944]{1,0:T(8,128)(2,1)S(1)}, u32[]{:S(2)}, u32[]{:S(2)}) %collective-permute-start.9) | collective-permute-done | bytes 471072 | tf_op jit(solution)/shard_map/ppermute | solution.py:32
  78.1 1.9 collective-permute-done.10.refs_3_.refs_2_
  80.8 4.2 %collective-permute-done.11.refs_4_.refs_3_ = bf16[80,2944]{1,0:T(8,128)(2,1)S(1)} collective-permute-done((bf16[80,2944]{1,0:T(8,128)(2,1)S(1)}, bf16[80,2944]{1,0:T(8,128)(2,1)S(1)}, u32[]{:S(2)}, u32[]{:S(2)}) %collective-permute-start.11) | collective-permute-done | bytes 471072 | tf_op jit(solution)/shard_map/ppermute | solution.py:32
  88.9 1.5 copy-done.16
  90.4 2.4 shard_map.168
  92.8 9.3 %all-to-all-start.2 = ((bf16[8,64,512]{2,1,0:T(8,128)(2,1)}), bf16[8,64,512]{2,1,0:T(8,128)(2,1)}, u32[]{:S(2)}, u32[]{:S(2)}) async-start(bf16[8,64,512]{2,1,0:T(8,128)(2,1)} %bitcast.9), calls=%async_computation.2 | async-start | bytes 1048576 | tf_op jit(solution)/shard_map/all_to_all | solution.py:603
  105.2 1.1 copy-done.22
  106.4 1.1 shard_map.167.refs_1_
  108.3 3.5 %all-to-all-done.2.refs_2_ = bf16[8,64,512]{2,1,0:T(8,128)(2,1)} async-done(((bf16[8,64,512]{2,1,0:T(8,128)(2,1)}), bf16[8,64,512]{2,1,0:T(8,128)(2,1)}, u32[]{:S(2)}, u32[]{:S(2)}) %all-to-all-start.2) | async-done | bytes 524320 | tf_op jit(solution)/shard_map/all_to_all | solution.py:603
  113.9 4.0 %shard_map.169 = (bf16[128,2432]{1,0:T(8,128)(2,1)S(1)}, bf16[128,2432]{1,0:T(8,128)(2,1)}, bf16[128,2432]{1,0:T(8,128)(2,1)}, bf16[128,2432]{1,0:T(8,128)(2,1)S(1)}, bf16[2,512,512]{2,1,0:T(8,128)(2,1)S(1)}) custom-call(s32[16]{0:T(128)S(1)} %broadcast_select_fusion.refs_0_, bf16[512,512]{1,0:T(8,128)(2,1)S(1)} %copy-done.27, ...), custom_call_target="tpu_custom_call" | custom-call | flops 1073741824 | bytes 5210176 | tf_op jit(solution)/shard_map/pallas_call | solution.py:66
  119.7 1.1 shard_map.170
  120.8 9.4 %all_to_all.25 = bf16[8,64,128]{2,1,0:T(8,128)(2,1)S(1)} all-to-all(bf16[8,64,128]{2,1,0:T(8,128)(2,1)S(1)} %shard_map.170), channel_id=1, replica_groups=mesh['grp'=8,'tp'=16] {'grp'}, dimensions={0} | all-to-all | bytes 262144 | tf_op jit(solution)/shard_map/all_to_all | solution.py:619
  130.3 1.9 shard_map.171
  133.8 1.3 collective-permute-start.15
  136.7 4.3 %collective-permute-done.15.refs_5_ = bf16[80,2432]{1,0:T(8,128)(2,1)} collective-permute-done((bf16[80,2432]{1,0:T(8,128)(2,1)}, bf16[80,2432]{1,0:T(8,128)(2,1)}, u32[]{:S(2)}, u32[]{:S(2)}) %collective-permute-start.15) | collective-permute-done | bytes 389152 | tf_op jit(solution)/shard_map/ppermute | solution.py:32
  141.0 2.8 %collective-permute-done.16.refs_6_ = bf16[80,2432]{1,0:T(8,128)(2,1)} collective-permute-done((bf16[80,2432]{1,0:T(8,128)(2,1)}, bf16[80,2432]{1,0:T(8,128)(2,1)}, u32[]{:S(2)}, u32[]{:S(2)}) %collective-permute-start.16) | collective-permute-done | bytes 389152 | tf_op jit(solution)/shard_map/ppermute | solution.py:32
  143.8 4.1 %collective-permute-done.17.refs_7_ = bf16[80,2432]{1,0:T(8,128)(2,1)} collective-permute-done((bf16[80,2432]{1,0:T(8,128)(2,1)}, bf16[80,2432]{1,0:T(8,128)(2,1)}, u32[]{:S(2)}, u32[]{:S(2)}) %collective-permute-start.17) | collective-permute-done | bytes 389152 | tf_op jit(solution)/shard_map/ppermute | solution.py:32
  147.9 1.1 copy-done.8
  151.1 2.6 shard_map.172
  153.7 2.3 collective-permute-start.18
  158.0 4.3 %collective-permute-done.18.refs_3_ = bf16[52,2432]{1,0:T(8,128)(2,1)S(1)} collective-permute-done((bf16[52,2432]{1,0:T(8,128)(2,1)S(1)}, bf16[52,2432]{1,0:T(8,128)(2,1)S(1)}, u32[]{:S(2)}, u32[]{:S(2)}) %collective-permute-start.18) | collective-permute-done | bytes 252960 | tf_op jit(solution)/shard_map/ppermute | solution.py:32
  163.2 2.9 %collective-permute-done.20.refs_5_ = bf16[52,2432]{1,0:T(8,128)(2,1)S(1)} collective-permute-done((bf16[52,2432]{1,0:T(8,128)(2,1)S(1)}, bf16[52,2432]{1,0:T(8,128)(2,1)S(1)}, u32[]{:S(2)}, u32[]{:S(2)}) %collective-permute-start.20) | collective-permute-done | bytes 252960 | tf_op jit(solution)/shard_map/ppermute | solution.py:32
  168.2 4.1 %collective-permute-done.21.refs_1_ = bf16[52,2432]{1,0:T(8,128)(2,1)S(1)} collective-permute-done((bf16[52,2432]{1,0:T(8,128)(2,1)S(1)}, bf16[52,2432]{1,0:T(8,128)(2,1)S(1)}, u32[]{:S(2)}, u32[]{:S(2)}) %collective-permute-start.21) | collective-permute-done | bytes 252960 | tf_op jit(solution)/shard_map/ppermute | solution.py:32
  172.3 1.9 collective-permute-done.22.refs_2_
  174.1 2.9 %collective-permute-done.23.refs_3_ = bf16[52,2432]{1,0:T(8,128)(2,1)S(1)} collective-permute-done((bf16[52,2432]{1,0:T(8,128)(2,1)S(1)}, bf16[52,2432]{1,0:T(8,128)(2,1)S(1)}, u32[]{:S(2)}, u32[]{:S(2)}) %collective-permute-start.23) | collective-permute-done | bytes 252960 | tf_op jit(solution)/shard_map/ppermute | solution.py:32
  177.8 2.3 collective-permute-start.25
  180.2 10.6 %collective-permute-done.24.in1._ = bf16[208,2432]{1,0:T(8,128)(2,1)S(1)} collective-permute-done((bf16[208,2432]{1,0:T(8,128)(2,1)S(1)}, bf16[208,2432]{1,0:T(8,128)(2,1)S(1)}, u32[]{:S(2)}, u32[]{:S(2)}) %collective-permute-start.24) | collective-permute-done | bytes 1011744 | tf_op jit(solution)/shard_map/ppermute | solution.py:32
  190.8 2.2 collective-permute-done.25.in2
  192.9 10.8 %collective-permute-done.26.in3 = bf16[208,2432]{1,0:T(8,128)(2,1)S(1)} collective-permute-done((bf16[208,2432]{1,0:T(8,128)(2,1)S(1)}, bf16[208,2432]{1,0:T(8,128)(2,1)S(1)}, u32[]{:S(2)}, u32[]{:S(2)}) %collective-permute-start.26) | collective-permute-done | bytes 1011744 | tf_op jit(solution)/shard_map/ppermute | solution.py:32
  203.7 2.7 copy-done
  206.4 4.9 %shard_map.175 = (bf16[128,2432]{1,0:T(8,128)(2,1)S(1)}, bf16[128,2432]{1,0:T(8,128)(2,1)S(1)}, bf16[128,2432]{1,0:T(8,128)(2,1)S(1)}, bf16[128,2432]{1,0:T(8,128)(2,1)S(1)}) custom-call(bf16[208,2432]{1,0:T(8,128)(2,1)S(1)} %shard_map.174.in0, bf16[208,2432]{1,0:T(8,128)(2,1)S(1)} %collective-permute-done.24.in1._, ...), custom_call_target="tpu_custom_call" | custom-call | flops 3028287488 | bytes 10895360 | tf_op jit(solution)/shard_map/pallas_call | solution.py:435
  211.3 3.2 %shard_map.176 = (bf16[80,2432]{1,0:T(8,128)(2,1)S(1)}, bf16[80,2432]{1,0:T(8,128)(2,1)S(1)}, bf16[80,2432]{1,0:T(8,128)(2,1)S(1)}, bf16[80,2432]{1,0:T(8,128)(2,1)S(1)}) custom-call(bf16[208,2432]{1,0:T(8,128)(2,1)S(1)} %shard_map.174.in0, bf16[208,2432]{1,0:T(8,128)(2,1)S(1)} %collective-permute-done.24.in1._, ...), custom_call_target="tpu_custom_call" | custom-call | flops 1892679680 | bytes 9027584 | tf_op jit(solution)/shard_map/pallas_call | solution.py:435
  215.0 1.4 collective-permute-start.27
  216.4 1.5 collective-permute-start.28
  218.2 1.8 collective-permute-start.31
  220.0 1.2 collective-permute-done.30.refs_5_
  221.2 1.2 collective-permute-start.32
  222.4 15.6 %collective-permute-done.31.refs_6_ = bf16[80,2432]{1,0:T(8,128)(2,1)S(1)} collective-permute-done((bf16[80,2432]{1,0:T(8,128)(2,1)S(1)}, bf16[80,2432]{1,0:T(8,128)(2,1)S(1)}, u32[]{:S(2)}, u32[]{:S(2)}) %collective-permute-start.31) | collective-permute-done | bytes 389152 | tf_op jit(solution)/shard_map/ppermute | solution.py:32
  238.0 4.3 %collective-permute-done.32.refs_7_ = bf16[80,2432]{1,0:T(8,128)(2,1)S(1)} collective-permute-done((bf16[80,2432]{1,0:T(8,128)(2,1)S(1)}, bf16[80,2432]{1,0:T(8,128)(2,1)S(1)}, u32[]{:S(2)}, u32[]{:S(2)}) %collective-permute-start.32) | collective-permute-done | bytes 389152 | tf_op jit(solution)/shard_map/ppermute | solution.py:32
  242.3 2.2 shard_map.177
  246.2 3.7 %collective-permute-done.33.refs_3_ = bf16[52,2432]{1,0:T(8,128)(2,1)S(1)} collective-permute-done((bf16[52,2432]{1,0:T(8,128)(2,1)S(1)}, bf16[52,2432]{1,0:T(8,128)(2,1)S(1)}, u32[]{:S(2)}, u32[]{:S(2)}) %collective-permute-start.33) | collective-permute-done | bytes 252960 | tf_op jit(solution)/shard_map/ppermute | solution.py:32
  249.9 2.2 collective-permute-done.34.refs_4_
  252.1 2.8 %collective-permute-done.35.refs_5_ = bf16[52,2432]{1,0:T(8,128)(2,1)S(1)} collective-permute-done((bf16[52,2432]{1,0:T(8,128)(2,1)S(1)}, bf16[52,2432]{1,0:T(8,128)(2,1)S(1)}, u32[]{:S(2)}, u32[]{:S(2)}) %collective-permute-start.35) | collective-permute-done | bytes 252960 | tf_op jit(solution)/shard_map/ppermute | solution.py:32
  255.9 14.9 %all_to_all.26 = bf16[8,4,2432]{2,1,0:T(4,128)(2,1)S(1)} all-to-all(bf16[8,4,2432]{2,1,0:T(4,128)(2,1)S(1)} %reshape.60), channel_id=1, replica_groups=mesh['grp'=8,'tp'=16] {'grp'}, dimensions={0} | all-to-all | bytes 311296 | tf_op jit(solution)/shard_map/all_to_all | solution.py:650
  (135 shorter events, 41.1 us)
Async XLA Ops:
  3.1 19.2 %all-to-all-start = ((bf16[16,32,256]{2,1,0:T(8,128)(2,1)}), bf16[16,32,256]{2,1,0:T(8,128)(2,1)S(1)}, u32[]{:S(2)}, u32[]{:S(2)}) async-start(bf16[16,32,256]{2,1,0:T(8,128)(2,1)} %shard_map.158._), calls=%async_computation | async-start | bytes 524288 | tf_op jit(solution)/shard_map/all_to_all | solution.py:495
  11.8 1.7 copy-start.5
  13.5 1.5 copy-start.15
  15.9 4.4 %copy-start.6 = (bf16[32,152,192]{2,1,0:T(8,128)(2,1)S(1)}, bf16[32,152,192]{2,1,0:T(8,128)(2,1)}, u32[]{:S(2)}) copy-start(bf16[32,152,192]{2,1,0:T(8,128)(2,1)} %down_ref.1) | copy-start | bytes 5603332
  15.9 4.4 %copy-start.33 = (s32[2]{0:T(128)S(1)}, s32[2]{0:T(128)}, u32[]{:S(2)}) copy-start(s32[2]{0:T(128)} %ids_ref.1) | copy-start | bytes 28
  22.3 4.4 %copy-start.18 = (f32[2,2,6,2432]{3,1,2,0:T(2,128)S(1)}, f32[2,2,6,2432]{3,1,2,0:T(2,128)}, u32[]{:S(2)}) copy-start(f32[2,2,6,2432]{3,1,2,0:T(2,128)} %param.19) | copy-start | bytes 700420
  22.3 1.4 copy-start.20
  25.9 2.1 copy-start.37
  28.0 27.4 %copy-start.35 = (s32[20,1]{0,1:T(1,128)S(1)}, s32[20,1]{0,1:T(1,128)}, u32[]{:S(2)}) copy-start(s32[20,1]{0,1:T(1,128)} %param.17) | copy-start | bytes 244
  28.0 27.4 %all-to-all-start.1 = ((f32[8,2,8,2432]{3,2,1,0:T(8,128)}), f32[8,2,8,2432]{3,2,1,0:T(8,128)S(1)}, u32[]{:S(2)}, u32[]{:S(2)}) async-start(f32[8,2,8,2432]{3,2,1,0:T(8,128)} %shard_map.163), calls=%async_computation.1 | async-start | bytes 2490368 | tf_op jit(solution)/shard_map/all_to_all | solution.py:553
  33.4 13.7 %collective-permute-start = (bf16[80,2944]{1,0:T(8,128)(2,1)}, bf16[80,2944]{1,0:T(8,128)(2,1)S(1)}, u32[]{:S(2)}, u32[]{:S(2)}) collective-permute-start(bf16[80,2944]{1,0:T(8,128)(2,1)} %get-tuple-element.47), channel_id=1, source_target_pairs={{0,12},{1,13},{2,14},{3,15},{4,0},{5,1},{6,2},{7,3},{8,4},{9,5},{1... | collective-permute-start | bytes 1413128 | tf_op jit(solution)/shard_map/ppermute | solution.py:32
  36.2 10.9 %collective-permute-start.1 = (bf16[80,2944]{1,0:T(8,128)(2,1)}, bf16[80,2944]{1,0:T(8,128)(2,1)S(1)}, u32[]{:S(2)}, u32[]{:S(2)}) collective-permute-start(bf16[80,2944]{1,0:T(8,128)(2,1)} %copy-done.38), channel_id=1, source_target_pairs={{0,8},{1,9},{2,10},{3,11},{4,12},{5,13},{6,14},{7,15},{8,0},{9,1},... | collective-permute-start | bytes 1413128 | tf_op jit(solution)/shard_map/ppermute | solution.py:32
  36.8 13.9 %collective-permute-start.2 = (bf16[80,2944]{1,0:T(8,128)(2,1)}, bf16[80,2944]{1,0:T(8,128)(2,1)S(1)}, u32[]{:S(2)}, u32[]{:S(2)}) collective-permute-start(bf16[80,2944]{1,0:T(8,128)(2,1)} %copy-done.37), channel_id=1, source_target_pairs={{0,4},{1,5},{2,6},{3,7},{4,8},{5,9},{6,10},{7,11},{8,12},{9,13},{1... | collective-permute-start | bytes 1413128 | tf_op jit(solution)/shard_map/ppermute | solution.py:32
  51.9 6.3 %collective-permute-start.3 = (bf16[20,2944]{1,0:T(8,128)(2,1)}, bf16[20,2944]{1,0:T(8,128)(2,1)S(1)}, u32[]{:S(2)}, u32[]{:S(2)}) collective-permute-start(bf16[20,2944]{1,0:T(8,128)(2,1)} %get-tuple-element.51), channel_id=1, source_target_pairs={{0,3},{1,0},{2,1},{3,2},{4,7},{5,4},{6,5},{7,6},{8,11},{9,8},{10,9... | collective-permute-start | bytes 353288 | tf_op jit(solution)/shard_map/ppermute | solution.py:32
  54.3 5.7 %collective-permute-start.4 = (bf16[20,2944]{1,0:T(8,128)(2,1)}, bf16[20,2944]{1,0:T(8,128)(2,1)S(1)}, u32[]{:S(2)}, u32[]{:S(2)}) collective-permute-start(bf16[20,2944]{1,0:T(8,128)(2,1)} %get-tuple-element.52), channel_id=1, source_target_pairs={{0,2},{1,3},{2,0},{3,1},{4,6},{5,7},{6,4},{7,5},{8,10},{9,11},{10,... | collective-permute-start | bytes 353288 | tf_op jit(solution)/shard_map/ppermute | solution.py:32
  54.8 6.9 %collective-permute-start.5 = (bf16[20,2944]{1,0:T(8,128)(2,1)S(1)}, bf16[20,2944]{1,0:T(8,128)(2,1)S(1)}, u32[]{:S(2)}, u32[]{:S(2)}) collective-permute-start(bf16[20,2944]{1,0:T(8,128)(2,1)S(1)} %get-tuple-element.53), channel_id=1, source_target_pairs={{0,1},{1,2},{2,3},{3,0},{4,5},{5,6},{6,7},{7,4},{8,9},{9,10},{10,1... | collective-permute-start | bytes 353288 | tf_op jit(solution)/shard_map/ppermute | solution.py:32
  56.3 16.3 %copy-start.39 = (f32[2,2,64]{2,1,0:T(2,128)S(1)}, f32[2,2,64]{2,1,0:T(2,128)}, u32[]{:S(2)}) copy-start(f32[2,2,64]{2,1,0:T(2,128)} %param.20) | copy-start | bytes 3076
  62.7 3.9 %collective-permute-start.6 = (bf16[20,2944]{1,0:T(8,128)(2,1)S(1)}, bf16[20,2944]{1,0:T(8,128)(2,1)S(1)}, u32[]{:S(2)}, u32[]{:S(2)}) collective-permute-start(bf16[20,2944]{1,0:T(8,128)(2,1)S(1)} %get-tuple-element.55.refs_0_), channel_id=1, source_target_pairs={{0,3},{1,0},{2,1},{3,2},{4,7},{5,4},{6,5},{7,6},{8,11},{9,8},{10,9... | collective-permute-start | bytes 353288 | tf_op jit(solution)/shard_map/ppermute | solution.py:32
  63.0 5.5 %collective-permute-start.7 = (bf16[20,2944]{1,0:T(8,128)(2,1)S(1)}, bf16[20,2944]{1,0:T(8,128)(2,1)S(1)}, u32[]{:S(2)}, u32[]{:S(2)}) collective-permute-start(bf16[20,2944]{1,0:T(8,128)(2,1)S(1)} %get-tuple-element.55.refs_0_), channel_id=1, source_target_pairs={{0,2},{1,3},{2,0},{3,1},{4,6},{5,7},{6,4},{7,5},{8,10},{9,11},{10,... | collective-permute-start | bytes 353288 | tf_op jit(solution)/shard_map/ppermute | solution.py:32
  63.5 6.7 %collective-permute-start.8 = (bf16[20,2944]{1,0:T(8,128)(2,1)S(1)}, bf16[20,2944]{1,0:T(8,128)(2,1)S(1)}, u32[]{:S(2)}, u32[]{:S(2)}) collective-permute-start(bf16[20,2944]{1,0:T(8,128)(2,1)S(1)} %get-tuple-element.55.refs_0_), channel_id=1, source_target_pairs={{0,1},{1,2},{2,3},{3,0},{4,5},{5,6},{6,7},{7,4},{8,9},{9,10},{10,1... | collective-permute-start | bytes 353288 | tf_op jit(solution)/shard_map/ppermute | solution.py:32
  70.3 7.8 %collective-permute-start.9 = (bf16[80,2944]{1,0:T(8,128)(2,1)S(1)}, bf16[80,2944]{1,0:T(8,128)(2,1)S(1)}, u32[]{:S(2)}, u32[]{:S(2)}) collective-permute-start(bf16[80,2944]{1,0:T(8,128)(2,1)S(1)} %shard_map.166.refs_1_.refs_0_), channel_id=1, source_target_pairs={{0,12},{1,13},{2,14},{3,15},{4,0},{5,1},{6,2},{7,3},{8,4},{9,5},{1... | collective-permute-start | bytes 1413128 | tf_op jit(solution)/shard_map/ppermute | solution.py:32
  70.7 9.3 %collective-permute-start.10 = (bf16[80,2944]{1,0:T(8,128)(2,1)S(1)}, bf16[80,2944]{1,0:T(8,128)(2,1)S(1)}, u32[]{:S(2)}, u32[]{:S(2)}) collective-permute-start(bf16[80,2944]{1,0:T(8,128)(2,1)S(1)} %shard_map.166.refs_1_.refs_0_), channel_id=1, source_target_pairs={{0,8},{1,9},{2,10},{3,11},{4,12},{5,13},{6,14},{7,15},{8,0},{9,1},... | collective-permute-start | bytes 1413128 | tf_op jit(solution)/shard_map/ppermute | solution.py:32
  71.0 14.0 %collective-permute-start.11 = (bf16[80,2944]{1,0:T(8,128)(2,1)S(1)}, bf16[80,2944]{1,0:T(8,128)(2,1)S(1)}, u32[]{:S(2)}, u32[]{:S(2)}) collective-permute-start(bf16[80,2944]{1,0:T(8,128)(2,1)S(1)} %shard_map.166.refs_1_.refs_0_), channel_id=1, source_target_pairs={{0,4},{1,5},{2,6},{3,7},{4,8},{5,9},{6,10},{7,11},{8,12},{9,13},{1... | collective-permute-start | bytes 1413128 | tf_op jit(solution)/shard_map/ppermute | solution.py:32
  85.8 1.0 copy-start.3
  88.9 1.5 copy-start.16
  90.4 11.8 %copy-start.1 = (bf16[32,3,64,128]{3,2,1,0:T(8,128)(2,1)S(1)}, bf16[32,3,64,128]{3,2,1,0:T(8,128)(2,1)}, u32[]{:S(2)}) copy-start(bf16[32,3,64,128]{3,2,1,0:T(8,128)(2,1)} %refs_7_.1) | copy-start | bytes 4718596
  92.8 18.9 %all-to-all-start.2 = ((bf16[8,64,512]{2,1,0:T(8,128)(2,1)}), bf16[8,64,512]{2,1,0:T(8,128)(2,1)}, u32[]{:S(2)}, u32[]{:S(2)}) async-start(bf16[8,64,512]{2,1,0:T(8,128)(2,1)} %bitcast.9), calls=%async_computation.2 | async-start | bytes 1048576 | tf_op jit(solution)/shard_map/all_to_all | solution.py:603
  102.2 1.0 copy-start.4
  105.2 1.1 copy-start.22
  111.7 1.0 copy-start.27
  112.8 1.1 copy-start.36
  117.8 12.4 %copy-start.24 = (bf16[128,2432]{1,0:T(8,128)(2,1)}, bf16[128,2432]{1,0:T(8,128)(2,1)S(1)}, u32[]{:S(2)}) copy-start(bf16[128,2432]{1,0:T(8,128)(2,1)S(1)} %get-tuple-element.58.refs_0_) | copy-start | bytes 1867780
  117.8 12.4 %copy-start.23 = (bf16[128,2432]{1,0:T(8,128)(2,1)S(1)}, bf16[128,2432]{1,0:T(8,128)(2,1)}, u32[]{:S(2)}) copy-start(bf16[128,2432]{1,0:T(8,128)(2,1)} %refs_2_.3) | copy-start | bytes 1867780
  117.9 18.7 %copy-start.19 = (f32[2,2,6,2432]{3,1,2,0:T(2,128)S(1)}, f32[2,2,6,2432]{3,1,2,0:T(2,128)}, u32[]{:S(2)}) copy-start(f32[2,2,6,2432]{3,1,2,0:T(2,128)} %param.19) | copy-start | bytes 700420
  117.9 12.4 %collective-permute-start.12 = (bf16[128,2432]{1,0:T(8,128)(2,1)S(1)}, bf16[128,2432]{1,0:T(8,128)(2,1)S(1)}, u32[]{:S(2)}, u32[]{:S(2)}) collective-permute-start(bf16[128,2432]{1,0:T(8,128)(2,1)S(1)} %get-tuple-element.59), channel_id=1, source_target_pairs={{0,12},{1,13},{2,14},{3,15},{4,0},{5,1},{6,2},{7,3},{8,4},{9,5},{1... | collective-permute-start | bytes 1867784 | tf_op jit(solution)/shard_map/ppermute | solution.py:32
  118.7 17.9 %collective-permute-start.13 = (bf16[128,2432]{1,0:T(8,128)(2,1)}, bf16[128,2432]{1,0:T(8,128)(2,1)}, u32[]{:S(2)}, u32[]{:S(2)}) collective-permute-start(bf16[128,2432]{1,0:T(8,128)(2,1)} %get-tuple-element.60), channel_id=1, source_target_pairs={{0,8},{1,9},{2,10},{3,11},{4,12},{5,13},{6,14},{7,15},{8,0},{9,1},... | collective-permute-start | bytes 1867784 | tf_op jit(solution)/shard_map/ppermute | solution.py:32
  119.7 17.0 %collective-permute-start.14 = (bf16[128,2432]{1,0:T(8,128)(2,1)}, bf16[128,2432]{1,0:T(8,128)(2,1)}, u32[]{:S(2)}, u32[]{:S(2)}) collective-permute-start(bf16[128,2432]{1,0:T(8,128)(2,1)} %get-tuple-element.61), channel_id=1, source_target_pairs={{0,4},{1,5},{2,6},{3,7},{4,8},{5,9},{6,10},{7,11},{8,12},{9,13},{1... | collective-permute-start | bytes 1867784 | tf_op jit(solution)/shard_map/ppermute | solution.py:32
  130.3 73.4 %slice-start = ((s8[5914624]{0:T(1024)(128)(4,1)}), s8[1720320]{0:T(1024)(128)(4,1)S(1)}, s32[]{:S(2)}) async-start(s8[5914624]{0:T(1024)(128)(4,1)} %bitcast.20), calls=%async_computation.5 | async-start | bytes 3440640
  133.8 7.2 %collective-permute-start.15 = (bf16[80,2432]{1,0:T(8,128)(2,1)}, bf16[80,2432]{1,0:T(8,128)(2,1)}, u32[]{:S(2)}, u32[]{:S(2)}) collective-permute-start(bf16[80,2432]{1,0:T(8,128)(2,1)} %get-tuple-element.64), channel_id=1, source_target_pairs={{0,12},{1,13},{2,14},{3,15},{4,0},{5,1},{6,2},{7,3},{8,4},{9,5},{1... | collective-permute-start | bytes 1167368 | tf_op jit(solution)/shard_map/ppermute | solution.py:32
  135.1 8.7 %collective-permute-start.16 = (bf16[80,2432]{1,0:T(8,128)(2,1)}, bf16[80,2432]{1,0:T(8,128)(2,1)}, u32[]{:S(2)}, u32[]{:S(2)}) collective-permute-start(bf16[80,2432]{1,0:T(8,128)(2,1)} %get-tuple-element.65), channel_id=1, source_target_pairs={{0,8},{1,9},{2,10},{3,11},{4,12},{5,13},{6,14},{7,15},{8,0},{9,1},... | collective-permute-start | bytes 1167368 | tf_op jit(solution)/shard_map/ppermute | solution.py:32
  135.9 12.0 %collective-permute-start.17 = (bf16[80,2432]{1,0:T(8,128)(2,1)}, bf16[80,2432]{1,0:T(8,128)(2,1)}, u32[]{:S(2)}, u32[]{:S(2)}) collective-permute-start(bf16[80,2432]{1,0:T(8,128)(2,1)} %get-tuple-element.66), channel_id=1, source_target_pairs={{0,4},{1,5},{2,6},{3,7},{4,8},{5,9},{6,10},{7,11},{8,12},{9,13},{1... | collective-permute-start | bytes 1167368 | tf_op jit(solution)/shard_map/ppermute | solution.py:32
  147.9 1.1 copy-start.8
  149.0 1.1 copy-start.25
  151.1 15.0 %copy-start.32 = (bf16[20,2432]{1,0:T(8,128)(2,1)S(1)}, bf16[20,2432]{1,0:T(8,128)(2,1)}, u32[]{:S(2)}) copy-start(bf16[20,2432]{1,0:T(8,128)(2,1)} %copy-done.31) | copy-start | bytes 291844
  151.1 52.6 %slice-start.1 = ((s8[5914624]{0:T(1024)(128)(4,1)}), s8[4194304]{0:T(1024)(128)(4,1)S(1)}, s32[]{:S(2)}) async-start(s8[5914624]{0:T(1024)(128)(4,1)} %bitcast.20), calls=%async_computation.6 | async-start | bytes 8388608
  153.7 8.7 %collective-permute-start.18 = (bf16[52,2432]{1,0:T(8,128)(2,1)S(1)}, bf16[52,2432]{1,0:T(8,128)(2,1)S(1)}, u32[]{:S(2)}, u32[]{:S(2)}) collective-permute-start(bf16[52,2432]{1,0:T(8,128)(2,1)S(1)} %get-tuple-element.68), channel_id=1, source_target_pairs={{0,3},{1,0},{2,1},{3,2},{4,7},{5,4},{6,5},{7,6},{8,11},{9,8},{10,9... | collective-permute-start | bytes 758792 | tf_op jit(solution)/shard_map/ppermute | solution.py:32
  156.0 7.2 %collective-permute-start.19 = (bf16[52,2432]{1,0:T(8,128)(2,1)S(1)}, bf16[52,2432]{1,0:T(8,128)(2,1)S(1)}, u32[]{:S(2)}, u32[]{:S(2)}) collective-permute-start(bf16[52,2432]{1,0:T(8,128)(2,1)S(1)} %get-tuple-element.69), channel_id=1, source_target_pairs={{0,2},{1,3},{2,0},{3,1},{4,6},{5,7},{6,4},{7,5},{8,10},{9,11},{10,... | collective-permute-start | bytes 758792 | tf_op jit(solution)/shard_map/ppermute | solution.py:32
  156.7 9.4 %collective-permute-start.20 = (bf16[52,2432]{1,0:T(8,128)(2,1)S(1)}, bf16[52,2432]{1,0:T(8,128)(2,1)S(1)}, u32[]{:S(2)}, u32[]{:S(2)}) collective-permute-start(bf16[52,2432]{1,0:T(8,128)(2,1)S(1)} %get-tuple-element.70), channel_id=1, source_target_pairs={{0,1},{1,2},{2,3},{3,0},{4,5},{5,6},{6,7},{7,4},{8,9},{9,10},{10,1... | collective-permute-start | bytes 758792 | tf_op jit(solution)/shard_map/ppermute | solution.py:32
  166.6 5.7 %collective-permute-start.21 = (bf16[52,2432]{1,0:T(8,128)(2,1)S(1)}, bf16[52,2432]{1,0:T(8,128)(2,1)S(1)}, u32[]{:S(2)}, u32[]{:S(2)}) collective-permute-start(bf16[52,2432]{1,0:T(8,128)(2,1)S(1)} %get-tuple-element.73.refs_0_), channel_id=1, source_target_pairs={{0,3},{1,0},{2,1},{3,2},{4,7},{5,4},{6,5},{7,6},{8,11},{9,8},{10,9... | collective-permute-start | bytes 758792 | tf_op jit(solution)/shard_map/ppermute | solution.py:32
  167.0 7.2 %collective-permute-start.22 = (bf16[52,2432]{1,0:T(8,128)(2,1)S(1)}, bf16[52,2432]{1,0:T(8,128)(2,1)S(1)}, u32[]{:S(2)}, u32[]{:S(2)}) collective-permute-start(bf16[52,2432]{1,0:T(8,128)(2,1)S(1)} %get-tuple-element.73.refs_0_), channel_id=1, source_target_pairs={{0,2},{1,3},{2,0},{3,1},{4,6},{5,7},{6,4},{7,5},{8,10},{9,11},{10,... | collective-permute-start | bytes 758792 | tf_op jit(solution)/shard_map/ppermute | solution.py:32
  167.7 9.4 %collective-permute-start.23 = (bf16[52,2432]{1,0:T(8,128)(2,1)S(1)}, bf16[52,2432]{1,0:T(8,128)(2,1)S(1)}, u32[]{:S(2)}, u32[]{:S(2)}) collective-permute-start(bf16[52,2432]{1,0:T(8,128)(2,1)S(1)} %get-tuple-element.73.refs_0_), channel_id=1, source_target_pairs={{0,1},{1,2},{2,3},{3,0},{4,5},{5,6},{6,7},{7,4},{8,9},{9,10},{10,1... | collective-permute-start | bytes 758792 | tf_op jit(solution)/shard_map/ppermute | solution.py:32
  177.1 13.6 %collective-permute-start.24 = (bf16[208,2432]{1,0:T(8,128)(2,1)S(1)}, bf16[208,2432]{1,0:T(8,128)(2,1)S(1)}, u32[]{:S(2)}, u32[]{:S(2)}) collective-permute-start(bf16[208,2432]{1,0:T(8,128)(2,1)S(1)} %shard_map.174.in0), channel_id=1, source_target_pairs={{0,12},{1,13},{2,14},{3,15},{4,0},{5,1},{6,2},{7,3},{8,4},{9,5},{1... | collective-permute-start | bytes 3035144 | tf_op jit(solution)/shard_map/ppermute | solution.py:32
  177.8 15.1 %collective-permute-start.25 = (bf16[208,2432]{1,0:T(8,128)(2,1)S(1)}, bf16[208,2432]{1,0:T(8,128)(2,1)S(1)}, u32[]{:S(2)}, u32[]{:S(2)}) collective-permute-start(bf16[208,2432]{1,0:T(8,128)(2,1)S(1)} %shard_map.174.in0), channel_id=1, source_target_pairs={{0,8},{1,9},{2,10},{3,11},{4,12},{5,13},{6,14},{7,15},{8,0},{9,1},... | collective-permute-start | bytes 3035144 | tf_op jit(solution)/shard_map/ppermute | solution.py:32
  180.2 23.6 %collective-permute-start.26 = (bf16[208,2432]{1,0:T(8,128)(2,1)S(1)}, bf16[208,2432]{1,0:T(8,128)(2,1)S(1)}, u32[]{:S(2)}, u32[]{:S(2)}) collective-permute-start(bf16[208,2432]{1,0:T(8,128)(2,1)S(1)} %shard_map.174.in0), channel_id=1, source_target_pairs={{0,4},{1,5},{2,6},{3,7},{4,8},{5,9},{6,10},{7,11},{8,12},{9,13},{1... | collective-permute-start | bytes 3035144 | tf_op jit(solution)/shard_map/ppermute | solution.py:32
  203.7 2.7 copy-start
  214.6 6.7 %collective-permute-start.30 = (bf16[80,2432]{1,0:T(8,128)(2,1)S(1)}, bf16[80,2432]{1,0:T(8,128)(2,1)S(1)}, u32[]{:S(2)}, u32[]{:S(2)}) collective-permute-start(bf16[80,2432]{1,0:T(8,128)(2,1)S(1)} %get-tuple-element.79), channel_id=1, source_target_pairs={{0,12},{1,13},{2,14},{3,15},{4,0},{5,1},{6,2},{7,3},{8,4},{9,5},{1... | collective-permute-start | bytes 1167368 | tf_op jit(solution)/shard_map/ppermute | solution.py:32
  215.0 27.3 %collective-permute-start.27 = (bf16[128,2432]{1,0:T(8,128)(2,1)S(1)}, bf16[128,2432]{1,0:T(8,128)(2,1)S(1)}, u32[]{:S(2)}, u32[]{:S(2)}) collective-permute-start(bf16[128,2432]{1,0:T(8,128)(2,1)S(1)} %get-tuple-element.75), channel_id=1, source_target_pairs={{0,12},{1,13},{2,14},{3,15},{4,0},{5,1},{6,2},{7,3},{8,4},{9,5},{1... | collective-permute-start | bytes 1867784 | tf_op jit(solution)/shard_map/ppermute | solution.py:32
  216.4 25.9 %collective-permute-start.28 = (bf16[128,2432]{1,0:T(8,128)(2,1)S(1)}, bf16[128,2432]{1,0:T(8,128)(2,1)S(1)}, u32[]{:S(2)}, u32[]{:S(2)}) collective-permute-start(bf16[128,2432]{1,0:T(8,128)(2,1)S(1)} %get-tuple-element.76), channel_id=1, source_target_pairs={{0,8},{1,9},{2,10},{3,11},{4,12},{5,13},{6,14},{7,15},{8,0},{9,1},... | collective-permute-start | bytes 1867784 | tf_op jit(solution)/shard_map/ppermute | solution.py:32
  217.9 24.4 %collective-permute-start.29 = (bf16[128,2432]{1,0:T(8,128)(2,1)S(1)}, bf16[128,2432]{1,0:T(8,128)(2,1)S(1)}, u32[]{:S(2)}, u32[]{:S(2)}) collective-permute-start(bf16[128,2432]{1,0:T(8,128)(2,1)S(1)} %get-tuple-element.77), channel_id=1, source_target_pairs={{0,4},{1,5},{2,6},{3,7},{4,8},{5,9},{6,10},{7,11},{8,12},{9,13},{1... | collective-permute-start | bytes 1867784 | tf_op jit(solution)/shard_map/ppermute | solution.py:32
  218.2 19.8 %collective-permute-start.31 = (bf16[80,2432]{1,0:T(8,128)(2,1)S(1)}, bf16[80,2432]{1,0:T(8,128)(2,1)S(1)}, u32[]{:S(2)}, u32[]{:S(2)}) collective-permute-start(bf16[80,2432]{1,0:T(8,128)(2,1)S(1)} %get-tuple-element.80), channel_id=1, source_target_pairs={{0,8},{1,9},{2,10},{3,11},{4,12},{5,13},{6,14},{7,15},{8,0},{9,1},... | collective-permute-start | bytes 1167368 | tf_op jit(solution)/shard_map/ppermute | solution.py:32
  221.2 21.1 %collective-permute-start.32 = (bf16[80,2432]{1,0:T(8,128)(2,1)S(1)}, bf16[80,2432]{1,0:T(8,128)(2,1)S(1)}, u32[]{:S(2)}, u32[]{:S(2)}) collective-permute-start(bf16[80,2432]{1,0:T(8,128)(2,1)S(1)} %get-tuple-element.81), channel_id=1, source_target_pairs={{0,4},{1,5},{2,6},{3,7},{4,8},{5,9},{6,10},{7,11},{8,12},{9,13},{1... | collective-permute-start | bytes 1167368 | tf_op jit(solution)/shard_map/ppermute | solution.py:32
  244.5 5.4 %collective-permute-start.33 = (bf16[52,2432]{1,0:T(8,128)(2,1)S(1)}, bf16[52,2432]{1,0:T(8,128)(2,1)S(1)}, u32[]{:S(2)}, u32[]{:S(2)}) collective-permute-start(bf16[52,2432]{1,0:T(8,128)(2,1)S(1)} %get-tuple-element.83), channel_id=1, source_target_pairs={{0,3},{1,0},{2,1},{3,2},{4,7},{5,4},{6,5},{7,6},{8,11},{9,8},{10,9... | collective-permute-start | bytes 758792 | tf_op jit(solution)/shard_map/ppermute | solution.py:32
  245.2 6.9 %collective-permute-start.34 = (bf16[52,2432]{1,0:T(8,128)(2,1)S(1)}, bf16[52,2432]{1,0:T(8,128)(2,1)S(1)}, u32[]{:S(2)}, u32[]{:S(2)}) collective-permute-start(bf16[52,2432]{1,0:T(8,128)(2,1)S(1)} %get-tuple-element.84), channel_id=1, source_target_pairs={{0,2},{1,3},{2,0},{3,1},{4,6},{5,7},{6,4},{7,5},{8,10},{9,11},{10,... | collective-permute-start | bytes 758792 | tf_op jit(solution)/shard_map/ppermute | solution.py:32
  245.5 9.4 %collective-permute-start.35 = (bf16[52,2432]{1,0:T(8,128)(2,1)S(1)}, bf16[52,2432]{1,0:T(8,128)(2,1)S(1)}, u32[]{:S(2)}, u32[]{:S(2)}) collective-permute-start(bf16[52,2432]{1,0:T(8,128)(2,1)S(1)} %get-tuple-element.85), channel_id=1, source_target_pairs={{0,1},{1,2},{2,3},{3,0},{4,5},{5,6},{6,7},{7,4},{8,9},{9,10},{10,1... | collective-permute-start | bytes 758792 | tf_op jit(solution)/shard_map/ppermute | solution.py:32
  (17 other events, 14.7 us)

commit v3 on v2

v3 whole, which is shorter than its diff:
```python
import functools

import jax
import jax.numpy as jnp
from jax import lax
from jax.experimental import pallas as pl
from jax.experimental.pallas import tpu as pltpu
from jax.sharding import PartitionSpec as P

HEAD_DIM = 64
CAP = 2
EPSILON = 1e-06
ADAPTER_SCALE = 0.5
SIDE = 4
POOL = 20
WIDTH = 2432
EXTRA = 512
F32 = jnp.float32
BF16 = jnp.bfloat16


def torus_shift(values, stage, step):
    pairs = []
    for grp in range(8):
        for tp in range(16):
            z, y = divmod(tp, SIDE)
            if (grp + stage) % 2 == 0:
                y = (y + step) % SIDE
            else:
                z = (z + step) % SIDE
            pairs.append((grp * 16 + tp, grp * 16 + z * SIDE + y))
    return lax.ppermute(values, ("grp", "tp"), pairs)


def core_swap(values):
    return lax.ppermute(values, "grp", [(grp, grp ^ 1) for grp in range(8)])


def chip_swap(values, far):
    pairs = []
    for grp in range(8):
        chip = 3 - grp // 2 if far else (grp // 2) ^ 1
        pairs.append((grp, chip * 2 + grp % 2))
    return lax.ppermute(values, "grp", pairs)


def spread(rows, stage):
    return [
        rows,
        torus_shift(rows, stage, -1),
        torus_shift(rows, stage, 2),
        torus_shift(rows, stage, 1),
    ]


def exchange(parts, stage):
    return [
        parts[0],
        torus_shift(parts[3], stage, -1),
        torus_shift(parts[2], stage, 2),
        torus_shift(parts[1], stage, 1),
    ]


def run(kernel, outs, args, smem=0, scratch=(), flops=0, limit=8, after=(), hbm=()):
    count = len(args)
    spaces = [pltpu.SMEM] * smem + [pltpu.VMEM] * (count - smem)
    for index in hbm:
        spaces[index] = pl.ANY
    specs = [pl.BlockSpec(memory_space=space) for space in spaces]
    specs += [pl.BlockSpec(memory_space=pl.ANY)] * len(after)
    single = not isinstance(outs, list)
    shapes = [outs] if single else outs
    moved = sum(a.size * a.dtype.itemsize for a in args)
    moved += sum(s.size * s.dtype.itemsize for s in shapes)

    def body(*refs):
        kernel(*refs[:count], *refs[count + len(after) :])

    result = pl.pallas_call(
        body,
        out_shape=shapes,
        in_specs=specs,
        out_specs=[pl.BlockSpec(memory_space=pltpu.VMEM)] * len(shapes),
        scratch_shapes=list(scratch),
        compiler_params=pltpu.CompilerParams(vmem_limit_bytes=limit << 20),
        cost_estimate=pl.CostEstimate(flops=flops, bytes_accessed=moved, transcendentals=0),
    )(*args, *after)
    return result[0] if single else result


def like(shape, dtype=BF16):
    return jax.ShapeDtypeStruct(shape, dtype)


def normed(values):
    centred = values - jnp.mean(values, -1, keepdims=True)
    return centred * lax.rsqrt(jnp.mean(centred * centred, -1, keepdims=True) + EPSILON)


def low_half(shape):
    return lax.broadcasted_iota(jnp.int32, shape, len(shape) - 1) < HEAD_DIM


def head_norm(values, gains):
    first = low_half(values.shape)
    squares = values * values
    head0 = jnp.sum(jnp.where(first, squares, 0.0), -1, keepdims=True)
    head1 = jnp.sum(jnp.where(first, 0.0, squares), -1, keepdims=True)
    scale = jnp.where(
        first,
        lax.rsqrt(head0 * (1.0 / HEAD_DIM) + EPSILON),
        lax.rsqrt(head1 * (1.0 / HEAD_DIM) + EPSILON),
    )
    return values * scale * gains


def pack_kernel(rows_ref, line_ref, out_ref, slot_ref, held, wide):
    wide[...] = jnp.full(wide.shape, -1, jnp.int32)
    wide[0:1, 0:POOL] = line_ref[...]
    line = wide[0:1, :]
    first = lax.broadcasted_iota(jnp.int32, (POOL, 256), 0)
    second = lax.broadcasted_iota(jnp.int32, (POOL, 256), 1)
    column = jnp.sum(jnp.where(first == second, line, 0), 1, keepdims=True)
    rank = jnp.sum(jnp.where((column == line) & (first < second), 1, 0), 0, keepdims=True)
    slot_ref[...] = line * CAP + rank
    held[...] = jnp.zeros_like(held)
    held[POOL : POOL + 1, :] = (line * CAP + rank).astype(F32)
    for block in range(16):
        held[0:POOL, :] = rows_ref[:, block * 256 : (block + 1) * 256].astype(F32)
        out_ref[block] = held[...].astype(BF16)


def embed_kernel(
    places_ref, arrived_ref, weight_ref, low_ref, out0, out1, out2, out3, slot_ref, held, label
):
    for far, out in enumerate((out0, out1, out2, out3)):
        for near in range(SIDE):
            place = far * SIDE + near
            block = arrived_ref[places_ref[place]].astype(F32)
            held[near * POOL : (near + 1) * POOL, :] = block[0:POOL]
            label[place : place + 1, :] = block[POOL : POOL + 1, 0:128]
        out[:, 0:WIDTH] = jnp.dot(
            held[...].astype(BF16), weight_ref[...], preferred_element_type=F32
        ).astype(BF16)
        out[:, WIDTH:] = jnp.zeros((SIDE * POOL, EXTRA), BF16)
        for near in range(SIDE):
            left = WIDTH + near // 2 * 256
            top = near % 2 * 32
            out[top : top + 32, left : left + 192] = low_ref[places_ref[far * SIDE + near]]
    line = (128, 16 * POOL)
    offset = lax.broadcasted_iota(jnp.int32, line, 1) - lax.broadcasted_iota(jnp.int32, line, 0)
    taken = offset == 0
    for place in range(1, 16):
        taken = taken | (offset == place * POOL)
    taken = taken & (lax.broadcasted_iota(jnp.int32, line, 0) < POOL)
    spot = jnp.dot(
        label[...].astype(BF16),
        jnp.where(taken, 1.0, 0.0).astype(BF16),
        preferred_element_type=F32,
    )
    place = lax.broadcasted_iota(jnp.int32, spot.shape, 0)
    start = place * POOL
    column = lax.broadcasted_iota(jnp.int32, spot.shape, 1)
    inside = (column >= start) & (column < start + POOL)
    target = jnp.sum(jnp.where(inside, spot, 0.0), 0, keepdims=True).astype(jnp.int32)
    block = jnp.sum(jnp.where(inside, place, 0), 0, keepdims=True)
    slot_ref[...] = (
        (target >> 2) * 64 + ((target >> 1) & 1) * 32 + (target & 1) + 2 * block
    )


def middle_kernel(in0, in1, in2, in3, out0, out1, out2, out3, held):
    held[...] = total_of((in0, in1, in2, in3))
    for near, out in enumerate((out0, out1, out2, out3)):
        out[:, 0:WIDTH] = held[near * POOL : (near + 1) * POOL, 0:WIDTH].astype(BF16)
        left = WIDTH + near // 2 * 256
        for half in range(2):
            top = near % 2 * 32 + half * 16
            out[0:16, WIDTH + half * 256 : WIDTH + half * 256 + 256] = held[
                top : top + 16, left : left + 256
            ].astype(BF16)
        out[16:POOL, WIDTH:] = jnp.zeros((POOL - 16, EXTRA), BF16)


def both_middle_kernel(*refs):
    img, txt, outs, held = refs[0:4], refs[4:8], refs[8:12], refs[12]
    held[...] = total_of(txt)
    for near, out in enumerate(outs):
        rows = slice(near * 32, (near + 1) * 32)
        out[0:32, :] = functools.reduce(
            jnp.add, [piece[rows, :].astype(F32) for piece in img]
        ).astype(BF16)
        out[32 : 32 + POOL, :] = held[near * POOL : (near + 1) * POOL, :].astype(BF16)


def join_kernel(in0, in1, in2, in3, out_ref, held):
    for place, piece in enumerate((in0, in1, in2, in3)):
        held[place * POOL : (place + 1) * POOL, :] = piece[...].astype(F32)
    out_ref[...] = held[...].astype(BF16)


def both_join_kernel(in0, in1, in2, in3, out_ref, held):
    for place, piece in enumerate((in0, in1, in2, in3)):
        out_ref[place * 32 : (place + 1) * 32, :] = piece[0:32, :]
        held[place * POOL : (place + 1) * POOL, :] = piece[32:, :].astype(F32)
    out_ref[128:, :] = held[...].astype(BF16)


def prompt_mod_kernel(mod_ref, out_ref):
    for own in range(2):
        for place in range(6):
            out_ref[own, place : place + 1, :] = mod_ref[own, place, 1:2, :]
        out_ref[own, 6:8, :] = jnp.zeros((2, out_ref.shape[2]), F32)


def mod_pair_kernel(first_ref, second_ref, out_ref):
    count = first_ref.shape[0]
    out_ref[0:count] = first_ref[...]
    out_ref[count : 2 * count] = second_ref[...]


def row_mod_kernel(index_ref, near_ref, far_ref, out_ref):
    for row in range(POOL):
        index = index_ref[row]
        within = lax.rem(index, 8)
        values = jnp.where(index < 8, near_ref[within], far_ref[within])
        for place in range(6):
            out_ref[place, row : row + 1, :] = values[place : place + 1]


def total_of(parts):
    return functools.reduce(jnp.add, [part[...].astype(F32) for part in parts])


def embed_norm_kernel(in0, in1, in2, in3, mod_ref, embedded_ref, out_ref):
    total = total_of((in0, in1, in2, in3))
    embedded = total[:, 0:WIDTH].astype(BF16)
    embedded_ref[...] = embedded
    modded = normed(embedded.astype(F32)) * (1.0 + mod_ref[1]) + mod_ref[0]
    out_ref[:, 0:WIDTH] = modded.astype(BF16)
    out_ref[:, WIDTH:] = total[:, WIDTH:].astype(BF16)


def both_norm_kernel(
    image_ref, embedded_ref, in0, in1, in2, in3, img_mod_ref, txt_mod_ref,
    img_ref, txt_ref, out_ref,
):
    projected = total_of((in0, in1, in2, in3))
    gate, shift, scale = img_mod_ref[2:3, :], img_mod_ref[3:4, :], img_mod_ref[4:5, :]
    mixed = (image_ref[...].astype(F32) + gate * projected[0:32]).astype(BF16)
    img_ref[...] = mixed
    out_ref[0:32, :] = (normed(mixed.astype(F32)) * (1.0 + scale) + shift).astype(BF16)
    mixed = (embedded_ref[...].astype(F32) + txt_mod_ref[2] * projected[32:]).astype(BF16)
    txt_ref[...] = mixed
    hidden = normed(mixed.astype(F32)) * (1.0 + txt_mod_ref[4]) + txt_mod_ref[3]
    out_ref[32 : 32 + POOL, :] = hidden.astype(BF16)


def one_hot(line, count):
    shape = (count, line.shape[1])
    return jnp.where(lax.broadcasted_iota(jnp.int32, shape, 0) == line, 1.0, 0.0)


def with_keep(values, keep):
    first = low_half(values.shape)
    return jnp.where(first, values, keep), jnp.where(first, keep, values)


def project(rows, weight_ref):
    both = jnp.concatenate([weight_ref[0], weight_ref[1]], -1)
    first = jnp.dot(rows, both, preferred_element_type=F32)
    return first, jnp.dot(rows, weight_ref[2], preferred_element_type=F32)


def txt_qkv_kernel(
    places_ref, in0, in1, in2, in3, weight_ref, gain_ref, slot_ref, out_ref, low_ref, held, rows_ref
):
    part = in0.shape[0]
    for place, piece in enumerate((in0, in1, in2, in3)):
        rows_ref[place * part : (place + 1) * part, :] = piece[:, 0:WIDTH]
        wide = piece[:, WIDTH:].astype(F32)
        for near in range(SIDE):
            rows = wide[near * POOL : near * POOL + 16]
            start = pl.multiple_of(places_ref[place * SIDE + near] * 32, 32)
            low_ref[pl.ds(start, 16), :] = rows[:, 0:192]
            low_ref[pl.ds(start + 16, 16), :] = rows[:, 256:448]
    projected, values = project(rows_ref[...], weight_ref)
    held[:, 0:128] = head_norm(projected[:, 0:128], gain_ref[0:1, :]).astype(BF16)
    held[:, 128:256] = head_norm(projected[:, 128:256], gain_ref[1:2, :]).astype(BF16)
    held[:, 256:384] = values.astype(BF16)
    hot = one_hot(slot_ref[...], 512)
    keep = jnp.sum(hot, -1, keepdims=True)
    slots = jnp.dot(hot.astype(BF16), held[...], preferred_element_type=F32)
    val0, val1 = with_keep(slots[:, 256:384], keep)
    out_ref[:, 0:256] = slots[:, 0:256].astype(BF16)
    out_ref[:, 256:384] = val0.astype(BF16)
    out_ref[:, 384:512] = val1.astype(BF16)


def img_project_kernel(
    ids_ref, tp_ref, image_hbm, mod_ref, weight_hbm, down_hbm,
    projected_ref, low_ref, own_ref, own_mod_ref, image, weight, down, wide, modded, sems,
):
    copies = [pltpu.make_async_copy(image_hbm, image, sems.at[0])]
    copies.append(pltpu.make_async_copy(weight_hbm, weight, sems.at[1]))
    for own in range(2):
        copies.append(
            pltpu.make_async_copy(down_hbm.at[ids_ref[own]], down.at[own], sems.at[2 + own])
        )
    for copy in copies:
        copy.start()
    copies[0].wait()
    depth = down.shape[1]
    tp = tp_ref[0]
    own_ref[...] = image[pl.ds(pl.multiple_of(tp * 32, 32), 32), :]
    for place in range(6):
        own_mod_ref[place : place + 1, :] = mod_ref[tp // 8, place, 0:1, :]
    for own in range(2):
        for part in range(2):
            rows = image[own * 256 + part * 128 : own * 256 + (part + 1) * 128, :].astype(F32)
            scaled = normed(rows) * (1.0 + mod_ref[own, 1, 0:1, :]) + mod_ref[own, 0, 0:1, :]
            modded[part * 128 : (part + 1) * 128, :] = scaled.astype(BF16)
        if own == 0:
            copies[1].wait()
        copies[2 + own].wait()
        wide[...] = jnp.zeros_like(wide)
        start = pl.multiple_of(tp * depth, 8)
        wide[pl.ds(start, depth), :] = down[own].astype(F32)
        projected, values = project(modded[...], weight)
        projected_ref[own * 256 : (own + 1) * 256, 0:256] = projected
        projected_ref[own * 256 : (own + 1) * 256, 256:384] = values
        low = jnp.dot(modded[...], wide[...].astype(BF16), preferred_element_type=F32)
        for block in range(8):
            low_ref[own * 8 + block] = low[block * 32 : (block + 1) * 32].astype(BF16)


def img_adapt_kernel(ids_ref, low_ref, projected_ref, up_hbm, gain_ref, out_ref, up, lift, sems):
    copies = []
    for own in range(2):
        copies.append(
            pltpu.make_async_copy(up_hbm.at[ids_ref[own]], up.at[own], sems.at[own])
        )
        copies[own].start()
    for own in range(2):
        copies[own].wait()
        lift[...] = jnp.zeros_like(lift)
        for part in range(3):
            lift[part * 64 : (part + 1) * 64, part * 128 : (part + 1) * 128] = up[own, part]
        rows = slice(own * 256, (own + 1) * 256)
        projected = projected_ref[rows, :] + ADAPTER_SCALE * jnp.dot(
            low_ref[rows, :].astype(BF16), lift[...], preferred_element_type=F32
        )
        out_ref[rows, 0:128] = head_norm(projected[:, 0:128], gain_ref[0:1, :]).astype(BF16)
        out_ref[rows, 128:256] = head_norm(projected[:, 128:256], gain_ref[1:2, :]).astype(BF16)
        val0, val1 = with_keep(projected[:, 256:384], 1.0)
        out_ref[rows, 256:384] = val0.astype(BF16)
        out_ref[rows, 384:512] = val1.astype(BF16)


def attend(queries, tokens):
    scaled = queries.astype(F32) * HEAD_DIM ** (-0.5)
    first = low_half(scaled.shape)
    keys = tokens[:, 128:256]
    results = []
    for head in range(2):
        own = jnp.where(first if head == 0 else ~first, scaled, 0.0).astype(BF16)
        scores = lax.dot_general(
            own, keys, (((1,), (1,)), ((), ())), preferred_element_type=F32
        )
        weights = jnp.exp(scores).astype(BF16)
        summed = jnp.dot(
            weights, tokens[:, 256 + head * 128 : 384 + head * 128], preferred_element_type=F32
        )
        results.append(summed / pltpu.roll(summed, HEAD_DIM, 1))
    return jnp.where(first, results[0], results[1]).astype(BF16)


def img_attend_kernel(
    places_ref, img_ref, slot_ref, weight_ref,
    out0, out1, out2, out3, token_ref, tokens, held, ranked,
):
    for own in range(2):
        tokens[own, 0:256, :] = img_ref[own * 256 : (own + 1) * 256, :]
        for source in range(8):
            start = 256 + source * 32
            tokens[own, start : start + 32, :] = slot_ref[source, own * 32 : (own + 1) * 32, :]
    token_ref[...] = tokens[...]
    for own in range(2):
        held[own * 256 : (own + 1) * 256, :] = attend(tokens[own, 0:256, 0:128], tokens[own])
    for place in range(16):
        start = pl.multiple_of(places_ref[place] * 32, 32)
        ranked[place * 32 : (place + 1) * 32, :] = held[pl.ds(start, 32), :]
    result = jnp.dot(ranked[...], weight_ref[...], preferred_element_type=F32)
    for place, out in enumerate((out0, out1, out2, out3)):
        out[...] = result[place * 128 : (place + 1) * 128].astype(BF16)


def txt_attend_kernel(token_ref, out_ref):
    for own in range(2):
        attended = attend(token_ref[own, 256:512, 0:128], token_ref[own])
        for source in range(8):
            start = source * 32
            out_ref[source, own * 32 : (own + 1) * 32, :] = attended[start : start + 32]


def txt_project_kernel(att_ref, slot_ref, weight_ref, out0, out1, out2, out3):
    hot = one_hot(slot_ref[...], 512).astype(BF16)
    rows = lax.dot_general(
        hot, att_ref[...], (((0,), (0,)), ((), ())), preferred_element_type=F32
    ).astype(BF16)
    part = out0.shape[0]
    result = jnp.dot(rows, weight_ref[...], preferred_element_type=F32)
    for place, out in enumerate((out0, out1, out2, out3)):
        out[...] = result[place * part : (place + 1) * part].astype(BF16)


def feed_kernel(
    start, stream, in0, in1, in2, in3, win_ref, wout_ref, out0, out1, out2, out3, rows_ref
):
    part, width = out0.shape
    for place, piece in enumerate((in0, in1, in2, in3)):
        rows_ref[place * part : (place + 1) * part, :] = piece[start : start + part, :]
    hidden = lax.dot_general(
        rows_ref[...], win_ref[stream], (((1,), (1,)), ((), ())), preferred_element_type=F32
    )
    hidden = jax.nn.gelu(hidden, approximate=True).astype(BF16)
    for columns in (slice(0, 1280), slice(1280, width)):
        result = jnp.dot(hidden, wout_ref[stream, :, columns], preferred_element_type=F32)
        for place, out in enumerate((out0, out1, out2, out3)):
            out[:, columns] = result[place * part : (place + 1) * part].astype(BF16)


def both_final_kernel(
    img_ref, txt_ref, in0, in1, in2, in3, img_mod_ref, txt_mod_ref, slot_ref, out_ref, placed_ref
):
    total = total_of((in0, in1, in2, in3))
    out_ref[...] = (img_ref[...].astype(F32) + img_mod_ref[5:6, :] * total[0:32]).astype(BF16)
    rows = txt_ref[...].astype(F32) + txt_mod_ref[5] * total[32:]
    hot = one_hot(slot_ref[:, 0:POOL], 32).astype(BF16)
    placed_ref[...] = jnp.dot(hot, rows.astype(BF16), preferred_element_type=F32).astype(BF16)


def middle(parts):
    rows, width = parts[0].shape
    return run(
        middle_kernel,
        [like((rows // SIDE, width))] * SIDE,
        parts,
        scratch=[pltpu.VMEM((rows, width), F32)],
    )


def both_middle(img_parts, txt_parts):
    rows, width = txt_parts[0].shape
    return run(
        both_middle_kernel,
        [like((32 + POOL, width))] * SIDE,
        (*img_parts, *txt_parts),
        scratch=[pltpu.VMEM((rows, width), F32)],
    )


def join(kernel, parts):
    width = parts[0].shape[1]
    return run(
        kernel,
        like((SIDE * parts[0].shape[0], width)),
        parts,
        scratch=[pltpu.VMEM((SIDE * POOL, width), F32)],
    )


def feed(parts, start, rows, weight_in, weight_out, stream, after=()):
    width = parts[0].shape[1]
    return run(
        functools.partial(feed_kernel, start, stream),
        [like((rows, width))] * SIDE,
        (*parts, weight_in, weight_out),
        scratch=[pltpu.VMEM((rows * SIDE, width), BF16)],
        flops=rows * SIDE * width * weight_in.shape[1] * 4,
        limit=14,
        after=after,
    )


def shards(
    image,
    prompt_encoder_rows,
    prompt_row_request,
    request_adapter,
    modulation,
    query_key_gain,
    prompt_embed_weight,
    image_query_key_value,
    prompt_query_key_value,
    image_out_weight,
    prompt_out_weight,
    feed_in_weight,
    feed_out_weight,
    adapter_down,
    adapter_up,
):
    grp = lax.axis_index("grp")
    tp = lax.axis_index("tp")
    chip, core = grp // 2, grp % 2
    z, y = tp // SIDE, tp % SIDE
    width = image.shape[1]

    steps = jnp.arange(16)
    far, near = steps // SIDE, steps % SIDE
    places = jnp.where(
        core == 0,
        ((z + far) % SIDE) * SIDE + (y + near) % SIDE,
        ((z + near) % SIDE) * SIDE + (y + far) % SIDE,
    ).astype(jnp.int32)
    gains = jnp.concatenate([query_key_gain, query_key_gain], -1)

    request = prompt_row_request[:, 0]
    outgoing, slots_own = run(
        pack_kernel,
        [like((16, 32, 256)), like((1, 256), jnp.int32)],
        (prompt_encoder_rows, prompt_row_request.reshape(1, POOL)),
        scratch=[pltpu.VMEM((32, 256), F32), pltpu.VMEM((8, 256), jnp.int32)],
    )
    arrived = lax.all_to_all(outgoing, "tp", 0, 0, tiled=True)
    img_projected, low_part, own_image, own_mod = run(
        img_project_kernel,
        [
            like((512, 384), F32),
            like((16, 32, 192)),
            like((32, width)),
            like((6, width), F32),
        ],
        (
            request_adapter,
            tp.reshape(1).astype(jnp.int32),
            image,
            modulation.transpose(0, 2, 1, 3),
            image_query_key_value.transpose(1, 0, 2),
            adapter_down,
        ),
        smem=2,
        scratch=[
            pltpu.VMEM(image.shape, BF16),
            pltpu.VMEM((3, width, 128), BF16),
            pltpu.VMEM((2, *adapter_down.shape[1:]), BF16),
            pltpu.VMEM((width, 192), F32),
            pltpu.VMEM((256, width), BF16),
            pltpu.SemaphoreType.DMA((4,)),
        ],
        flops=512 * width * 576 * 2,
        limit=56,
        after=(outgoing,),
        hbm=(2, 4, 5),
    )
    prompt_mod = run(
        prompt_mod_kernel, like((2, 8, width), F32), (modulation.transpose(0, 2, 1, 3),)
    )
    mod_own = run(
        mod_pair_kernel, like((4, 8, width), F32), (prompt_mod, core_swap(prompt_mod))
    )
    home = request // 4
    row_index = jnp.where(
        home == chip, 0, jnp.where(home == (chip ^ 1), 1, jnp.where(home == 3 - chip, 2, 3))
    )
    row_index = row_index * 4 + (request // 2 % 2 + core) % 2 * 2 + request % 2

    *embed_parts, slots_all = run(
        embed_kernel,
        [like((SIDE * POOL, width + EXTRA))] * SIDE + [like((1, 16 * POOL), jnp.int32)],
        (places, arrived, prompt_embed_weight, low_part),
        smem=1,
        scratch=[pltpu.VMEM((SIDE * POOL, 256), F32), pltpu.VMEM((16, 128), F32)],
        flops=320 * 256 * width * 2,
        after=(mod_own,),
    )
    embed_pieces = exchange(embed_parts, 1)

    embed_sums = exchange(middle(embed_pieces), 0)
    mod_near = run(
        mod_pair_kernel, like((8, 8, width), F32), (mod_own, chip_swap(mod_own, False))
    )
    row_mod = run(
        row_mod_kernel,
        like((6, POOL, width), F32),
        (row_index, mod_near, chip_swap(mod_near, True)),
        smem=1,
    )
    embedded, txt_mod = run(
        embed_norm_kernel,
        [like((POOL, width)), like((POOL, width + EXTRA))],
        (*embed_sums, row_mod),
    )
    txt_mods = spread(join(join_kernel, spread(txt_mod, 0)), 1)

    slot_parts, low = run(
        txt_qkv_kernel,
        [like((512, 512)), like((512, 192), F32)],
        (places, *txt_mods, prompt_query_key_value.transpose(1, 0, 2), gains[1], slots_all),
        smem=1,
        scratch=[pltpu.VMEM((16 * POOL, 384), BF16), pltpu.VMEM((16 * POOL, width), BF16)],
        flops=320 * width * 384 * 2,
        limit=14,
    )
    img_parts = run(
        img_adapt_kernel,
        like((512, 512)),
        (request_adapter, low, img_projected, adapter_up, gains[0]),
        smem=1,
        scratch=[
            pltpu.VMEM((2, 3, 64, 128), BF16),
            pltpu.VMEM((192, 384), BF16),
            pltpu.SemaphoreType.DMA((2,)),
        ],
        flops=512 * 384 * 192 * 2,
        hbm=(3,),
    )
    slot_parts = lax.all_to_all(slot_parts.reshape(8, 64, 512), "grp", 0, 0, tiled=True)

    *img_terms, tokens = run(
        img_attend_kernel,
        [like((128, width))] * SIDE + [like((2, 512, 512))],
        (places, img_parts, slot_parts, image_out_weight),
        smem=1,
        scratch=[
            pltpu.VMEM((2, 512, 512), BF16),
            pltpu.VMEM((512, 128), BF16),
            pltpu.VMEM((512, 128), BF16),
        ],
        flops=1 << 30,
        limit=16,
    )
    img_sums = exchange(img_terms, 1)
    att_parts = run(txt_attend_kernel, like((8, 64, 128)), (tokens,), flops=1 << 29)
    att_parts = lax.all_to_all(att_parts, "grp", 0, 0, tiled=True).reshape(512, 128)
    txt_terms = run(
        txt_project_kernel,
        [like((SIDE * POOL, width))] * SIDE,
        (att_parts, slots_all, prompt_out_weight),
        flops=320 * 128 * width * 2,
        after=(img_sums[1],),
    )
    txt_sums = exchange(txt_terms, 1)

    sums = exchange(both_middle(img_sums, txt_sums), 0)
    mixed_img, mixed_txt, norm_rows = run(
        both_norm_kernel,
        [like((32, width)), like((POOL, width)), like((32 + POOL, width))],
        (own_image, embedded, *sums, own_mod, row_mod),
    )
    rows = spread(join(both_join_kernel, spread(norm_rows, 0)), 1)
    weight_in = feed_in_weight.transpose(0, 2, 1)
    img_terms = feed(rows, 0, 128, weight_in, feed_out_weight, 0)
    txt_terms = feed(
        rows, 128, SIDE * POOL, weight_in, feed_out_weight, 1, (img_terms[0],)
    )
    sums = exchange(both_middle(exchange(img_terms, 1), exchange(txt_terms, 1)), 0)
    image_out, placed = run(
        both_final_kernel,
        [like((32, width))] * 2,
        (mixed_img, mixed_txt, *sums, own_mod, row_mod, slots_own),
    )

    placed = lax.all_to_all(placed.reshape(8, 4, width), "grp", 0, 0, tiled=True)
    prompt_out = placed.reshape(32, width)

    return (image_out, prompt_out)


def solution(mesh):
    placed = (
        P("grp", None),
        P(("grp", "tp"), None),
        P(("grp", "tp"), None),
        P("grp"),
        P("grp", None, None, None),
        P(),
        P("tp", None),
        P(None, None, "tp"),
        P(None, None, "tp"),
        P("tp", None),
        P("tp", None),
        P(None, None, "tp"),
        P(None, "tp", None),
        P(None, "tp", None),
        P(None, None, None, "tp"),
    )
    return jax.shard_map(
        shards,
        mesh=mesh,
        in_specs=placed,
        out_specs=(P(("grp", "tp"), None), P(("grp", "tp"), None)),
        check_vma=False,
    )
```

time: 273 us -> 265 us (0.971)
  local copies, waits for them, and re-layouts: 32.7 us -> 16.1 us
  blocking collectives: 24.4 us -> 30.9 us
  starting transfers between devices: 54.6 us -> 60.6 us
  Pallas kernels: 37.5 us -> 34.1 us
    pallas_call x7 -> x0, Pallas kernels: 19.5 us -> none  [the longest x2 8.17 us: feed(): pl.pallas_call(functools.partial(feed_kernel, start), grid=(1,), out_shap...]
    pallas_call x14 -> x22, Pallas kernels: 18 us -> 34.1 us  [run(): pl.pallas_call(body, out_shape=shapes, in_specs=specs, out_specs=[pl.Bloc...]
    unnamed x85 -> x54, local copies, waits for them, and re-layouts: 30.9 us -> 15.3 us
    ppermute x36, starting transfers between devices: 31.3 us -> 38.3 us  [torus_shift(): return lax.ppermute(values, ('grp', 'tp'), pairs)]
    all_to_all x1, blocking collectives: 14.9 us -> 21.4 us  [shards(): lax.all_to_all(placed.reshape(8, 4, width), 'grp', 0, 0, tiled=True)]
    all_to_all x1 -> x0, starting transfers between devices: 5.38 us -> none  [shards(): lax.all_to_all(mod_all, 'grp', 0, 0, tiled=True).reshape(16, 8, width)]
    ppermute x0 -> x3, starting transfers between devices: none -> 4.69 us  [the longest x2 3.19 us: chip_swap(): return lax.ppermute(values, 'grp', pairs)]
  transfers between devices with their start and end apart: 39 -> 41, of which waited for: 30 -> 25; matrix products, arithmetic and copies ran while one was open for 1% -> 0% of each run, Pallas kernels for 4% -> 7%
where the time goes in v3:
time: 265 us; the launch traced here: 264 us
  waiting for transfers between devices  122 us (46%)
  starting transfers between devices  60.6 us (23%)
  Pallas kernels  34.1 us (13%)
  blocking collectives  30.9 us (12%)
  local copies, waits for them, and re-layouts  16.1 us (6%)
    ppermute x36, waiting for transfers between devices, torus_shift(): return lax.ppermute(values, ('grp', 'tp'), pairs)  117 us
    ppermute x36, starting transfers between devices, torus_shift(): return lax.ppermute(values, ('grp', 'tp'), pairs)  38.3 us
    pallas_call x22, Pallas kernels, run(): pl.pallas_call(body, out_shape=shapes, in_specs=specs, out_specs=[pl.Bloc...  34.1 us
    all_to_all x1, blocking collectives, shards(): lax.all_to_all(placed.reshape(8, 4, width), 'grp', 0, 0, tiled=True)  21.4 us
    unnamed x54, local copies, waits for them, and re-layouts  15.3 us
    all_to_all x1, starting transfers between devices, shards(): lax.all_to_all(slot_parts.reshape(8, 64, 512), 'grp', 0, 0, tiled=True)  9.79 us
    all_to_all x1, blocking collectives, shards(): lax.all_to_all(att_parts, 'grp', 0, 0, tiled=True).reshape(512, 128)  9.53 us
    all_to_all x1, starting transfers between devices, shards(): arrived = lax.all_to_all(outgoing, 'tp', 0, 0, tiled=True)  7.85 us
  transfers between devices with their start and end apart: 41, of which 25 were waited for; matrix products, arithmetic and copies ran while one was open for 0% of the time, Pallas kernels for 7%

profile of v3, /device:TPU:1, one launch (start us, length us, event | category | flops | bytes accessed | tf_op | source)
XLA Modules:
  0.0 264.4 jit_solution(12969174057294589008)
XLA Ops:
  0.6 0.9 copy-done.4
  1.6 1.5 collective-permute-start
  3.1 0.9 copy-done.16
  4.7 0.9 shard_map.158
  5.6 7.9 %all-to-all-start = ((bf16[16,32,256]{2,1,0:T(8,128)(2,1)}), bf16[16,32,256]{2,1,0:T(8,128)(2,1)S(1)}, u32[]{:S(2)}, u32[]{:S(2)}) async-start(bf16[16,32,256]{2,1,0:T(8,128)(2,1)} %get-tuple-element.51.refs_6_), calls=%async_computation | async-start | bytes 524288 | tf_op jit(solution)/shard_map/all_to_all | solution.py:526
  13.5 1.3 collective-permute-start.7
  14.8 7.8 %shard_map.159 = (f32[512,384]{1,0:T(8,128)}, bf16[16,32,192]{2,1,0:T(8,128)(2,1)}, bf16[32,2432]{1,0:T(8,128)(2,1)}, f32[6,2432]{1,0:T(8,128)}) custom-call(s32[2]{0:T(128)} %refs_0_.5, s32[1]{0:T(128)} %bitcast.refs_1_, bf16[512,2432]{1,0:T(8,128)(2,1)} %refs_2_.3, f32[2,6,2,2432]{3,2,1,0:T(2,128)} %bitcast.33, bf16[3,2432,128]{2,1,0:T(8,128)(2,1)} %bitcast.38, ...), custom_call_target="tpu_custom_call" | custom-call | flops 1434451968 | bytes 7656460 | tf_op jit(solution)/shard_map/pallas_call | solution.py:80
  22.7 0.9 copy-done.15
  23.7 2.5 shard_map.162
  26.1 2.5 collective-permute-start.1
  29.9 1.9 collective-permute-start.8
  31.8 7.8 %collective-permute-done.1.refs_1_ = bf16[80,2944]{1,0:T(8,128)(2,1)S(1)} collective-permute-done((bf16[80,2944]{1,0:T(8,128)(2,1)}, bf16[80,2944]{1,0:T(8,128)(2,1)S(1)}, u32[]{:S(2)}, u32[]{:S(2)}) %collective-permute-start.1) | collective-permute-done | bytes 471072 | tf_op jit(solution)/shard_map/ppermute | solution.py:32
  40.4 2.9 %collective-permute-done.3.refs_3_ = bf16[80,2944]{1,0:T(8,128)(2,1)} collective-permute-done((bf16[80,2944]{1,0:T(8,128)(2,1)}, bf16[80,2944]{1,0:T(8,128)(2,1)}, u32[]{:S(2)}, u32[]{:S(2)}) %collective-permute-start.3) | collective-permute-done | bytes 471072 | tf_op jit(solution)/shard_map/ppermute | solution.py:32
  43.3 1.0 copy-done.13
  44.3 1.6 shard_map.163
  45.9 2.4 collective-permute-start.4
  49.5 1.0 shard_map.165.refs_4_.refs_7_
  50.5 1.3 collective-permute-done.4.refs_1_
  51.8 2.0 collective-permute-done.5.refs_2_
  53.8 1.7 collective-permute-done.6.refs_3_
  56.5 1.5 collective-permute-start.10
  58.0 1.2 collective-permute-start.9
  59.2 4.0 %collective-permute-done.11.refs_3_ = bf16[20,2944]{1,0:T(8,128)(2,1)S(1)} collective-permute-done((bf16[20,2944]{1,0:T(8,128)(2,1)S(1)}, bf16[20,2944]{1,0:T(8,128)(2,1)S(1)}, u32[]{:S(2)}, u32[]{:S(2)}) %collective-permute-start.11) | collective-permute-done | bytes 117792 | tf_op jit(solution)/shard_map/ppermute | solution.py:32
  64.0 2.1 collective-permute-start.13
  66.9 11.0 %collective-permute-done.14.refs_4_ = bf16[80,2944]{1,0:T(8,128)(2,1)S(1)} collective-permute-done((bf16[80,2944]{1,0:T(8,128)(2,1)S(1)}, bf16[80,2944]{1,0:T(8,128)(2,1)S(1)}, u32[]{:S(2)}, u32[]{:S(2)}) %collective-permute-start.14) | collective-permute-done | bytes 471072 | tf_op jit(solution)/shard_map/ppermute | solution.py:32
  78.6 2.2 shard_map.168
  82.4 9.8 %all-to-all-start.1 = ((bf16[8,64,512]{2,1,0:T(8,128)(2,1)}), bf16[8,64,512]{2,1,0:T(8,128)(2,1)S(1)}, u32[]{:S(2)}, u32[]{:S(2)}) async-start(bf16[8,64,512]{2,1,0:T(8,128)(2,1)} %bitcast.36), calls=%async_computation.1 | async-start | bytes 1048576 | tf_op jit(solution)/shard_map/all_to_all | solution.py:619
  92.3 1.1 copy-done.5
  93.4 1.0 copy-done.9
  94.4 1.5 shard_map.169.refs_1_
  96.7 5.0 %all-to-all-done.1.refs_2_ = bf16[8,64,512]{2,1,0:T(8,128)(2,1)S(1)} async-done(((bf16[8,64,512]{2,1,0:T(8,128)(2,1)}), bf16[8,64,512]{2,1,0:T(8,128)(2,1)S(1)}, u32[]{:S(2)}, u32[]{:S(2)}) %all-to-all-start.1) | async-done | bytes 524320 | tf_op jit(solution)/shard_map/all_to_all | solution.py:619
  101.7 1.0 copy-done.11
  102.8 1.1 copy-done.23
  103.8 2.5 shard_map.170
  106.3 2.4 collective-permute-start.15
  109.4 1.1 shard_map.171
  110.5 9.5 %all_to_all.20 = bf16[8,64,128]{2,1,0:T(8,128)(2,1)S(1)} all-to-all(bf16[8,64,128]{2,1,0:T(8,128)(2,1)S(1)} %shard_map.171), channel_id=1, replica_groups=mesh['grp'=8,'tp'=16] {'grp'}, dimensions={0} | all-to-all | bytes 262144 | tf_op jit(solution)/shard_map/all_to_all | solution.py:636
  120.1 2.5 collective-permute-done.15.refs_3_.refs_1_
  122.6 0.9 shard_map.172
  123.5 3.5 %collective-permute-start.18 = (bf16[80,2432]{1,0:T(8,128)(2,1)S(1)}, bf16[80,2432]{1,0:T(8,128)(2,1)S(1)}, u32[]{:S(2)}, u32[]{:S(2)}) collective-permute-start(bf16[80,2432]{1,0:T(8,128)(2,1)S(1)} %get-tuple-element.74), channel_id=1, source_target_pairs={{0,12},{1,13},{2,14},{3,15},{4,0},{5,1},{6,2},{7,3},{8,4},{9,5},{1... | collective-permute-start | bytes 1167368 | tf_op jit(solution)/shard_map/ppermute | solution.py:32
  127.6 8.2 %collective-permute-done.18.refs_5_ = bf16[80,2432]{1,0:T(8,128)(2,1)S(1)} collective-permute-done((bf16[80,2432]{1,0:T(8,128)(2,1)S(1)}, bf16[80,2432]{1,0:T(8,128)(2,1)S(1)}, u32[]{:S(2)}, u32[]{:S(2)}) %collective-permute-start.18) | collective-permute-done | bytes 389152 | tf_op jit(solution)/shard_map/ppermute | solution.py:32
  135.8 3.4 %collective-permute-done.20.refs_7_ = bf16[80,2432]{1,0:T(8,128)(2,1)S(1)} collective-permute-done((bf16[80,2432]{1,0:T(8,128)(2,1)S(1)}, bf16[80,2432]{1,0:T(8,128)(2,1)S(1)}, u32[]{:S(2)}, u32[]{:S(2)}) %collective-permute-start.20) | collective-permute-done | bytes 389152 | tf_op jit(solution)/shard_map/ppermute | solution.py:32
  140.1 2.3 collective-permute-start.21
  143.0 5.7 %collective-permute-done.21.refs_3_ = bf16[52,2432]{1,0:T(8,128)(2,1)S(1)} collective-permute-done((bf16[52,2432]{1,0:T(8,128)(2,1)S(1)}, bf16[52,2432]{1,0:T(8,128)(2,1)S(1)}, u32[]{:S(2)}, u32[]{:S(2)}) %collective-permute-start.21) | collective-permute-done | bytes 252960 | tf_op jit(solution)/shard_map/ppermute | solution.py:32
  149.3 2.8 %collective-permute-done.23.refs_5_ = bf16[52,2432]{1,0:T(8,128)(2,1)S(1)} collective-permute-done((bf16[52,2432]{1,0:T(8,128)(2,1)S(1)}, bf16[52,2432]{1,0:T(8,128)(2,1)S(1)}, u32[]{:S(2)}, u32[]{:S(2)}) %collective-permute-start.23) | collective-permute-done | bytes 252960 | tf_op jit(solution)/shard_map/ppermute | solution.py:32
  152.8 1.8 collective-permute-start.25
  154.5 0.9 collective-permute-start.24
  155.4 7.1 %collective-permute-done.26.refs_3_ = bf16[52,2432]{1,0:T(8,128)(2,1)S(1)} collective-permute-done((bf16[52,2432]{1,0:T(8,128)(2,1)S(1)}, bf16[52,2432]{1,0:T(8,128)(2,1)S(1)}, u32[]{:S(2)}, u32[]{:S(2)}) %collective-permute-start.26) | collective-permute-done | bytes 252960 | tf_op jit(solution)/shard_map/ppermute | solution.py:32
  163.3 1.6 collective-permute-start.28
  164.9 1.1 collective-permute-start.27
  166.0 22.9 %collective-permute-done.29.refs_3_ = bf16[208,2432]{1,0:T(8,128)(2,1)S(1)} collective-permute-done((bf16[208,2432]{1,0:T(8,128)(2,1)S(1)}, bf16[208,2432]{1,0:T(8,128)(2,1)S(1)}, u32[]{:S(2)}, u32[]{:S(2)}) %collective-permute-start.29) | collective-permute-done | bytes 1011744 | tf_op jit(solution)/shard_map/ppermute | solution.py:32
  189.7 2.7 %copy-done = bf16[2,608,2432]{2,1,0:T(8,128)(2,1)S(1)} copy-done((bf16[2,608,2432]{2,1,0:T(8,128)(2,1)S(1)}, bf16[2,608,2432]{2,1,0:T(8,128)(2,1)}, u32[]{:S(2)}) %copy-start) | copy-done | bytes 5914648
  192.4 4.9 %shard_map.176 = (bf16[128,2432]{1,0:T(8,128)(2,1)S(1)}, bf16[128,2432]{1,0:T(8,128)(2,1)S(1)}, bf16[128,2432]{1,0:T(8,128)(2,1)S(1)}, bf16[128,2432]{1,0:T(8,128)(2,1)S(1)}) custom-call(bf16[208,2432]{1,0:T(8,128)(2,1)S(1)} %shard_map.175.refs_0_, bf16[208,2432]{1,0:T(8,128)(2,1)S(1)} %collective-permute-done.27.refs_1_, ...), custom_call_target="tpu_custom_call" | custom-call | flops 3028287488 | bytes 18366464 | tf_op jit(solution)/shard_map/pallas_call | solution.py:80
  197.3 3.2 %shard_map.177 = (bf16[80,2432]{1,0:T(8,128)(2,1)S(1)}, bf16[80,2432]{1,0:T(8,128)(2,1)S(1)}, bf16[80,2432]{1,0:T(8,128)(2,1)S(1)}, bf16[80,2432]{1,0:T(8,128)(2,1)S(1)}) custom-call(bf16[208,2432]{1,0:T(8,128)(2,1)S(1)} %shard_map.175.refs_0_, bf16[208,2432]{1,0:T(8,128)(2,1)S(1)} %collective-permute-done.27.refs_1_, ...), custom_call_target="tpu_custom_call" | custom-call | flops 1892679680 | bytes 17432576 | tf_op jit(solution)/shard_map/pallas_call | solution.py:80
  200.6 2.1 collective-permute-start.33
  202.7 1.2 collective-permute-start.31
  204.1 3.6 %collective-permute-start.34 = (bf16[80,2432]{1,0:T(8,128)(2,1)S(1)}, bf16[80,2432]{1,0:T(8,128)(2,1)S(1)}, u32[]{:S(2)}, u32[]{:S(2)}) collective-permute-start(bf16[80,2432]{1,0:T(8,128)(2,1)S(1)} %get-tuple-element.91), channel_id=1, source_target_pairs={{0,8},{1,9},{2,10},{3,11},{4,12},{5,13},{6,14},{7,15},{8,0},{9,1},... | collective-permute-start | bytes 1167368 | tf_op jit(solution)/shard_map/ppermute | solution.py:32
  207.7 16.6 %collective-permute-done.34.refs_6_ = bf16[80,2432]{1,0:T(8,128)(2,1)S(1)} collective-permute-done((bf16[80,2432]{1,0:T(8,128)(2,1)S(1)}, bf16[80,2432]{1,0:T(8,128)(2,1)S(1)}, u32[]{:S(2)}, u32[]{:S(2)}) %collective-permute-start.34) | collective-permute-done | bytes 389152 | tf_op jit(solution)/shard_map/ppermute | solution.py:32
  224.3 4.3 %collective-permute-done.35.refs_7_ = bf16[80,2432]{1,0:T(8,128)(2,1)S(1)} collective-permute-done((bf16[80,2432]{1,0:T(8,128)(2,1)S(1)}, bf16[80,2432]{1,0:T(8,128)(2,1)S(1)}, u32[]{:S(2)}, u32[]{:S(2)}) %collective-permute-start.35) | collective-permute-done | bytes 389152 | tf_op jit(solution)/shard_map/ppermute | solution.py:32
  229.5 2.0 collective-permute-start.36
  232.2 5.7 %collective-permute-done.36.refs_3_ = bf16[52,2432]{1,0:T(8,128)(2,1)S(1)} collective-permute-done((bf16[52,2432]{1,0:T(8,128)(2,1)S(1)}, bf16[52,2432]{1,0:T(8,128)(2,1)S(1)}, u32[]{:S(2)}, u32[]{:S(2)}) %collective-permute-start.36) | collective-permute-done | bytes 252960 | tf_op jit(solution)/shard_map/ppermute | solution.py:32
  238.5 2.7 %collective-permute-done.38.refs_5_ = bf16[52,2432]{1,0:T(8,128)(2,1)S(1)} collective-permute-done((bf16[52,2432]{1,0:T(8,128)(2,1)S(1)}, bf16[52,2432]{1,0:T(8,128)(2,1)S(1)}, u32[]{:S(2)}, u32[]{:S(2)}) %collective-permute-start.38) | collective-permute-done | bytes 252960 | tf_op jit(solution)/shard_map/ppermute | solution.py:32
  241.3 1.0 shard_map.179
  242.3 21.4 %all_to_all.21 = bf16[8,4,2432]{2,1,0:T(4,128)(2,1)S(1)} all-to-all(bf16[8,4,2432]{2,1,0:T(4,128)(2,1)S(1)} %reshape.26), channel_id=1, replica_groups=mesh['grp'=8,'tp'=16] {'grp'}, dimensions={0} | all-to-all | bytes 311296 | tf_op jit(solution)/shard_map/all_to_all | solution.py:665
  (102 shorter events, 18.6 us)
Async XLA Ops:
  0.6 0.9 copy-start.4
  1.6 11.9 %collective-permute-start = (f32[2,8,2432]{2,1,0:T(8,128)S(1)}, f32[2,8,2432]{2,1,0:T(8,128)S(1)}, u32[]{:S(2)}, u32[]{:S(2)}) collective-permute-start(f32[2,8,2432]{2,1,0:T(8,128)S(1)} %shard_map.160.refs_0_), channel_id=1, source_target_pairs={{0,16},{16,0},{32,48},{48,32},{64,80},{80,64},{96,112},{112,96},{1... | collective-permute-start | bytes 466952 | tf_op jit(solution)/shard_map/ppermute | solution.py:36
  3.1 0.9 copy-start.16
  5.6 17.1 %all-to-all-start = ((bf16[16,32,256]{2,1,0:T(8,128)(2,1)}), bf16[16,32,256]{2,1,0:T(8,128)(2,1)S(1)}, u32[]{:S(2)}, u32[]{:S(2)}) async-start(bf16[16,32,256]{2,1,0:T(8,128)(2,1)} %get-tuple-element.51.refs_6_), calls=%async_computation | async-start | bytes 524288 | tf_op jit(solution)/shard_map/all_to_all | solution.py:526
  13.5 16.3 %collective-permute-start.7 = (f32[4,8,2432]{2,1,0:T(8,128)S(1)}, f32[4,8,2432]{2,1,0:T(8,128)S(1)}, u32[]{:S(2)}, u32[]{:S(2)}) collective-permute-start(f32[4,8,2432]{2,1,0:T(8,128)S(1)} %shard_map.161.refs_4_.refs_0_), channel_id=1, source_target_pairs={{0,32},{16,48},{32,0},{48,16},{64,96},{80,112},{96,64},{112,80},{1... | collective-permute-start | bytes 933896 | tf_op jit(solution)/shard_map/ppermute | solution.py:44
  14.8 7.9 %copy-start.3 = (bf16[256,2432]{1,0:T(8,128)(2,1)S(1)}, bf16[256,2432]{1,0:T(8,128)(2,1)}, u32[]{:S(2)}) copy-start(bf16[256,2432]{1,0:T(8,128)(2,1)} %refs_2_.4) | copy-start | bytes 3735556
  22.7 1.0 copy-start.15
  26.1 23.3 %copy-start.21 = (s32[20,1]{0,1:T(1,128)S(1)}, s32[20,1]{0,1:T(1,128)}, u32[]{:S(2)}) copy-start(s32[20,1]{0,1:T(1,128)} %param.17) | copy-start | bytes 244
  26.1 13.5 %collective-permute-start.1 = (bf16[80,2944]{1,0:T(8,128)(2,1)}, bf16[80,2944]{1,0:T(8,128)(2,1)S(1)}, u32[]{:S(2)}, u32[]{:S(2)}) collective-permute-start(bf16[80,2944]{1,0:T(8,128)(2,1)} %get-tuple-element.55), channel_id=1, source_target_pairs={{0,12},{1,13},{2,14},{3,15},{4,0},{5,1},{6,2},{7,3},{8,4},{9,5},{1... | collective-permute-start | bytes 1413128 | tf_op jit(solution)/shard_map/ppermute | solution.py:32
  28.7 11.7 %collective-permute-start.2 = (bf16[80,2944]{1,0:T(8,128)(2,1)}, bf16[80,2944]{1,0:T(8,128)(2,1)}, u32[]{:S(2)}, u32[]{:S(2)}) collective-permute-start(bf16[80,2944]{1,0:T(8,128)(2,1)} %get-tuple-element.56), channel_id=1, source_target_pairs={{0,8},{1,9},{2,10},{3,11},{4,12},{5,13},{6,14},{7,15},{8,0},{9,1},... | collective-permute-start | bytes 1413128 | tf_op jit(solution)/shard_map/ppermute | solution.py:32
  29.2 14.0 %collective-permute-start.3 = (bf16[80,2944]{1,0:T(8,128)(2,1)}, bf16[80,2944]{1,0:T(8,128)(2,1)}, u32[]{:S(2)}, u32[]{:S(2)}) collective-permute-start(bf16[80,2944]{1,0:T(8,128)(2,1)} %get-tuple-element.57), channel_id=1, source_target_pairs={{0,4},{1,5},{2,6},{3,7},{4,8},{5,9},{6,10},{7,11},{8,12},{9,13},{1... | collective-permute-start | bytes 1413128 | tf_op jit(solution)/shard_map/ppermute | solution.py:32
  29.9 19.6 %collective-permute-start.8 = (f32[8,8,2432]{2,1,0:T(8,128)S(1)}, f32[8,8,2432]{2,1,0:T(8,128)S(1)}, u32[]{:S(2)}, u32[]{:S(2)}) collective-permute-start(f32[8,8,2432]{2,1,0:T(8,128)S(1)} %shard_map.164.refs_1_), channel_id=1, source_target_pairs={{0,96},{16,112},{32,64},{48,80},{64,32},{80,48},{96,0},{112,16},{1... | collective-permute-start | bytes 1867784 | tf_op jit(solution)/shard_map/ppermute | solution.py:44
  43.3 1.0 copy-start.13
  45.9 5.9 %collective-permute-start.4 = (bf16[20,2944]{1,0:T(8,128)(2,1)S(1)}, bf16[20,2944]{1,0:T(8,128)(2,1)S(1)}, u32[]{:S(2)}, u32[]{:S(2)}) collective-permute-start(bf16[20,2944]{1,0:T(8,128)(2,1)S(1)} %get-tuple-element.59), channel_id=1, source_target_pairs={{0,3},{1,0},{2,1},{3,2},{4,7},{5,4},{6,5},{7,6},{8,11},{9,8},{10,9... | collective-permute-start | bytes 353288 | tf_op jit(solution)/shard_map/ppermute | solution.py:32
  48.3 5.5 %collective-permute-start.5 = (bf16[20,2944]{1,0:T(8,128)(2,1)S(1)}, bf16[20,2944]{1,0:T(8,128)(2,1)S(1)}, u32[]{:S(2)}, u32[]{:S(2)}) collective-permute-start(bf16[20,2944]{1,0:T(8,128)(2,1)S(1)} %get-tuple-element.60), channel_id=1, source_target_pairs={{0,2},{1,3},{2,0},{3,1},{4,6},{5,7},{6,4},{7,5},{8,10},{9,11},{10,... | collective-permute-start | bytes 353288 | tf_op jit(solution)/shard_map/ppermute | solution.py:32
  48.9 6.7 %collective-permute-start.6 = (bf16[20,2944]{1,0:T(8,128)(2,1)S(1)}, bf16[20,2944]{1,0:T(8,128)(2,1)S(1)}, u32[]{:S(2)}, u32[]{:S(2)}) collective-permute-start(bf16[20,2944]{1,0:T(8,128)(2,1)S(1)} %get-tuple-element.61), channel_id=1, source_target_pairs={{0,1},{1,2},{2,3},{3,0},{4,5},{5,6},{6,7},{7,4},{8,9},{9,10},{10,1... | collective-permute-start | bytes 353288 | tf_op jit(solution)/shard_map/ppermute | solution.py:32
  50.5 16.4 %copy-start.24 = (f32[2,2,64]{2,1,0:T(2,128)S(1)}, f32[2,2,64]{2,1,0:T(2,128)}, u32[]{:S(2)}) copy-start(f32[2,2,64]{2,1,0:T(2,128)} %param.20) | copy-start | bytes 3076
  50.5 28.1 %copy-start.1 = (bf16[2432,3,128]{2,0,1:T(8,128)(2,1)S(1)}, bf16[2432,3,128]{2,0,1:T(8,128)(2,1)}, u32[]{:S(2)}) copy-start(bf16[2432,3,128]{2,0,1:T(8,128)(2,1)} %param.23) | copy-start | bytes 5603332
  56.5 6.7 %collective-permute-start.11 = (bf16[20,2944]{1,0:T(8,128)(2,1)S(1)}, bf16[20,2944]{1,0:T(8,128)(2,1)S(1)}, u32[]{:S(2)}, u32[]{:S(2)}) collective-permute-start(bf16[20,2944]{1,0:T(8,128)(2,1)S(1)} %get-tuple-element.63.refs_0_), channel_id=1, source_target_pairs={{0,1},{1,2},{2,3},{3,0},{4,5},{5,6},{6,7},{7,4},{8,9},{9,10},{10,1... | collective-permute-start | bytes 353288 | tf_op jit(solution)/shard_map/ppermute | solution.py:32
  56.5 6.7 %collective-permute-start.10 = (bf16[20,2944]{1,0:T(8,128)(2,1)S(1)}, bf16[20,2944]{1,0:T(8,128)(2,1)S(1)}, u32[]{:S(2)}, u32[]{:S(2)}) collective-permute-start(bf16[20,2944]{1,0:T(8,128)(2,1)S(1)} %get-tuple-element.63.refs_0_), channel_id=1, source_target_pairs={{0,2},{1,3},{2,0},{3,1},{4,6},{5,7},{6,4},{7,5},{8,10},{9,11},{10,... | collective-permute-start | bytes 353288 | tf_op jit(solution)/shard_map/ppermute | solution.py:32
  58.0 5.8 %collective-permute-start.9 = (bf16[20,2944]{1,0:T(8,128)(2,1)S(1)}, bf16[20,2944]{1,0:T(8,128)(2,1)S(1)}, u32[]{:S(2)}, u32[]{:S(2)}) collective-permute-start(bf16[20,2944]{1,0:T(8,128)(2,1)S(1)} %get-tuple-element.63.refs_0_), channel_id=1, source_target_pairs={{0,3},{1,0},{2,1},{3,2},{4,7},{5,4},{6,5},{7,6},{8,11},{9,8},{10,9... | collective-permute-start | bytes 353288 | tf_op jit(solution)/shard_map/ppermute | solution.py:32
  63.9 14.1 %collective-permute-start.14 = (bf16[80,2944]{1,0:T(8,128)(2,1)S(1)}, bf16[80,2944]{1,0:T(8,128)(2,1)S(1)}, u32[]{:S(2)}, u32[]{:S(2)}) collective-permute-start(bf16[80,2944]{1,0:T(8,128)(2,1)S(1)} %shard_map.167.refs_1_), channel_id=1, source_target_pairs={{0,4},{1,5},{2,6},{3,7},{4,8},{5,9},{6,10},{7,11},{8,12},{9,13},{1... | collective-permute-start | bytes 1413128 | tf_op jit(solution)/shard_map/ppermute | solution.py:32
  64.0 14.0 %collective-permute-start.13 = (bf16[80,2944]{1,0:T(8,128)(2,1)S(1)}, bf16[80,2944]{1,0:T(8,128)(2,1)S(1)}, u32[]{:S(2)}, u32[]{:S(2)}) collective-permute-start(bf16[80,2944]{1,0:T(8,128)(2,1)S(1)} %shard_map.167.refs_1_), channel_id=1, source_target_pairs={{0,8},{1,9},{2,10},{3,11},{4,12},{5,13},{6,14},{7,15},{8,0},{9,1},... | collective-permute-start | bytes 1413128 | tf_op jit(solution)/shard_map/ppermute | solution.py:32
  66.0 12.6 %collective-permute-start.12 = (bf16[80,2944]{1,0:T(8,128)(2,1)S(1)}, bf16[80,2944]{1,0:T(8,128)(2,1)S(1)}, u32[]{:S(2)}, u32[]{:S(2)}) collective-permute-start(bf16[80,2944]{1,0:T(8,128)(2,1)S(1)} %shard_map.167.refs_1_), channel_id=1, source_target_pairs={{0,12},{1,13},{2,14},{3,15},{4,0},{5,1},{6,2},{7,3},{8,4},{9,5},{1... | collective-permute-start | bytes 1413128 | tf_op jit(solution)/shard_map/ppermute | solution.py:32
  78.6 13.6 %copy-start.2 = (bf16[32,3,64,128]{3,2,1,0:T(8,128)(2,1)S(1)}, bf16[32,3,64,128]{3,2,1,0:T(8,128)(2,1)}, u32[]{:S(2)}) copy-start(bf16[32,3,64,128]{3,2,1,0:T(8,128)(2,1)} %refs_3_.2) | copy-start | bytes 4718596
  78.6 13.6 %copy-start.22 = (s32[2]{0:T(128)S(1)}, s32[2]{0:T(128)}, u32[]{:S(2)}) copy-start(s32[2]{0:T(128)} %refs_0_.5) | copy-start | bytes 28
  80.8 0.8 copy-start.7
  81.6 0.8 copy-start.8
  82.4 19.3 %all-to-all-start.1 = ((bf16[8,64,512]{2,1,0:T(8,128)(2,1)}), bf16[8,64,512]{2,1,0:T(8,128)(2,1)S(1)}, u32[]{:S(2)}, u32[]{:S(2)}) async-start(bf16[8,64,512]{2,1,0:T(8,128)(2,1)} %bitcast.36), calls=%async_computation.1 | async-start | bytes 1048576 | tf_op jit(solution)/shard_map/all_to_all | solution.py:619
  92.2 1.1 copy-start.5
  93.4 1.0 copy-start.9
  101.7 1.0 copy-start.11
  102.8 1.1 copy-start.23
  106.3 16.2 %copy-start.6 = (bf16[128,2432]{1,0:T(8,128)(2,1)S(1)}, bf16[128,2432]{1,0:T(8,128)(2,1)}, u32[]{:S(2)}) copy-start(bf16[128,2432]{1,0:T(8,128)(2,1)} %refs_2_.5) | copy-start | bytes 1867780
  106.3 16.2 %collective-permute-start.15 = (bf16[128,2432]{1,0:T(8,128)(2,1)S(1)}, bf16[128,2432]{1,0:T(8,128)(2,1)S(1)}, u32[]{:S(2)}, u32[]{:S(2)}) collective-permute-start(bf16[128,2432]{1,0:T(8,128)(2,1)S(1)} %get-tuple-element.69), channel_id=1, source_target_pairs={{0,12},{1,13},{2,14},{3,15},{4,0},{5,1},{6,2},{7,3},{8,4},{9,5},{1... | collective-permute-start | bytes 1867784 | tf_op jit(solution)/shard_map/ppermute | solution.py:32
  108.7 18.9 %collective-permute-start.16 = (bf16[128,2432]{1,0:T(8,128)(2,1)S(1)}, bf16[128,2432]{1,0:T(8,128)(2,1)S(1)}, u32[]{:S(2)}, u32[]{:S(2)}) collective-permute-start(bf16[128,2432]{1,0:T(8,128)(2,1)S(1)} %get-tuple-element.70), channel_id=1, source_target_pairs={{0,8},{1,9},{2,10},{3,11},{4,12},{5,13},{6,14},{7,15},{8,0},{9,1},... | collective-permute-start | bytes 1867784 | tf_op jit(solution)/shard_map/ppermute | solution.py:32
  108.7 18.9 %collective-permute-start.17 = (bf16[128,2432]{1,0:T(8,128)(2,1)S(1)}, bf16[128,2432]{1,0:T(8,128)(2,1)S(1)}, u32[]{:S(2)}, u32[]{:S(2)}) collective-permute-start(bf16[128,2432]{1,0:T(8,128)(2,1)S(1)} %get-tuple-element.71), channel_id=1, source_target_pairs={{0,4},{1,5},{2,6},{3,7},{4,8},{5,9},{6,10},{7,11},{8,12},{9,13},{1... | collective-permute-start | bytes 1867784 | tf_op jit(solution)/shard_map/ppermute | solution.py:32
  109.4 80.3 %slice-start = ((s8[5914624]{0:T(1024)(128)(4,1)}), s8[4194304]{0:T(1024)(128)(4,1)S(1)}, s32[]{:S(2)}) async-start(s8[5914624]{0:T(1024)(128)(4,1)} %bitcast.28), calls=%async_computation.4 | async-start | bytes 8388608
  123.5 12.3 %collective-permute-start.18 = (bf16[80,2432]{1,0:T(8,128)(2,1)S(1)}, bf16[80,2432]{1,0:T(8,128)(2,1)S(1)}, u32[]{:S(2)}, u32[]{:S(2)}) collective-permute-start(bf16[80,2432]{1,0:T(8,128)(2,1)S(1)} %get-tuple-element.74), channel_id=1, source_target_pairs={{0,12},{1,13},{2,14},{3,15},{4,0},{5,1},{6,2},{7,3},{8,4},{9,5},{1... | collective-permute-start | bytes 1167368 | tf_op jit(solution)/shard_map/ppermute | solution.py:32
  127.0 8.8 %collective-permute-start.19 = (bf16[80,2432]{1,0:T(8,128)(2,1)S(1)}, bf16[80,2432]{1,0:T(8,128)(2,1)S(1)}, u32[]{:S(2)}, u32[]{:S(2)}) collective-permute-start(bf16[80,2432]{1,0:T(8,128)(2,1)S(1)} %get-tuple-element.75), channel_id=1, source_target_pairs={{0,8},{1,9},{2,10},{3,11},{4,12},{5,13},{6,14},{7,15},{8,0},{9,1},... | collective-permute-start | bytes 1167368 | tf_op jit(solution)/shard_map/ppermute | solution.py:32
  127.0 12.3 %collective-permute-start.20 = (bf16[80,2432]{1,0:T(8,128)(2,1)S(1)}, bf16[80,2432]{1,0:T(8,128)(2,1)S(1)}, u32[]{:S(2)}, u32[]{:S(2)}) collective-permute-start(bf16[80,2432]{1,0:T(8,128)(2,1)S(1)} %get-tuple-element.76), channel_id=1, source_target_pairs={{0,4},{1,5},{2,6},{3,7},{4,8},{5,9},{6,10},{7,11},{8,12},{9,13},{1... | collective-permute-start | bytes 1167368 | tf_op jit(solution)/shard_map/ppermute | solution.py:32
  139.2 12.9 %copy-start.14 = (f32[6,2432]{1,0:T(8,128)S(1)}, f32[6,2432]{1,0:T(8,128)}, u32[]{:S(2)}) copy-start(f32[6,2432]{1,0:T(8,128)} %get-tuple-element.81.refs_6_) | copy-start | bytes 175108
  139.2 12.9 %copy-start.17 = (bf16[32,2432]{1,0:T(8,128)(2,1)S(1)}, bf16[32,2432]{1,0:T(8,128)(2,1)}, u32[]{:S(2)}) copy-start(bf16[32,2432]{1,0:T(8,128)(2,1)} %get-tuple-element.52.refs_0_) | copy-start | bytes 466948
  139.2 12.9 %copy-start.19 = (bf16[20,2432]{1,0:T(8,128)(2,1)S(1)}, bf16[20,2432]{1,0:T(8,128)(2,1)}, u32[]{:S(2)}) copy-start(bf16[20,2432]{1,0:T(8,128)(2,1)} %copy-done.18) | copy-start | bytes 291844
  139.2 50.5 %slice-start.1 = ((s8[5914624]{0:T(1024)(128)(4,1)}), s8[1720320]{0:T(1024)(128)(4,1)S(1)}, s32[]{:S(2)}) async-start(s8[5914624]{0:T(1024)(128)(4,1)} %bitcast.28), calls=%async_computation.5 | async-start | bytes 3440640
  140.1 8.6 %collective-permute-start.21 = (bf16[52,2432]{1,0:T(8,128)(2,1)S(1)}, bf16[52,2432]{1,0:T(8,128)(2,1)S(1)}, u32[]{:S(2)}, u32[]{:S(2)}) collective-permute-start(bf16[52,2432]{1,0:T(8,128)(2,1)S(1)} %get-tuple-element.78), channel_id=1, source_target_pairs={{0,3},{1,0},{2,1},{3,2},{4,7},{5,4},{6,5},{7,6},{8,11},{9,8},{10,9... | collective-permute-start | bytes 758792 | tf_op jit(solution)/shard_map/ppermute | solution.py:32
  142.4 6.9 %collective-permute-start.22 = (bf16[52,2432]{1,0:T(8,128)(2,1)S(1)}, bf16[52,2432]{1,0:T(8,128)(2,1)S(1)}, u32[]{:S(2)}, u32[]{:S(2)}) collective-permute-start(bf16[52,2432]{1,0:T(8,128)(2,1)S(1)} %get-tuple-element.79), channel_id=1, source_target_pairs={{0,2},{1,3},{2,0},{3,1},{4,6},{5,7},{6,4},{7,5},{8,10},{9,11},{10,... | collective-permute-start | bytes 758792 | tf_op jit(solution)/shard_map/ppermute | solution.py:32
  142.4 9.8 %collective-permute-start.23 = (bf16[52,2432]{1,0:T(8,128)(2,1)S(1)}, bf16[52,2432]{1,0:T(8,128)(2,1)S(1)}, u32[]{:S(2)}, u32[]{:S(2)}) collective-permute-start(bf16[52,2432]{1,0:T(8,128)(2,1)S(1)} %get-tuple-element.80), channel_id=1, source_target_pairs={{0,1},{1,2},{2,3},{3,0},{4,5},{5,6},{6,7},{7,4},{8,9},{9,10},{10,1... | collective-permute-start | bytes 758792 | tf_op jit(solution)/shard_map/ppermute | solution.py:32
  152.7 9.8 %collective-permute-start.26 = (bf16[52,2432]{1,0:T(8,128)(2,1)S(1)}, bf16[52,2432]{1,0:T(8,128)(2,1)S(1)}, u32[]{:S(2)}, u32[]{:S(2)}) collective-permute-start(bf16[52,2432]{1,0:T(8,128)(2,1)S(1)} %get-tuple-element.84.refs_0_), channel_id=1, source_target_pairs={{0,1},{1,2},{2,3},{3,0},{4,5},{5,6},{6,7},{7,4},{8,9},{9,10},{10,1... | collective-permute-start | bytes 758792 | tf_op jit(solution)/shard_map/ppermute | solution.py:32
  152.8 9.7 %collective-permute-start.25 = (bf16[52,2432]{1,0:T(8,128)(2,1)S(1)}, bf16[52,2432]{1,0:T(8,128)(2,1)S(1)}, u32[]{:S(2)}, u32[]{:S(2)}) collective-permute-start(bf16[52,2432]{1,0:T(8,128)(2,1)S(1)} %get-tuple-element.84.refs_0_), channel_id=1, source_target_pairs={{0,2},{1,3},{2,0},{3,1},{4,6},{5,7},{6,4},{7,5},{8,10},{9,11},{10,... | collective-permute-start | bytes 758792 | tf_op jit(solution)/shard_map/ppermute | solution.py:32
  154.5 8.6 %collective-permute-start.24 = (bf16[52,2432]{1,0:T(8,128)(2,1)S(1)}, bf16[52,2432]{1,0:T(8,128)(2,1)S(1)}, u32[]{:S(2)}, u32[]{:S(2)}) collective-permute-start(bf16[52,2432]{1,0:T(8,128)(2,1)S(1)} %get-tuple-element.84.refs_0_), channel_id=1, source_target_pairs={{0,3},{1,0},{2,1},{3,2},{4,7},{5,4},{6,5},{7,6},{8,11},{9,8},{10,9... | collective-permute-start | bytes 758792 | tf_op jit(solution)/shard_map/ppermute | solution.py:32
  163.3 25.7 %collective-permute-start.29 = (bf16[208,2432]{1,0:T(8,128)(2,1)S(1)}, bf16[208,2432]{1,0:T(8,128)(2,1)S(1)}, u32[]{:S(2)}, u32[]{:S(2)}) collective-permute-start(bf16[208,2432]{1,0:T(8,128)(2,1)S(1)} %shard_map.175.refs_0_), channel_id=1, source_target_pairs={{0,4},{1,5},{2,6},{3,7},{4,8},{5,9},{6,10},{7,11},{8,12},{9,13},{1... | collective-permute-start | bytes 3035144 | tf_op jit(solution)/shard_map/ppermute | solution.py:32
  163.3 25.6 %collective-permute-start.28 = (bf16[208,2432]{1,0:T(8,128)(2,1)S(1)}, bf16[208,2432]{1,0:T(8,128)(2,1)S(1)}, u32[]{:S(2)}, u32[]{:S(2)}) collective-permute-start(bf16[208,2432]{1,0:T(8,128)(2,1)S(1)} %shard_map.175.refs_0_), channel_id=1, source_target_pairs={{0,8},{1,9},{2,10},{3,11},{4,12},{5,13},{6,14},{7,15},{8,0},{9,1},... | collective-permute-start | bytes 3035144 | tf_op jit(solution)/shard_map/ppermute | solution.py:32
  164.9 24.8 %collective-permute-start.27 = (bf16[208,2432]{1,0:T(8,128)(2,1)S(1)}, bf16[208,2432]{1,0:T(8,128)(2,1)S(1)}, u32[]{:S(2)}, u32[]{:S(2)}) collective-permute-start(bf16[208,2432]{1,0:T(8,128)(2,1)S(1)} %shard_map.175.refs_0_), channel_id=1, source_target_pairs={{0,12},{1,13},{2,14},{3,15},{4,0},{5,1},{6,2},{7,3},{8,4},{9,5},{1... | collective-permute-start | bytes 3035144 | tf_op jit(solution)/shard_map/ppermute | solution.py:32
  189.7 2.7 %copy-start = (bf16[2,608,2432]{2,1,0:T(8,128)(2,1)S(1)}, bf16[2,608,2432]{2,1,0:T(8,128)(2,1)}, u32[]{:S(2)}) copy-start(bf16[2,608,2432]{2,1,0:T(8,128)(2,1)} %refs_5_.5) | copy-start | bytes 17743876
  200.6 7.1 %collective-permute-start.33 = (bf16[80,2432]{1,0:T(8,128)(2,1)S(1)}, bf16[80,2432]{1,0:T(8,128)(2,1)S(1)}, u32[]{:S(2)}, u32[]{:S(2)}) collective-permute-start(bf16[80,2432]{1,0:T(8,128)(2,1)S(1)} %get-tuple-element.90), channel_id=1, source_target_pairs={{0,12},{1,13},{2,14},{3,15},{4,0},{5,1},{6,2},{7,3},{8,4},{9,5},{1... | collective-permute-start | bytes 1167368 | tf_op jit(solution)/shard_map/ppermute | solution.py:32
  202.6 26.0 %collective-permute-start.30 = (bf16[128,2432]{1,0:T(8,128)(2,1)S(1)}, bf16[128,2432]{1,0:T(8,128)(2,1)S(1)}, u32[]{:S(2)}, u32[]{:S(2)}) collective-permute-start(bf16[128,2432]{1,0:T(8,128)(2,1)S(1)} %get-tuple-element.86), channel_id=1, source_target_pairs={{0,12},{1,13},{2,14},{3,15},{4,0},{5,1},{6,2},{7,3},{8,4},{9,5},{1... | collective-permute-start | bytes 1867784 | tf_op jit(solution)/shard_map/ppermute | solution.py:32
  202.7 25.9 %collective-permute-start.31 = (bf16[128,2432]{1,0:T(8,128)(2,1)S(1)}, bf16[128,2432]{1,0:T(8,128)(2,1)S(1)}, u32[]{:S(2)}, u32[]{:S(2)}) collective-permute-start(bf16[128,2432]{1,0:T(8,128)(2,1)S(1)} %get-tuple-element.87), channel_id=1, source_target_pairs={{0,8},{1,9},{2,10},{3,11},{4,12},{5,13},{6,14},{7,15},{8,0},{9,1},... | collective-permute-start | bytes 1867784 | tf_op jit(solution)/shard_map/ppermute | solution.py:32
  203.9 24.7 %collective-permute-start.32 = (bf16[128,2432]{1,0:T(8,128)(2,1)S(1)}, bf16[128,2432]{1,0:T(8,128)(2,1)S(1)}, u32[]{:S(2)}, u32[]{:S(2)}) collective-permute-start(bf16[128,2432]{1,0:T(8,128)(2,1)S(1)} %get-tuple-element.88), channel_id=1, source_target_pairs={{0,4},{1,5},{2,6},{3,7},{4,8},{5,9},{6,10},{7,11},{8,12},{9,13},{1... | collective-permute-start | bytes 1867784 | tf_op jit(solution)/shard_map/ppermute | solution.py:32
  204.1 20.2 %collective-permute-start.34 = (bf16[80,2432]{1,0:T(8,128)(2,1)S(1)}, bf16[80,2432]{1,0:T(8,128)(2,1)S(1)}, u32[]{:S(2)}, u32[]{:S(2)}) collective-permute-start(bf16[80,2432]{1,0:T(8,128)(2,1)S(1)} %get-tuple-element.91), channel_id=1, source_target_pairs={{0,8},{1,9},{2,10},{3,11},{4,12},{5,13},{6,14},{7,15},{8,0},{9,1},... | collective-permute-start | bytes 1167368 | tf_op jit(solution)/shard_map/ppermute | solution.py:32
  207.7 20.9 %collective-permute-start.35 = (bf16[80,2432]{1,0:T(8,128)(2,1)S(1)}, bf16[80,2432]{1,0:T(8,128)(2,1)S(1)}, u32[]{:S(2)}, u32[]{:S(2)}) collective-permute-start(bf16[80,2432]{1,0:T(8,128)(2,1)S(1)} %get-tuple-element.92), channel_id=1, source_target_pairs={{0,4},{1,5},{2,6},{3,7},{4,8},{5,9},{6,10},{7,11},{8,12},{9,13},{1... | collective-permute-start | bytes 1167368 | tf_op jit(solution)/shard_map/ppermute | solution.py:32
  229.5 8.4 %collective-permute-start.36 = (bf16[52,2432]{1,0:T(8,128)(2,1)S(1)}, bf16[52,2432]{1,0:T(8,128)(2,1)S(1)}, u32[]{:S(2)}, u32[]{:S(2)}) collective-permute-start(bf16[52,2432]{1,0:T(8,128)(2,1)S(1)} %get-tuple-element.94), channel_id=1, source_target_pairs={{0,3},{1,0},{2,1},{3,2},{4,7},{5,4},{6,5},{7,6},{8,11},{9,8},{10,9... | collective-permute-start | bytes 758792 | tf_op jit(solution)/shard_map/ppermute | solution.py:32
  231.5 7.0 %collective-permute-start.37 = (bf16[52,2432]{1,0:T(8,128)(2,1)S(1)}, bf16[52,2432]{1,0:T(8,128)(2,1)S(1)}, u32[]{:S(2)}, u32[]{:S(2)}) collective-permute-start(bf16[52,2432]{1,0:T(8,128)(2,1)S(1)} %get-tuple-element.95), channel_id=1, source_target_pairs={{0,2},{1,3},{2,0},{3,1},{4,6},{5,7},{6,4},{7,5},{8,10},{9,11},{10,... | collective-permute-start | bytes 758792 | tf_op jit(solution)/shard_map/ppermute | solution.py:32
  231.5 9.7 %collective-permute-start.38 = (bf16[52,2432]{1,0:T(8,128)(2,1)S(1)}, bf16[52,2432]{1,0:T(8,128)(2,1)S(1)}, u32[]{:S(2)}, u32[]{:S(2)}) collective-permute-start(bf16[52,2432]{1,0:T(8,128)(2,1)S(1)} %get-tuple-element.96), channel_id=1, source_target_pairs={{0,1},{1,2},{2,3},{3,0},{4,5},{5,6},{6,7},{7,4},{8,9},{9,10},{10,1... | collective-permute-start | bytes 758792 | tf_op jit(solution)/shard_map/ppermute | solution.py:32
  (4 other events, 2.9 us)

commit v4 on v3

--- a/solution.py
+++ b/solution.py
@@ -192,6 +192,20 @@
             jnp.add, [piece[rows, :].astype(F32) for piece in img]
         ).astype(BF16)
         out[32 : 32 + POOL, :] = held[near * POOL : (near + 1) * POOL, :].astype(BF16)
+
+
+def part_middle_kernel(
+    in0, in1, in2, in3, txt0, txt1, txt2, txt3, img0, img1, img2, img3, held
+):
+    pieces = (in0, in1, in2, in3)
+    held[...] = functools.reduce(jnp.add, [piece[128:, :].astype(F32) for piece in pieces])
+    for near, out in enumerate((txt0, txt1, txt2, txt3)):
+        out[...] = held[near * POOL : (near + 1) * POOL, :].astype(BF16)
+    for near, out in enumerate((img0, img1, img2, img3)):
+        rows = slice(near * 32, (near + 1) * 32)
+        out[...] = functools.reduce(
+            jnp.add, [piece[rows, :].astype(F32) for piece in pieces]
+        ).astype(BF16)
 
 
 def join_kernel(in0, in1, in2, in3, out_ref, held):
@@ -415,28 +429,35 @@
         out[...] = result[place * part : (place + 1) * part].astype(BF16)
 
 
-def feed_kernel(
-    start, stream, in0, in1, in2, in3, win_ref, wout_ref, out0, out1, out2, out3, rows_ref
-):
-    part, width = out0.shape
-    for place, piece in enumerate((in0, in1, in2, in3)):
-        rows_ref[place * part : (place + 1) * part, :] = piece[start : start + part, :]
-    hidden = lax.dot_general(
-        rows_ref[...], win_ref[stream], (((1,), (1,)), ((), ())), preferred_element_type=F32
-    )
-    hidden = jax.nn.gelu(hidden, approximate=True).astype(BF16)
-    for columns in (slice(0, 1280), slice(1280, width)):
-        result = jnp.dot(hidden, wout_ref[stream, :, columns], preferred_element_type=F32)
-        for place, out in enumerate((out0, out1, out2, out3)):
-            out[:, columns] = result[place * part : (place + 1) * part].astype(BF16)
-
-
-def both_final_kernel(
-    img_ref, txt_ref, in0, in1, in2, in3, img_mod_ref, txt_mod_ref, slot_ref, out_ref, placed_ref
-):
+def feed_kernel(in0, in1, in2, in3, win_ref, wout_ref, out0, out1, out2, out3, rows_ref):
+    pieces, outs = (in0, in1, in2, in3), (out0, out1, out2, out3)
+    width = out0.shape[1]
+    for stream, (start, part) in enumerate(((0, 128), (128, SIDE * POOL))):
+        for place, piece in enumerate(pieces):
+            rows_ref[place * part : (place + 1) * part, :] = piece[start : start + part, :]
+        hidden = lax.dot_general(
+            rows_ref[0 : SIDE * part, :],
+            win_ref[stream],
+            (((1,), (1,)), ((), ())),
+            preferred_element_type=F32,
+        )
+        hidden = jax.nn.gelu(hidden, approximate=True).astype(BF16)
+        for columns in (slice(0, 1280), slice(1280, width)):
+            result = jnp.dot(hidden, wout_ref[stream, :, columns], preferred_element_type=F32)
+            for place, out in enumerate(outs):
+                out[start : start + part, columns] = result[
+                    place * part : (place + 1) * part
+                ].astype(BF16)
+
+
+def img_final_kernel(mixed_ref, in0, in1, in2, in3, mod_ref, out_ref):
     total = total_of((in0, in1, in2, in3))
-    out_ref[...] = (img_ref[...].astype(F32) + img_mod_ref[5:6, :] * total[0:32]).astype(BF16)
-    rows = txt_ref[...].astype(F32) + txt_mod_ref[5] * total[32:]
+    out_ref[...] = (mixed_ref[...].astype(F32) + mod_ref[5:6, :] * total).astype(BF16)
+
+
+def txt_final_kernel(mixed_ref, in0, in1, in2, in3, mod_ref, slot_ref, placed_ref):
+    total = total_of((in0, in1, in2, in3))
+    rows = mixed_ref[...].astype(F32) + mod_ref[5] * total
     hot = one_hot(slot_ref[:, 0:POOL], 32).astype(BF16)
     placed_ref[...] = jnp.dot(hot, rows.astype(BF16), preferred_element_type=F32).astype(BF16)
 
@@ -471,16 +492,15 @@
     )
 
 
-def feed(parts, start, rows, weight_in, weight_out, stream, after=()):
-    width = parts[0].shape[1]
+def feed(parts, weight_in, weight_out):
+    rows, width = parts[0].shape
     return run(
-        functools.partial(feed_kernel, start, stream),
+        feed_kernel,
         [like((rows, width))] * SIDE,
         (*parts, weight_in, weight_out),
-        scratch=[pltpu.VMEM((rows * SIDE, width), BF16)],
+        scratch=[pltpu.VMEM((SIDE * 128, width), BF16)],
         flops=rows * SIDE * width * weight_in.shape[1] * 4,
         limit=14,
-        after=after,
     )
 
 
@@ -651,17 +671,22 @@
     )
     rows = spread(join(both_join_kernel, spread(norm_rows, 0)), 1)
     weight_in = feed_in_weight.transpose(0, 2, 1)
-    img_terms = feed(rows, 0, 128, weight_in, feed_out_weight, 0)
-    txt_terms = feed(
-        rows, 128, SIDE * POOL, weight_in, feed_out_weight, 1, (img_terms[0],)
-    )
-    sums = exchange(both_middle(exchange(img_terms, 1), exchange(txt_terms, 1)), 0)
-    image_out, placed = run(
-        both_final_kernel,
-        [like((32, width))] * 2,
-        (mixed_img, mixed_txt, *sums, own_mod, row_mod, slots_own),
-    )
-
+    pieces = exchange(feed(rows, weight_in, feed_out_weight), 1)
+    parts = run(
+        part_middle_kernel,
+        [like((POOL, width))] * SIDE + [like((32, width))] * SIDE,
+        pieces,
+        scratch=[pltpu.VMEM((SIDE * POOL, width), F32)],
+    )
+
+    placed = run(
+        txt_final_kernel,
+        like((32, width)),
+        (mixed_txt, *exchange(parts[:SIDE], 0), row_mod, slots_own),
+    )
+    image_out = run(
+        img_final_kernel, like((32, width)), (mixed_img, *exchange(parts[SIDE:], 0), own_mod)
+    )
     placed = lax.all_to_all(placed.reshape(8, 4, width), "grp", 0, 0, tiled=True)
     prompt_out = placed.reshape(32, width)
 

time: 265 us -> 259 us (0.977)
  blocking collectives: 30.9 us -> 9.37 us
  starting transfers between devices: 60.6 us -> 74.5 us
    all_to_all x1 -> x0, blocking collectives: 21.4 us -> none  [shards(): lax.all_to_all(placed.reshape(8, 4, width), 'grp', 0, 0, tiled=True)]
    all_to_all x0 -> x1, starting transfers between devices: none -> 14.5 us  [shards(): lax.all_to_all(placed.reshape(8, 4, width), 'grp', 0, 0, tiled=True)]
    all_to_all x0 -> x1, waiting for transfers between devices: none -> 4.72 us  [shards(): lax.all_to_all(placed.reshape(8, 4, width), 'grp', 0, 0, tiled=True)]
    unnamed x54 -> x48, local copies, waits for them, and re-layouts: 15.3 us -> 13.5 us
  transfers between devices with their start and end apart: 41 -> 42, of which waited for: 25 -> 25; matrix products, arithmetic and copies ran while one was open for 0% -> 0% of each run, Pallas kernels for 7% -> 7%
where the time goes in v4:
time: 259 us; the launch traced here: 258 us
  waiting for transfers between devices  124 us (48%)
  starting transfers between devices  74.5 us (29%)
  Pallas kernels  34.4 us (13%)
  local copies, waits for them, and re-layouts  14.9 us (6%)
  blocking collectives  9.37 us (4%)
    ppermute x36, waiting for transfers between devices, torus_shift(): return lax.ppermute(values, ('grp', 'tp'), pairs)  114 us
    ppermute x36, starting transfers between devices, torus_shift(): return lax.ppermute(values, ('grp', 'tp'), pairs)  37.6 us
    pallas_call x22, Pallas kernels, run(): pl.pallas_call(body, out_shape=shapes, in_specs=specs, out_specs=[pl.Bloc...  34.4 us
    all_to_all x1, starting transfers between devices, shards(): lax.all_to_all(placed.reshape(8, 4, width), 'grp', 0, 0, tiled=True)  14.5 us
    unnamed x48, local copies, waits for them, and re-layouts  13.5 us
    all_to_all x1, starting transfers between devices, shards(): lax.all_to_all(slot_parts.reshape(8, 64, 512), 'grp', 0, 0, tiled=True)  9.81 us
    all_to_all x1, blocking collectives, shards(): lax.all_to_all(att_parts, 'grp', 0, 0, tiled=True).reshape(512, 128)  9.37 us
    all_to_all x1, starting transfers between devices, shards(): arrived = lax.all_to_all(outgoing, 'tp', 0, 0, tiled=True)  7.85 us
  transfers between devices with their start and end apart: 42, of which 25 were waited for; matrix products, arithmetic and copies ran while one was open for 0% of the time, Pallas kernels for 7%

profile of v4, /device:TPU:1, one launch (start us, length us, event | category | flops | bytes accessed | tf_op | source)
XLA Modules:
  0.0 258.4 jit_solution(30037343225403880)
XLA Ops:
  0.6 0.9 copy-done.3
  1.6 1.5 collective-permute-start
  3.1 0.9 copy-done.13
  4.7 0.9 shard_map.158
  5.6 7.9 %all-to-all-start = ((bf16[16,32,256]{2,1,0:T(8,128)(2,1)}), bf16[16,32,256]{2,1,0:T(8,128)(2,1)S(1)}, u32[]{:S(2)}, u32[]{:S(2)}) async-start(bf16[16,32,256]{2,1,0:T(8,128)(2,1)} %get-tuple-element.49.refs_6_), calls=%async_computation | async-start | bytes 524288 | tf_op jit(solution)/shard_map/all_to_all | solution.py:546
  13.6 1.3 collective-permute-start.7
  14.9 7.8 %shard_map.159 = (f32[512,384]{1,0:T(8,128)}, bf16[16,32,192]{2,1,0:T(8,128)(2,1)}, bf16[32,2432]{1,0:T(8,128)(2,1)}, f32[6,2432]{1,0:T(8,128)}) custom-call(s32[2]{0:T(128)} %refs_0_.5, s32[1]{0:T(128)} %bitcast.refs_1_, bf16[512,2432]{1,0:T(8,128)(2,1)} %refs_2_.3, f32[2,6,2,2432]{3,2,1,0:T(2,128)} %bitcast.29, bf16[3,2432,128]{2,1,0:T(8,128)(2,1)} %bitcast.35, ...), custom_call_target="tpu_custom_call" | custom-call | flops 1434451968 | bytes 7656460 | tf_op jit(solution)/shard_map/pallas_call | solution.py:80
  22.8 0.9 copy-done.12
  23.7 2.5 shard_map.162
  26.2 2.5 collective-permute-start.1
  29.9 1.9 collective-permute-start.8
  31.8 7.8 %collective-permute-done.1.refs_1_ = bf16[80,2944]{1,0:T(8,128)(2,1)} collective-permute-done((bf16[80,2944]{1,0:T(8,128)(2,1)}, bf16[80,2944]{1,0:T(8,128)(2,1)}, u32[]{:S(2)}, u32[]{:S(2)}) %collective-permute-start.1) | collective-permute-done | bytes 471072 | tf_op jit(solution)/shard_map/ppermute | solution.py:32
  39.6 3.7 %collective-permute-done.3.refs_3_ = bf16[80,2944]{1,0:T(8,128)(2,1)} collective-permute-done((bf16[80,2944]{1,0:T(8,128)(2,1)}, bf16[80,2944]{1,0:T(8,128)(2,1)}, u32[]{:S(2)}, u32[]{:S(2)}) %collective-permute-start.3) | collective-permute-done | bytes 471072 | tf_op jit(solution)/shard_map/ppermute | solution.py:32
  43.3 1.8 shard_map.163
  45.1 2.4 collective-permute-start.4
  48.6 1.0 shard_map.165.refs_4_.refs_7_.refs_5_
  49.7 1.3 collective-permute-done.4.refs_1_
  51.0 2.0 collective-permute-done.5.refs_2_
  53.0 1.7 collective-permute-done.6.refs_3_
  55.6 1.5 collective-permute-start.10
  57.1 1.2 collective-permute-start.9
  58.3 4.0 %collective-permute-done.11.refs_3_ = bf16[20,2944]{1,0:T(8,128)(2,1)S(1)} collective-permute-done((bf16[20,2944]{1,0:T(8,128)(2,1)S(1)}, bf16[20,2944]{1,0:T(8,128)(2,1)S(1)}, u32[]{:S(2)}, u32[]{:S(2)}) %collective-permute-start.11) | collective-permute-done | bytes 117792 | tf_op jit(solution)/shard_map/ppermute | solution.py:32
  63.1 1.9 collective-permute-start.13
  65.0 1.0 collective-permute-start.12
  66.1 11.0 %collective-permute-done.14.refs_4_ = bf16[80,2944]{1,0:T(8,128)(2,1)S(1)} collective-permute-done((bf16[80,2944]{1,0:T(8,128)(2,1)S(1)}, bf16[80,2944]{1,0:T(8,128)(2,1)S(1)}, u32[]{:S(2)}, u32[]{:S(2)}) %collective-permute-start.14) | collective-permute-done | bytes 471072 | tf_op jit(solution)/shard_map/ppermute | solution.py:32
  77.7 2.2 shard_map.168
  81.6 9.8 %all-to-all-start.1 = ((bf16[8,64,512]{2,1,0:T(8,128)(2,1)}), bf16[8,64,512]{2,1,0:T(8,128)(2,1)S(1)}, u32[]{:S(2)}, u32[]{:S(2)}) async-start(bf16[8,64,512]{2,1,0:T(8,128)(2,1)} %bitcast.32), calls=%async_computation.1 | async-start | bytes 1048576 | tf_op jit(solution)/shard_map/all_to_all | solution.py:639
  91.4 1.1 copy-done.4
  92.5 1.0 copy-done.8
  93.6 1.5 shard_map.169.refs_1_
  95.9 5.0 %all-to-all-done.1.refs_2_ = bf16[8,64,512]{2,1,0:T(8,128)(2,1)S(1)} async-done(((bf16[8,64,512]{2,1,0:T(8,128)(2,1)}), bf16[8,64,512]{2,1,0:T(8,128)(2,1)S(1)}, u32[]{:S(2)}, u32[]{:S(2)}) %all-to-all-start.1) | async-done | bytes 524320 | tf_op jit(solution)/shard_map/all_to_all | solution.py:639
  100.9 1.0 copy-done.10
  101.9 1.1 copy-done.22
  103.0 2.5 shard_map.170
  105.5 2.4 collective-permute-start.15
  108.5 1.1 shard_map.171
  109.7 9.4 %all_to_all.20 = bf16[8,64,128]{2,1,0:T(8,128)(2,1)S(1)} all-to-all(bf16[8,64,128]{2,1,0:T(8,128)(2,1)S(1)} %shard_map.171), channel_id=1, replica_groups=mesh['grp'=8,'tp'=16] {'grp'}, dimensions={0} | all-to-all | bytes 262144 | tf_op jit(solution)/shard_map/all_to_all | solution.py:656
  119.0 2.7 %collective-permute-done.15.refs_3_.refs_1_ = bf16[128,2432]{1,0:T(8,128)(2,1)S(1)} collective-permute-done((bf16[128,2432]{1,0:T(8,128)(2,1)S(1)}, bf16[128,2432]{1,0:T(8,128)(2,1)S(1)}, u32[]{:S(2)}, u32[]{:S(2)}) %collective-permute-start.15) | collective-permute-done | bytes 622624 | tf_op jit(solution)/shard_map/ppermute | solution.py:32
  121.7 0.9 shard_map.172
  122.6 3.5 %collective-permute-start.18 = (bf16[80,2432]{1,0:T(8,128)(2,1)S(1)}, bf16[80,2432]{1,0:T(8,128)(2,1)S(1)}, u32[]{:S(2)}, u32[]{:S(2)}) collective-permute-start(bf16[80,2432]{1,0:T(8,128)(2,1)S(1)} %get-tuple-element.72), channel_id=1, source_target_pairs={{0,12},{1,13},{2,14},{3,15},{4,0},{5,1},{6,2},{7,3},{8,4},{9,5},{1... | collective-permute-start | bytes 1167368 | tf_op jit(solution)/shard_map/ppermute | solution.py:32
  126.8 8.2 %collective-permute-done.18.refs_5_ = bf16[80,2432]{1,0:T(8,128)(2,1)S(1)} collective-permute-done((bf16[80,2432]{1,0:T(8,128)(2,1)S(1)}, bf16[80,2432]{1,0:T(8,128)(2,1)S(1)}, u32[]{:S(2)}, u32[]{:S(2)}) %collective-permute-start.18) | collective-permute-done | bytes 389152 | tf_op jit(solution)/shard_map/ppermute | solution.py:32
  135.0 3.4 %collective-permute-done.20.refs_7_ = bf16[80,2432]{1,0:T(8,128)(2,1)S(1)} collective-permute-done((bf16[80,2432]{1,0:T(8,128)(2,1)S(1)}, bf16[80,2432]{1,0:T(8,128)(2,1)S(1)}, u32[]{:S(2)}, u32[]{:S(2)}) %collective-permute-start.20) | collective-permute-done | bytes 389152 | tf_op jit(solution)/shard_map/ppermute | solution.py:32
  138.4 0.9 shard_map.173
  139.2 2.2 collective-permute-start.21
  142.2 5.7 %collective-permute-done.21.refs_3_ = bf16[52,2432]{1,0:T(8,128)(2,1)S(1)} collective-permute-done((bf16[52,2432]{1,0:T(8,128)(2,1)S(1)}, bf16[52,2432]{1,0:T(8,128)(2,1)S(1)}, u32[]{:S(2)}, u32[]{:S(2)}) %collective-permute-start.21) | collective-permute-done | bytes 252960 | tf_op jit(solution)/shard_map/ppermute | solution.py:32
  148.4 2.8 %collective-permute-done.23.refs_5_ = bf16[52,2432]{1,0:T(8,128)(2,1)S(1)} collective-permute-done((bf16[52,2432]{1,0:T(8,128)(2,1)S(1)}, bf16[52,2432]{1,0:T(8,128)(2,1)S(1)}, u32[]{:S(2)}, u32[]{:S(2)}) %collective-permute-start.23) | collective-permute-done | bytes 252960 | tf_op jit(solution)/shard_map/ppermute | solution.py:32
  151.9 1.8 collective-permute-start.25
  153.7 0.9 collective-permute-start.24
  154.5 7.1 %collective-permute-done.26.refs_3_ = bf16[52,2432]{1,0:T(8,128)(2,1)S(1)} collective-permute-done((bf16[52,2432]{1,0:T(8,128)(2,1)S(1)}, bf16[52,2432]{1,0:T(8,128)(2,1)S(1)}, u32[]{:S(2)}, u32[]{:S(2)}) %collective-permute-start.26) | collective-permute-done | bytes 252960 | tf_op jit(solution)/shard_map/ppermute | solution.py:32
  162.5 1.6 collective-permute-start.28
  164.1 1.0 collective-permute-start.27
  165.1 22.9 %collective-permute-done.29.refs_3_ = bf16[208,2432]{1,0:T(8,128)(2,1)S(1)} collective-permute-done((bf16[208,2432]{1,0:T(8,128)(2,1)S(1)}, bf16[208,2432]{1,0:T(8,128)(2,1)S(1)}, u32[]{:S(2)}, u32[]{:S(2)}) %collective-permute-start.29) | collective-permute-done | bytes 1011744 | tf_op jit(solution)/shard_map/ppermute | solution.py:32
  188.8 2.7 %copy-done.21 = bf16[2,608,2432]{2,1,0:T(8,128)(2,1)S(1)} copy-done((bf16[2,608,2432]{2,1,0:T(8,128)(2,1)S(1)}, bf16[2,608,2432]{2,1,0:T(8,128)(2,1)}, u32[]{:S(2)}) %copy-start.21) | copy-done | bytes 5914648
  191.5 8.3 %shard_map.176 = (bf16[208,2432]{1,0:T(8,128)(2,1)S(1)}, bf16[208,2432]{1,0:T(8,128)(2,1)S(1)}, bf16[208,2432]{1,0:T(8,128)(2,1)S(1)}, bf16[208,2432]{1,0:T(8,128)(2,1)S(1)}) custom-call(bf16[208,2432]{1,0:T(8,128)(2,1)S(1)} %shard_map.175.refs_0_, bf16[208,2432]{1,0:T(8,128)(2,1)S(1)} %collective-permute-done.27.refs_1_, ...), custom_call_target="tpu_custom_call" | custom-call | flops 4920967168 | bytes 19922944 | tf_op jit(solution)/shard_map/pallas_call | solution.py:80
  199.8 2.1 collective-permute-start.30
  202.5 21.5 %collective-permute-done.30.refs_1_ = bf16[208,2432]{1,0:T(8,128)(2,1)S(1)} collective-permute-done((bf16[208,2432]{1,0:T(8,128)(2,1)S(1)}, bf16[208,2432]{1,0:T(8,128)(2,1)S(1)}, u32[]{:S(2)}, u32[]{:S(2)}) %collective-permute-start.30) | collective-permute-done | bytes 1011744 | tf_op jit(solution)/shard_map/ppermute | solution.py:32
  224.1 3.4 %collective-permute-done.32.refs_3_ = bf16[208,2432]{1,0:T(8,128)(2,1)S(1)} collective-permute-done((bf16[208,2432]{1,0:T(8,128)(2,1)S(1)}, bf16[208,2432]{1,0:T(8,128)(2,1)S(1)}, u32[]{:S(2)}, u32[]{:S(2)}) %collective-permute-start.32) | collective-permute-done | bytes 1011744 | tf_op jit(solution)/shard_map/ppermute | solution.py:32
  227.5 0.9 shard_map.177
  228.3 2.0 collective-permute-start.36
  231.0 2.0 collective-permute-start.33
  233.0 1.8 collective-permute-start.34
  234.8 1.2 collective-permute-done.37.refs_3_
  237.7 14.5 %all-to-all-start.3 = ((bf16[8,4,2432]{2,1,0:T(4,128)(2,1)}), bf16[8,4,2432]{2,1,0:T(4,128)(2,1)S(1)}, u32[]{:S(2)}, u32[]{:S(2)}) async-start(bf16[8,4,2432]{2,1,0:T(4,128)(2,1)} %reshape.26), calls=%async_computation.3 | async-start | bytes 311296 | tf_op jit(solution)/shard_map/all_to_all | solution.py:690
  253.0 4.7 %all-to-all-done.3 = bf16[8,4,2432]{2,1,0:T(4,128)(2,1)S(1)} async-done(((bf16[8,4,2432]{2,1,0:T(4,128)(2,1)}), bf16[8,4,2432]{2,1,0:T(4,128)(2,1)S(1)}, u32[]{:S(2)}, u32[]{:S(2)}) %all-to-all-start.3) | async-done | bytes 155680 | tf_op jit(solution)/shard_map/all_to_all | solution.py:690
  (96 shorter events, 17.4 us)
Async XLA Ops:
  0.6 0.9 copy-start.3
  1.6 11.9 %collective-permute-start = (f32[2,8,2432]{2,1,0:T(8,128)S(1)}, f32[2,8,2432]{2,1,0:T(8,128)S(1)}, u32[]{:S(2)}, u32[]{:S(2)}) collective-permute-start(f32[2,8,2432]{2,1,0:T(8,128)S(1)} %shard_map.160.refs_0_), channel_id=1, source_target_pairs={{0,16},{16,0},{32,48},{48,32},{64,80},{80,64},{96,112},{112,96},{1... | collective-permute-start | bytes 466952 | tf_op jit(solution)/shard_map/ppermute | solution.py:36
  3.1 0.9 copy-start.13
  5.6 17.1 %all-to-all-start = ((bf16[16,32,256]{2,1,0:T(8,128)(2,1)}), bf16[16,32,256]{2,1,0:T(8,128)(2,1)S(1)}, u32[]{:S(2)}, u32[]{:S(2)}) async-start(bf16[16,32,256]{2,1,0:T(8,128)(2,1)} %get-tuple-element.49.refs_6_), calls=%async_computation | async-start | bytes 524288 | tf_op jit(solution)/shard_map/all_to_all | solution.py:546
  13.6 16.3 %collective-permute-start.7 = (f32[4,8,2432]{2,1,0:T(8,128)S(1)}, f32[4,8,2432]{2,1,0:T(8,128)S(1)}, u32[]{:S(2)}, u32[]{:S(2)}) collective-permute-start(f32[4,8,2432]{2,1,0:T(8,128)S(1)} %shard_map.161.refs_4_.refs_0_), channel_id=1, source_target_pairs={{0,32},{16,48},{32,0},{48,16},{64,96},{80,112},{96,64},{112,80},{1... | collective-permute-start | bytes 933896 | tf_op jit(solution)/shard_map/ppermute | solution.py:44
  14.9 7.9 %copy-start.2 = (bf16[256,2432]{1,0:T(8,128)(2,1)S(1)}, bf16[256,2432]{1,0:T(8,128)(2,1)}, u32[]{:S(2)}) copy-start(bf16[256,2432]{1,0:T(8,128)(2,1)} %refs_2_.4) | copy-start | bytes 3735556
  22.7 1.0 copy-start.12
  26.2 22.4 %copy-start.18 = (s32[20,1]{0,1:T(1,128)S(1)}, s32[20,1]{0,1:T(1,128)}, u32[]{:S(2)}) copy-start(s32[20,1]{0,1:T(1,128)} %param.17) | copy-start | bytes 244
  26.2 13.5 %collective-permute-start.1 = (bf16[80,2944]{1,0:T(8,128)(2,1)}, bf16[80,2944]{1,0:T(8,128)(2,1)}, u32[]{:S(2)}, u32[]{:S(2)}) collective-permute-start(bf16[80,2944]{1,0:T(8,128)(2,1)} %get-tuple-element.53), channel_id=1, source_target_pairs={{0,12},{1,13},{2,14},{3,15},{4,0},{5,1},{6,2},{7,3},{8,4},{9,5},{1... | collective-permute-start | bytes 1413128 | tf_op jit(solution)/shard_map/ppermute | solution.py:32
  28.7 10.9 %collective-permute-start.2 = (bf16[80,2944]{1,0:T(8,128)(2,1)}, bf16[80,2944]{1,0:T(8,128)(2,1)}, u32[]{:S(2)}, u32[]{:S(2)}) collective-permute-start(bf16[80,2944]{1,0:T(8,128)(2,1)} %get-tuple-element.54), channel_id=1, source_target_pairs={{0,8},{1,9},{2,10},{3,11},{4,12},{5,13},{6,14},{7,15},{8,0},{9,1},... | collective-permute-start | bytes 1413128 | tf_op jit(solution)/shard_map/ppermute | solution.py:32
  29.3 14.0 %collective-permute-start.3 = (bf16[80,2944]{1,0:T(8,128)(2,1)}, bf16[80,2944]{1,0:T(8,128)(2,1)}, u32[]{:S(2)}, u32[]{:S(2)}) collective-permute-start(bf16[80,2944]{1,0:T(8,128)(2,1)} %get-tuple-element.55), channel_id=1, source_target_pairs={{0,4},{1,5},{2,6},{3,7},{4,8},{5,9},{6,10},{7,11},{8,12},{9,13},{1... | collective-permute-start | bytes 1413128 | tf_op jit(solution)/shard_map/ppermute | solution.py:32
  29.9 18.7 %collective-permute-start.8 = (f32[8,8,2432]{2,1,0:T(8,128)S(1)}, f32[8,8,2432]{2,1,0:T(8,128)S(1)}, u32[]{:S(2)}, u32[]{:S(2)}) collective-permute-start(f32[8,8,2432]{2,1,0:T(8,128)S(1)} %shard_map.164.refs_1_), channel_id=1, source_target_pairs={{0,96},{16,112},{32,64},{48,80},{64,32},{80,48},{96,0},{112,16},{1... | collective-permute-start | bytes 1867784 | tf_op jit(solution)/shard_map/ppermute | solution.py:44
  45.1 5.9 %collective-permute-start.4 = (bf16[20,2944]{1,0:T(8,128)(2,1)S(1)}, bf16[20,2944]{1,0:T(8,128)(2,1)S(1)}, u32[]{:S(2)}, u32[]{:S(2)}) collective-permute-start(bf16[20,2944]{1,0:T(8,128)(2,1)S(1)} %get-tuple-element.57), channel_id=1, source_target_pairs={{0,3},{1,0},{2,1},{3,2},{4,7},{5,4},{6,5},{7,6},{8,11},{9,8},{10,9... | collective-permute-start | bytes 353288 | tf_op jit(solution)/shard_map/ppermute | solution.py:32
  47.4 5.5 %collective-permute-start.5 = (bf16[20,2944]{1,0:T(8,128)(2,1)S(1)}, bf16[20,2944]{1,0:T(8,128)(2,1)S(1)}, u32[]{:S(2)}, u32[]{:S(2)}) collective-permute-start(bf16[20,2944]{1,0:T(8,128)(2,1)S(1)} %get-tuple-element.58), channel_id=1, source_target_pairs={{0,2},{1,3},{2,0},{3,1},{4,6},{5,7},{6,4},{7,5},{8,10},{9,11},{10,... | collective-permute-start | bytes 353288 | tf_op jit(solution)/shard_map/ppermute | solution.py:32
  48.0 6.7 %collective-permute-start.6 = (bf16[20,2944]{1,0:T(8,128)(2,1)S(1)}, bf16[20,2944]{1,0:T(8,128)(2,1)S(1)}, u32[]{:S(2)}, u32[]{:S(2)}) collective-permute-start(bf16[20,2944]{1,0:T(8,128)(2,1)S(1)} %get-tuple-element.59), channel_id=1, source_target_pairs={{0,1},{1,2},{2,3},{3,0},{4,5},{5,6},{6,7},{7,4},{8,9},{9,10},{10,1... | collective-permute-start | bytes 353288 | tf_op jit(solution)/shard_map/ppermute | solution.py:32
  49.6 16.4 %copy-start.23 = (f32[2,2,64]{2,1,0:T(2,128)S(1)}, f32[2,2,64]{2,1,0:T(2,128)}, u32[]{:S(2)}) copy-start(f32[2,2,64]{2,1,0:T(2,128)} %param.20) | copy-start | bytes 3076
  49.6 28.1 %copy-start = (bf16[2432,3,128]{2,0,1:T(8,128)(2,1)S(1)}, bf16[2432,3,128]{2,0,1:T(8,128)(2,1)}, u32[]{:S(2)}) copy-start(bf16[2432,3,128]{2,0,1:T(8,128)(2,1)} %param.23) | copy-start | bytes 5603332
  55.6 6.7 %collective-permute-start.11 = (bf16[20,2944]{1,0:T(8,128)(2,1)S(1)}, bf16[20,2944]{1,0:T(8,128)(2,1)S(1)}, u32[]{:S(2)}, u32[]{:S(2)}) collective-permute-start(bf16[20,2944]{1,0:T(8,128)(2,1)S(1)} %get-tuple-element.61.refs_0_), channel_id=1, source_target_pairs={{0,1},{1,2},{2,3},{3,0},{4,5},{5,6},{6,7},{7,4},{8,9},{9,10},{10,1... | collective-permute-start | bytes 353288 | tf_op jit(solution)/shard_map/ppermute | solution.py:32
  55.6 6.7 %collective-permute-start.10 = (bf16[20,2944]{1,0:T(8,128)(2,1)S(1)}, bf16[20,2944]{1,0:T(8,128)(2,1)S(1)}, u32[]{:S(2)}, u32[]{:S(2)}) collective-permute-start(bf16[20,2944]{1,0:T(8,128)(2,1)S(1)} %get-tuple-element.61.refs_0_), channel_id=1, source_target_pairs={{0,2},{1,3},{2,0},{3,1},{4,6},{5,7},{6,4},{7,5},{8,10},{9,11},{10,... | collective-permute-start | bytes 353288 | tf_op jit(solution)/shard_map/ppermute | solution.py:32
  57.1 5.8 %collective-permute-start.9 = (bf16[20,2944]{1,0:T(8,128)(2,1)S(1)}, bf16[20,2944]{1,0:T(8,128)(2,1)S(1)}, u32[]{:S(2)}, u32[]{:S(2)}) collective-permute-start(bf16[20,2944]{1,0:T(8,128)(2,1)S(1)} %get-tuple-element.61.refs_0_), channel_id=1, source_target_pairs={{0,3},{1,0},{2,1},{3,2},{4,7},{5,4},{6,5},{7,6},{8,11},{9,8},{10,9... | collective-permute-start | bytes 353288 | tf_op jit(solution)/shard_map/ppermute | solution.py:32
  63.0 14.1 %collective-permute-start.14 = (bf16[80,2944]{1,0:T(8,128)(2,1)S(1)}, bf16[80,2944]{1,0:T(8,128)(2,1)S(1)}, u32[]{:S(2)}, u32[]{:S(2)}) collective-permute-start(bf16[80,2944]{1,0:T(8,128)(2,1)S(1)} %shard_map.167.refs_1_), channel_id=1, source_target_pairs={{0,4},{1,5},{2,6},{3,7},{4,8},{5,9},{6,10},{7,11},{8,12},{9,13},{1... | collective-permute-start | bytes 1413128 | tf_op jit(solution)/shard_map/ppermute | solution.py:32
  63.1 14.0 %collective-permute-start.13 = (bf16[80,2944]{1,0:T(8,128)(2,1)S(1)}, bf16[80,2944]{1,0:T(8,128)(2,1)S(1)}, u32[]{:S(2)}, u32[]{:S(2)}) collective-permute-start(bf16[80,2944]{1,0:T(8,128)(2,1)S(1)} %shard_map.167.refs_1_), channel_id=1, source_target_pairs={{0,8},{1,9},{2,10},{3,11},{4,12},{5,13},{6,14},{7,15},{8,0},{9,1},... | collective-permute-start | bytes 1413128 | tf_op jit(solution)/shard_map/ppermute | solution.py:32
  65.0 12.7 %collective-permute-start.12 = (bf16[80,2944]{1,0:T(8,128)(2,1)S(1)}, bf16[80,2944]{1,0:T(8,128)(2,1)S(1)}, u32[]{:S(2)}, u32[]{:S(2)}) collective-permute-start(bf16[80,2944]{1,0:T(8,128)(2,1)S(1)} %shard_map.167.refs_1_), channel_id=1, source_target_pairs={{0,12},{1,13},{2,14},{3,15},{4,0},{5,1},{6,2},{7,3},{8,4},{9,5},{1... | collective-permute-start | bytes 1413128 | tf_op jit(solution)/shard_map/ppermute | solution.py:32
  77.7 13.6 %copy-start.1 = (bf16[32,3,64,128]{3,2,1,0:T(8,128)(2,1)S(1)}, bf16[32,3,64,128]{3,2,1,0:T(8,128)(2,1)}, u32[]{:S(2)}) copy-start(bf16[32,3,64,128]{3,2,1,0:T(8,128)(2,1)} %refs_3_.2) | copy-start | bytes 4718596
  77.7 13.6 %copy-start.19 = (s32[2]{0:T(128)S(1)}, s32[2]{0:T(128)}, u32[]{:S(2)}) copy-start(s32[2]{0:T(128)} %refs_0_.5) | copy-start | bytes 28
  80.0 0.8 copy-start.6
  80.8 0.8 copy-start.7
  81.6 19.3 %all-to-all-start.1 = ((bf16[8,64,512]{2,1,0:T(8,128)(2,1)}), bf16[8,64,512]{2,1,0:T(8,128)(2,1)S(1)}, u32[]{:S(2)}, u32[]{:S(2)}) async-start(bf16[8,64,512]{2,1,0:T(8,128)(2,1)} %bitcast.32), calls=%async_computation.1 | async-start | bytes 1048576 | tf_op jit(solution)/shard_map/all_to_all | solution.py:639
  91.4 1.1 copy-start.4
  92.5 1.0 copy-start.8
  95.1 0.8 copy-start.9
  100.9 1.0 copy-start.10
  101.9 1.1 copy-start.22
  105.5 16.2 %copy-start.5 = (bf16[128,2432]{1,0:T(8,128)(2,1)S(1)}, bf16[128,2432]{1,0:T(8,128)(2,1)}, u32[]{:S(2)}) copy-start(bf16[128,2432]{1,0:T(8,128)(2,1)} %refs_2_.5) | copy-start | bytes 1867780
  105.5 16.2 %collective-permute-start.15 = (bf16[128,2432]{1,0:T(8,128)(2,1)S(1)}, bf16[128,2432]{1,0:T(8,128)(2,1)S(1)}, u32[]{:S(2)}, u32[]{:S(2)}) collective-permute-start(bf16[128,2432]{1,0:T(8,128)(2,1)S(1)} %get-tuple-element.67), channel_id=1, source_target_pairs={{0,12},{1,13},{2,14},{3,15},{4,0},{5,1},{6,2},{7,3},{8,4},{9,5},{1... | collective-permute-start | bytes 1867784 | tf_op jit(solution)/shard_map/ppermute | solution.py:32
  107.9 18.9 %collective-permute-start.16 = (bf16[128,2432]{1,0:T(8,128)(2,1)S(1)}, bf16[128,2432]{1,0:T(8,128)(2,1)S(1)}, u32[]{:S(2)}, u32[]{:S(2)}) collective-permute-start(bf16[128,2432]{1,0:T(8,128)(2,1)S(1)} %get-tuple-element.68), channel_id=1, source_target_pairs={{0,8},{1,9},{2,10},{3,11},{4,12},{5,13},{6,14},{7,15},{8,0},{9,1},... | collective-permute-start | bytes 1867784 | tf_op jit(solution)/shard_map/ppermute | solution.py:32
  107.9 18.9 %collective-permute-start.17 = (bf16[128,2432]{1,0:T(8,128)(2,1)S(1)}, bf16[128,2432]{1,0:T(8,128)(2,1)S(1)}, u32[]{:S(2)}, u32[]{:S(2)}) collective-permute-start(bf16[128,2432]{1,0:T(8,128)(2,1)S(1)} %get-tuple-element.69), channel_id=1, source_target_pairs={{0,4},{1,5},{2,6},{3,7},{4,8},{5,9},{6,10},{7,11},{8,12},{9,13},{1... | collective-permute-start | bytes 1867784 | tf_op jit(solution)/shard_map/ppermute | solution.py:32
  122.6 12.3 %collective-permute-start.18 = (bf16[80,2432]{1,0:T(8,128)(2,1)S(1)}, bf16[80,2432]{1,0:T(8,128)(2,1)S(1)}, u32[]{:S(2)}, u32[]{:S(2)}) collective-permute-start(bf16[80,2432]{1,0:T(8,128)(2,1)S(1)} %get-tuple-element.72), channel_id=1, source_target_pairs={{0,12},{1,13},{2,14},{3,15},{4,0},{5,1},{6,2},{7,3},{8,4},{9,5},{1... | collective-permute-start | bytes 1167368 | tf_op jit(solution)/shard_map/ppermute | solution.py:32
  126.1 8.8 %collective-permute-start.19 = (bf16[80,2432]{1,0:T(8,128)(2,1)S(1)}, bf16[80,2432]{1,0:T(8,128)(2,1)S(1)}, u32[]{:S(2)}, u32[]{:S(2)}) collective-permute-start(bf16[80,2432]{1,0:T(8,128)(2,1)S(1)} %get-tuple-element.73), channel_id=1, source_target_pairs={{0,8},{1,9},{2,10},{3,11},{4,12},{5,13},{6,14},{7,15},{8,0},{9,1},... | collective-permute-start | bytes 1167368 | tf_op jit(solution)/shard_map/ppermute | solution.py:32
  126.1 12.3 %collective-permute-start.20 = (bf16[80,2432]{1,0:T(8,128)(2,1)S(1)}, bf16[80,2432]{1,0:T(8,128)(2,1)S(1)}, u32[]{:S(2)}, u32[]{:S(2)}) collective-permute-start(bf16[80,2432]{1,0:T(8,128)(2,1)S(1)} %get-tuple-element.74), channel_id=1, source_target_pairs={{0,4},{1,5},{2,6},{3,7},{4,8},{5,9},{6,10},{7,11},{8,12},{9,13},{1... | collective-permute-start | bytes 1167368 | tf_op jit(solution)/shard_map/ppermute | solution.py:32
  138.4 12.9 %copy-start.11 = (f32[6,2432]{1,0:T(8,128)S(1)}, f32[6,2432]{1,0:T(8,128)}, u32[]{:S(2)}) copy-start(f32[6,2432]{1,0:T(8,128)} %get-tuple-element.79.refs_6_.refs_5_) | copy-start | bytes 175108
  138.4 12.9 %copy-start.14 = (bf16[32,2432]{1,0:T(8,128)(2,1)S(1)}, bf16[32,2432]{1,0:T(8,128)(2,1)}, u32[]{:S(2)}) copy-start(bf16[32,2432]{1,0:T(8,128)(2,1)} %get-tuple-element.50.refs_0_) | copy-start | bytes 466948
  138.4 12.9 %copy-start.16 = (bf16[20,2432]{1,0:T(8,128)(2,1)S(1)}, bf16[20,2432]{1,0:T(8,128)(2,1)}, u32[]{:S(2)}) copy-start(bf16[20,2432]{1,0:T(8,128)(2,1)} %copy-done.15) | copy-start | bytes 291844
  138.4 50.5 %copy-start.20 = (bf16[2,2432,608]{1,2,0:T(8,128)(2,1)S(1)}, bf16[2,2432,608]{1,2,0:T(8,128)(2,1)}, u32[]{:S(2)}) copy-start(bf16[2,2432,608]{1,2,0:T(8,128)(2,1)} %param.26) | copy-start | bytes 17743876
  139.2 8.6 %collective-permute-start.21 = (bf16[52,2432]{1,0:T(8,128)(2,1)S(1)}, bf16[52,2432]{1,0:T(8,128)(2,1)S(1)}, u32[]{:S(2)}, u32[]{:S(2)}) collective-permute-start(bf16[52,2432]{1,0:T(8,128)(2,1)S(1)} %get-tuple-element.76), channel_id=1, source_target_pairs={{0,3},{1,0},{2,1},{3,2},{4,7},{5,4},{6,5},{7,6},{8,11},{9,8},{10,9... | collective-permute-start | bytes 758792 | tf_op jit(solution)/shard_map/ppermute | solution.py:32
  141.5 6.9 %collective-permute-start.22 = (bf16[52,2432]{1,0:T(8,128)(2,1)S(1)}, bf16[52,2432]{1,0:T(8,128)(2,1)S(1)}, u32[]{:S(2)}, u32[]{:S(2)}) collective-permute-start(bf16[52,2432]{1,0:T(8,128)(2,1)S(1)} %get-tuple-element.77), channel_id=1, source_target_pairs={{0,2},{1,3},{2,0},{3,1},{4,6},{5,7},{6,4},{7,5},{8,10},{9,11},{10,... | collective-permute-start | bytes 758792 | tf_op jit(solution)/shard_map/ppermute | solution.py:32
  141.5 9.8 %collective-permute-start.23 = (bf16[52,2432]{1,0:T(8,128)(2,1)S(1)}, bf16[52,2432]{1,0:T(8,128)(2,1)S(1)}, u32[]{:S(2)}, u32[]{:S(2)}) collective-permute-start(bf16[52,2432]{1,0:T(8,128)(2,1)S(1)} %get-tuple-element.78), channel_id=1, source_target_pairs={{0,1},{1,2},{2,3},{3,0},{4,5},{5,6},{6,7},{7,4},{8,9},{9,10},{10,1... | collective-permute-start | bytes 758792 | tf_op jit(solution)/shard_map/ppermute | solution.py:32
  151.8 9.8 %collective-permute-start.26 = (bf16[52,2432]{1,0:T(8,128)(2,1)S(1)}, bf16[52,2432]{1,0:T(8,128)(2,1)S(1)}, u32[]{:S(2)}, u32[]{:S(2)}) collective-permute-start(bf16[52,2432]{1,0:T(8,128)(2,1)S(1)} %get-tuple-element.81.refs_0_), channel_id=1, source_target_pairs={{0,1},{1,2},{2,3},{3,0},{4,5},{5,6},{6,7},{7,4},{8,9},{9,10},{10,1... | collective-permute-start | bytes 758792 | tf_op jit(solution)/shard_map/ppermute | solution.py:32
  151.9 9.7 %collective-permute-start.25 = (bf16[52,2432]{1,0:T(8,128)(2,1)S(1)}, bf16[52,2432]{1,0:T(8,128)(2,1)S(1)}, u32[]{:S(2)}, u32[]{:S(2)}) collective-permute-start(bf16[52,2432]{1,0:T(8,128)(2,1)S(1)} %get-tuple-element.81.refs_0_), channel_id=1, source_target_pairs={{0,2},{1,3},{2,0},{3,1},{4,6},{5,7},{6,4},{7,5},{8,10},{9,11},{10,... | collective-permute-start | bytes 758792 | tf_op jit(solution)/shard_map/ppermute | solution.py:32
  153.7 8.6 %collective-permute-start.24 = (bf16[52,2432]{1,0:T(8,128)(2,1)S(1)}, bf16[52,2432]{1,0:T(8,128)(2,1)S(1)}, u32[]{:S(2)}, u32[]{:S(2)}) collective-permute-start(bf16[52,2432]{1,0:T(8,128)(2,1)S(1)} %get-tuple-element.81.refs_0_), channel_id=1, source_target_pairs={{0,3},{1,0},{2,1},{3,2},{4,7},{5,4},{6,5},{7,6},{8,11},{9,8},{10,9... | collective-permute-start | bytes 758792 | tf_op jit(solution)/shard_map/ppermute | solution.py:32
  162.4 25.7 %collective-permute-start.29 = (bf16[208,2432]{1,0:T(8,128)(2,1)S(1)}, bf16[208,2432]{1,0:T(8,128)(2,1)S(1)}, u32[]{:S(2)}, u32[]{:S(2)}) collective-permute-start(bf16[208,2432]{1,0:T(8,128)(2,1)S(1)} %shard_map.175.refs_0_), channel_id=1, source_target_pairs={{0,4},{1,5},{2,6},{3,7},{4,8},{5,9},{6,10},{7,11},{8,12},{9,13},{1... | collective-permute-start | bytes 3035144 | tf_op jit(solution)/shard_map/ppermute | solution.py:32
  162.5 25.6 %collective-permute-start.28 = (bf16[208,2432]{1,0:T(8,128)(2,1)S(1)}, bf16[208,2432]{1,0:T(8,128)(2,1)S(1)}, u32[]{:S(2)}, u32[]{:S(2)}) collective-permute-start(bf16[208,2432]{1,0:T(8,128)(2,1)S(1)} %shard_map.175.refs_0_), channel_id=1, source_target_pairs={{0,8},{1,9},{2,10},{3,11},{4,12},{5,13},{6,14},{7,15},{8,0},{9,1},... | collective-permute-start | bytes 3035144 | tf_op jit(solution)/shard_map/ppermute | solution.py:32
  164.1 24.7 %collective-permute-start.27 = (bf16[208,2432]{1,0:T(8,128)(2,1)S(1)}, bf16[208,2432]{1,0:T(8,128)(2,1)S(1)}, u32[]{:S(2)}, u32[]{:S(2)}) collective-permute-start(bf16[208,2432]{1,0:T(8,128)(2,1)S(1)} %shard_map.175.refs_0_), channel_id=1, source_target_pairs={{0,12},{1,13},{2,14},{3,15},{4,0},{5,1},{6,2},{7,3},{8,4},{9,5},{1... | collective-permute-start | bytes 3035144 | tf_op jit(solution)/shard_map/ppermute | solution.py:32
  188.8 2.7 %copy-start.21 = (bf16[2,608,2432]{2,1,0:T(8,128)(2,1)S(1)}, bf16[2,608,2432]{2,1,0:T(8,128)(2,1)}, u32[]{:S(2)}) copy-start(bf16[2,608,2432]{2,1,0:T(8,128)(2,1)} %refs_5_.3) | copy-start | bytes 17743876
  199.8 24.3 %collective-permute-start.30 = (bf16[208,2432]{1,0:T(8,128)(2,1)S(1)}, bf16[208,2432]{1,0:T(8,128)(2,1)S(1)}, u32[]{:S(2)}, u32[]{:S(2)}) collective-permute-start(bf16[208,2432]{1,0:T(8,128)(2,1)S(1)} %get-tuple-element.83), channel_id=1, source_target_pairs={{0,12},{1,13},{2,14},{3,15},{4,0},{5,1},{6,2},{7,3},{8,4},{9,5},{1... | collective-permute-start | bytes 3035144 | tf_op jit(solution)/shard_map/ppermute | solution.py:32
  201.9 22.2 %collective-permute-start.31 = (bf16[208,2432]{1,0:T(8,128)(2,1)S(1)}, bf16[208,2432]{1,0:T(8,128)(2,1)S(1)}, u32[]{:S(2)}, u32[]{:S(2)}) collective-permute-start(bf16[208,2432]{1,0:T(8,128)(2,1)S(1)} %get-tuple-element.84), channel_id=1, source_target_pairs={{0,8},{1,9},{2,10},{3,11},{4,12},{5,13},{6,14},{7,15},{8,0},{9,1},... | collective-permute-start | bytes 3035144 | tf_op jit(solution)/shard_map/ppermute | solution.py:32
  201.9 25.6 %collective-permute-start.32 = (bf16[208,2432]{1,0:T(8,128)(2,1)S(1)}, bf16[208,2432]{1,0:T(8,128)(2,1)S(1)}, u32[]{:S(2)}, u32[]{:S(2)}) collective-permute-start(bf16[208,2432]{1,0:T(8,128)(2,1)S(1)} %get-tuple-element.85), channel_id=1, source_target_pairs={{0,4},{1,5},{2,6},{3,7},{4,8},{5,9},{6,10},{7,11},{8,12},{9,13},{1... | collective-permute-start | bytes 3035144 | tf_op jit(solution)/shard_map/ppermute | solution.py:32
  228.3 6.4 %collective-permute-start.36 = (bf16[20,2432]{1,0:T(8,128)(2,1)S(1)}, bf16[20,2432]{1,0:T(8,128)(2,1)S(1)}, u32[]{:S(2)}, u32[]{:S(2)}) collective-permute-start(bf16[20,2432]{1,0:T(8,128)(2,1)S(1)} %get-tuple-element.92), channel_id=1, source_target_pairs={{0,3},{1,0},{2,1},{3,2},{4,7},{5,4},{6,5},{7,6},{8,11},{9,8},{10,9... | collective-permute-start | bytes 291848 | tf_op jit(solution)/shard_map/ppermute | solution.py:32
  230.4 5.6 %collective-permute-start.37 = (bf16[20,2432]{1,0:T(8,128)(2,1)S(1)}, bf16[20,2432]{1,0:T(8,128)(2,1)S(1)}, u32[]{:S(2)}, u32[]{:S(2)}) collective-permute-start(bf16[20,2432]{1,0:T(8,128)(2,1)S(1)} %get-tuple-element.93), channel_id=1, source_target_pairs={{0,2},{1,3},{2,0},{3,1},{4,6},{5,7},{6,4},{7,5},{8,10},{9,11},{10,... | collective-permute-start | bytes 291848 | tf_op jit(solution)/shard_map/ppermute | solution.py:32
  230.4 6.4 %collective-permute-start.38 = (bf16[20,2432]{1,0:T(8,128)(2,1)S(1)}, bf16[20,2432]{1,0:T(8,128)(2,1)S(1)}, u32[]{:S(2)}, u32[]{:S(2)}) collective-permute-start(bf16[20,2432]{1,0:T(8,128)(2,1)S(1)} %get-tuple-element.94), channel_id=1, source_target_pairs={{0,1},{1,2},{2,3},{3,0},{4,5},{5,6},{6,7},{7,4},{8,9},{9,10},{10,1... | collective-permute-start | bytes 291848 | tf_op jit(solution)/shard_map/ppermute | solution.py:32
  231.0 21.2 %collective-permute-start.33 = (bf16[32,2432]{1,0:T(8,128)(2,1)S(1)}, bf16[32,2432]{1,0:T(8,128)(2,1)S(1)}, u32[]{:S(2)}, u32[]{:S(2)}) collective-permute-start(bf16[32,2432]{1,0:T(8,128)(2,1)S(1)} %get-tuple-element.87), channel_id=1, source_target_pairs={{0,3},{1,0},{2,1},{3,2},{4,7},{5,4},{6,5},{7,6},{8,11},{9,8},{10,9... | collective-permute-start | bytes 466952 | tf_op jit(solution)/shard_map/ppermute | solution.py:32
  233.0 19.2 %collective-permute-start.34 = (bf16[32,2432]{1,0:T(8,128)(2,1)S(1)}, bf16[32,2432]{1,0:T(8,128)(2,1)S(1)}, u32[]{:S(2)}, u32[]{:S(2)}) collective-permute-start(bf16[32,2432]{1,0:T(8,128)(2,1)S(1)} %get-tuple-element.88), channel_id=1, source_target_pairs={{0,2},{1,3},{2,0},{3,1},{4,6},{5,7},{6,4},{7,5},{8,10},{9,11},{10,... | collective-permute-start | bytes 466952 | tf_op jit(solution)/shard_map/ppermute | solution.py:32
  234.8 17.4 %collective-permute-start.35 = (bf16[32,2432]{1,0:T(8,128)(2,1)S(1)}, bf16[32,2432]{1,0:T(8,128)(2,1)S(1)}, u32[]{:S(2)}, u32[]{:S(2)}) collective-permute-start(bf16[32,2432]{1,0:T(8,128)(2,1)S(1)} %get-tuple-element.89), channel_id=1, source_target_pairs={{0,1},{1,2},{2,3},{3,0},{4,5},{5,6},{6,7},{7,4},{8,9},{9,10},{10,1... | collective-permute-start | bytes 466952 | tf_op jit(solution)/shard_map/ppermute | solution.py:32
  237.7 20.0 %all-to-all-start.3 = ((bf16[8,4,2432]{2,1,0:T(4,128)(2,1)}), bf16[8,4,2432]{2,1,0:T(4,128)(2,1)S(1)}, u32[]{:S(2)}, u32[]{:S(2)}) async-start(bf16[8,4,2432]{2,1,0:T(4,128)(2,1)} %reshape.26), calls=%async_computation.3 | async-start | bytes 311296 | tf_op jit(solution)/shard_map/all_to_all | solution.py:690
  (2 other events, 1.3 us)

commit v5 on v4

--- a/solution.py
+++ b/solution.py
@@ -429,14 +429,17 @@
         out[...] = result[place * part : (place + 1) * part].astype(BF16)
 
 
-def feed_kernel(in0, in1, in2, in3, win_ref, wout_ref, out0, out1, out2, out3, rows_ref):
-    pieces, outs = (in0, in1, in2, in3), (out0, out1, out2, out3)
-    width = out0.shape[1]
+def feed_kernel(*refs):
+    rows_ref = refs[-1]
+    count = (len(refs) - 3) // 2
+    pieces, outs = refs[0:count], refs[count + 2 : 2 * count + 2]
+    win_ref, wout_ref = refs[count], refs[count + 1]
+    width = outs[0].shape[1]
     for stream, (start, part) in enumerate(((0, 128), (128, SIDE * POOL))):
         for place, piece in enumerate(pieces):
             rows_ref[place * part : (place + 1) * part, :] = piece[start : start + part, :]
         hidden = lax.dot_general(
-            rows_ref[0 : SIDE * part, :],
+            rows_ref[0 : count * part, :],
             win_ref[stream],
             (((1,), (1,)), ((), ())),
             preferred_element_type=F32,
@@ -492,15 +495,16 @@
     )
 
 
-def feed(parts, weight_in, weight_out):
+def feed(parts, weight_in, weight_out, after=()):
     rows, width = parts[0].shape
     return run(
         feed_kernel,
-        [like((rows, width))] * SIDE,
+        [like((rows, width))] * len(parts),
         (*parts, weight_in, weight_out),
-        scratch=[pltpu.VMEM((SIDE * 128, width), BF16)],
-        flops=rows * SIDE * width * weight_in.shape[1] * 4,
+        scratch=[pltpu.VMEM((len(parts) * 128, width), BF16)],
+        flops=rows * len(parts) * width * weight_in.shape[1] * 4,
         limit=14,
+        after=after,
     )
 
 
@@ -575,7 +579,8 @@
         hbm=(2, 4, 5),
     )
     prompt_mod = run(
-        prompt_mod_kernel, like((2, 8, width), F32), (modulation.transpose(0, 2, 1, 3),)
+        prompt_mod_kernel, like((2, 8, width), F32), (modulation.transpose(0, 2, 1, 3),),
+        after=(outgoing,),
     )
     mod_own = run(
         mod_pair_kernel, like((4, 8, width), F32), (prompt_mod, core_swap(prompt_mod))
@@ -671,7 +676,9 @@
     )
     rows = spread(join(both_join_kernel, spread(norm_rows, 0)), 1)
     weight_in = feed_in_weight.transpose(0, 2, 1)
-    pieces = exchange(feed(rows, weight_in, feed_out_weight), 1)
+    own_term = feed(rows[:1], weight_in, feed_out_weight)
+    terms = feed(rows[1:], weight_in, feed_out_weight, after=(own_term[0],))
+    pieces = exchange([*own_term, *terms], 1)
     parts = run(
         part_middle_kernel,
         [like((POOL, width))] * SIDE + [like((32, width))] * SIDE,

time: 259 us -> 255 us (0.985)
  waiting for transfers between devices: 124 us -> 118 us
    ppermute x36, waiting for transfers between devices: 114 us -> 108 us  [torus_shift(): return lax.ppermute(values, ('grp', 'tp'), pairs)]
    pallas_call x22 -> x23, Pallas kernels: 34.4 us -> 36 us  [run(): pl.pallas_call(body, out_shape=shapes, in_specs=specs, out_specs=[pl.Bloc...]
    unnamed x48 -> x50, local copies, waits for them, and re-layouts: 13.5 us -> 13.5 us
  transfers between devices with their start and end apart: 42 -> 42, of which waited for: 25 -> 25; matrix products, arithmetic and copies ran while one was open for 0% -> 0% of each run, Pallas kernels for 7% -> 8%
where the time goes in v5:
time: 255 us; the launch traced here: 254 us
  waiting for transfers between devices  118 us (46%)
  starting transfers between devices  74.5 us (29%)
  Pallas kernels  36 us (14%)
  local copies, waits for them, and re-layouts  14.9 us (6%)
  blocking collectives  9.53 us (4%)
    ppermute x36, waiting for transfers between devices, torus_shift(): return lax.ppermute(values, ('grp', 'tp'), pairs)  108 us
    ppermute x36, starting transfers between devices, torus_shift(): return lax.ppermute(values, ('grp', 'tp'), pairs)  37.6 us
    pallas_call x23, Pallas kernels, run(): pl.pallas_call(body, out_shape=shapes, in_specs=specs, out_specs=[pl.Bloc...  36 us
    all_to_all x1, starting transfers between devices, shards(): lax.all_to_all(placed.reshape(8, 4, width), 'grp', 0, 0, tiled=True)  14.5 us
    unnamed x50, local copies, waits for them, and re-layouts  13.5 us
    all_to_all x1, starting transfers between devices, shards(): lax.all_to_all(slot_parts.reshape(8, 64, 512), 'grp', 0, 0, tiled=True)  9.81 us
    all_to_all x1, blocking collectives, shards(): lax.all_to_all(att_parts, 'grp', 0, 0, tiled=True).reshape(512, 128)  9.53 us
    all_to_all x1, starting transfers between devices, shards(): arrived = lax.all_to_all(outgoing, 'tp', 0, 0, tiled=True)  7.85 us
  transfers between devices with their start and end apart: 42, of which 25 were waited for; matrix products, arithmetic and copies ran while one was open for 0% of the time, Pallas kernels for 8%

profile of v5, /device:TPU:1, one launch (start us, length us, event | category | flops | bytes accessed | tf_op | source)
XLA Modules:
  0.0 253.9 jit_solution(8787600107410753851)
XLA Ops:
  0.6 0.9 copy-done.14
  2.2 0.9 shard_map.158
  3.1 0.9 copy-done.4
  4.1 1.5 collective-permute-start
  5.6 7.9 %all-to-all-start = ((bf16[16,32,256]{2,1,0:T(8,128)(2,1)}), bf16[16,32,256]{2,1,0:T(8,128)(2,1)S(1)}, u32[]{:S(2)}, u32[]{:S(2)}) async-start(bf16[16,32,256]{2,1,0:T(8,128)(2,1)} %get-tuple-element.48.refs_6_.refs_1_), calls=%async_computation | async-start | bytes 524288 | tf_op jit(solution)/shard_map/all_to_all | solution.py:550
  13.5 1.3 collective-permute-start.7
  14.9 7.8 %shard_map.159 = (f32[512,384]{1,0:T(8,128)}, bf16[16,32,192]{2,1,0:T(8,128)(2,1)}, bf16[32,2432]{1,0:T(8,128)(2,1)}, f32[6,2432]{1,0:T(8,128)}) custom-call(s32[2]{0:T(128)} %refs_0_.5, s32[1]{0:T(128)} %bitcast.refs_1_, bf16[512,2432]{1,0:T(8,128)(2,1)} %refs_2_.4, f32[2,6,2,2432]{3,2,1,0:T(2,128)} %bitcast.33, bf16[3,2432,128]{2,1,0:T(8,128)(2,1)} %bitcast.38, ...), custom_call_target="tpu_custom_call" | custom-call | flops 1434451968 | bytes 7656460 | tf_op jit(solution)/shard_map/pallas_call | solution.py:80
  22.7 0.9 copy-done.13
  23.7 2.5 shard_map.162
  26.2 2.5 collective-permute-start.1
  29.9 1.9 collective-permute-start.8
  31.8 7.8 %collective-permute-done.1.refs_1_ = bf16[80,2944]{1,0:T(8,128)(2,1)} collective-permute-done((bf16[80,2944]{1,0:T(8,128)(2,1)}, bf16[80,2944]{1,0:T(8,128)(2,1)}, u32[]{:S(2)}, u32[]{:S(2)}) %collective-permute-start.1) | collective-permute-done | bytes 471072 | tf_op jit(solution)/shard_map/ppermute | solution.py:32
  39.6 3.7 %collective-permute-done.3.refs_3_ = bf16[80,2944]{1,0:T(8,128)(2,1)} collective-permute-done((bf16[80,2944]{1,0:T(8,128)(2,1)}, bf16[80,2944]{1,0:T(8,128)(2,1)}, u32[]{:S(2)}, u32[]{:S(2)}) %collective-permute-start.3) | collective-permute-done | bytes 471072 | tf_op jit(solution)/shard_map/ppermute | solution.py:32
  43.3 1.8 shard_map.163
  45.1 2.4 collective-permute-start.4
  48.6 1.0 shard_map.165.refs_4_.refs_7_.refs_5_
  49.6 1.3 collective-permute-done.4.refs_1_
  51.0 2.0 collective-permute-done.5.refs_2_
  53.0 1.7 collective-permute-done.6.refs_3_
  55.6 1.5 collective-permute-start.10
  57.1 1.2 collective-permute-start.9
  58.3 4.0 %collective-permute-done.11.refs_3_ = bf16[20,2944]{1,0:T(8,128)(2,1)S(1)} collective-permute-done((bf16[20,2944]{1,0:T(8,128)(2,1)S(1)}, bf16[20,2944]{1,0:T(8,128)(2,1)S(1)}, u32[]{:S(2)}, u32[]{:S(2)}) %collective-permute-start.11) | collective-permute-done | bytes 117792 | tf_op jit(solution)/shard_map/ppermute | solution.py:32
  63.1 1.9 collective-permute-start.13
  65.0 1.0 collective-permute-start.12
  66.1 11.0 %collective-permute-done.14.refs_4_ = bf16[80,2944]{1,0:T(8,128)(2,1)S(1)} collective-permute-done((bf16[80,2944]{1,0:T(8,128)(2,1)S(1)}, bf16[80,2944]{1,0:T(8,128)(2,1)S(1)}, u32[]{:S(2)}, u32[]{:S(2)}) %collective-permute-start.14) | collective-permute-done | bytes 471072 | tf_op jit(solution)/shard_map/ppermute | solution.py:32
  77.7 2.2 shard_map.168
  81.6 9.8 %all-to-all-start.1 = ((bf16[8,64,512]{2,1,0:T(8,128)(2,1)}), bf16[8,64,512]{2,1,0:T(8,128)(2,1)S(1)}, u32[]{:S(2)}, u32[]{:S(2)}) async-start(bf16[8,64,512]{2,1,0:T(8,128)(2,1)} %bitcast.36), calls=%async_computation.1 | async-start | bytes 1048576 | tf_op jit(solution)/shard_map/all_to_all | solution.py:644
  91.4 1.1 copy-done.5
  92.5 1.0 copy-done.9
  93.6 1.5 shard_map.169.refs_1_
  95.9 5.0 %all-to-all-done.1.refs_2_ = bf16[8,64,512]{2,1,0:T(8,128)(2,1)S(1)} async-done(((bf16[8,64,512]{2,1,0:T(8,128)(2,1)}), bf16[8,64,512]{2,1,0:T(8,128)(2,1)S(1)}, u32[]{:S(2)}, u32[]{:S(2)}) %all-to-all-start.1) | async-done | bytes 524320 | tf_op jit(solution)/shard_map/all_to_all | solution.py:644
  100.9 1.0 copy-done.11
  101.9 1.1 copy-done.21
  103.0 2.5 shard_map.170
  105.5 2.4 collective-permute-start.15
  108.5 1.1 shard_map.171
  109.7 9.5 %all_to_all.20 = bf16[8,64,128]{2,1,0:T(8,128)(2,1)S(1)} all-to-all(bf16[8,64,128]{2,1,0:T(8,128)(2,1)S(1)} %shard_map.171), channel_id=1, replica_groups=mesh['grp'=8,'tp'=16] {'grp'}, dimensions={0} | all-to-all | bytes 262144 | tf_op jit(solution)/shard_map/all_to_all | solution.py:661
  119.2 2.5 collective-permute-done.15.refs_3_.refs_1_
  121.7 0.9 shard_map.172
  122.6 3.5 %collective-permute-start.18 = (bf16[80,2432]{1,0:T(8,128)(2,1)S(1)}, bf16[80,2432]{1,0:T(8,128)(2,1)S(1)}, u32[]{:S(2)}, u32[]{:S(2)}) collective-permute-start(bf16[80,2432]{1,0:T(8,128)(2,1)S(1)} %get-tuple-element.71), channel_id=1, source_target_pairs={{0,12},{1,13},{2,14},{3,15},{4,0},{5,1},{6,2},{7,3},{8,4},{9,5},{1... | collective-permute-start | bytes 1167368 | tf_op jit(solution)/shard_map/ppermute | solution.py:32
  126.8 8.2 %collective-permute-done.18.refs_5_ = bf16[80,2432]{1,0:T(8,128)(2,1)S(1)} collective-permute-done((bf16[80,2432]{1,0:T(8,128)(2,1)S(1)}, bf16[80,2432]{1,0:T(8,128)(2,1)S(1)}, u32[]{:S(2)}, u32[]{:S(2)}) %collective-permute-start.18) | collective-permute-done | bytes 389152 | tf_op jit(solution)/shard_map/ppermute | solution.py:32
  135.0 3.4 %collective-permute-done.20.refs_7_ = bf16[80,2432]{1,0:T(8,128)(2,1)S(1)} collective-permute-done((bf16[80,2432]{1,0:T(8,128)(2,1)S(1)}, bf16[80,2432]{1,0:T(8,128)(2,1)S(1)}, u32[]{:S(2)}, u32[]{:S(2)}) %collective-permute-start.20) | collective-permute-done | bytes 389152 | tf_op jit(solution)/shard_map/ppermute | solution.py:32
  139.3 2.3 collective-permute-start.21
  142.2 5.7 %collective-permute-done.21.refs_3_ = bf16[52,2432]{1,0:T(8,128)(2,1)S(1)} collective-permute-done((bf16[52,2432]{1,0:T(8,128)(2,1)S(1)}, bf16[52,2432]{1,0:T(8,128)(2,1)S(1)}, u32[]{:S(2)}, u32[]{:S(2)}) %collective-permute-start.21) | collective-permute-done | bytes 252960 | tf_op jit(solution)/shard_map/ppermute | solution.py:32
  148.5 2.8 %collective-permute-done.23.refs_5_ = bf16[52,2432]{1,0:T(8,128)(2,1)S(1)} collective-permute-done((bf16[52,2432]{1,0:T(8,128)(2,1)S(1)}, bf16[52,2432]{1,0:T(8,128)(2,1)S(1)}, u32[]{:S(2)}, u32[]{:S(2)}) %collective-permute-start.23) | collective-permute-done | bytes 252960 | tf_op jit(solution)/shard_map/ppermute | solution.py:32
  151.9 1.8 collective-permute-start.25
  153.7 0.9 collective-permute-start.24
  154.6 7.1 %collective-permute-done.26.refs_3_ = bf16[52,2432]{1,0:T(8,128)(2,1)S(1)} collective-permute-done((bf16[52,2432]{1,0:T(8,128)(2,1)S(1)}, bf16[52,2432]{1,0:T(8,128)(2,1)S(1)}, u32[]{:S(2)}, u32[]{:S(2)}) %collective-permute-start.26) | collective-permute-done | bytes 252960 | tf_op jit(solution)/shard_map/ppermute | solution.py:32
  162.5 1.6 collective-permute-start.28
  164.1 1.1 collective-permute-start.27
  165.2 2.7 %copy-done = bf16[2,608,2432]{2,1,0:T(8,128)(2,1)S(1)} copy-done((bf16[2,608,2432]{2,1,0:T(8,128)(2,1)S(1)}, bf16[2,608,2432]{2,1,0:T(8,128)(2,1)}, u32[]{:S(2)}) %copy-start) | copy-done | bytes 5914648
  167.8 3.4 %shard_map.176.refs_5_.refs_0_ = bf16[208,2432]{1,0:T(8,128)(2,1)S(1)} custom-call(bf16[208,2432]{1,0:T(8,128)(2,1)S(1)} %shard_map.175.refs_0_, bf16[2,608,2432]{2,1,0:T(8,128)(2,1)S(1)} %bitcast.30, bf16[2,608,2432]{2,1,0:T(8,128)(2,1)S(1)} %copy-done), custom_call_target="tpu_custom_call" | custom-call | flops 1230241792 | bytes 13852672 | tf_op jit(solution)/shard_map/pallas_call | solution.py:80
  171.2 16.8 %collective-permute-done.29.refs_2_ = bf16[208,2432]{1,0:T(8,128)(2,1)S(1)} collective-permute-done((bf16[208,2432]{1,0:T(8,128)(2,1)S(1)}, bf16[208,2432]{1,0:T(8,128)(2,1)S(1)}, u32[]{:S(2)}, u32[]{:S(2)}) %collective-permute-start.29) | collective-permute-done | bytes 1011744 | tf_op jit(solution)/shard_map/ppermute | solution.py:32
  188.8 6.5 %shard_map.177 = (bf16[208,2432]{1,0:T(8,128)(2,1)S(1)}, bf16[208,2432]{1,0:T(8,128)(2,1)S(1)}, bf16[208,2432]{1,0:T(8,128)(2,1)S(1)}) custom-call(bf16[208,2432]{1,0:T(8,128)(2,1)S(1)} %collective-permute-done.27.refs_0_, bf16[208,2432]{1,0:T(8,128)(2,1)S(1)} %collective-permute-done.28.refs_1_, bf16[208,2432]{1,0:T(8,128)(2,1)S(1)} %collective-permute-done.29.refs_2_, ...), custom_call_target="tpu_custom_call" | custom-call | flops 3690725376 | bytes 17899520 | tf_op jit(solution)/shard_map/pallas_call | solution.py:80
  195.3 2.1 collective-permute-start.30
  198.1 21.5 %collective-permute-done.30.refs_1_ = bf16[208,2432]{1,0:T(8,128)(2,1)S(1)} collective-permute-done((bf16[208,2432]{1,0:T(8,128)(2,1)S(1)}, bf16[208,2432]{1,0:T(8,128)(2,1)S(1)}, u32[]{:S(2)}, u32[]{:S(2)}) %collective-permute-start.30) | collective-permute-done | bytes 1011744 | tf_op jit(solution)/shard_map/ppermute | solution.py:32
  219.6 3.4 %collective-permute-done.32.refs_3_ = bf16[208,2432]{1,0:T(8,128)(2,1)S(1)} collective-permute-done((bf16[208,2432]{1,0:T(8,128)(2,1)S(1)}, bf16[208,2432]{1,0:T(8,128)(2,1)S(1)}, u32[]{:S(2)}, u32[]{:S(2)}) %collective-permute-start.32) | collective-permute-done | bytes 1011744 | tf_op jit(solution)/shard_map/ppermute | solution.py:32
  223.0 0.9 shard_map.178
  223.9 2.0 collective-permute-start.36
  226.6 2.0 collective-permute-start.33
  228.6 1.8 collective-permute-start.34
  230.3 1.2 collective-permute-done.37.refs_3_
  233.2 14.5 %all-to-all-start.3 = ((bf16[8,4,2432]{2,1,0:T(4,128)(2,1)}), bf16[8,4,2432]{2,1,0:T(4,128)(2,1)S(1)}, u32[]{:S(2)}, u32[]{:S(2)}) async-start(bf16[8,4,2432]{2,1,0:T(4,128)(2,1)} %reshape.26), calls=%async_computation.3 | async-start | bytes 311296 | tf_op jit(solution)/shard_map/all_to_all | solution.py:697
  248.5 4.7 %all-to-all-done.3 = bf16[8,4,2432]{2,1,0:T(4,128)(2,1)S(1)} async-done(((bf16[8,4,2432]{2,1,0:T(4,128)(2,1)}), bf16[8,4,2432]{2,1,0:T(4,128)(2,1)S(1)}, u32[]{:S(2)}, u32[]{:S(2)}) %all-to-all-start.3) | async-done | bytes 155680 | tf_op jit(solution)/shard_map/all_to_all | solution.py:697
  (100 shorter events, 18.3 us)
Async XLA Ops:
  0.6 0.9 copy-start.14
  3.1 0.9 copy-start.4
  4.1 9.4 %collective-permute-start = (f32[2,8,2432]{2,1,0:T(8,128)S(1)}, f32[2,8,2432]{2,1,0:T(8,128)S(1)}, u32[]{:S(2)}, u32[]{:S(2)}) collective-permute-start(f32[2,8,2432]{2,1,0:T(8,128)S(1)} %shard_map.160.refs_0_), channel_id=1, source_target_pairs={{0,16},{16,0},{32,48},{48,32},{64,80},{80,64},{96,112},{112,96},{1... | collective-permute-start | bytes 466952 | tf_op jit(solution)/shard_map/ppermute | solution.py:36
  5.6 17.1 %all-to-all-start = ((bf16[16,32,256]{2,1,0:T(8,128)(2,1)}), bf16[16,32,256]{2,1,0:T(8,128)(2,1)S(1)}, u32[]{:S(2)}, u32[]{:S(2)}) async-start(bf16[16,32,256]{2,1,0:T(8,128)(2,1)} %get-tuple-element.48.refs_6_.refs_1_), calls=%async_computation | async-start | bytes 524288 | tf_op jit(solution)/shard_map/all_to_all | solution.py:550
  13.5 16.3 %collective-permute-start.7 = (f32[4,8,2432]{2,1,0:T(8,128)S(1)}, f32[4,8,2432]{2,1,0:T(8,128)S(1)}, u32[]{:S(2)}, u32[]{:S(2)}) collective-permute-start(f32[4,8,2432]{2,1,0:T(8,128)S(1)} %shard_map.161.refs_4_.refs_0_), channel_id=1, source_target_pairs={{0,32},{16,48},{32,0},{48,16},{64,96},{80,112},{96,64},{112,80},{1... | collective-permute-start | bytes 933896 | tf_op jit(solution)/shard_map/ppermute | solution.py:44
  14.8 7.9 %copy-start.3 = (bf16[256,2432]{1,0:T(8,128)(2,1)S(1)}, bf16[256,2432]{1,0:T(8,128)(2,1)}, u32[]{:S(2)}) copy-start(bf16[256,2432]{1,0:T(8,128)(2,1)} %refs_2_.5) | copy-start | bytes 3735556
  22.7 1.0 copy-start.13
  26.2 22.4 %copy-start.19 = (s32[20,1]{0,1:T(1,128)S(1)}, s32[20,1]{0,1:T(1,128)}, u32[]{:S(2)}) copy-start(s32[20,1]{0,1:T(1,128)} %param.17) | copy-start | bytes 244
  26.2 13.5 %collective-permute-start.1 = (bf16[80,2944]{1,0:T(8,128)(2,1)}, bf16[80,2944]{1,0:T(8,128)(2,1)}, u32[]{:S(2)}, u32[]{:S(2)}) collective-permute-start(bf16[80,2944]{1,0:T(8,128)(2,1)} %get-tuple-element.52), channel_id=1, source_target_pairs={{0,12},{1,13},{2,14},{3,15},{4,0},{5,1},{6,2},{7,3},{8,4},{9,5},{1... | collective-permute-start | bytes 1413128 | tf_op jit(solution)/shard_map/ppermute | solution.py:32
  28.7 10.9 %collective-permute-start.2 = (bf16[80,2944]{1,0:T(8,128)(2,1)}, bf16[80,2944]{1,0:T(8,128)(2,1)}, u32[]{:S(2)}, u32[]{:S(2)}) collective-permute-start(bf16[80,2944]{1,0:T(8,128)(2,1)} %get-tuple-element.53), channel_id=1, source_target_pairs={{0,8},{1,9},{2,10},{3,11},{4,12},{5,13},{6,14},{7,15},{8,0},{9,1},... | collective-permute-start | bytes 1413128 | tf_op jit(solution)/shard_map/ppermute | solution.py:32
  29.3 14.0 %collective-permute-start.3 = (bf16[80,2944]{1,0:T(8,128)(2,1)}, bf16[80,2944]{1,0:T(8,128)(2,1)}, u32[]{:S(2)}, u32[]{:S(2)}) collective-permute-start(bf16[80,2944]{1,0:T(8,128)(2,1)} %get-tuple-element.54), channel_id=1, source_target_pairs={{0,4},{1,5},{2,6},{3,7},{4,8},{5,9},{6,10},{7,11},{8,12},{9,13},{1... | collective-permute-start | bytes 1413128 | tf_op jit(solution)/shard_map/ppermute | solution.py:32
  29.9 18.7 %collective-permute-start.8 = (f32[8,8,2432]{2,1,0:T(8,128)S(1)}, f32[8,8,2432]{2,1,0:T(8,128)S(1)}, u32[]{:S(2)}, u32[]{:S(2)}) collective-permute-start(f32[8,8,2432]{2,1,0:T(8,128)S(1)} %shard_map.164.refs_1_), channel_id=1, source_target_pairs={{0,96},{16,112},{32,64},{48,80},{64,32},{80,48},{96,0},{112,16},{1... | collective-permute-start | bytes 1867784 | tf_op jit(solution)/shard_map/ppermute | solution.py:44
  45.1 5.9 %collective-permute-start.4 = (bf16[20,2944]{1,0:T(8,128)(2,1)S(1)}, bf16[20,2944]{1,0:T(8,128)(2,1)S(1)}, u32[]{:S(2)}, u32[]{:S(2)}) collective-permute-start(bf16[20,2944]{1,0:T(8,128)(2,1)S(1)} %get-tuple-element.56), channel_id=1, source_target_pairs={{0,3},{1,0},{2,1},{3,2},{4,7},{5,4},{6,5},{7,6},{8,11},{9,8},{10,9... | collective-permute-start | bytes 353288 | tf_op jit(solution)/shard_map/ppermute | solution.py:32
  47.4 5.5 %collective-permute-start.5 = (bf16[20,2944]{1,0:T(8,128)(2,1)S(1)}, bf16[20,2944]{1,0:T(8,128)(2,1)S(1)}, u32[]{:S(2)}, u32[]{:S(2)}) collective-permute-start(bf16[20,2944]{1,0:T(8,128)(2,1)S(1)} %get-tuple-element.57), channel_id=1, source_target_pairs={{0,2},{1,3},{2,0},{3,1},{4,6},{5,7},{6,4},{7,5},{8,10},{9,11},{10,... | collective-permute-start | bytes 353288 | tf_op jit(solution)/shard_map/ppermute | solution.py:32
  48.0 6.7 %collective-permute-start.6 = (bf16[20,2944]{1,0:T(8,128)(2,1)S(1)}, bf16[20,2944]{1,0:T(8,128)(2,1)S(1)}, u32[]{:S(2)}, u32[]{:S(2)}) collective-permute-start(bf16[20,2944]{1,0:T(8,128)(2,1)S(1)} %get-tuple-element.58), channel_id=1, source_target_pairs={{0,1},{1,2},{2,3},{3,0},{4,5},{5,6},{6,7},{7,4},{8,9},{9,10},{10,1... | collective-permute-start | bytes 353288 | tf_op jit(solution)/shard_map/ppermute | solution.py:32
  49.6 16.4 %copy-start.22 = (f32[2,2,64]{2,1,0:T(2,128)S(1)}, f32[2,2,64]{2,1,0:T(2,128)}, u32[]{:S(2)}) copy-start(f32[2,2,64]{2,1,0:T(2,128)} %param.20) | copy-start | bytes 3076
  49.6 28.1 %copy-start.1 = (bf16[2432,3,128]{2,0,1:T(8,128)(2,1)S(1)}, bf16[2432,3,128]{2,0,1:T(8,128)(2,1)}, u32[]{:S(2)}) copy-start(bf16[2432,3,128]{2,0,1:T(8,128)(2,1)} %param.23) | copy-start | bytes 5603332
  55.6 6.7 %collective-permute-start.11 = (bf16[20,2944]{1,0:T(8,128)(2,1)S(1)}, bf16[20,2944]{1,0:T(8,128)(2,1)S(1)}, u32[]{:S(2)}, u32[]{:S(2)}) collective-permute-start(bf16[20,2944]{1,0:T(8,128)(2,1)S(1)} %get-tuple-element.60.refs_0_), channel_id=1, source_target_pairs={{0,1},{1,2},{2,3},{3,0},{4,5},{5,6},{6,7},{7,4},{8,9},{9,10},{10,1... | collective-permute-start | bytes 353288 | tf_op jit(solution)/shard_map/ppermute | solution.py:32
  55.6 6.7 %collective-permute-start.10 = (bf16[20,2944]{1,0:T(8,128)(2,1)S(1)}, bf16[20,2944]{1,0:T(8,128)(2,1)S(1)}, u32[]{:S(2)}, u32[]{:S(2)}) collective-permute-start(bf16[20,2944]{1,0:T(8,128)(2,1)S(1)} %get-tuple-element.60.refs_0_), channel_id=1, source_target_pairs={{0,2},{1,3},{2,0},{3,1},{4,6},{5,7},{6,4},{7,5},{8,10},{9,11},{10,... | collective-permute-start | bytes 353288 | tf_op jit(solution)/shard_map/ppermute | solution.py:32
  57.1 5.8 %collective-permute-start.9 = (bf16[20,2944]{1,0:T(8,128)(2,1)S(1)}, bf16[20,2944]{1,0:T(8,128)(2,1)S(1)}, u32[]{:S(2)}, u32[]{:S(2)}) collective-permute-start(bf16[20,2944]{1,0:T(8,128)(2,1)S(1)} %get-tuple-element.60.refs_0_), channel_id=1, source_target_pairs={{0,3},{1,0},{2,1},{3,2},{4,7},{5,4},{6,5},{7,6},{8,11},{9,8},{10,9... | collective-permute-start | bytes 353288 | tf_op jit(solution)/shard_map/ppermute | solution.py:32
  63.0 14.1 %collective-permute-start.14 = (bf16[80,2944]{1,0:T(8,128)(2,1)S(1)}, bf16[80,2944]{1,0:T(8,128)(2,1)S(1)}, u32[]{:S(2)}, u32[]{:S(2)}) collective-permute-start(bf16[80,2944]{1,0:T(8,128)(2,1)S(1)} %shard_map.167.refs_1_), channel_id=1, source_target_pairs={{0,4},{1,5},{2,6},{3,7},{4,8},{5,9},{6,10},{7,11},{8,12},{9,13},{1... | collective-permute-start | bytes 1413128 | tf_op jit(solution)/shard_map/ppermute | solution.py:32
  63.1 14.0 %collective-permute-start.13 = (bf16[80,2944]{1,0:T(8,128)(2,1)S(1)}, bf16[80,2944]{1,0:T(8,128)(2,1)S(1)}, u32[]{:S(2)}, u32[]{:S(2)}) collective-permute-start(bf16[80,2944]{1,0:T(8,128)(2,1)S(1)} %shard_map.167.refs_1_), channel_id=1, source_target_pairs={{0,8},{1,9},{2,10},{3,11},{4,12},{5,13},{6,14},{7,15},{8,0},{9,1},... | collective-permute-start | bytes 1413128 | tf_op jit(solution)/shard_map/ppermute | solution.py:32
  65.0 12.7 %collective-permute-start.12 = (bf16[80,2944]{1,0:T(8,128)(2,1)S(1)}, bf16[80,2944]{1,0:T(8,128)(2,1)S(1)}, u32[]{:S(2)}, u32[]{:S(2)}) collective-permute-start(bf16[80,2944]{1,0:T(8,128)(2,1)S(1)} %shard_map.167.refs_1_), channel_id=1, source_target_pairs={{0,12},{1,13},{2,14},{3,15},{4,0},{5,1},{6,2},{7,3},{8,4},{9,5},{1... | collective-permute-start | bytes 1413128 | tf_op jit(solution)/shard_map/ppermute | solution.py:32
  77.7 13.6 %copy-start.2 = (bf16[32,3,64,128]{3,2,1,0:T(8,128)(2,1)S(1)}, bf16[32,3,64,128]{3,2,1,0:T(8,128)(2,1)}, u32[]{:S(2)}) copy-start(bf16[32,3,64,128]{3,2,1,0:T(8,128)(2,1)} %refs_3_.2) | copy-start | bytes 4718596
  77.7 13.6 %copy-start.20 = (s32[2]{0:T(128)S(1)}, s32[2]{0:T(128)}, u32[]{:S(2)}) copy-start(s32[2]{0:T(128)} %refs_0_.5) | copy-start | bytes 28
  80.8 0.8 copy-start.8
  81.6 19.3 %all-to-all-start.1 = ((bf16[8,64,512]{2,1,0:T(8,128)(2,1)}), bf16[8,64,512]{2,1,0:T(8,128)(2,1)S(1)}, u32[]{:S(2)}, u32[]{:S(2)}) async-start(bf16[8,64,512]{2,1,0:T(8,128)(2,1)} %bitcast.36), calls=%async_computation.1 | async-start | bytes 1048576 | tf_op jit(solution)/shard_map/all_to_all | solution.py:644
  91.4 1.1 copy-start.5
  92.5 1.0 copy-start.9
  95.1 0.8 copy-start.10
  100.9 1.0 copy-start.11
  101.9 1.1 copy-start.21
  105.5 16.2 %copy-start.6 = (bf16[128,2432]{1,0:T(8,128)(2,1)S(1)}, bf16[128,2432]{1,0:T(8,128)(2,1)}, u32[]{:S(2)}) copy-start(bf16[128,2432]{1,0:T(8,128)(2,1)} %refs_2_.6) | copy-start | bytes 1867780
  105.5 16.2 %collective-permute-start.15 = (bf16[128,2432]{1,0:T(8,128)(2,1)S(1)}, bf16[128,2432]{1,0:T(8,128)(2,1)S(1)}, u32[]{:S(2)}, u32[]{:S(2)}) collective-permute-start(bf16[128,2432]{1,0:T(8,128)(2,1)S(1)} %get-tuple-element.66), channel_id=1, source_target_pairs={{0,12},{1,13},{2,14},{3,15},{4,0},{5,1},{6,2},{7,3},{8,4},{9,5},{1... | collective-permute-start | bytes 1867784 | tf_op jit(solution)/shard_map/ppermute | solution.py:32
  107.9 18.9 %collective-permute-start.16 = (bf16[128,2432]{1,0:T(8,128)(2,1)S(1)}, bf16[128,2432]{1,0:T(8,128)(2,1)S(1)}, u32[]{:S(2)}, u32[]{:S(2)}) collective-permute-start(bf16[128,2432]{1,0:T(8,128)(2,1)S(1)} %get-tuple-element.67), channel_id=1, source_target_pairs={{0,8},{1,9},{2,10},{3,11},{4,12},{5,13},{6,14},{7,15},{8,0},{9,1},... | collective-permute-start | bytes 1867784 | tf_op jit(solution)/shard_map/ppermute | solution.py:32
  107.9 18.9 %collective-permute-start.17 = (bf16[128,2432]{1,0:T(8,128)(2,1)S(1)}, bf16[128,2432]{1,0:T(8,128)(2,1)S(1)}, u32[]{:S(2)}, u32[]{:S(2)}) collective-permute-start(bf16[128,2432]{1,0:T(8,128)(2,1)S(1)} %get-tuple-element.68), channel_id=1, source_target_pairs={{0,4},{1,5},{2,6},{3,7},{4,8},{5,9},{6,10},{7,11},{8,12},{9,13},{1... | collective-permute-start | bytes 1867784 | tf_op jit(solution)/shard_map/ppermute | solution.py:32
  108.5 56.6 %slice-start = ((s8[5914624]{0:T(1024)(128)(4,1)}), s8[4194304]{0:T(1024)(128)(4,1)S(1)}, s32[]{:S(2)}) async-start(s8[5914624]{0:T(1024)(128)(4,1)} %bitcast.28), calls=%async_computation.4 | async-start | bytes 8388608
  122.6 12.3 %collective-permute-start.18 = (bf16[80,2432]{1,0:T(8,128)(2,1)S(1)}, bf16[80,2432]{1,0:T(8,128)(2,1)S(1)}, u32[]{:S(2)}, u32[]{:S(2)}) collective-permute-start(bf16[80,2432]{1,0:T(8,128)(2,1)S(1)} %get-tuple-element.71), channel_id=1, source_target_pairs={{0,12},{1,13},{2,14},{3,15},{4,0},{5,1},{6,2},{7,3},{8,4},{9,5},{1... | collective-permute-start | bytes 1167368 | tf_op jit(solution)/shard_map/ppermute | solution.py:32
  126.1 8.8 %collective-permute-start.19 = (bf16[80,2432]{1,0:T(8,128)(2,1)S(1)}, bf16[80,2432]{1,0:T(8,128)(2,1)S(1)}, u32[]{:S(2)}, u32[]{:S(2)}) collective-permute-start(bf16[80,2432]{1,0:T(8,128)(2,1)S(1)} %get-tuple-element.72), channel_id=1, source_target_pairs={{0,8},{1,9},{2,10},{3,11},{4,12},{5,13},{6,14},{7,15},{8,0},{9,1},... | collective-permute-start | bytes 1167368 | tf_op jit(solution)/shard_map/ppermute | solution.py:32
  126.1 12.3 %collective-permute-start.20 = (bf16[80,2432]{1,0:T(8,128)(2,1)S(1)}, bf16[80,2432]{1,0:T(8,128)(2,1)S(1)}, u32[]{:S(2)}, u32[]{:S(2)}) collective-permute-start(bf16[80,2432]{1,0:T(8,128)(2,1)S(1)} %get-tuple-element.73), channel_id=1, source_target_pairs={{0,4},{1,5},{2,6},{3,7},{4,8},{5,9},{6,10},{7,11},{8,12},{9,13},{1... | collective-permute-start | bytes 1167368 | tf_op jit(solution)/shard_map/ppermute | solution.py:32
  138.4 12.9 %copy-start.12 = (f32[6,2432]{1,0:T(8,128)S(1)}, f32[6,2432]{1,0:T(8,128)}, u32[]{:S(2)}) copy-start(f32[6,2432]{1,0:T(8,128)} %get-tuple-element.78.refs_6_.refs_5_) | copy-start | bytes 175108
  138.4 12.9 %copy-start.15 = (bf16[32,2432]{1,0:T(8,128)(2,1)S(1)}, bf16[32,2432]{1,0:T(8,128)(2,1)}, u32[]{:S(2)}) copy-start(bf16[32,2432]{1,0:T(8,128)(2,1)} %get-tuple-element.49.refs_0_) | copy-start | bytes 466948
  138.4 12.9 %copy-start.17 = (bf16[20,2432]{1,0:T(8,128)(2,1)S(1)}, bf16[20,2432]{1,0:T(8,128)(2,1)}, u32[]{:S(2)}) copy-start(bf16[20,2432]{1,0:T(8,128)(2,1)} %copy-done.16) | copy-start | bytes 291844
  138.4 26.8 %slice-start.1 = ((s8[5914624]{0:T(1024)(128)(4,1)}), s8[1720320]{0:T(1024)(128)(4,1)S(1)}, s32[]{:S(2)}) async-start(s8[5914624]{0:T(1024)(128)(4,1)} %bitcast.28), calls=%async_computation.5 | async-start | bytes 3440640
  139.3 8.6 %collective-permute-start.21 = (bf16[52,2432]{1,0:T(8,128)(2,1)S(1)}, bf16[52,2432]{1,0:T(8,128)(2,1)S(1)}, u32[]{:S(2)}, u32[]{:S(2)}) collective-permute-start(bf16[52,2432]{1,0:T(8,128)(2,1)S(1)} %get-tuple-element.75), channel_id=1, source_target_pairs={{0,3},{1,0},{2,1},{3,2},{4,7},{5,4},{6,5},{7,6},{8,11},{9,8},{10,9... | collective-permute-start | bytes 758792 | tf_op jit(solution)/shard_map/ppermute | solution.py:32
  141.5 6.9 %collective-permute-start.22 = (bf16[52,2432]{1,0:T(8,128)(2,1)S(1)}, bf16[52,2432]{1,0:T(8,128)(2,1)S(1)}, u32[]{:S(2)}, u32[]{:S(2)}) collective-permute-start(bf16[52,2432]{1,0:T(8,128)(2,1)S(1)} %get-tuple-element.76), channel_id=1, source_target_pairs={{0,2},{1,3},{2,0},{3,1},{4,6},{5,7},{6,4},{7,5},{8,10},{9,11},{10,... | collective-permute-start | bytes 758792 | tf_op jit(solution)/shard_map/ppermute | solution.py:32
  141.5 9.8 %collective-permute-start.23 = (bf16[52,2432]{1,0:T(8,128)(2,1)S(1)}, bf16[52,2432]{1,0:T(8,128)(2,1)S(1)}, u32[]{:S(2)}, u32[]{:S(2)}) collective-permute-start(bf16[52,2432]{1,0:T(8,128)(2,1)S(1)} %get-tuple-element.77), channel_id=1, source_target_pairs={{0,1},{1,2},{2,3},{3,0},{4,5},{5,6},{6,7},{7,4},{8,9},{9,10},{10,1... | collective-permute-start | bytes 758792 | tf_op jit(solution)/shard_map/ppermute | solution.py:32
  151.8 9.8 %collective-permute-start.26 = (bf16[52,2432]{1,0:T(8,128)(2,1)S(1)}, bf16[52,2432]{1,0:T(8,128)(2,1)S(1)}, u32[]{:S(2)}, u32[]{:S(2)}) collective-permute-start(bf16[52,2432]{1,0:T(8,128)(2,1)S(1)} %get-tuple-element.80.refs_0_), channel_id=1, source_target_pairs={{0,1},{1,2},{2,3},{3,0},{4,5},{5,6},{6,7},{7,4},{8,9},{9,10},{10,1... | collective-permute-start | bytes 758792 | tf_op jit(solution)/shard_map/ppermute | solution.py:32
  151.9 9.7 %collective-permute-start.25 = (bf16[52,2432]{1,0:T(8,128)(2,1)S(1)}, bf16[52,2432]{1,0:T(8,128)(2,1)S(1)}, u32[]{:S(2)}, u32[]{:S(2)}) collective-permute-start(bf16[52,2432]{1,0:T(8,128)(2,1)S(1)} %get-tuple-element.80.refs_0_), channel_id=1, source_target_pairs={{0,2},{1,3},{2,0},{3,1},{4,6},{5,7},{6,4},{7,5},{8,10},{9,11},{10,... | collective-permute-start | bytes 758792 | tf_op jit(solution)/shard_map/ppermute | solution.py:32
  153.7 8.6 %collective-permute-start.24 = (bf16[52,2432]{1,0:T(8,128)(2,1)S(1)}, bf16[52,2432]{1,0:T(8,128)(2,1)S(1)}, u32[]{:S(2)}, u32[]{:S(2)}) collective-permute-start(bf16[52,2432]{1,0:T(8,128)(2,1)S(1)} %get-tuple-element.80.refs_0_), channel_id=1, source_target_pairs={{0,3},{1,0},{2,1},{3,2},{4,7},{5,4},{6,5},{7,6},{8,11},{9,8},{10,9... | collective-permute-start | bytes 758792 | tf_op jit(solution)/shard_map/ppermute | solution.py:32
  162.4 25.7 %collective-permute-start.29 = (bf16[208,2432]{1,0:T(8,128)(2,1)S(1)}, bf16[208,2432]{1,0:T(8,128)(2,1)S(1)}, u32[]{:S(2)}, u32[]{:S(2)}) collective-permute-start(bf16[208,2432]{1,0:T(8,128)(2,1)S(1)} %shard_map.175.refs_0_), channel_id=1, source_target_pairs={{0,4},{1,5},{2,6},{3,7},{4,8},{5,9},{6,10},{7,11},{8,12},{9,13},{1... | collective-permute-start | bytes 3035144 | tf_op jit(solution)/shard_map/ppermute | solution.py:32
  162.5 25.6 %collective-permute-start.28 = (bf16[208,2432]{1,0:T(8,128)(2,1)S(1)}, bf16[208,2432]{1,0:T(8,128)(2,1)S(1)}, u32[]{:S(2)}, u32[]{:S(2)}) collective-permute-start(bf16[208,2432]{1,0:T(8,128)(2,1)S(1)} %shard_map.175.refs_0_), channel_id=1, source_target_pairs={{0,8},{1,9},{2,10},{3,11},{4,12},{5,13},{6,14},{7,15},{8,0},{9,1},... | collective-permute-start | bytes 3035144 | tf_op jit(solution)/shard_map/ppermute | solution.py:32
  164.1 24.8 %collective-permute-start.27 = (bf16[208,2432]{1,0:T(8,128)(2,1)S(1)}, bf16[208,2432]{1,0:T(8,128)(2,1)S(1)}, u32[]{:S(2)}, u32[]{:S(2)}) collective-permute-start(bf16[208,2432]{1,0:T(8,128)(2,1)S(1)} %shard_map.175.refs_0_), channel_id=1, source_target_pairs={{0,12},{1,13},{2,14},{3,15},{4,0},{5,1},{6,2},{7,3},{8,4},{9,5},{1... | collective-permute-start | bytes 3035144 | tf_op jit(solution)/shard_map/ppermute | solution.py:32
  165.1 2.7 %copy-start = (bf16[2,608,2432]{2,1,0:T(8,128)(2,1)S(1)}, bf16[2,608,2432]{2,1,0:T(8,128)(2,1)}, u32[]{:S(2)}) copy-start(bf16[2,608,2432]{2,1,0:T(8,128)(2,1)} %refs_4_.1) | copy-start | bytes 17743876
  195.3 24.3 %collective-permute-start.30 = (bf16[208,2432]{1,0:T(8,128)(2,1)S(1)}, bf16[208,2432]{1,0:T(8,128)(2,1)S(1)}, u32[]{:S(2)}, u32[]{:S(2)}) collective-permute-start(bf16[208,2432]{1,0:T(8,128)(2,1)S(1)} %get-tuple-element.81), channel_id=1, source_target_pairs={{0,12},{1,13},{2,14},{3,15},{4,0},{5,1},{6,2},{7,3},{8,4},{9,5},{1... | collective-permute-start | bytes 3035144 | tf_op jit(solution)/shard_map/ppermute | solution.py:32
  197.4 22.2 %collective-permute-start.31 = (bf16[208,2432]{1,0:T(8,128)(2,1)S(1)}, bf16[208,2432]{1,0:T(8,128)(2,1)S(1)}, u32[]{:S(2)}, u32[]{:S(2)}) collective-permute-start(bf16[208,2432]{1,0:T(8,128)(2,1)S(1)} %get-tuple-element.82), channel_id=1, source_target_pairs={{0,8},{1,9},{2,10},{3,11},{4,12},{5,13},{6,14},{7,15},{8,0},{9,1},... | collective-permute-start | bytes 3035144 | tf_op jit(solution)/shard_map/ppermute | solution.py:32
  197.4 25.6 %collective-permute-start.32 = (bf16[208,2432]{1,0:T(8,128)(2,1)S(1)}, bf16[208,2432]{1,0:T(8,128)(2,1)S(1)}, u32[]{:S(2)}, u32[]{:S(2)}) collective-permute-start(bf16[208,2432]{1,0:T(8,128)(2,1)S(1)} %get-tuple-element.83), channel_id=1, source_target_pairs={{0,4},{1,5},{2,6},{3,7},{4,8},{5,9},{6,10},{7,11},{8,12},{9,13},{1... | collective-permute-start | bytes 3035144 | tf_op jit(solution)/shard_map/ppermute | solution.py:32
  223.9 6.5 %collective-permute-start.36 = (bf16[20,2432]{1,0:T(8,128)(2,1)S(1)}, bf16[20,2432]{1,0:T(8,128)(2,1)S(1)}, u32[]{:S(2)}, u32[]{:S(2)}) collective-permute-start(bf16[20,2432]{1,0:T(8,128)(2,1)S(1)} %get-tuple-element.90), channel_id=1, source_target_pairs={{0,3},{1,0},{2,1},{3,2},{4,7},{5,4},{6,5},{7,6},{8,11},{9,8},{10,9... | collective-permute-start | bytes 291848 | tf_op jit(solution)/shard_map/ppermute | solution.py:32
  225.9 5.6 %collective-permute-start.37 = (bf16[20,2432]{1,0:T(8,128)(2,1)S(1)}, bf16[20,2432]{1,0:T(8,128)(2,1)S(1)}, u32[]{:S(2)}, u32[]{:S(2)}) collective-permute-start(bf16[20,2432]{1,0:T(8,128)(2,1)S(1)} %get-tuple-element.91), channel_id=1, source_target_pairs={{0,2},{1,3},{2,0},{3,1},{4,6},{5,7},{6,4},{7,5},{8,10},{9,11},{10,... | collective-permute-start | bytes 291848 | tf_op jit(solution)/shard_map/ppermute | solution.py:32
  225.9 6.4 %collective-permute-start.38 = (bf16[20,2432]{1,0:T(8,128)(2,1)S(1)}, bf16[20,2432]{1,0:T(8,128)(2,1)S(1)}, u32[]{:S(2)}, u32[]{:S(2)}) collective-permute-start(bf16[20,2432]{1,0:T(8,128)(2,1)S(1)} %get-tuple-element.92), channel_id=1, source_target_pairs={{0,1},{1,2},{2,3},{3,0},{4,5},{5,6},{6,7},{7,4},{8,9},{9,10},{10,1... | collective-permute-start | bytes 291848 | tf_op jit(solution)/shard_map/ppermute | solution.py:32
  226.6 21.2 %collective-permute-start.33 = (bf16[32,2432]{1,0:T(8,128)(2,1)S(1)}, bf16[32,2432]{1,0:T(8,128)(2,1)S(1)}, u32[]{:S(2)}, u32[]{:S(2)}) collective-permute-start(bf16[32,2432]{1,0:T(8,128)(2,1)S(1)} %get-tuple-element.85), channel_id=1, source_target_pairs={{0,3},{1,0},{2,1},{3,2},{4,7},{5,4},{6,5},{7,6},{8,11},{9,8},{10,9... | collective-permute-start | bytes 466952 | tf_op jit(solution)/shard_map/ppermute | solution.py:32
  228.6 19.1 %collective-permute-start.34 = (bf16[32,2432]{1,0:T(8,128)(2,1)S(1)}, bf16[32,2432]{1,0:T(8,128)(2,1)S(1)}, u32[]{:S(2)}, u32[]{:S(2)}) collective-permute-start(bf16[32,2432]{1,0:T(8,128)(2,1)S(1)} %get-tuple-element.86), channel_id=1, source_target_pairs={{0,2},{1,3},{2,0},{3,1},{4,6},{5,7},{6,4},{7,5},{8,10},{9,11},{10,... | collective-permute-start | bytes 466952 | tf_op jit(solution)/shard_map/ppermute | solution.py:32
  230.3 17.4 %collective-permute-start.35 = (bf16[32,2432]{1,0:T(8,128)(2,1)S(1)}, bf16[32,2432]{1,0:T(8,128)(2,1)S(1)}, u32[]{:S(2)}, u32[]{:S(2)}) collective-permute-start(bf16[32,2432]{1,0:T(8,128)(2,1)S(1)} %get-tuple-element.87), channel_id=1, source_target_pairs={{0,1},{1,2},{2,3},{3,0},{4,5},{5,6},{6,7},{7,4},{8,9},{9,10},{10,1... | collective-permute-start | bytes 466952 | tf_op jit(solution)/shard_map/ppermute | solution.py:32
  233.2 20.0 %all-to-all-start.3 = ((bf16[8,4,2432]{2,1,0:T(4,128)(2,1)}), bf16[8,4,2432]{2,1,0:T(4,128)(2,1)S(1)}, u32[]{:S(2)}, u32[]{:S(2)}) async-start(bf16[8,4,2432]{2,1,0:T(4,128)(2,1)} %reshape.26), calls=%async_computation.3 | async-start | bytes 311296 | tf_op jit(solution)/shard_map/all_to_all | solution.py:697
  (3 other events, 2.1 us)

commit v6 on v5

--- a/solution.py
+++ b/solution.py
@@ -462,7 +462,9 @@
     total = total_of((in0, in1, in2, in3))
     rows = mixed_ref[...].astype(F32) + mod_ref[5] * total
     hot = one_hot(slot_ref[:, 0:POOL], 32).astype(BF16)
-    placed_ref[...] = jnp.dot(hot, rows.astype(BF16), preferred_element_type=F32).astype(BF16)
+    placed = jnp.dot(hot, rows.astype(BF16), preferred_element_type=F32)
+    for group in range(8):
+        placed_ref[group] = placed[group * 4 : (group + 1) * 4].astype(BF16)
 
 
 def middle(parts):
@@ -548,6 +550,12 @@
         scratch=[pltpu.VMEM((32, 256), F32), pltpu.VMEM((8, 256), jnp.int32)],
     )
     arrived = lax.all_to_all(outgoing, "tp", 0, 0, tiled=True)
+    home = request // 4
+    row_index = jnp.where(
+        home == chip, 0, jnp.where(home == (chip ^ 1), 1, jnp.where(home == 3 - chip, 2, 3))
+    )
+    row_index = row_index * 4 + (request // 2 % 2 + core) % 2 * 2 + request % 2
+
     img_projected, low_part, own_image, own_mod = run(
         img_project_kernel,
         [
@@ -575,7 +583,7 @@
         ],
         flops=512 * width * 576 * 2,
         limit=56,
-        after=(outgoing,),
+        after=(outgoing, row_index),
         hbm=(2, 4, 5),
     )
     prompt_mod = run(
@@ -585,12 +593,6 @@
     mod_own = run(
         mod_pair_kernel, like((4, 8, width), F32), (prompt_mod, core_swap(prompt_mod))
     )
-    home = request // 4
-    row_index = jnp.where(
-        home == chip, 0, jnp.where(home == (chip ^ 1), 1, jnp.where(home == 3 - chip, 2, 3))
-    )
-    row_index = row_index * 4 + (request // 2 % 2 + core) % 2 * 2 + request % 2
-
     *embed_parts, slots_all = run(
         embed_kernel,
         [like((SIDE * POOL, width + EXTRA))] * SIDE + [like((1, 16 * POOL), jnp.int32)],
@@ -604,7 +606,10 @@
 
     embed_sums = exchange(middle(embed_pieces), 0)
     mod_near = run(
-        mod_pair_kernel, like((8, 8, width), F32), (mod_own, chip_swap(mod_own, False))
+        mod_pair_kernel,
+        like((8, 8, width), F32),
+        (mod_own, chip_swap(mod_own, False)),
+        after=(embed_pieces[1],),
     )
     row_mod = run(
         row_mod_kernel,
@@ -688,13 +693,13 @@
 
     placed = run(
         txt_final_kernel,
-        like((32, width)),
+        like((8, 4, width)),
         (mixed_txt, *exchange(parts[:SIDE], 0), row_mod, slots_own),
     )
     image_out = run(
         img_final_kernel, like((32, width)), (mixed_img, *exchange(parts[SIDE:], 0), own_mod)
     )
-    placed = lax.all_to_all(placed.reshape(8, 4, width), "grp", 0, 0, tiled=True)
+    placed = lax.all_to_all(placed, "grp", 0, 0, tiled=True)
     prompt_out = placed.reshape(32, width)
 
     return (image_out, prompt_out)

time: 255 us -> 261 us (1.024)
  waiting for transfers between devices: 118 us -> 128 us
    ppermute x2, waiting for transfers between devices: 0.01 us -> 7.41 us  [chip_swap(): return lax.ppermute(values, 'grp', pairs)]
  transfers between devices with their start and end apart: 42 -> 42, of which waited for: 25 -> 26; matrix products, arithmetic and copies ran while one was open for 0% -> 1% of each run, Pallas kernels for 8% -> 7%
where the time goes in v6:
time: 261 us; the launch traced here: 260 us
  waiting for transfers between devices  128 us (49%)
  starting transfers between devices  72.8 us (28%)
  Pallas kernels  34.3 us (13%)
  local copies, waits for them, and re-layouts  13.6 us (5%)
  blocking collectives  9.8 us (4%)
    ppermute x36, waiting for transfers between devices, torus_shift(): return lax.ppermute(values, ('grp', 'tp'), pairs)  110 us
    ppermute x36, starting transfers between devices, torus_shift(): return lax.ppermute(values, ('grp', 'tp'), pairs)  36.9 us
    pallas_call x23, Pallas kernels, run(): pl.pallas_call(body, out_shape=shapes, in_specs=specs, out_specs=[pl.Bloc...  34.3 us
    all_to_all x1, starting transfers between devices, shards(): placed = lax.all_to_all(placed, 'grp', 0, 0, tiled=True)  14.5 us
    unnamed x50, local copies, waits for them, and re-layouts  12.9 us
    all_to_all x1, blocking collectives, shards(): lax.all_to_all(att_parts, 'grp', 0, 0, tiled=True).reshape(512, 128)  9.8 us
    all_to_all x1, starting transfers between devices, shards(): arrived = lax.all_to_all(outgoing, 'tp', 0, 0, tiled=True)  8.6 us
    all_to_all x1, starting transfers between devices, shards(): lax.all_to_all(slot_parts.reshape(8, 64, 512), 'grp', 0, 0, tiled=True)  8.02 us
  transfers between devices with their start and end apart: 42, of which 26 were waited for; matrix products, arithmetic and copies ran while one was open for 1% of the time, Pallas kernels for 7%

profile of v6, /device:TPU:1, one launch (start us, length us, event | category | flops | bytes accessed | tf_op | source)
XLA Modules:
  0.0 260.4 jit_solution(10169794362133293036)
XLA Ops:
  0.6 0.9 copy-done.14
  2.2 0.9 shard_map.158
  3.1 8.6 %all-to-all-start = ((bf16[16,32,256]{2,1,0:T(8,128)(2,1)}), bf16[16,32,256]{2,1,0:T(8,128)(2,1)S(1)}, u32[]{:S(2)}, u32[]{:S(2)}) async-start(bf16[16,32,256]{2,1,0:T(8,128)(2,1)} %get-tuple-element.48.refs_6_.refs_1_), calls=%async_computation | async-start | bytes 524288 | tf_op jit(solution)/shard_map/all_to_all | solution.py:552
  11.7 0.9 copy-done.4
  12.7 1.0 collective-permute-start
  13.7 1.3 fusion.3.refs_7_.refs_0_
  15.0 7.8 %shard_map.159 = (f32[512,384]{1,0:T(8,128)}, bf16[16,32,192]{2,1,0:T(8,128)(2,1)}, bf16[32,2432]{1,0:T(8,128)(2,1)}, f32[6,2432]{1,0:T(8,128)}) custom-call(s32[2]{0:T(128)} %refs_0_.5, s32[1]{0:T(128)} %bitcast.refs_1_, bf16[512,2432]{1,0:T(8,128)(2,1)} %refs_2_.4, f32[2,6,2,2432]{3,2,1,0:T(2,128)} %bitcast.33, bf16[3,2432,128]{2,1,0:T(8,128)(2,1)} %bitcast.38, ...), custom_call_target="tpu_custom_call" | custom-call | flops 1434451968 | bytes 7656460 | tf_op jit(solution)/shard_map/pallas_call | solution.py:80
  23.0 0.9 copy-done.13
  23.9 1.4 shard_map.162
  25.4 2.9 %collective-permute-start.1 = (bf16[80,2944]{1,0:T(8,128)(2,1)S(1)}, bf16[80,2944]{1,0:T(8,128)(2,1)S(1)}, u32[]{:S(2)}, u32[]{:S(2)}) collective-permute-start(bf16[80,2944]{1,0:T(8,128)(2,1)S(1)} %get-tuple-element.52), channel_id=1, source_target_pairs={{0,12},{1,13},{2,14},{3,15},{4,0},{5,1},{6,2},{7,3},{8,4},{9,5},{1... | collective-permute-start | bytes 1413128 | tf_op jit(solution)/shard_map/ppermute | solution.py:32
  28.3 1.2 collective-permute-start.7
  29.5 7.4 %collective-permute-done.7.refs_1_ = f32[4,8,2432]{2,1,0:T(8,128)S(1)} collective-permute-done((f32[4,8,2432]{2,1,0:T(8,128)S(1)}, f32[4,8,2432]{2,1,0:T(8,128)S(1)}, u32[]{:S(2)}, u32[]{:S(2)}) %collective-permute-start.7) | collective-permute-done | bytes 311328 | tf_op jit(solution)/shard_map/ppermute | solution.py:44
  36.9 2.6 collective-permute-start.8
  40.1 8.7 %collective-permute-done.2.refs_2_ = bf16[80,2944]{1,0:T(8,128)(2,1)S(1)} collective-permute-done((bf16[80,2944]{1,0:T(8,128)(2,1)S(1)}, bf16[80,2944]{1,0:T(8,128)(2,1)S(1)}, u32[]{:S(2)}, u32[]{:S(2)}) %collective-permute-start.2) | collective-permute-done | bytes 471072 | tf_op jit(solution)/shard_map/ppermute | solution.py:32
  48.8 4.7 %collective-permute-done.3.refs_3_ = bf16[80,2944]{1,0:T(8,128)(2,1)S(1)} collective-permute-done((bf16[80,2944]{1,0:T(8,128)(2,1)S(1)}, bf16[80,2944]{1,0:T(8,128)(2,1)S(1)}, u32[]{:S(2)}, u32[]{:S(2)}) %collective-permute-start.3) | collective-permute-done | bytes 471072 | tf_op jit(solution)/shard_map/ppermute | solution.py:32
  54.0 2.2 collective-permute-start.4
  57.1 1.0 shard_map.165.refs_4_.refs_7_.refs_5_
  58.1 1.7 collective-permute-done.4.refs_1_
  59.7 2.0 collective-permute-done.5.refs_2_
  61.7 1.5 collective-permute-done.6.refs_3_
  63.6 1.7 collective-permute-start.10
  65.3 1.0 collective-permute-start.9
  66.3 4.3 %collective-permute-done.11.refs_3_ = bf16[20,2944]{1,0:T(8,128)(2,1)S(1)} collective-permute-done((bf16[20,2944]{1,0:T(8,128)(2,1)S(1)}, bf16[20,2944]{1,0:T(8,128)(2,1)S(1)}, u32[]{:S(2)}, u32[]{:S(2)}) %collective-permute-start.11) | collective-permute-done | bytes 117792 | tf_op jit(solution)/shard_map/ppermute | solution.py:32
  71.4 1.2 collective-permute-start.13
  72.6 1.5 collective-permute-start.12
  74.1 11.3 %collective-permute-done.14.refs_4_ = bf16[80,2944]{1,0:T(8,128)(2,1)S(1)} collective-permute-done((bf16[80,2944]{1,0:T(8,128)(2,1)S(1)}, bf16[80,2944]{1,0:T(8,128)(2,1)S(1)}, u32[]{:S(2)}, u32[]{:S(2)}) %collective-permute-start.14) | collective-permute-done | bytes 471072 | tf_op jit(solution)/shard_map/ppermute | solution.py:32
  86.0 2.2 shard_map.168
  89.8 8.0 %all-to-all-start.1 = ((bf16[8,64,512]{2,1,0:T(8,128)(2,1)}), bf16[8,64,512]{2,1,0:T(8,128)(2,1)S(1)}, u32[]{:S(2)}, u32[]{:S(2)}) async-start(bf16[8,64,512]{2,1,0:T(8,128)(2,1)} %bitcast.36), calls=%async_computation.1 | async-start | bytes 1048576 | tf_op jit(solution)/shard_map/all_to_all | solution.py:649
  97.9 1.1 copy-done.5
  99.0 1.0 copy-done.9
  100.1 1.5 shard_map.169.refs_1_
  102.4 5.0 %all-to-all-done.1.refs_2_ = bf16[8,64,512]{2,1,0:T(8,128)(2,1)S(1)} async-done(((bf16[8,64,512]{2,1,0:T(8,128)(2,1)}), bf16[8,64,512]{2,1,0:T(8,128)(2,1)S(1)}, u32[]{:S(2)}, u32[]{:S(2)}) %all-to-all-start.1) | async-done | bytes 524320 | tf_op jit(solution)/shard_map/all_to_all | solution.py:649
  107.4 1.0 copy-done.11
  108.4 1.1 copy-done.21
  109.5 2.5 shard_map.170
  112.0 2.1 collective-permute-start.15
  114.8 1.1 shard_map.171
  115.9 9.8 %all_to_all.20 = bf16[8,64,128]{2,1,0:T(8,128)(2,1)S(1)} all-to-all(bf16[8,64,128]{2,1,0:T(8,128)(2,1)S(1)} %shard_map.171), channel_id=1, replica_groups=mesh['grp'=8,'tp'=16] {'grp'}, dimensions={0} | all-to-all | bytes 262144 | tf_op jit(solution)/shard_map/all_to_all | solution.py:666
  125.7 2.2 collective-permute-done.15.refs_3_.refs_1_
  128.0 0.9 shard_map.172
  128.9 3.5 %collective-permute-start.18 = (bf16[80,2432]{1,0:T(8,128)(2,1)S(1)}, bf16[80,2432]{1,0:T(8,128)(2,1)S(1)}, u32[]{:S(2)}, u32[]{:S(2)}) collective-permute-start(bf16[80,2432]{1,0:T(8,128)(2,1)S(1)} %get-tuple-element.71), channel_id=1, source_target_pairs={{0,12},{1,13},{2,14},{3,15},{4,0},{5,1},{6,2},{7,3},{8,4},{9,5},{1... | collective-permute-start | bytes 1167368 | tf_op jit(solution)/shard_map/ppermute | solution.py:32
  133.0 8.2 %collective-permute-done.18.refs_5_ = bf16[80,2432]{1,0:T(8,128)(2,1)S(1)} collective-permute-done((bf16[80,2432]{1,0:T(8,128)(2,1)S(1)}, bf16[80,2432]{1,0:T(8,128)(2,1)S(1)}, u32[]{:S(2)}, u32[]{:S(2)}) %collective-permute-start.18) | collective-permute-done | bytes 389152 | tf_op jit(solution)/shard_map/ppermute | solution.py:32
  141.2 3.4 %collective-permute-done.20.refs_7_ = bf16[80,2432]{1,0:T(8,128)(2,1)S(1)} collective-permute-done((bf16[80,2432]{1,0:T(8,128)(2,1)S(1)}, bf16[80,2432]{1,0:T(8,128)(2,1)S(1)}, u32[]{:S(2)}, u32[]{:S(2)}) %collective-permute-start.20) | collective-permute-done | bytes 389152 | tf_op jit(solution)/shard_map/ppermute | solution.py:32
  145.5 2.4 collective-permute-start.21
  148.6 5.7 %collective-permute-done.21.refs_3_ = bf16[52,2432]{1,0:T(8,128)(2,1)S(1)} collective-permute-done((bf16[52,2432]{1,0:T(8,128)(2,1)S(1)}, bf16[52,2432]{1,0:T(8,128)(2,1)S(1)}, u32[]{:S(2)}, u32[]{:S(2)}) %collective-permute-start.21) | collective-permute-done | bytes 252960 | tf_op jit(solution)/shard_map/ppermute | solution.py:32
  154.9 2.9 %collective-permute-done.23.refs_5_ = bf16[52,2432]{1,0:T(8,128)(2,1)S(1)} collective-permute-done((bf16[52,2432]{1,0:T(8,128)(2,1)S(1)}, bf16[52,2432]{1,0:T(8,128)(2,1)S(1)}, u32[]{:S(2)}, u32[]{:S(2)}) %collective-permute-start.23) | collective-permute-done | bytes 252960 | tf_op jit(solution)/shard_map/ppermute | solution.py:32
  158.4 1.7 collective-permute-start.25
  160.1 1.0 collective-permute-start.24
  161.1 7.1 %collective-permute-done.26.refs_3_ = bf16[52,2432]{1,0:T(8,128)(2,1)S(1)} collective-permute-done((bf16[52,2432]{1,0:T(8,128)(2,1)S(1)}, bf16[52,2432]{1,0:T(8,128)(2,1)S(1)}, u32[]{:S(2)}, u32[]{:S(2)}) %collective-permute-start.26) | collective-permute-done | bytes 252960 | tf_op jit(solution)/shard_map/ppermute | solution.py:32
  169.0 1.7 collective-permute-start.28
  170.7 1.0 collective-permute-start.27
  171.7 2.7 %copy-done = bf16[2,608,2432]{2,1,0:T(8,128)(2,1)S(1)} copy-done((bf16[2,608,2432]{2,1,0:T(8,128)(2,1)S(1)}, bf16[2,608,2432]{2,1,0:T(8,128)(2,1)}, u32[]{:S(2)}) %copy-start) | copy-done | bytes 5914648
  174.4 3.4 %shard_map.176.refs_5_.refs_0_ = bf16[208,2432]{1,0:T(8,128)(2,1)S(1)} custom-call(bf16[208,2432]{1,0:T(8,128)(2,1)S(1)} %shard_map.175.refs_0_, bf16[2,608,2432]{2,1,0:T(8,128)(2,1)S(1)} %bitcast.30, bf16[2,608,2432]{2,1,0:T(8,128)(2,1)S(1)} %copy-done), custom_call_target="tpu_custom_call" | custom-call | flops 1230241792 | bytes 13852672 | tf_op jit(solution)/shard_map/pallas_call | solution.py:80
  177.8 16.9 %collective-permute-done.29.refs_2_ = bf16[208,2432]{1,0:T(8,128)(2,1)S(1)} collective-permute-done((bf16[208,2432]{1,0:T(8,128)(2,1)S(1)}, bf16[208,2432]{1,0:T(8,128)(2,1)S(1)}, u32[]{:S(2)}, u32[]{:S(2)}) %collective-permute-start.29) | collective-permute-done | bytes 1011744 | tf_op jit(solution)/shard_map/ppermute | solution.py:32
  195.3 6.4 %shard_map.177 = (bf16[208,2432]{1,0:T(8,128)(2,1)S(1)}, bf16[208,2432]{1,0:T(8,128)(2,1)S(1)}, bf16[208,2432]{1,0:T(8,128)(2,1)S(1)}) custom-call(bf16[208,2432]{1,0:T(8,128)(2,1)S(1)} %collective-permute-done.27.refs_0_, bf16[208,2432]{1,0:T(8,128)(2,1)S(1)} %collective-permute-done.28.refs_1_, bf16[208,2432]{1,0:T(8,128)(2,1)S(1)} %collective-permute-done.29.refs_2_, ...), custom_call_target="tpu_custom_call" | custom-call | flops 3690725376 | bytes 17899520 | tf_op jit(solution)/shard_map/pallas_call | solution.py:80
  201.8 2.1 collective-permute-start.30
  204.5 21.5 %collective-permute-done.30.refs_1_ = bf16[208,2432]{1,0:T(8,128)(2,1)S(1)} collective-permute-done((bf16[208,2432]{1,0:T(8,128)(2,1)S(1)}, bf16[208,2432]{1,0:T(8,128)(2,1)S(1)}, u32[]{:S(2)}, u32[]{:S(2)}) %collective-permute-start.30) | collective-permute-done | bytes 1011744 | tf_op jit(solution)/shard_map/ppermute | solution.py:32
  226.1 3.4 %collective-permute-done.32.refs_3_ = bf16[208,2432]{1,0:T(8,128)(2,1)S(1)} collective-permute-done((bf16[208,2432]{1,0:T(8,128)(2,1)S(1)}, bf16[208,2432]{1,0:T(8,128)(2,1)S(1)}, u32[]{:S(2)}, u32[]{:S(2)}) %collective-permute-start.32) | collective-permute-done | bytes 1011744 | tf_op jit(solution)/shard_map/ppermute | solution.py:32
  230.3 2.1 collective-permute-start.36
  233.1 2.0 collective-permute-start.33
  235.1 1.8 collective-permute-start.34
  236.9 1.0 collective-permute-done.37.refs_3_
  239.6 14.5 %all-to-all-start.3 = ((bf16[8,4,2432]{2,1,0:T(4,128)(2,1)}), bf16[8,4,2432]{2,1,0:T(4,128)(2,1)S(1)}, u32[]{:S(2)}, u32[]{:S(2)}) async-start(bf16[8,4,2432]{2,1,0:T(4,128)(2,1)} %shard_map.180), calls=%async_computation.3 | async-start | bytes 311296 | tf_op jit(solution)/shard_map/all_to_all | solution.py:702
  254.9 4.7 %all-to-all-done.3 = bf16[8,4,2432]{2,1,0:T(4,128)(2,1)S(1)} async-done(((bf16[8,4,2432]{2,1,0:T(4,128)(2,1)}), bf16[8,4,2432]{2,1,0:T(4,128)(2,1)S(1)}, u32[]{:S(2)}, u32[]{:S(2)}) %all-to-all-start.3) | async-done | bytes 155680 | tf_op jit(solution)/shard_map/all_to_all | solution.py:702
  (99 shorter events, 18.1 us)
Async XLA Ops:
  0.6 0.9 copy-start.14
  3.1 19.8 %all-to-all-start = ((bf16[16,32,256]{2,1,0:T(8,128)(2,1)}), bf16[16,32,256]{2,1,0:T(8,128)(2,1)S(1)}, u32[]{:S(2)}, u32[]{:S(2)}) async-start(bf16[16,32,256]{2,1,0:T(8,128)(2,1)} %get-tuple-element.48.refs_6_.refs_1_), calls=%async_computation | async-start | bytes 524288 | tf_op jit(solution)/shard_map/all_to_all | solution.py:552
  11.7 0.9 copy-start.4
  12.7 10.2 %collective-permute-start = (f32[2,8,2432]{2,1,0:T(8,128)S(1)}, f32[2,8,2432]{2,1,0:T(8,128)S(1)}, u32[]{:S(2)}, u32[]{:S(2)}) collective-permute-start(f32[2,8,2432]{2,1,0:T(8,128)S(1)} %shard_map.160.refs_0_), channel_id=1, source_target_pairs={{0,16},{16,0},{32,48},{48,32},{64,80},{80,64},{96,112},{112,96},{1... | collective-permute-start | bytes 466952 | tf_op jit(solution)/shard_map/ppermute | solution.py:36
  15.0 7.9 %copy-start.3 = (bf16[256,2432]{1,0:T(8,128)(2,1)S(1)}, bf16[256,2432]{1,0:T(8,128)(2,1)}, u32[]{:S(2)}) copy-start(bf16[256,2432]{1,0:T(8,128)(2,1)} %refs_2_.5) | copy-start | bytes 3735556
  22.9 1.0 copy-start.13
  25.3 31.7 %copy-start.18 = (s32[20]{0:T(128)S(1)}, s32[20]{0:T(128)}, u32[]{:S(2)}) copy-start(s32[20]{0:T(128)} %fusion.3.refs_7_.refs_0_) | copy-start | bytes 244
  25.4 11.5 %collective-permute-start.1 = (bf16[80,2944]{1,0:T(8,128)(2,1)S(1)}, bf16[80,2944]{1,0:T(8,128)(2,1)S(1)}, u32[]{:S(2)}, u32[]{:S(2)}) collective-permute-start(bf16[80,2944]{1,0:T(8,128)(2,1)S(1)} %get-tuple-element.52), channel_id=1, source_target_pairs={{0,12},{1,13},{2,14},{3,15},{4,0},{5,1},{6,2},{7,3},{8,4},{9,5},{1... | collective-permute-start | bytes 1413128 | tf_op jit(solution)/shard_map/ppermute | solution.py:32
  28.3 8.6 %collective-permute-start.7 = (f32[4,8,2432]{2,1,0:T(8,128)S(1)}, f32[4,8,2432]{2,1,0:T(8,128)S(1)}, u32[]{:S(2)}, u32[]{:S(2)}) collective-permute-start(f32[4,8,2432]{2,1,0:T(8,128)S(1)} %shard_map.161.refs_4_.refs_0_), channel_id=1, source_target_pairs={{0,32},{16,48},{32,0},{48,16},{64,96},{80,112},{96,64},{112,80},{1... | collective-permute-start | bytes 933896 | tf_op jit(solution)/shard_map/ppermute | solution.py:44
  36.9 20.1 %collective-permute-start.8 = (f32[8,8,2432]{2,1,0:T(8,128)S(1)}, f32[8,8,2432]{2,1,0:T(8,128)S(1)}, u32[]{:S(2)}, u32[]{:S(2)}) collective-permute-start(f32[8,8,2432]{2,1,0:T(8,128)S(1)} %shard_map.164.refs_1_), channel_id=1, source_target_pairs={{0,96},{16,112},{32,64},{48,80},{64,32},{80,48},{96,0},{112,16},{1... | collective-permute-start | bytes 1867784 | tf_op jit(solution)/shard_map/ppermute | solution.py:44
  39.5 9.3 %collective-permute-start.2 = (bf16[80,2944]{1,0:T(8,128)(2,1)S(1)}, bf16[80,2944]{1,0:T(8,128)(2,1)S(1)}, u32[]{:S(2)}, u32[]{:S(2)}) collective-permute-start(bf16[80,2944]{1,0:T(8,128)(2,1)S(1)} %get-tuple-element.53), channel_id=1, source_target_pairs={{0,8},{1,9},{2,10},{3,11},{4,12},{5,13},{6,14},{7,15},{8,0},{9,1},... | collective-permute-start | bytes 1413128 | tf_op jit(solution)/shard_map/ppermute | solution.py:32
  39.5 14.0 %collective-permute-start.3 = (bf16[80,2944]{1,0:T(8,128)(2,1)S(1)}, bf16[80,2944]{1,0:T(8,128)(2,1)S(1)}, u32[]{:S(2)}, u32[]{:S(2)}) collective-permute-start(bf16[80,2944]{1,0:T(8,128)(2,1)S(1)} %get-tuple-element.54), channel_id=1, source_target_pairs={{0,4},{1,5},{2,6},{3,7},{4,8},{5,9},{6,10},{7,11},{8,12},{9,13},{1... | collective-permute-start | bytes 1413128 | tf_op jit(solution)/shard_map/ppermute | solution.py:32
  54.0 5.7 %collective-permute-start.4 = (bf16[20,2944]{1,0:T(8,128)(2,1)S(1)}, bf16[20,2944]{1,0:T(8,128)(2,1)S(1)}, u32[]{:S(2)}, u32[]{:S(2)}) collective-permute-start(bf16[20,2944]{1,0:T(8,128)(2,1)S(1)} %get-tuple-element.56), channel_id=1, source_target_pairs={{0,3},{1,0},{2,1},{3,2},{4,7},{5,4},{6,5},{7,6},{8,11},{9,8},{10,9... | collective-permute-start | bytes 353288 | tf_op jit(solution)/shard_map/ppermute | solution.py:32
  56.2 5.5 %collective-permute-start.5 = (bf16[20,2944]{1,0:T(8,128)(2,1)S(1)}, bf16[20,2944]{1,0:T(8,128)(2,1)S(1)}, u32[]{:S(2)}, u32[]{:S(2)}) collective-permute-start(bf16[20,2944]{1,0:T(8,128)(2,1)S(1)} %get-tuple-element.57), channel_id=1, source_target_pairs={{0,2},{1,3},{2,0},{3,1},{4,6},{5,7},{6,4},{7,5},{8,10},{9,11},{10,... | collective-permute-start | bytes 353288 | tf_op jit(solution)/shard_map/ppermute | solution.py:32
  56.3 6.9 %collective-permute-start.6 = (bf16[20,2944]{1,0:T(8,128)(2,1)S(1)}, bf16[20,2944]{1,0:T(8,128)(2,1)S(1)}, u32[]{:S(2)}, u32[]{:S(2)}) collective-permute-start(bf16[20,2944]{1,0:T(8,128)(2,1)S(1)} %get-tuple-element.58), channel_id=1, source_target_pairs={{0,1},{1,2},{2,3},{3,0},{4,5},{5,6},{6,7},{7,4},{8,9},{9,10},{10,1... | collective-permute-start | bytes 353288 | tf_op jit(solution)/shard_map/ppermute | solution.py:32
  58.0 16.0 %copy-start.22 = (f32[2,2,64]{2,1,0:T(2,128)S(1)}, f32[2,2,64]{2,1,0:T(2,128)}, u32[]{:S(2)}) copy-start(f32[2,2,64]{2,1,0:T(2,128)} %param.20) | copy-start | bytes 3076
  58.1 28.0 %copy-start.1 = (bf16[2432,3,128]{2,0,1:T(8,128)(2,1)S(1)}, bf16[2432,3,128]{2,0,1:T(8,128)(2,1)}, u32[]{:S(2)}) copy-start(bf16[2432,3,128]{2,0,1:T(8,128)(2,1)} %param.23) | copy-start | bytes 5603332
  63.5 7.8 %copy-start.16 = (bf16[20,2432]{1,0:T(8,128)(2,1)}, bf16[20,2432]{1,0:T(8,128)(2,1)S(1)}, u32[]{:S(2)}) copy-start(bf16[20,2432]{1,0:T(8,128)(2,1)S(1)} %get-tuple-element.59.refs_1_) | copy-start | bytes 291844
  63.6 7.0 %collective-permute-start.11 = (bf16[20,2944]{1,0:T(8,128)(2,1)S(1)}, bf16[20,2944]{1,0:T(8,128)(2,1)S(1)}, u32[]{:S(2)}, u32[]{:S(2)}) collective-permute-start(bf16[20,2944]{1,0:T(8,128)(2,1)S(1)} %get-tuple-element.60.refs_0_), channel_id=1, source_target_pairs={{0,1},{1,2},{2,3},{3,0},{4,5},{5,6},{6,7},{7,4},{8,9},{9,10},{10,1... | collective-permute-start | bytes 353288 | tf_op jit(solution)/shard_map/ppermute | solution.py:32
  63.6 6.9 %collective-permute-start.10 = (bf16[20,2944]{1,0:T(8,128)(2,1)S(1)}, bf16[20,2944]{1,0:T(8,128)(2,1)S(1)}, u32[]{:S(2)}, u32[]{:S(2)}) collective-permute-start(bf16[20,2944]{1,0:T(8,128)(2,1)S(1)} %get-tuple-element.60.refs_0_), channel_id=1, source_target_pairs={{0,2},{1,3},{2,0},{3,1},{4,6},{5,7},{6,4},{7,5},{8,10},{9,11},{10,... | collective-permute-start | bytes 353288 | tf_op jit(solution)/shard_map/ppermute | solution.py:32
  65.3 5.9 %collective-permute-start.9 = (bf16[20,2944]{1,0:T(8,128)(2,1)S(1)}, bf16[20,2944]{1,0:T(8,128)(2,1)S(1)}, u32[]{:S(2)}, u32[]{:S(2)}) collective-permute-start(bf16[20,2944]{1,0:T(8,128)(2,1)S(1)} %get-tuple-element.60.refs_0_), channel_id=1, source_target_pairs={{0,3},{1,0},{2,1},{3,2},{4,7},{5,4},{6,5},{7,6},{8,11},{9,8},{10,9... | collective-permute-start | bytes 353288 | tf_op jit(solution)/shard_map/ppermute | solution.py:32
  71.3 14.1 %collective-permute-start.14 = (bf16[80,2944]{1,0:T(8,128)(2,1)S(1)}, bf16[80,2944]{1,0:T(8,128)(2,1)S(1)}, u32[]{:S(2)}, u32[]{:S(2)}) collective-permute-start(bf16[80,2944]{1,0:T(8,128)(2,1)S(1)} %shard_map.167.refs_1_), channel_id=1, source_target_pairs={{0,4},{1,5},{2,6},{3,7},{4,8},{5,9},{6,10},{7,11},{8,12},{9,13},{1... | collective-permute-start | bytes 1413128 | tf_op jit(solution)/shard_map/ppermute | solution.py:32
  71.4 14.0 %collective-permute-start.13 = (bf16[80,2944]{1,0:T(8,128)(2,1)S(1)}, bf16[80,2944]{1,0:T(8,128)(2,1)S(1)}, u32[]{:S(2)}, u32[]{:S(2)}) collective-permute-start(bf16[80,2944]{1,0:T(8,128)(2,1)S(1)} %shard_map.167.refs_1_), channel_id=1, source_target_pairs={{0,8},{1,9},{2,10},{3,11},{4,12},{5,13},{6,14},{7,15},{8,0},{9,1},... | collective-permute-start | bytes 1413128 | tf_op jit(solution)/shard_map/ppermute | solution.py:32
  72.6 13.4 %collective-permute-start.12 = (bf16[80,2944]{1,0:T(8,128)(2,1)S(1)}, bf16[80,2944]{1,0:T(8,128)(2,1)S(1)}, u32[]{:S(2)}, u32[]{:S(2)}) collective-permute-start(bf16[80,2944]{1,0:T(8,128)(2,1)S(1)} %shard_map.167.refs_1_), channel_id=1, source_target_pairs={{0,12},{1,13},{2,14},{3,15},{4,0},{5,1},{6,2},{7,3},{8,4},{9,5},{1... | collective-permute-start | bytes 1413128 | tf_op jit(solution)/shard_map/ppermute | solution.py:32
  86.0 11.9 %copy-start.2 = (bf16[32,3,64,128]{3,2,1,0:T(8,128)(2,1)S(1)}, bf16[32,3,64,128]{3,2,1,0:T(8,128)(2,1)}, u32[]{:S(2)}) copy-start(bf16[32,3,64,128]{3,2,1,0:T(8,128)(2,1)} %refs_3_.2) | copy-start | bytes 4718596
  86.0 11.9 %copy-start.20 = (s32[2]{0:T(128)S(1)}, s32[2]{0:T(128)}, u32[]{:S(2)}) copy-start(s32[2]{0:T(128)} %refs_0_.5) | copy-start | bytes 28
  89.8 17.5 %all-to-all-start.1 = ((bf16[8,64,512]{2,1,0:T(8,128)(2,1)}), bf16[8,64,512]{2,1,0:T(8,128)(2,1)S(1)}, u32[]{:S(2)}, u32[]{:S(2)}) async-start(bf16[8,64,512]{2,1,0:T(8,128)(2,1)} %bitcast.36), calls=%async_computation.1 | async-start | bytes 1048576 | tf_op jit(solution)/shard_map/all_to_all | solution.py:649
  97.9 1.1 copy-start.5
  99.0 1.0 copy-start.9
  101.6 0.8 copy-start.10
  107.4 1.0 copy-start.11
  108.4 1.1 copy-start.21
  112.0 16.0 %copy-start.6 = (bf16[128,2432]{1,0:T(8,128)(2,1)S(1)}, bf16[128,2432]{1,0:T(8,128)(2,1)}, u32[]{:S(2)}) copy-start(bf16[128,2432]{1,0:T(8,128)(2,1)} %refs_2_.6) | copy-start | bytes 1867780
  112.0 16.0 %collective-permute-start.15 = (bf16[128,2432]{1,0:T(8,128)(2,1)S(1)}, bf16[128,2432]{1,0:T(8,128)(2,1)S(1)}, u32[]{:S(2)}, u32[]{:S(2)}) collective-permute-start(bf16[128,2432]{1,0:T(8,128)(2,1)S(1)} %get-tuple-element.66), channel_id=1, source_target_pairs={{0,12},{1,13},{2,14},{3,15},{4,0},{5,1},{6,2},{7,3},{8,4},{9,5},{1... | collective-permute-start | bytes 1867784 | tf_op jit(solution)/shard_map/ppermute | solution.py:32
  114.1 18.9 %collective-permute-start.16 = (bf16[128,2432]{1,0:T(8,128)(2,1)S(1)}, bf16[128,2432]{1,0:T(8,128)(2,1)S(1)}, u32[]{:S(2)}, u32[]{:S(2)}) collective-permute-start(bf16[128,2432]{1,0:T(8,128)(2,1)S(1)} %get-tuple-element.67), channel_id=1, source_target_pairs={{0,8},{1,9},{2,10},{3,11},{4,12},{5,13},{6,14},{7,15},{8,0},{9,1},... | collective-permute-start | bytes 1867784 | tf_op jit(solution)/shard_map/ppermute | solution.py:32
  114.1 18.9 %collective-permute-start.17 = (bf16[128,2432]{1,0:T(8,128)(2,1)S(1)}, bf16[128,2432]{1,0:T(8,128)(2,1)S(1)}, u32[]{:S(2)}, u32[]{:S(2)}) collective-permute-start(bf16[128,2432]{1,0:T(8,128)(2,1)S(1)} %get-tuple-element.68), channel_id=1, source_target_pairs={{0,4},{1,5},{2,6},{3,7},{4,8},{5,9},{6,10},{7,11},{8,12},{9,13},{1... | collective-permute-start | bytes 1867784 | tf_op jit(solution)/shard_map/ppermute | solution.py:32
  114.8 56.9 %slice-start = ((s8[5914624]{0:T(1024)(128)(4,1)}), s8[4194304]{0:T(1024)(128)(4,1)S(1)}, s32[]{:S(2)}) async-start(s8[5914624]{0:T(1024)(128)(4,1)} %bitcast.28), calls=%async_computation.4 | async-start | bytes 8388608
  128.9 12.3 %collective-permute-start.18 = (bf16[80,2432]{1,0:T(8,128)(2,1)S(1)}, bf16[80,2432]{1,0:T(8,128)(2,1)S(1)}, u32[]{:S(2)}, u32[]{:S(2)}) collective-permute-start(bf16[80,2432]{1,0:T(8,128)(2,1)S(1)} %get-tuple-element.71), channel_id=1, source_target_pairs={{0,12},{1,13},{2,14},{3,15},{4,0},{5,1},{6,2},{7,3},{8,4},{9,5},{1... | collective-permute-start | bytes 1167368 | tf_op jit(solution)/shard_map/ppermute | solution.py:32
  132.4 8.8 %collective-permute-start.19 = (bf16[80,2432]{1,0:T(8,128)(2,1)S(1)}, bf16[80,2432]{1,0:T(8,128)(2,1)S(1)}, u32[]{:S(2)}, u32[]{:S(2)}) collective-permute-start(bf16[80,2432]{1,0:T(8,128)(2,1)S(1)} %get-tuple-element.72), channel_id=1, source_target_pairs={{0,8},{1,9},{2,10},{3,11},{4,12},{5,13},{6,14},{7,15},{8,0},{9,1},... | collective-permute-start | bytes 1167368 | tf_op jit(solution)/shard_map/ppermute | solution.py:32
  132.4 12.3 %collective-permute-start.20 = (bf16[80,2432]{1,0:T(8,128)(2,1)S(1)}, bf16[80,2432]{1,0:T(8,128)(2,1)S(1)}, u32[]{:S(2)}, u32[]{:S(2)}) collective-permute-start(bf16[80,2432]{1,0:T(8,128)(2,1)S(1)} %get-tuple-element.73), channel_id=1, source_target_pairs={{0,4},{1,5},{2,6},{3,7},{4,8},{5,9},{6,10},{7,11},{8,12},{9,13},{1... | collective-permute-start | bytes 1167368 | tf_op jit(solution)/shard_map/ppermute | solution.py:32
  144.6 13.2 %copy-start.12 = (f32[6,2432]{1,0:T(8,128)S(1)}, f32[6,2432]{1,0:T(8,128)}, u32[]{:S(2)}) copy-start(f32[6,2432]{1,0:T(8,128)} %get-tuple-element.78.refs_6_.refs_5_) | copy-start | bytes 175108
  144.6 13.2 %copy-start.15 = (bf16[32,2432]{1,0:T(8,128)(2,1)S(1)}, bf16[32,2432]{1,0:T(8,128)(2,1)}, u32[]{:S(2)}) copy-start(bf16[32,2432]{1,0:T(8,128)(2,1)} %get-tuple-element.49.refs_0_) | copy-start | bytes 466948
  144.6 13.2 %copy-start.17 = (bf16[20,2432]{1,0:T(8,128)(2,1)S(1)}, bf16[20,2432]{1,0:T(8,128)(2,1)}, u32[]{:S(2)}) copy-start(bf16[20,2432]{1,0:T(8,128)(2,1)} %copy-done.16) | copy-start | bytes 291844
  144.6 27.1 %slice-start.1 = ((s8[5914624]{0:T(1024)(128)(4,1)}), s8[1720320]{0:T(1024)(128)(4,1)S(1)}, s32[]{:S(2)}) async-start(s8[5914624]{0:T(1024)(128)(4,1)} %bitcast.28), calls=%async_computation.5 | async-start | bytes 3440640
  145.5 8.8 %collective-permute-start.21 = (bf16[52,2432]{1,0:T(8,128)(2,1)S(1)}, bf16[52,2432]{1,0:T(8,128)(2,1)S(1)}, u32[]{:S(2)}, u32[]{:S(2)}) collective-permute-start(bf16[52,2432]{1,0:T(8,128)(2,1)S(1)} %get-tuple-element.75), channel_id=1, source_target_pairs={{0,3},{1,0},{2,1},{3,2},{4,7},{5,4},{6,5},{7,6},{8,11},{9,8},{10,9... | collective-permute-start | bytes 758792 | tf_op jit(solution)/shard_map/ppermute | solution.py:32
  147.9 6.9 %collective-permute-start.22 = (bf16[52,2432]{1,0:T(8,128)(2,1)S(1)}, bf16[52,2432]{1,0:T(8,128)(2,1)S(1)}, u32[]{:S(2)}, u32[]{:S(2)}) collective-permute-start(bf16[52,2432]{1,0:T(8,128)(2,1)S(1)} %get-tuple-element.76), channel_id=1, source_target_pairs={{0,2},{1,3},{2,0},{3,1},{4,6},{5,7},{6,4},{7,5},{8,10},{9,11},{10,... | collective-permute-start | bytes 758792 | tf_op jit(solution)/shard_map/ppermute | solution.py:32
  148.1 9.8 %collective-permute-start.23 = (bf16[52,2432]{1,0:T(8,128)(2,1)S(1)}, bf16[52,2432]{1,0:T(8,128)(2,1)S(1)}, u32[]{:S(2)}, u32[]{:S(2)}) collective-permute-start(bf16[52,2432]{1,0:T(8,128)(2,1)S(1)} %get-tuple-element.77), channel_id=1, source_target_pairs={{0,1},{1,2},{2,3},{3,0},{4,5},{5,6},{6,7},{7,4},{8,9},{9,10},{10,1... | collective-permute-start | bytes 758792 | tf_op jit(solution)/shard_map/ppermute | solution.py:32
  158.4 9.8 %collective-permute-start.26 = (bf16[52,2432]{1,0:T(8,128)(2,1)S(1)}, bf16[52,2432]{1,0:T(8,128)(2,1)S(1)}, u32[]{:S(2)}, u32[]{:S(2)}) collective-permute-start(bf16[52,2432]{1,0:T(8,128)(2,1)S(1)} %get-tuple-element.80.refs_0_), channel_id=1, source_target_pairs={{0,1},{1,2},{2,3},{3,0},{4,5},{5,6},{6,7},{7,4},{8,9},{9,10},{10,1... | collective-permute-start | bytes 758792 | tf_op jit(solution)/shard_map/ppermute | solution.py:32
  158.4 9.7 %collective-permute-start.25 = (bf16[52,2432]{1,0:T(8,128)(2,1)S(1)}, bf16[52,2432]{1,0:T(8,128)(2,1)S(1)}, u32[]{:S(2)}, u32[]{:S(2)}) collective-permute-start(bf16[52,2432]{1,0:T(8,128)(2,1)S(1)} %get-tuple-element.80.refs_0_), channel_id=1, source_target_pairs={{0,2},{1,3},{2,0},{3,1},{4,6},{5,7},{6,4},{7,5},{8,10},{9,11},{10,... | collective-permute-start | bytes 758792 | tf_op jit(solution)/shard_map/ppermute | solution.py:32
  160.1 8.7 %collective-permute-start.24 = (bf16[52,2432]{1,0:T(8,128)(2,1)S(1)}, bf16[52,2432]{1,0:T(8,128)(2,1)S(1)}, u32[]{:S(2)}, u32[]{:S(2)}) collective-permute-start(bf16[52,2432]{1,0:T(8,128)(2,1)S(1)} %get-tuple-element.80.refs_0_), channel_id=1, source_target_pairs={{0,3},{1,0},{2,1},{3,2},{4,7},{5,4},{6,5},{7,6},{8,11},{9,8},{10,9... | collective-permute-start | bytes 758792 | tf_op jit(solution)/shard_map/ppermute | solution.py:32
  168.9 25.7 %collective-permute-start.29 = (bf16[208,2432]{1,0:T(8,128)(2,1)S(1)}, bf16[208,2432]{1,0:T(8,128)(2,1)S(1)}, u32[]{:S(2)}, u32[]{:S(2)}) collective-permute-start(bf16[208,2432]{1,0:T(8,128)(2,1)S(1)} %shard_map.175.refs_0_), channel_id=1, source_target_pairs={{0,4},{1,5},{2,6},{3,7},{4,8},{5,9},{6,10},{7,11},{8,12},{9,13},{1... | collective-permute-start | bytes 3035144 | tf_op jit(solution)/shard_map/ppermute | solution.py:32
  169.0 25.6 %collective-permute-start.28 = (bf16[208,2432]{1,0:T(8,128)(2,1)S(1)}, bf16[208,2432]{1,0:T(8,128)(2,1)S(1)}, u32[]{:S(2)}, u32[]{:S(2)}) collective-permute-start(bf16[208,2432]{1,0:T(8,128)(2,1)S(1)} %shard_map.175.refs_0_), channel_id=1, source_target_pairs={{0,8},{1,9},{2,10},{3,11},{4,12},{5,13},{6,14},{7,15},{8,0},{9,1},... | collective-permute-start | bytes 3035144 | tf_op jit(solution)/shard_map/ppermute | solution.py:32
  170.7 24.6 %collective-permute-start.27 = (bf16[208,2432]{1,0:T(8,128)(2,1)S(1)}, bf16[208,2432]{1,0:T(8,128)(2,1)S(1)}, u32[]{:S(2)}, u32[]{:S(2)}) collective-permute-start(bf16[208,2432]{1,0:T(8,128)(2,1)S(1)} %shard_map.175.refs_0_), channel_id=1, source_target_pairs={{0,12},{1,13},{2,14},{3,15},{4,0},{5,1},{6,2},{7,3},{8,4},{9,5},{1... | collective-permute-start | bytes 3035144 | tf_op jit(solution)/shard_map/ppermute | solution.py:32
  171.7 2.7 %copy-start = (bf16[2,608,2432]{2,1,0:T(8,128)(2,1)S(1)}, bf16[2,608,2432]{2,1,0:T(8,128)(2,1)}, u32[]{:S(2)}) copy-start(bf16[2,608,2432]{2,1,0:T(8,128)(2,1)} %refs_4_.1) | copy-start | bytes 17743876
  201.8 24.3 %collective-permute-start.30 = (bf16[208,2432]{1,0:T(8,128)(2,1)S(1)}, bf16[208,2432]{1,0:T(8,128)(2,1)S(1)}, u32[]{:S(2)}, u32[]{:S(2)}) collective-permute-start(bf16[208,2432]{1,0:T(8,128)(2,1)S(1)} %get-tuple-element.81), channel_id=1, source_target_pairs={{0,12},{1,13},{2,14},{3,15},{4,0},{5,1},{6,2},{7,3},{8,4},{9,5},{1... | collective-permute-start | bytes 3035144 | tf_op jit(solution)/shard_map/ppermute | solution.py:32
  203.9 22.2 %collective-permute-start.31 = (bf16[208,2432]{1,0:T(8,128)(2,1)S(1)}, bf16[208,2432]{1,0:T(8,128)(2,1)S(1)}, u32[]{:S(2)}, u32[]{:S(2)}) collective-permute-start(bf16[208,2432]{1,0:T(8,128)(2,1)S(1)} %get-tuple-element.82), channel_id=1, source_target_pairs={{0,8},{1,9},{2,10},{3,11},{4,12},{5,13},{6,14},{7,15},{8,0},{9,1},... | collective-permute-start | bytes 3035144 | tf_op jit(solution)/shard_map/ppermute | solution.py:32
  203.9 25.6 %collective-permute-start.32 = (bf16[208,2432]{1,0:T(8,128)(2,1)S(1)}, bf16[208,2432]{1,0:T(8,128)(2,1)S(1)}, u32[]{:S(2)}, u32[]{:S(2)}) collective-permute-start(bf16[208,2432]{1,0:T(8,128)(2,1)S(1)} %get-tuple-element.83), channel_id=1, source_target_pairs={{0,4},{1,5},{2,6},{3,7},{4,8},{5,9},{6,10},{7,11},{8,12},{9,13},{1... | collective-permute-start | bytes 3035144 | tf_op jit(solution)/shard_map/ppermute | solution.py:32
  230.3 6.5 %collective-permute-start.36 = (bf16[20,2432]{1,0:T(8,128)(2,1)S(1)}, bf16[20,2432]{1,0:T(8,128)(2,1)S(1)}, u32[]{:S(2)}, u32[]{:S(2)}) collective-permute-start(bf16[20,2432]{1,0:T(8,128)(2,1)S(1)} %get-tuple-element.90), channel_id=1, source_target_pairs={{0,3},{1,0},{2,1},{3,2},{4,7},{5,4},{6,5},{7,6},{8,11},{9,8},{10,9... | collective-permute-start | bytes 291848 | tf_op jit(solution)/shard_map/ppermute | solution.py:32
  232.4 5.5 %collective-permute-start.37 = (bf16[20,2432]{1,0:T(8,128)(2,1)S(1)}, bf16[20,2432]{1,0:T(8,128)(2,1)S(1)}, u32[]{:S(2)}, u32[]{:S(2)}) collective-permute-start(bf16[20,2432]{1,0:T(8,128)(2,1)S(1)} %get-tuple-element.91), channel_id=1, source_target_pairs={{0,2},{1,3},{2,0},{3,1},{4,6},{5,7},{6,4},{7,5},{8,10},{9,11},{10,... | collective-permute-start | bytes 291848 | tf_op jit(solution)/shard_map/ppermute | solution.py:32
  232.4 6.3 %collective-permute-start.38 = (bf16[20,2432]{1,0:T(8,128)(2,1)S(1)}, bf16[20,2432]{1,0:T(8,128)(2,1)S(1)}, u32[]{:S(2)}, u32[]{:S(2)}) collective-permute-start(bf16[20,2432]{1,0:T(8,128)(2,1)S(1)} %get-tuple-element.92), channel_id=1, source_target_pairs={{0,1},{1,2},{2,3},{3,0},{4,5},{5,6},{6,7},{7,4},{8,9},{9,10},{10,1... | collective-permute-start | bytes 291848 | tf_op jit(solution)/shard_map/ppermute | solution.py:32
  233.1 21.0 %collective-permute-start.33 = (bf16[32,2432]{1,0:T(8,128)(2,1)S(1)}, bf16[32,2432]{1,0:T(8,128)(2,1)S(1)}, u32[]{:S(2)}, u32[]{:S(2)}) collective-permute-start(bf16[32,2432]{1,0:T(8,128)(2,1)S(1)} %get-tuple-element.85), channel_id=1, source_target_pairs={{0,3},{1,0},{2,1},{3,2},{4,7},{5,4},{6,5},{7,6},{8,11},{9,8},{10,9... | collective-permute-start | bytes 466952 | tf_op jit(solution)/shard_map/ppermute | solution.py:32
  235.1 19.0 %collective-permute-start.34 = (bf16[32,2432]{1,0:T(8,128)(2,1)S(1)}, bf16[32,2432]{1,0:T(8,128)(2,1)S(1)}, u32[]{:S(2)}, u32[]{:S(2)}) collective-permute-start(bf16[32,2432]{1,0:T(8,128)(2,1)S(1)} %get-tuple-element.86), channel_id=1, source_target_pairs={{0,2},{1,3},{2,0},{3,1},{4,6},{5,7},{6,4},{7,5},{8,10},{9,11},{10,... | collective-permute-start | bytes 466952 | tf_op jit(solution)/shard_map/ppermute | solution.py:32
  236.9 17.3 %collective-permute-start.35 = (bf16[32,2432]{1,0:T(8,128)(2,1)S(1)}, bf16[32,2432]{1,0:T(8,128)(2,1)S(1)}, u32[]{:S(2)}, u32[]{:S(2)}) collective-permute-start(bf16[32,2432]{1,0:T(8,128)(2,1)S(1)} %get-tuple-element.87), channel_id=1, source_target_pairs={{0,1},{1,2},{2,3},{3,0},{4,5},{5,6},{6,7},{7,4},{8,9},{9,10},{10,1... | collective-permute-start | bytes 466952 | tf_op jit(solution)/shard_map/ppermute | solution.py:32
  239.6 20.0 %all-to-all-start.3 = ((bf16[8,4,2432]{2,1,0:T(4,128)(2,1)}), bf16[8,4,2432]{2,1,0:T(4,128)(2,1)S(1)}, u32[]{:S(2)}, u32[]{:S(2)}) async-start(bf16[8,4,2432]{2,1,0:T(4,128)(2,1)} %shard_map.180), calls=%async_computation.3 | async-start | bytes 311296 | tf_op jit(solution)/shard_map/all_to_all | solution.py:702
  (3 other events, 2.3 us)

commit v7 on v6

--- a/solution.py
+++ b/solution.py
@@ -609,7 +609,6 @@
         mod_pair_kernel,
         like((8, 8, width), F32),
         (mod_own, chip_swap(mod_own, False)),
-        after=(embed_pieces[1],),
     )
     row_mod = run(
         row_mod_kernel,

time: 261 us -> 254 us (0.973)
  waiting for transfers between devices: 128 us -> 117 us
    ppermute x2, waiting for transfers between devices: 7.41 us -> 0.01 us  [chip_swap(): return lax.ppermute(values, 'grp', pairs)]
    ppermute x36, waiting for transfers between devices: 110 us -> 107 us  [torus_shift(): return lax.ppermute(values, ('grp', 'tp'), pairs)]
    unnamed x50 -> x56, local copies, waits for them, and re-layouts: 12.9 us -> 14.8 us
  transfers between devices with their start and end apart: 42 -> 42, of which waited for: 26 -> 24; matrix products, arithmetic and copies ran while one was open for 1% -> 0% of each run, Pallas kernels for 7% -> 8%
where the time goes in v7:
time: 254 us; the launch traced here: 253 us
  waiting for transfers between devices  117 us (46%)
  starting transfers between devices  75 us (30%)
  Pallas kernels  34.3 us (14%)
  local copies, waits for them, and re-layouts  15.5 us (6%)
  blocking collectives  9.54 us (4%)
    ppermute x36, waiting for transfers between devices, torus_shift(): return lax.ppermute(values, ('grp', 'tp'), pairs)  107 us
    ppermute x36, starting transfers between devices, torus_shift(): return lax.ppermute(values, ('grp', 'tp'), pairs)  38 us
    pallas_call x23, Pallas kernels, run(): pl.pallas_call(body, out_shape=shapes, in_specs=specs, out_specs=[pl.Bloc...  34.3 us
    unnamed x56, local copies, waits for them, and re-layouts  14.8 us
    all_to_all x1, starting transfers between devices, shards(): placed = lax.all_to_all(placed, 'grp', 0, 0, tiled=True)  14.5 us
    all_to_all x1, starting transfers between devices, shards(): lax.all_to_all(slot_parts.reshape(8, 64, 512), 'grp', 0, 0, tiled=True)  9.9 us
    all_to_all x1, blocking collectives, shards(): lax.all_to_all(att_parts, 'grp', 0, 0, tiled=True).reshape(512, 128)  9.54 us
    all_to_all x1, starting transfers between devices, shards(): arrived = lax.all_to_all(outgoing, 'tp', 0, 0, tiled=True)  7.85 us
  transfers between devices with their start and end apart: 42, of which 24 were waited for; matrix products, arithmetic and copies ran while one was open for 0% of the time, Pallas kernels for 8%

profile of v7, /device:TPU:1, one launch (start us, length us, event | category | flops | bytes accessed | tf_op | source)
XLA Modules:
  0.0 253.1 jit_solution(10400969888081574154)
XLA Ops:
  0.6 0.9 copy-done.16
  2.2 0.9 shard_map.158
  3.1 0.9 copy-done.4
  4.1 1.5 collective-permute-start
  5.6 7.9 %all-to-all-start = ((bf16[16,32,256]{2,1,0:T(8,128)(2,1)}), bf16[16,32,256]{2,1,0:T(8,128)(2,1)S(1)}, u32[]{:S(2)}, u32[]{:S(2)}) async-start(bf16[16,32,256]{2,1,0:T(8,128)(2,1)} %get-tuple-element.48.refs_6_.refs_1_), calls=%async_computation | async-start | bytes 524288 | tf_op jit(solution)/shard_map/all_to_all | solution.py:552
  13.5 1.3 collective-permute-start.7
  15.3 7.8 %shard_map.159 = (f32[512,384]{1,0:T(8,128)}, bf16[16,32,192]{2,1,0:T(8,128)(2,1)}, bf16[32,2432]{1,0:T(8,128)(2,1)}, f32[6,2432]{1,0:T(8,128)}) custom-call(s32[2]{0:T(128)} %refs_0_.5, s32[1]{0:T(128)} %bitcast.refs_1_, bf16[512,2432]{1,0:T(8,128)(2,1)} %refs_2_.4, f32[2,6,2,2432]{3,2,1,0:T(2,128)} %bitcast.33, bf16[3,2432,128]{2,1,0:T(8,128)(2,1)} %bitcast.38, ...), custom_call_target="tpu_custom_call" | custom-call | flops 1434451968 | bytes 7656460 | tf_op jit(solution)/shard_map/pallas_call | solution.py:80
  23.3 1.9 collective-permute-start.8
  25.2 0.9 copy-done.15
  26.1 1.5 shard_map.162
  27.6 2.6 %collective-permute-start.1 = (bf16[80,2944]{1,0:T(8,128)(2,1)S(1)}, bf16[80,2944]{1,0:T(8,128)(2,1)S(1)}, u32[]{:S(2)}, u32[]{:S(2)}) collective-permute-start(bf16[80,2944]{1,0:T(8,128)(2,1)S(1)} %get-tuple-element.52), channel_id=1, source_target_pairs={{0,12},{1,13},{2,14},{3,15},{4,0},{5,1},{6,2},{7,3},{8,4},{9,5},{1... | collective-permute-start | bytes 1413128 | tf_op jit(solution)/shard_map/ppermute | solution.py:32
  31.3 9.5 %collective-permute-done.1.refs_1_ = bf16[80,2944]{1,0:T(8,128)(2,1)S(1)} collective-permute-done((bf16[80,2944]{1,0:T(8,128)(2,1)S(1)}, bf16[80,2944]{1,0:T(8,128)(2,1)S(1)}, u32[]{:S(2)}, u32[]{:S(2)}) %collective-permute-start.1) | collective-permute-done | bytes 471072 | tf_op jit(solution)/shard_map/ppermute | solution.py:32
  40.8 3.7 %collective-permute-done.3.refs_3_ = bf16[80,2944]{1,0:T(8,128)(2,1)S(1)} collective-permute-done((bf16[80,2944]{1,0:T(8,128)(2,1)S(1)}, bf16[80,2944]{1,0:T(8,128)(2,1)S(1)}, u32[]{:S(2)}, u32[]{:S(2)}) %collective-permute-start.3) | collective-permute-done | bytes 471072 | tf_op jit(solution)/shard_map/ppermute | solution.py:32
  45.0 2.2 collective-permute-start.4
  49.1 1.1 copy-done.8
  50.2 1.0 shard_map.165.refs_4_.refs_7_.refs_5_
  51.3 1.4 collective-permute-done.5.refs_2_
  52.7 1.4 collective-permute-done.6.refs_3_
  54.5 1.5 collective-permute-start.10
  55.9 1.2 collective-permute-start.9
  57.2 4.0 %collective-permute-done.11.refs_3_ = bf16[20,2944]{1,0:T(8,128)(2,1)S(1)} collective-permute-done((bf16[20,2944]{1,0:T(8,128)(2,1)S(1)}, bf16[20,2944]{1,0:T(8,128)(2,1)S(1)}, u32[]{:S(2)}, u32[]{:S(2)}) %collective-permute-start.11) | collective-permute-done | bytes 117792 | tf_op jit(solution)/shard_map/ppermute | solution.py:32
  62.0 2.4 collective-permute-start.13
  65.3 10.7 %collective-permute-done.14.refs_4_ = bf16[80,2944]{1,0:T(8,128)(2,1)S(1)} collective-permute-done((bf16[80,2944]{1,0:T(8,128)(2,1)S(1)}, bf16[80,2944]{1,0:T(8,128)(2,1)S(1)}, u32[]{:S(2)}, u32[]{:S(2)}) %collective-permute-start.14) | collective-permute-done | bytes 471072 | tf_op jit(solution)/shard_map/ppermute | solution.py:32
  76.0 0.9 collective-permute-done.12.refs_2_
  76.9 2.2 shard_map.168
  80.8 9.9 %all-to-all-start.1 = ((bf16[8,64,512]{2,1,0:T(8,128)(2,1)}), bf16[8,64,512]{2,1,0:T(8,128)(2,1)S(1)}, u32[]{:S(2)}, u32[]{:S(2)}) async-start(bf16[8,64,512]{2,1,0:T(8,128)(2,1)} %bitcast.36), calls=%async_computation.1 | async-start | bytes 1048576 | tf_op jit(solution)/shard_map/all_to_all | solution.py:648
  90.7 1.1 copy-done.5
  91.8 1.0 copy-done.11
  92.8 1.5 shard_map.169.refs_1_
  95.2 5.0 %all-to-all-done.1.refs_2_ = bf16[8,64,512]{2,1,0:T(8,128)(2,1)S(1)} async-done(((bf16[8,64,512]{2,1,0:T(8,128)(2,1)}), bf16[8,64,512]{2,1,0:T(8,128)(2,1)S(1)}, u32[]{:S(2)}, u32[]{:S(2)}) %all-to-all-start.1) | async-done | bytes 524320 | tf_op jit(solution)/shard_map/all_to_all | solution.py:648
  100.2 1.0 copy-done.13
  101.2 1.1 copy-done.24
  102.3 2.5 shard_map.170
  104.8 2.4 collective-permute-start.15
  107.8 1.1 shard_map.171
  109.0 9.5 %all_to_all.20 = bf16[8,64,128]{2,1,0:T(8,128)(2,1)S(1)} all-to-all(bf16[8,64,128]{2,1,0:T(8,128)(2,1)S(1)} %shard_map.171), channel_id=1, replica_groups=mesh['grp'=8,'tp'=16] {'grp'}, dimensions={0} | all-to-all | bytes 262144 | tf_op jit(solution)/shard_map/all_to_all | solution.py:665
  118.5 2.5 collective-permute-done.15.refs_3_.refs_1_
  121.0 0.9 shard_map.172
  121.9 3.5 %collective-permute-start.18 = (bf16[80,2432]{1,0:T(8,128)(2,1)S(1)}, bf16[80,2432]{1,0:T(8,128)(2,1)S(1)}, u32[]{:S(2)}, u32[]{:S(2)}) collective-permute-start(bf16[80,2432]{1,0:T(8,128)(2,1)S(1)} %get-tuple-element.71), channel_id=1, source_target_pairs={{0,12},{1,13},{2,14},{3,15},{4,0},{5,1},{6,2},{7,3},{8,4},{9,5},{1... | collective-permute-start | bytes 1167368 | tf_op jit(solution)/shard_map/ppermute | solution.py:32
  126.1 8.2 %collective-permute-done.18.refs_5_ = bf16[80,2432]{1,0:T(8,128)(2,1)S(1)} collective-permute-done((bf16[80,2432]{1,0:T(8,128)(2,1)S(1)}, bf16[80,2432]{1,0:T(8,128)(2,1)S(1)}, u32[]{:S(2)}, u32[]{:S(2)}) %collective-permute-start.18) | collective-permute-done | bytes 389152 | tf_op jit(solution)/shard_map/ppermute | solution.py:32
  134.2 3.4 %collective-permute-done.20.refs_7_ = bf16[80,2432]{1,0:T(8,128)(2,1)S(1)} collective-permute-done((bf16[80,2432]{1,0:T(8,128)(2,1)S(1)}, bf16[80,2432]{1,0:T(8,128)(2,1)S(1)}, u32[]{:S(2)}, u32[]{:S(2)}) %collective-permute-start.20) | collective-permute-done | bytes 389152 | tf_op jit(solution)/shard_map/ppermute | solution.py:32
  138.5 2.3 collective-permute-start.21
  141.5 5.7 %collective-permute-done.21.refs_3_ = bf16[52,2432]{1,0:T(8,128)(2,1)S(1)} collective-permute-done((bf16[52,2432]{1,0:T(8,128)(2,1)S(1)}, bf16[52,2432]{1,0:T(8,128)(2,1)S(1)}, u32[]{:S(2)}, u32[]{:S(2)}) %collective-permute-start.21) | collective-permute-done | bytes 252960 | tf_op jit(solution)/shard_map/ppermute | solution.py:32
  147.7 2.8 %collective-permute-done.23.refs_5_ = bf16[52,2432]{1,0:T(8,128)(2,1)S(1)} collective-permute-done((bf16[52,2432]{1,0:T(8,128)(2,1)S(1)}, bf16[52,2432]{1,0:T(8,128)(2,1)S(1)}, u32[]{:S(2)}, u32[]{:S(2)}) %collective-permute-start.23) | collective-permute-done | bytes 252960 | tf_op jit(solution)/shard_map/ppermute | solution.py:32
  151.2 1.8 collective-permute-start.25
  153.0 0.9 collective-permute-start.24
  153.9 7.1 %collective-permute-done.26.refs_3_ = bf16[52,2432]{1,0:T(8,128)(2,1)S(1)} collective-permute-done((bf16[52,2432]{1,0:T(8,128)(2,1)S(1)}, bf16[52,2432]{1,0:T(8,128)(2,1)S(1)}, u32[]{:S(2)}, u32[]{:S(2)}) %collective-permute-start.26) | collective-permute-done | bytes 252960 | tf_op jit(solution)/shard_map/ppermute | solution.py:32
  161.8 1.5 collective-permute-start.28
  163.3 1.1 collective-permute-start.27
  164.4 2.7 %copy-done = bf16[2,608,2432]{2,1,0:T(8,128)(2,1)S(1)} copy-done((bf16[2,608,2432]{2,1,0:T(8,128)(2,1)S(1)}, bf16[2,608,2432]{2,1,0:T(8,128)(2,1)}, u32[]{:S(2)}) %copy-start) | copy-done | bytes 5914648
  167.1 3.4 %shard_map.176.refs_5_.refs_0_ = bf16[208,2432]{1,0:T(8,128)(2,1)S(1)} custom-call(bf16[208,2432]{1,0:T(8,128)(2,1)S(1)} %shard_map.175.refs_0_, bf16[2,608,2432]{2,1,0:T(8,128)(2,1)S(1)} %bitcast.30, bf16[2,608,2432]{2,1,0:T(8,128)(2,1)S(1)} %copy-done), custom_call_target="tpu_custom_call" | custom-call | flops 1230241792 | bytes 13852672 | tf_op jit(solution)/shard_map/pallas_call | solution.py:80
  170.5 16.8 %collective-permute-done.29.refs_2_ = bf16[208,2432]{1,0:T(8,128)(2,1)S(1)} collective-permute-done((bf16[208,2432]{1,0:T(8,128)(2,1)S(1)}, bf16[208,2432]{1,0:T(8,128)(2,1)S(1)}, u32[]{:S(2)}, u32[]{:S(2)}) %collective-permute-start.29) | collective-permute-done | bytes 1011744 | tf_op jit(solution)/shard_map/ppermute | solution.py:32
  188.0 6.5 %shard_map.177 = (bf16[208,2432]{1,0:T(8,128)(2,1)S(1)}, bf16[208,2432]{1,0:T(8,128)(2,1)S(1)}, bf16[208,2432]{1,0:T(8,128)(2,1)S(1)}) custom-call(bf16[208,2432]{1,0:T(8,128)(2,1)S(1)} %collective-permute-done.27.refs_0_, bf16[208,2432]{1,0:T(8,128)(2,1)S(1)} %collective-permute-done.28.refs_1_, bf16[208,2432]{1,0:T(8,128)(2,1)S(1)} %collective-permute-done.29.refs_2_, ...), custom_call_target="tpu_custom_call" | custom-call | flops 3690725376 | bytes 17899520 | tf_op jit(solution)/shard_map/pallas_call | solution.py:80
  194.5 2.1 collective-permute-start.30
  197.3 21.5 %collective-permute-done.30.refs_1_ = bf16[208,2432]{1,0:T(8,128)(2,1)S(1)} collective-permute-done((bf16[208,2432]{1,0:T(8,128)(2,1)S(1)}, bf16[208,2432]{1,0:T(8,128)(2,1)S(1)}, u32[]{:S(2)}, u32[]{:S(2)}) %collective-permute-start.30) | collective-permute-done | bytes 1011744 | tf_op jit(solution)/shard_map/ppermute | solution.py:32
  218.8 3.4 %collective-permute-done.32.refs_3_ = bf16[208,2432]{1,0:T(8,128)(2,1)S(1)} collective-permute-done((bf16[208,2432]{1,0:T(8,128)(2,1)S(1)}, bf16[208,2432]{1,0:T(8,128)(2,1)S(1)}, u32[]{:S(2)}, u32[]{:S(2)}) %collective-permute-start.32) | collective-permute-done | bytes 1011744 | tf_op jit(solution)/shard_map/ppermute | solution.py:32
  222.2 0.9 shard_map.178
  223.1 2.1 collective-permute-start.36
  225.8 2.0 collective-permute-start.33
  227.9 1.8 collective-permute-start.34
  229.6 1.0 collective-permute-done.37.refs_3_
  231.4 0.9 shard_map.180
  232.3 14.5 %all-to-all-start.3 = ((bf16[8,4,2432]{2,1,0:T(4,128)(2,1)}), bf16[8,4,2432]{2,1,0:T(4,128)(2,1)S(1)}, u32[]{:S(2)}, u32[]{:S(2)}) async-start(bf16[8,4,2432]{2,1,0:T(4,128)(2,1)} %shard_map.180), calls=%async_computation.3 | async-start | bytes 311296 | tf_op jit(solution)/shard_map/all_to_all | solution.py:701
  247.7 4.7 %all-to-all-done.3 = bf16[8,4,2432]{2,1,0:T(4,128)(2,1)S(1)} async-done(((bf16[8,4,2432]{2,1,0:T(4,128)(2,1)}), bf16[8,4,2432]{2,1,0:T(4,128)(2,1)S(1)}, u32[]{:S(2)}, u32[]{:S(2)}) %all-to-all-start.3) | async-done | bytes 155680 | tf_op jit(solution)/shard_map/all_to_all | solution.py:701
  (105 shorter events, 18.7 us)
Async XLA Ops:
  0.6 14.2 %copy-start.22 = (s32[20,1]{0,1:T(1,128)S(1)}, s32[20,1]{0,1:T(1,128)}, u32[]{:S(2)}) copy-start(s32[20,1]{0,1:T(1,128)} %param.17) | copy-start | bytes 244
  3.1 0.9 copy-start.4
  4.1 9.4 %collective-permute-start = (f32[2,8,2432]{2,1,0:T(8,128)S(1)}, f32[2,8,2432]{2,1,0:T(8,128)S(1)}, u32[]{:S(2)}, u32[]{:S(2)}) collective-permute-start(f32[2,8,2432]{2,1,0:T(8,128)S(1)} %shard_map.160.refs_0_), channel_id=1, source_target_pairs={{0,16},{16,0},{32,48},{48,32},{64,80},{80,64},{96,112},{112,96},{1... | collective-permute-start | bytes 466952 | tf_op jit(solution)/shard_map/ppermute | solution.py:36
  5.6 19.6 %all-to-all-start = ((bf16[16,32,256]{2,1,0:T(8,128)(2,1)}), bf16[16,32,256]{2,1,0:T(8,128)(2,1)S(1)}, u32[]{:S(2)}, u32[]{:S(2)}) async-start(bf16[16,32,256]{2,1,0:T(8,128)(2,1)} %get-tuple-element.48.refs_6_.refs_1_), calls=%async_computation | async-start | bytes 524288 | tf_op jit(solution)/shard_map/all_to_all | solution.py:552
  13.5 9.7 %collective-permute-start.7 = (f32[4,8,2432]{2,1,0:T(8,128)S(1)}, f32[4,8,2432]{2,1,0:T(8,128)S(1)}, u32[]{:S(2)}, u32[]{:S(2)}) collective-permute-start(f32[4,8,2432]{2,1,0:T(8,128)S(1)} %shard_map.161.refs_4_.refs_0_), channel_id=1, source_target_pairs={{0,32},{16,48},{32,0},{48,16},{64,96},{80,112},{96,64},{112,80},{1... | collective-permute-start | bytes 933896 | tf_op jit(solution)/shard_map/ppermute | solution.py:44
  15.3 9.8 %copy-start.3 = (bf16[256,2432]{1,0:T(8,128)(2,1)S(1)}, bf16[256,2432]{1,0:T(8,128)(2,1)}, u32[]{:S(2)}) copy-start(bf16[256,2432]{1,0:T(8,128)(2,1)} %refs_2_.5) | copy-start | bytes 3735556
  23.3 25.0 %collective-permute-start.8 = (f32[8,8,2432]{2,1,0:T(8,128)S(1)}, f32[8,8,2432]{2,1,0:T(8,128)S(1)}, u32[]{:S(2)}, u32[]{:S(2)}) collective-permute-start(f32[8,8,2432]{2,1,0:T(8,128)S(1)} %shard_map.164.refs_1_), channel_id=1, source_target_pairs={{0,96},{16,112},{32,64},{48,80},{64,32},{80,48},{96,0},{112,16},{1... | collective-permute-start | bytes 1867784 | tf_op jit(solution)/shard_map/ppermute | solution.py:44
  25.2 1.0 copy-start.15
  26.1 23.0 %copy-start.20 = (s32[20]{0:T(128)S(1)}, s32[20]{0:T(128)}, u32[]{:S(2)}) copy-start(s32[20]{0:T(128)} %fusion.3.refs_7_.refs_0_) | copy-start | bytes 244
  27.6 13.2 %collective-permute-start.1 = (bf16[80,2944]{1,0:T(8,128)(2,1)S(1)}, bf16[80,2944]{1,0:T(8,128)(2,1)S(1)}, u32[]{:S(2)}, u32[]{:S(2)}) collective-permute-start(bf16[80,2944]{1,0:T(8,128)(2,1)S(1)} %get-tuple-element.52), channel_id=1, source_target_pairs={{0,12},{1,13},{2,14},{3,15},{4,0},{5,1},{6,2},{7,3},{8,4},{9,5},{1... | collective-permute-start | bytes 1413128 | tf_op jit(solution)/shard_map/ppermute | solution.py:32
  30.2 10.6 %collective-permute-start.2 = (bf16[80,2944]{1,0:T(8,128)(2,1)S(1)}, bf16[80,2944]{1,0:T(8,128)(2,1)S(1)}, u32[]{:S(2)}, u32[]{:S(2)}) collective-permute-start(bf16[80,2944]{1,0:T(8,128)(2,1)S(1)} %get-tuple-element.53), channel_id=1, source_target_pairs={{0,8},{1,9},{2,10},{3,11},{4,12},{5,13},{6,14},{7,15},{8,0},{9,1},... | collective-permute-start | bytes 1413128 | tf_op jit(solution)/shard_map/ppermute | solution.py:32
  30.8 13.7 %collective-permute-start.3 = (bf16[80,2944]{1,0:T(8,128)(2,1)S(1)}, bf16[80,2944]{1,0:T(8,128)(2,1)S(1)}, u32[]{:S(2)}, u32[]{:S(2)}) collective-permute-start(bf16[80,2944]{1,0:T(8,128)(2,1)S(1)} %get-tuple-element.54), channel_id=1, source_target_pairs={{0,4},{1,5},{2,6},{3,7},{4,8},{5,9},{6,10},{7,11},{8,12},{9,13},{1... | collective-permute-start | bytes 1413128 | tf_op jit(solution)/shard_map/ppermute | solution.py:32
  45.0 6.3 %collective-permute-start.4 = (bf16[20,2944]{1,0:T(8,128)(2,1)S(1)}, bf16[20,2944]{1,0:T(8,128)(2,1)S(1)}, u32[]{:S(2)}, u32[]{:S(2)}) collective-permute-start(bf16[20,2944]{1,0:T(8,128)(2,1)S(1)} %get-tuple-element.56), channel_id=1, source_target_pairs={{0,3},{1,0},{2,1},{3,2},{4,7},{5,4},{6,5},{7,6},{8,11},{9,8},{10,9... | collective-permute-start | bytes 353288 | tf_op jit(solution)/shard_map/ppermute | solution.py:32
  47.1 5.5 %collective-permute-start.5 = (bf16[20,2944]{1,0:T(8,128)(2,1)S(1)}, bf16[20,2944]{1,0:T(8,128)(2,1)S(1)}, u32[]{:S(2)}, u32[]{:S(2)}) collective-permute-start(bf16[20,2944]{1,0:T(8,128)(2,1)S(1)} %get-tuple-element.57), channel_id=1, source_target_pairs={{0,2},{1,3},{2,0},{3,1},{4,6},{5,7},{6,4},{7,5},{8,10},{9,11},{10,... | collective-permute-start | bytes 353288 | tf_op jit(solution)/shard_map/ppermute | solution.py:32
  47.7 6.4 %collective-permute-start.6 = (bf16[20,2944]{1,0:T(8,128)(2,1)S(1)}, bf16[20,2944]{1,0:T(8,128)(2,1)S(1)}, u32[]{:S(2)}, u32[]{:S(2)}) collective-permute-start(bf16[20,2944]{1,0:T(8,128)(2,1)S(1)} %get-tuple-element.58), channel_id=1, source_target_pairs={{0,1},{1,2},{2,3},{3,0},{4,5},{5,6},{6,7},{7,4},{8,9},{9,10},{10,1... | collective-permute-start | bytes 353288 | tf_op jit(solution)/shard_map/ppermute | solution.py:32
  49.1 1.1 copy-start.8
  51.2 14.0 %copy-start.25 = (f32[2,2,64]{2,1,0:T(2,128)S(1)}, f32[2,2,64]{2,1,0:T(2,128)}, u32[]{:S(2)}) copy-start(f32[2,2,64]{2,1,0:T(2,128)} %param.20) | copy-start | bytes 3076
  51.2 25.7 %copy-start.1 = (bf16[2432,3,128]{2,0,1:T(8,128)(2,1)S(1)}, bf16[2432,3,128]{2,0,1:T(8,128)(2,1)}, u32[]{:S(2)}) copy-start(bf16[2432,3,128]{2,0,1:T(8,128)(2,1)} %param.23) | copy-start | bytes 5603332
  54.4 7.6 %copy-start.18 = (bf16[20,2432]{1,0:T(8,128)(2,1)}, bf16[20,2432]{1,0:T(8,128)(2,1)S(1)}, u32[]{:S(2)}) copy-start(bf16[20,2432]{1,0:T(8,128)(2,1)S(1)} %get-tuple-element.59.refs_1_) | copy-start | bytes 291844
  54.4 6.7 %collective-permute-start.11 = (bf16[20,2944]{1,0:T(8,128)(2,1)S(1)}, bf16[20,2944]{1,0:T(8,128)(2,1)S(1)}, u32[]{:S(2)}, u32[]{:S(2)}) collective-permute-start(bf16[20,2944]{1,0:T(8,128)(2,1)S(1)} %get-tuple-element.60.refs_0_), channel_id=1, source_target_pairs={{0,1},{1,2},{2,3},{3,0},{4,5},{5,6},{6,7},{7,4},{8,9},{9,10},{10,1... | collective-permute-start | bytes 353288 | tf_op jit(solution)/shard_map/ppermute | solution.py:32
  54.5 6.6 %collective-permute-start.10 = (bf16[20,2944]{1,0:T(8,128)(2,1)S(1)}, bf16[20,2944]{1,0:T(8,128)(2,1)S(1)}, u32[]{:S(2)}, u32[]{:S(2)}) collective-permute-start(bf16[20,2944]{1,0:T(8,128)(2,1)S(1)} %get-tuple-element.60.refs_0_), channel_id=1, source_target_pairs={{0,2},{1,3},{2,0},{3,1},{4,6},{5,7},{6,4},{7,5},{8,10},{9,11},{10,... | collective-permute-start | bytes 353288 | tf_op jit(solution)/shard_map/ppermute | solution.py:32
  55.9 5.8 %collective-permute-start.9 = (bf16[20,2944]{1,0:T(8,128)(2,1)S(1)}, bf16[20,2944]{1,0:T(8,128)(2,1)S(1)}, u32[]{:S(2)}, u32[]{:S(2)}) collective-permute-start(bf16[20,2944]{1,0:T(8,128)(2,1)S(1)} %get-tuple-element.60.refs_0_), channel_id=1, source_target_pairs={{0,3},{1,0},{2,1},{3,2},{4,7},{5,4},{6,5},{7,6},{8,11},{9,8},{10,9... | collective-permute-start | bytes 353288 | tf_op jit(solution)/shard_map/ppermute | solution.py:32
  61.9 14.1 %collective-permute-start.14 = (bf16[80,2944]{1,0:T(8,128)(2,1)S(1)}, bf16[80,2944]{1,0:T(8,128)(2,1)S(1)}, u32[]{:S(2)}, u32[]{:S(2)}) collective-permute-start(bf16[80,2944]{1,0:T(8,128)(2,1)S(1)} %shard_map.167.refs_1_), channel_id=1, source_target_pairs={{0,4},{1,5},{2,6},{3,7},{4,8},{5,9},{6,10},{7,11},{8,12},{9,13},{1... | collective-permute-start | bytes 1413128 | tf_op jit(solution)/shard_map/ppermute | solution.py:32
  62.0 14.0 %collective-permute-start.13 = (bf16[80,2944]{1,0:T(8,128)(2,1)S(1)}, bf16[80,2944]{1,0:T(8,128)(2,1)S(1)}, u32[]{:S(2)}, u32[]{:S(2)}) collective-permute-start(bf16[80,2944]{1,0:T(8,128)(2,1)S(1)} %shard_map.167.refs_1_), channel_id=1, source_target_pairs={{0,8},{1,9},{2,10},{3,11},{4,12},{5,13},{6,14},{7,15},{8,0},{9,1},... | collective-permute-start | bytes 1413128 | tf_op jit(solution)/shard_map/ppermute | solution.py:32
  64.3 12.6 %collective-permute-start.12 = (bf16[80,2944]{1,0:T(8,128)(2,1)S(1)}, bf16[80,2944]{1,0:T(8,128)(2,1)S(1)}, u32[]{:S(2)}, u32[]{:S(2)}) collective-permute-start(bf16[80,2944]{1,0:T(8,128)(2,1)S(1)} %shard_map.167.refs_1_), channel_id=1, source_target_pairs={{0,12},{1,13},{2,14},{3,15},{4,0},{5,1},{6,2},{7,3},{8,4},{9,5},{1... | collective-permute-start | bytes 1413128 | tf_op jit(solution)/shard_map/ppermute | solution.py:32
  76.9 13.7 %copy-start.2 = (bf16[32,3,64,128]{3,2,1,0:T(8,128)(2,1)S(1)}, bf16[32,3,64,128]{3,2,1,0:T(8,128)(2,1)}, u32[]{:S(2)}) copy-start(bf16[32,3,64,128]{3,2,1,0:T(8,128)(2,1)} %refs_3_.2) | copy-start | bytes 4718596
  76.9 13.7 %copy-start.23 = (s32[2]{0:T(128)S(1)}, s32[2]{0:T(128)}, u32[]{:S(2)}) copy-start(s32[2]{0:T(128)} %refs_0_.5) | copy-start | bytes 28
  80.8 19.4 %all-to-all-start.1 = ((bf16[8,64,512]{2,1,0:T(8,128)(2,1)}), bf16[8,64,512]{2,1,0:T(8,128)(2,1)S(1)}, u32[]{:S(2)}, u32[]{:S(2)}) async-start(bf16[8,64,512]{2,1,0:T(8,128)(2,1)} %bitcast.36), calls=%async_computation.1 | async-start | bytes 1048576 | tf_op jit(solution)/shard_map/all_to_all | solution.py:648
  90.7 1.1 copy-start.5
  91.8 1.0 copy-start.11
  100.2 1.0 copy-start.13
  101.2 1.1 copy-start.24
  104.8 16.2 %copy-start.6 = (bf16[128,2432]{1,0:T(8,128)(2,1)S(1)}, bf16[128,2432]{1,0:T(8,128)(2,1)}, u32[]{:S(2)}) copy-start(bf16[128,2432]{1,0:T(8,128)(2,1)} %refs_2_.6) | copy-start | bytes 1867780
  104.8 16.2 %collective-permute-start.15 = (bf16[128,2432]{1,0:T(8,128)(2,1)S(1)}, bf16[128,2432]{1,0:T(8,128)(2,1)S(1)}, u32[]{:S(2)}, u32[]{:S(2)}) collective-permute-start(bf16[128,2432]{1,0:T(8,128)(2,1)S(1)} %get-tuple-element.66), channel_id=1, source_target_pairs={{0,12},{1,13},{2,14},{3,15},{4,0},{5,1},{6,2},{7,3},{8,4},{9,5},{1... | collective-permute-start | bytes 1867784 | tf_op jit(solution)/shard_map/ppermute | solution.py:32
  107.1 18.9 %collective-permute-start.16 = (bf16[128,2432]{1,0:T(8,128)(2,1)S(1)}, bf16[128,2432]{1,0:T(8,128)(2,1)S(1)}, u32[]{:S(2)}, u32[]{:S(2)}) collective-permute-start(bf16[128,2432]{1,0:T(8,128)(2,1)S(1)} %get-tuple-element.67), channel_id=1, source_target_pairs={{0,8},{1,9},{2,10},{3,11},{4,12},{5,13},{6,14},{7,15},{8,0},{9,1},... | collective-permute-start | bytes 1867784 | tf_op jit(solution)/shard_map/ppermute | solution.py:32
  107.1 18.9 %collective-permute-start.17 = (bf16[128,2432]{1,0:T(8,128)(2,1)S(1)}, bf16[128,2432]{1,0:T(8,128)(2,1)S(1)}, u32[]{:S(2)}, u32[]{:S(2)}) collective-permute-start(bf16[128,2432]{1,0:T(8,128)(2,1)S(1)} %get-tuple-element.68), channel_id=1, source_target_pairs={{0,4},{1,5},{2,6},{3,7},{4,8},{5,9},{6,10},{7,11},{8,12},{9,13},{1... | collective-permute-start | bytes 1867784 | tf_op jit(solution)/shard_map/ppermute | solution.py:32
  107.8 56.6 %slice-start = ((s8[5914624]{0:T(1024)(128)(4,1)}), s8[4194304]{0:T(1024)(128)(4,1)S(1)}, s32[]{:S(2)}) async-start(s8[5914624]{0:T(1024)(128)(4,1)} %bitcast.28), calls=%async_computation.4 | async-start | bytes 8388608
  121.9 12.3 %collective-permute-start.18 = (bf16[80,2432]{1,0:T(8,128)(2,1)S(1)}, bf16[80,2432]{1,0:T(8,128)(2,1)S(1)}, u32[]{:S(2)}, u32[]{:S(2)}) collective-permute-start(bf16[80,2432]{1,0:T(8,128)(2,1)S(1)} %get-tuple-element.71), channel_id=1, source_target_pairs={{0,12},{1,13},{2,14},{3,15},{4,0},{5,1},{6,2},{7,3},{8,4},{9,5},{1... | collective-permute-start | bytes 1167368 | tf_op jit(solution)/shard_map/ppermute | solution.py:32
  125.4 8.8 %collective-permute-start.19 = (bf16[80,2432]{1,0:T(8,128)(2,1)S(1)}, bf16[80,2432]{1,0:T(8,128)(2,1)S(1)}, u32[]{:S(2)}, u32[]{:S(2)}) collective-permute-start(bf16[80,2432]{1,0:T(8,128)(2,1)S(1)} %get-tuple-element.72), channel_id=1, source_target_pairs={{0,8},{1,9},{2,10},{3,11},{4,12},{5,13},{6,14},{7,15},{8,0},{9,1},... | collective-permute-start | bytes 1167368 | tf_op jit(solution)/shard_map/ppermute | solution.py:32
  125.4 12.3 %collective-permute-start.20 = (bf16[80,2432]{1,0:T(8,128)(2,1)S(1)}, bf16[80,2432]{1,0:T(8,128)(2,1)S(1)}, u32[]{:S(2)}, u32[]{:S(2)}) collective-permute-start(bf16[80,2432]{1,0:T(8,128)(2,1)S(1)} %get-tuple-element.73), channel_id=1, source_target_pairs={{0,4},{1,5},{2,6},{3,7},{4,8},{5,9},{6,10},{7,11},{8,12},{9,13},{1... | collective-permute-start | bytes 1167368 | tf_op jit(solution)/shard_map/ppermute | solution.py:32
  137.6 12.9 %copy-start.14 = (f32[6,2432]{1,0:T(8,128)S(1)}, f32[6,2432]{1,0:T(8,128)}, u32[]{:S(2)}) copy-start(f32[6,2432]{1,0:T(8,128)} %get-tuple-element.78.refs_6_.refs_5_) | copy-start | bytes 175108
  137.7 12.9 %copy-start.17 = (bf16[32,2432]{1,0:T(8,128)(2,1)S(1)}, bf16[32,2432]{1,0:T(8,128)(2,1)}, u32[]{:S(2)}) copy-start(bf16[32,2432]{1,0:T(8,128)(2,1)} %get-tuple-element.49.refs_0_) | copy-start | bytes 466948
  137.7 12.9 %copy-start.19 = (bf16[20,2432]{1,0:T(8,128)(2,1)S(1)}, bf16[20,2432]{1,0:T(8,128)(2,1)}, u32[]{:S(2)}) copy-start(bf16[20,2432]{1,0:T(8,128)(2,1)} %copy-done.18) | copy-start | bytes 291844
  137.7 26.8 %slice-start.1 = ((s8[5914624]{0:T(1024)(128)(4,1)}), s8[1720320]{0:T(1024)(128)(4,1)S(1)}, s32[]{:S(2)}) async-start(s8[5914624]{0:T(1024)(128)(4,1)} %bitcast.28), calls=%async_computation.5 | async-start | bytes 3440640
  138.5 8.6 %collective-permute-start.21 = (bf16[52,2432]{1,0:T(8,128)(2,1)S(1)}, bf16[52,2432]{1,0:T(8,128)(2,1)S(1)}, u32[]{:S(2)}, u32[]{:S(2)}) collective-permute-start(bf16[52,2432]{1,0:T(8,128)(2,1)S(1)} %get-tuple-element.75), channel_id=1, source_target_pairs={{0,3},{1,0},{2,1},{3,2},{4,7},{5,4},{6,5},{7,6},{8,11},{9,8},{10,9... | collective-permute-start | bytes 758792 | tf_op jit(solution)/shard_map/ppermute | solution.py:32
  140.8 6.9 %collective-permute-start.22 = (bf16[52,2432]{1,0:T(8,128)(2,1)S(1)}, bf16[52,2432]{1,0:T(8,128)(2,1)S(1)}, u32[]{:S(2)}, u32[]{:S(2)}) collective-permute-start(bf16[52,2432]{1,0:T(8,128)(2,1)S(1)} %get-tuple-element.76), channel_id=1, source_target_pairs={{0,2},{1,3},{2,0},{3,1},{4,6},{5,7},{6,4},{7,5},{8,10},{9,11},{10,... | collective-permute-start | bytes 758792 | tf_op jit(solution)/shard_map/ppermute | solution.py:32
  140.8 9.8 %collective-permute-start.23 = (bf16[52,2432]{1,0:T(8,128)(2,1)S(1)}, bf16[52,2432]{1,0:T(8,128)(2,1)S(1)}, u32[]{:S(2)}, u32[]{:S(2)}) collective-permute-start(bf16[52,2432]{1,0:T(8,128)(2,1)S(1)} %get-tuple-element.77), channel_id=1, source_target_pairs={{0,1},{1,2},{2,3},{3,0},{4,5},{5,6},{6,7},{7,4},{8,9},{9,10},{10,1... | collective-permute-start | bytes 758792 | tf_op jit(solution)/shard_map/ppermute | solution.py:32
  151.1 9.8 %collective-permute-start.26 = (bf16[52,2432]{1,0:T(8,128)(2,1)S(1)}, bf16[52,2432]{1,0:T(8,128)(2,1)S(1)}, u32[]{:S(2)}, u32[]{:S(2)}) collective-permute-start(bf16[52,2432]{1,0:T(8,128)(2,1)S(1)} %get-tuple-element.80.refs_0_), channel_id=1, source_target_pairs={{0,1},{1,2},{2,3},{3,0},{4,5},{5,6},{6,7},{7,4},{8,9},{9,10},{10,1... | collective-permute-start | bytes 758792 | tf_op jit(solution)/shard_map/ppermute | solution.py:32
  151.2 9.7 %collective-permute-start.25 = (bf16[52,2432]{1,0:T(8,128)(2,1)S(1)}, bf16[52,2432]{1,0:T(8,128)(2,1)S(1)}, u32[]{:S(2)}, u32[]{:S(2)}) collective-permute-start(bf16[52,2432]{1,0:T(8,128)(2,1)S(1)} %get-tuple-element.80.refs_0_), channel_id=1, source_target_pairs={{0,2},{1,3},{2,0},{3,1},{4,6},{5,7},{6,4},{7,5},{8,10},{9,11},{10,... | collective-permute-start | bytes 758792 | tf_op jit(solution)/shard_map/ppermute | solution.py:32
  153.0 8.6 %collective-permute-start.24 = (bf16[52,2432]{1,0:T(8,128)(2,1)S(1)}, bf16[52,2432]{1,0:T(8,128)(2,1)S(1)}, u32[]{:S(2)}, u32[]{:S(2)}) collective-permute-start(bf16[52,2432]{1,0:T(8,128)(2,1)S(1)} %get-tuple-element.80.refs_0_), channel_id=1, source_target_pairs={{0,3},{1,0},{2,1},{3,2},{4,7},{5,4},{6,5},{7,6},{8,11},{9,8},{10,9... | collective-permute-start | bytes 758792 | tf_op jit(solution)/shard_map/ppermute | solution.py:32
  161.7 25.7 %collective-permute-start.29 = (bf16[208,2432]{1,0:T(8,128)(2,1)S(1)}, bf16[208,2432]{1,0:T(8,128)(2,1)S(1)}, u32[]{:S(2)}, u32[]{:S(2)}) collective-permute-start(bf16[208,2432]{1,0:T(8,128)(2,1)S(1)} %shard_map.175.refs_0_), channel_id=1, source_target_pairs={{0,4},{1,5},{2,6},{3,7},{4,8},{5,9},{6,10},{7,11},{8,12},{9,13},{1... | collective-permute-start | bytes 3035144 | tf_op jit(solution)/shard_map/ppermute | solution.py:32
  161.8 25.6 %collective-permute-start.28 = (bf16[208,2432]{1,0:T(8,128)(2,1)S(1)}, bf16[208,2432]{1,0:T(8,128)(2,1)S(1)}, u32[]{:S(2)}, u32[]{:S(2)}) collective-permute-start(bf16[208,2432]{1,0:T(8,128)(2,1)S(1)} %shard_map.175.refs_0_), channel_id=1, source_target_pairs={{0,8},{1,9},{2,10},{3,11},{4,12},{5,13},{6,14},{7,15},{8,0},{9,1},... | collective-permute-start | bytes 3035144 | tf_op jit(solution)/shard_map/ppermute | solution.py:32
  163.3 24.8 %collective-permute-start.27 = (bf16[208,2432]{1,0:T(8,128)(2,1)S(1)}, bf16[208,2432]{1,0:T(8,128)(2,1)S(1)}, u32[]{:S(2)}, u32[]{:S(2)}) collective-permute-start(bf16[208,2432]{1,0:T(8,128)(2,1)S(1)} %shard_map.175.refs_0_), channel_id=1, source_target_pairs={{0,12},{1,13},{2,14},{3,15},{4,0},{5,1},{6,2},{7,3},{8,4},{9,5},{1... | collective-permute-start | bytes 3035144 | tf_op jit(solution)/shard_map/ppermute | solution.py:32
  164.4 2.7 %copy-start = (bf16[2,608,2432]{2,1,0:T(8,128)(2,1)S(1)}, bf16[2,608,2432]{2,1,0:T(8,128)(2,1)}, u32[]{:S(2)}) copy-start(bf16[2,608,2432]{2,1,0:T(8,128)(2,1)} %refs_4_.1) | copy-start | bytes 17743876
  194.5 24.3 %collective-permute-start.30 = (bf16[208,2432]{1,0:T(8,128)(2,1)S(1)}, bf16[208,2432]{1,0:T(8,128)(2,1)S(1)}, u32[]{:S(2)}, u32[]{:S(2)}) collective-permute-start(bf16[208,2432]{1,0:T(8,128)(2,1)S(1)} %get-tuple-element.81), channel_id=1, source_target_pairs={{0,12},{1,13},{2,14},{3,15},{4,0},{5,1},{6,2},{7,3},{8,4},{9,5},{1... | collective-permute-start | bytes 3035144 | tf_op jit(solution)/shard_map/ppermute | solution.py:32
  196.6 22.2 %collective-permute-start.31 = (bf16[208,2432]{1,0:T(8,128)(2,1)S(1)}, bf16[208,2432]{1,0:T(8,128)(2,1)S(1)}, u32[]{:S(2)}, u32[]{:S(2)}) collective-permute-start(bf16[208,2432]{1,0:T(8,128)(2,1)S(1)} %get-tuple-element.82), channel_id=1, source_target_pairs={{0,8},{1,9},{2,10},{3,11},{4,12},{5,13},{6,14},{7,15},{8,0},{9,1},... | collective-permute-start | bytes 3035144 | tf_op jit(solution)/shard_map/ppermute | solution.py:32
  196.6 25.6 %collective-permute-start.32 = (bf16[208,2432]{1,0:T(8,128)(2,1)S(1)}, bf16[208,2432]{1,0:T(8,128)(2,1)S(1)}, u32[]{:S(2)}, u32[]{:S(2)}) collective-permute-start(bf16[208,2432]{1,0:T(8,128)(2,1)S(1)} %get-tuple-element.83), channel_id=1, source_target_pairs={{0,4},{1,5},{2,6},{3,7},{4,8},{5,9},{6,10},{7,11},{8,12},{9,13},{1... | collective-permute-start | bytes 3035144 | tf_op jit(solution)/shard_map/ppermute | solution.py:32
  223.1 6.5 %collective-permute-start.36 = (bf16[20,2432]{1,0:T(8,128)(2,1)S(1)}, bf16[20,2432]{1,0:T(8,128)(2,1)S(1)}, u32[]{:S(2)}, u32[]{:S(2)}) collective-permute-start(bf16[20,2432]{1,0:T(8,128)(2,1)S(1)} %get-tuple-element.90), channel_id=1, source_target_pairs={{0,3},{1,0},{2,1},{3,2},{4,7},{5,4},{6,5},{7,6},{8,11},{9,8},{10,9... | collective-permute-start | bytes 291848 | tf_op jit(solution)/shard_map/ppermute | solution.py:32
  225.2 5.4 %collective-permute-start.37 = (bf16[20,2432]{1,0:T(8,128)(2,1)S(1)}, bf16[20,2432]{1,0:T(8,128)(2,1)S(1)}, u32[]{:S(2)}, u32[]{:S(2)}) collective-permute-start(bf16[20,2432]{1,0:T(8,128)(2,1)S(1)} %get-tuple-element.91), channel_id=1, source_target_pairs={{0,2},{1,3},{2,0},{3,1},{4,6},{5,7},{6,4},{7,5},{8,10},{9,11},{10,... | collective-permute-start | bytes 291848 | tf_op jit(solution)/shard_map/ppermute | solution.py:32
  225.2 6.2 %collective-permute-start.38 = (bf16[20,2432]{1,0:T(8,128)(2,1)S(1)}, bf16[20,2432]{1,0:T(8,128)(2,1)S(1)}, u32[]{:S(2)}, u32[]{:S(2)}) collective-permute-start(bf16[20,2432]{1,0:T(8,128)(2,1)S(1)} %get-tuple-element.92), channel_id=1, source_target_pairs={{0,1},{1,2},{2,3},{3,0},{4,5},{5,6},{6,7},{7,4},{8,9},{9,10},{10,1... | collective-permute-start | bytes 291848 | tf_op jit(solution)/shard_map/ppermute | solution.py:32
  225.8 21.0 %collective-permute-start.33 = (bf16[32,2432]{1,0:T(8,128)(2,1)S(1)}, bf16[32,2432]{1,0:T(8,128)(2,1)S(1)}, u32[]{:S(2)}, u32[]{:S(2)}) collective-permute-start(bf16[32,2432]{1,0:T(8,128)(2,1)S(1)} %get-tuple-element.85), channel_id=1, source_target_pairs={{0,3},{1,0},{2,1},{3,2},{4,7},{5,4},{6,5},{7,6},{8,11},{9,8},{10,9... | collective-permute-start | bytes 466952 | tf_op jit(solution)/shard_map/ppermute | solution.py:32
  227.9 19.0 %collective-permute-start.34 = (bf16[32,2432]{1,0:T(8,128)(2,1)S(1)}, bf16[32,2432]{1,0:T(8,128)(2,1)S(1)}, u32[]{:S(2)}, u32[]{:S(2)}) collective-permute-start(bf16[32,2432]{1,0:T(8,128)(2,1)S(1)} %get-tuple-element.86), channel_id=1, source_target_pairs={{0,2},{1,3},{2,0},{3,1},{4,6},{5,7},{6,4},{7,5},{8,10},{9,11},{10,... | collective-permute-start | bytes 466952 | tf_op jit(solution)/shard_map/ppermute | solution.py:32
  229.6 17.3 %collective-permute-start.35 = (bf16[32,2432]{1,0:T(8,128)(2,1)S(1)}, bf16[32,2432]{1,0:T(8,128)(2,1)S(1)}, u32[]{:S(2)}, u32[]{:S(2)}) collective-permute-start(bf16[32,2432]{1,0:T(8,128)(2,1)S(1)} %get-tuple-element.87), channel_id=1, source_target_pairs={{0,1},{1,2},{2,3},{3,0},{4,5},{5,6},{6,7},{7,4},{8,9},{9,10},{10,1... | collective-permute-start | bytes 466952 | tf_op jit(solution)/shard_map/ppermute | solution.py:32
  232.3 20.1 %all-to-all-start.3 = ((bf16[8,4,2432]{2,1,0:T(4,128)(2,1)}), bf16[8,4,2432]{2,1,0:T(4,128)(2,1)S(1)}, u32[]{:S(2)}, u32[]{:S(2)}) async-start(bf16[8,4,2432]{2,1,0:T(4,128)(2,1)} %shard_map.180), calls=%async_computation.3 | async-start | bytes 311296 | tf_op jit(solution)/shard_map/all_to_all | solution.py:701
  (6 other events, 4.8 us)

commit v8 on v7

--- a/solution.py
+++ b/solution.py
@@ -609,6 +609,7 @@
         mod_pair_kernel,
         like((8, 8, width), F32),
         (mod_own, chip_swap(mod_own, False)),
+        after=(embed_parts[0],),
     )
     row_mod = run(
         row_mod_kernel,

time: 254 us -> 254 us (level)
    unnamed x56 -> x52, local copies, waits for them, and re-layouts: 14.8 us -> 12.9 us
  transfers between devices with their start and end apart: 42 -> 42, of which waited for: 24 -> 25; matrix products, arithmetic and copies ran while one was open for 0% -> 0% of each run, Pallas kernels for 8% -> 8%
where the time goes in v8:
time: 254 us; the launch traced here: 253 us
  waiting for transfers between devices  119 us (47%)
  starting transfers between devices  74.9 us (29%)
  Pallas kernels  34.3 us (14%)
  local copies, waits for them, and re-layouts  13.6 us (5%)
  blocking collectives  9.53 us (4%)
    ppermute x36, waiting for transfers between devices, torus_shift(): return lax.ppermute(values, ('grp', 'tp'), pairs)  109 us
    ppermute x36, starting transfers between devices, torus_shift(): return lax.ppermute(values, ('grp', 'tp'), pairs)  37.9 us
    pallas_call x23, Pallas kernels, run(): pl.pallas_call(body, out_shape=shapes, in_specs=specs, out_specs=[pl.Bloc...  34.3 us
    all_to_all x1, starting transfers between devices, shards(): placed = lax.all_to_all(placed, 'grp', 0, 0, tiled=True)  14.5 us
    unnamed x52, local copies, waits for them, and re-layouts  12.9 us
    all_to_all x1, starting transfers between devices, shards(): lax.all_to_all(slot_parts.reshape(8, 64, 512), 'grp', 0, 0, tiled=True)  9.9 us
    all_to_all x1, blocking collectives, shards(): lax.all_to_all(att_parts, 'grp', 0, 0, tiled=True).reshape(512, 128)  9.53 us
    all_to_all x1, starting transfers between devices, shards(): arrived = lax.all_to_all(outgoing, 'tp', 0, 0, tiled=True)  7.85 us
  transfers between devices with their start and end apart: 42, of which 25 were waited for; matrix products, arithmetic and copies ran while one was open for 0% of the time, Pallas kernels for 8%

profile of v8, /device:TPU:1, one launch (start us, length us, event | category | flops | bytes accessed | tf_op | source)
XLA Modules:
  0.0 253.1 jit_solution(4363280031744372137)
XLA Ops:
  0.6 0.9 copy-done.14
  2.2 0.9 shard_map.158
  3.1 0.9 copy-done.4
  4.1 1.5 collective-permute-start
  5.6 7.9 %all-to-all-start = ((bf16[16,32,256]{2,1,0:T(8,128)(2,1)}), bf16[16,32,256]{2,1,0:T(8,128)(2,1)S(1)}, u32[]{:S(2)}, u32[]{:S(2)}) async-start(bf16[16,32,256]{2,1,0:T(8,128)(2,1)} %get-tuple-element.48.refs_6_.refs_1_), calls=%async_computation | async-start | bytes 524288 | tf_op jit(solution)/shard_map/all_to_all | solution.py:552
  13.5 1.3 collective-permute-start.7
  15.5 7.8 %shard_map.159 = (f32[512,384]{1,0:T(8,128)}, bf16[16,32,192]{2,1,0:T(8,128)(2,1)}, bf16[32,2432]{1,0:T(8,128)(2,1)}, f32[6,2432]{1,0:T(8,128)}) custom-call(s32[2]{0:T(128)} %refs_0_.5, s32[1]{0:T(128)} %bitcast.refs_1_, bf16[512,2432]{1,0:T(8,128)(2,1)} %refs_2_.4, f32[2,6,2,2432]{3,2,1,0:T(2,128)} %bitcast.33, bf16[3,2432,128]{2,1,0:T(8,128)(2,1)} %bitcast.38, ...), custom_call_target="tpu_custom_call" | custom-call | flops 1434451968 | bytes 7656460 | tf_op jit(solution)/shard_map/pallas_call | solution.py:80
  23.3 0.9 copy-done.13
  24.3 1.4 shard_map.162
  25.8 1.9 collective-permute-start.8
  27.7 2.6 %collective-permute-start.1 = (bf16[80,2944]{1,0:T(8,128)(2,1)S(1)}, bf16[80,2944]{1,0:T(8,128)(2,1)S(1)}, u32[]{:S(2)}, u32[]{:S(2)}) collective-permute-start(bf16[80,2944]{1,0:T(8,128)(2,1)S(1)} %get-tuple-element.52), channel_id=1, source_target_pairs={{0,12},{1,13},{2,14},{3,15},{4,0},{5,1},{6,2},{7,3},{8,4},{9,5},{1... | collective-permute-start | bytes 1413128 | tf_op jit(solution)/shard_map/ppermute | solution.py:32
  31.4 9.5 %collective-permute-done.1.refs_1_ = bf16[80,2944]{1,0:T(8,128)(2,1)S(1)} collective-permute-done((bf16[80,2944]{1,0:T(8,128)(2,1)S(1)}, bf16[80,2944]{1,0:T(8,128)(2,1)S(1)}, u32[]{:S(2)}, u32[]{:S(2)}) %collective-permute-start.1) | collective-permute-done | bytes 471072 | tf_op jit(solution)/shard_map/ppermute | solution.py:32
  40.9 3.7 %collective-permute-done.3.refs_3_ = bf16[80,2944]{1,0:T(8,128)(2,1)S(1)} collective-permute-done((bf16[80,2944]{1,0:T(8,128)(2,1)S(1)}, bf16[80,2944]{1,0:T(8,128)(2,1)S(1)}, u32[]{:S(2)}, u32[]{:S(2)}) %collective-permute-start.3) | collective-permute-done | bytes 471072 | tf_op jit(solution)/shard_map/ppermute | solution.py:32
  45.0 2.2 collective-permute-start.4
  48.3 1.0 shard_map.165.refs_4_.refs_7_.refs_5_
  49.4 1.4 collective-permute-done.4.refs_1_
  50.7 2.0 collective-permute-done.5.refs_2_
  52.7 1.4 collective-permute-done.6.refs_3_
  54.5 1.5 collective-permute-start.10
  56.0 1.2 collective-permute-start.9
  57.2 4.0 %collective-permute-done.11.refs_3_ = bf16[20,2944]{1,0:T(8,128)(2,1)S(1)} collective-permute-done((bf16[20,2944]{1,0:T(8,128)(2,1)S(1)}, bf16[20,2944]{1,0:T(8,128)(2,1)S(1)}, u32[]{:S(2)}, u32[]{:S(2)}) %collective-permute-start.11) | collective-permute-done | bytes 117792 | tf_op jit(solution)/shard_map/ppermute | solution.py:32
  62.0 2.4 collective-permute-start.13
  65.3 10.7 %collective-permute-done.14.refs_4_ = bf16[80,2944]{1,0:T(8,128)(2,1)S(1)} collective-permute-done((bf16[80,2944]{1,0:T(8,128)(2,1)S(1)}, bf16[80,2944]{1,0:T(8,128)(2,1)S(1)}, u32[]{:S(2)}, u32[]{:S(2)}) %collective-permute-start.14) | collective-permute-done | bytes 471072 | tf_op jit(solution)/shard_map/ppermute | solution.py:32
  76.0 0.9 collective-permute-done.12.refs_2_
  77.0 2.2 shard_map.168
  80.8 9.9 %all-to-all-start.1 = ((bf16[8,64,512]{2,1,0:T(8,128)(2,1)}), bf16[8,64,512]{2,1,0:T(8,128)(2,1)S(1)}, u32[]{:S(2)}, u32[]{:S(2)}) async-start(bf16[8,64,512]{2,1,0:T(8,128)(2,1)} %bitcast.36), calls=%async_computation.1 | async-start | bytes 1048576 | tf_op jit(solution)/shard_map/all_to_all | solution.py:649
  90.7 1.1 copy-done.5
  91.8 1.0 copy-done.9
  92.9 1.5 shard_map.169.refs_1_
  95.2 5.0 %all-to-all-done.1.refs_2_ = bf16[8,64,512]{2,1,0:T(8,128)(2,1)S(1)} async-done(((bf16[8,64,512]{2,1,0:T(8,128)(2,1)}), bf16[8,64,512]{2,1,0:T(8,128)(2,1)S(1)}, u32[]{:S(2)}, u32[]{:S(2)}) %all-to-all-start.1) | async-done | bytes 524320 | tf_op jit(solution)/shard_map/all_to_all | solution.py:649
  100.2 1.0 copy-done.11
  101.2 1.1 copy-done.22
  102.3 2.5 shard_map.170
  104.8 2.4 collective-permute-start.15
  107.9 1.1 shard_map.171
  109.0 9.5 %all_to_all.20 = bf16[8,64,128]{2,1,0:T(8,128)(2,1)S(1)} all-to-all(bf16[8,64,128]{2,1,0:T(8,128)(2,1)S(1)} %shard_map.171), channel_id=1, replica_groups=mesh['grp'=8,'tp'=16] {'grp'}, dimensions={0} | all-to-all | bytes 262144 | tf_op jit(solution)/shard_map/all_to_all | solution.py:666
  118.5 2.5 collective-permute-done.15.refs_3_.refs_1_
  121.0 0.9 shard_map.172
  121.9 3.5 %collective-permute-start.18 = (bf16[80,2432]{1,0:T(8,128)(2,1)S(1)}, bf16[80,2432]{1,0:T(8,128)(2,1)S(1)}, u32[]{:S(2)}, u32[]{:S(2)}) collective-permute-start(bf16[80,2432]{1,0:T(8,128)(2,1)S(1)} %get-tuple-element.71), channel_id=1, source_target_pairs={{0,12},{1,13},{2,14},{3,15},{4,0},{5,1},{6,2},{7,3},{8,4},{9,5},{1... | collective-permute-start | bytes 1167368 | tf_op jit(solution)/shard_map/ppermute | solution.py:32
  126.1 8.2 %collective-permute-done.18.refs_5_ = bf16[80,2432]{1,0:T(8,128)(2,1)S(1)} collective-permute-done((bf16[80,2432]{1,0:T(8,128)(2,1)S(1)}, bf16[80,2432]{1,0:T(8,128)(2,1)S(1)}, u32[]{:S(2)}, u32[]{:S(2)}) %collective-permute-start.18) | collective-permute-done | bytes 389152 | tf_op jit(solution)/shard_map/ppermute | solution.py:32
  134.3 3.4 %collective-permute-done.20.refs_7_ = bf16[80,2432]{1,0:T(8,128)(2,1)S(1)} collective-permute-done((bf16[80,2432]{1,0:T(8,128)(2,1)S(1)}, bf16[80,2432]{1,0:T(8,128)(2,1)S(1)}, u32[]{:S(2)}, u32[]{:S(2)}) %collective-permute-start.20) | collective-permute-done | bytes 389152 | tf_op jit(solution)/shard_map/ppermute | solution.py:32
  138.6 2.3 collective-permute-start.21
  141.5 5.7 %collective-permute-done.21.refs_3_ = bf16[52,2432]{1,0:T(8,128)(2,1)S(1)} collective-permute-done((bf16[52,2432]{1,0:T(8,128)(2,1)S(1)}, bf16[52,2432]{1,0:T(8,128)(2,1)S(1)}, u32[]{:S(2)}, u32[]{:S(2)}) %collective-permute-start.21) | collective-permute-done | bytes 252960 | tf_op jit(solution)/shard_map/ppermute | solution.py:32
  147.8 2.8 %collective-permute-done.23.refs_5_ = bf16[52,2432]{1,0:T(8,128)(2,1)S(1)} collective-permute-done((bf16[52,2432]{1,0:T(8,128)(2,1)S(1)}, bf16[52,2432]{1,0:T(8,128)(2,1)S(1)}, u32[]{:S(2)}, u32[]{:S(2)}) %collective-permute-start.23) | collective-permute-done | bytes 252960 | tf_op jit(solution)/shard_map/ppermute | solution.py:32
  151.2 1.8 collective-permute-start.25
  153.0 0.9 collective-permute-start.24
  153.9 7.1 %collective-permute-done.26.refs_3_ = bf16[52,2432]{1,0:T(8,128)(2,1)S(1)} collective-permute-done((bf16[52,2432]{1,0:T(8,128)(2,1)S(1)}, bf16[52,2432]{1,0:T(8,128)(2,1)S(1)}, u32[]{:S(2)}, u32[]{:S(2)}) %collective-permute-start.26) | collective-permute-done | bytes 252960 | tf_op jit(solution)/shard_map/ppermute | solution.py:32
  161.8 1.5 collective-permute-start.28
  163.3 1.1 collective-permute-start.27
  164.5 2.7 %copy-done = bf16[2,608,2432]{2,1,0:T(8,128)(2,1)S(1)} copy-done((bf16[2,608,2432]{2,1,0:T(8,128)(2,1)S(1)}, bf16[2,608,2432]{2,1,0:T(8,128)(2,1)}, u32[]{:S(2)}) %copy-start) | copy-done | bytes 5914648
  167.2 3.4 %shard_map.176.refs_5_.refs_0_ = bf16[208,2432]{1,0:T(8,128)(2,1)S(1)} custom-call(bf16[208,2432]{1,0:T(8,128)(2,1)S(1)} %shard_map.175.refs_0_, bf16[2,608,2432]{2,1,0:T(8,128)(2,1)S(1)} %bitcast.30, bf16[2,608,2432]{2,1,0:T(8,128)(2,1)S(1)} %copy-done), custom_call_target="tpu_custom_call" | custom-call | flops 1230241792 | bytes 13852672 | tf_op jit(solution)/shard_map/pallas_call | solution.py:80
  170.5 16.8 %collective-permute-done.29.refs_2_ = bf16[208,2432]{1,0:T(8,128)(2,1)S(1)} collective-permute-done((bf16[208,2432]{1,0:T(8,128)(2,1)S(1)}, bf16[208,2432]{1,0:T(8,128)(2,1)S(1)}, u32[]{:S(2)}, u32[]{:S(2)}) %collective-permute-start.29) | collective-permute-done | bytes 1011744 | tf_op jit(solution)/shard_map/ppermute | solution.py:32
  188.1 6.5 %shard_map.177 = (bf16[208,2432]{1,0:T(8,128)(2,1)S(1)}, bf16[208,2432]{1,0:T(8,128)(2,1)S(1)}, bf16[208,2432]{1,0:T(8,128)(2,1)S(1)}) custom-call(bf16[208,2432]{1,0:T(8,128)(2,1)S(1)} %collective-permute-done.27.refs_0_, bf16[208,2432]{1,0:T(8,128)(2,1)S(1)} %collective-permute-done.28.refs_1_, bf16[208,2432]{1,0:T(8,128)(2,1)S(1)} %collective-permute-done.29.refs_2_, ...), custom_call_target="tpu_custom_call" | custom-call | flops 3690725376 | bytes 17899520 | tf_op jit(solution)/shard_map/pallas_call | solution.py:80
  194.5 2.1 collective-permute-start.30
  197.3 21.5 %collective-permute-done.30.refs_1_ = bf16[208,2432]{1,0:T(8,128)(2,1)S(1)} collective-permute-done((bf16[208,2432]{1,0:T(8,128)(2,1)S(1)}, bf16[208,2432]{1,0:T(8,128)(2,1)S(1)}, u32[]{:S(2)}, u32[]{:S(2)}) %collective-permute-start.30) | collective-permute-done | bytes 1011744 | tf_op jit(solution)/shard_map/ppermute | solution.py:32
  218.8 3.4 %collective-permute-done.32.refs_3_ = bf16[208,2432]{1,0:T(8,128)(2,1)S(1)} collective-permute-done((bf16[208,2432]{1,0:T(8,128)(2,1)S(1)}, bf16[208,2432]{1,0:T(8,128)(2,1)S(1)}, u32[]{:S(2)}, u32[]{:S(2)}) %collective-permute-start.32) | collective-permute-done | bytes 1011744 | tf_op jit(solution)/shard_map/ppermute | solution.py:32
  222.2 0.9 shard_map.178
  223.1 2.1 collective-permute-start.36
  225.9 2.0 collective-permute-start.33
  227.9 1.8 collective-permute-start.34
  229.7 1.0 collective-permute-done.37.refs_3_
  231.4 0.9 shard_map.180
  232.4 14.5 %all-to-all-start.3 = ((bf16[8,4,2432]{2,1,0:T(4,128)(2,1)}), bf16[8,4,2432]{2,1,0:T(4,128)(2,1)S(1)}, u32[]{:S(2)}, u32[]{:S(2)}) async-start(bf16[8,4,2432]{2,1,0:T(4,128)(2,1)} %shard_map.180), calls=%async_computation.3 | async-start | bytes 311296 | tf_op jit(solution)/shard_map/all_to_all | solution.py:702
  247.7 4.7 %all-to-all-done.3 = bf16[8,4,2432]{2,1,0:T(4,128)(2,1)S(1)} async-done(((bf16[8,4,2432]{2,1,0:T(4,128)(2,1)}), bf16[8,4,2432]{2,1,0:T(4,128)(2,1)S(1)}, u32[]{:S(2)}, u32[]{:S(2)}) %all-to-all-start.3) | async-done | bytes 155680 | tf_op jit(solution)/shard_map/all_to_all | solution.py:702
  (101 shorter events, 17.9 us)
Async XLA Ops:
  0.6 14.2 %copy-start.20 = (s32[20,1]{0,1:T(1,128)S(1)}, s32[20,1]{0,1:T(1,128)}, u32[]{:S(2)}) copy-start(s32[20,1]{0,1:T(1,128)} %param.17) | copy-start | bytes 244
  0.6 0.9 copy-start.14
  3.1 0.9 copy-start.4
  4.1 9.4 %collective-permute-start = (f32[2,8,2432]{2,1,0:T(8,128)S(1)}, f32[2,8,2432]{2,1,0:T(8,128)S(1)}, u32[]{:S(2)}, u32[]{:S(2)}) collective-permute-start(f32[2,8,2432]{2,1,0:T(8,128)S(1)} %shard_map.160.refs_0_), channel_id=1, source_target_pairs={{0,16},{16,0},{32,48},{48,32},{64,80},{80,64},{96,112},{112,96},{1... | collective-permute-start | bytes 466952 | tf_op jit(solution)/shard_map/ppermute | solution.py:36
  5.6 17.7 %all-to-all-start = ((bf16[16,32,256]{2,1,0:T(8,128)(2,1)}), bf16[16,32,256]{2,1,0:T(8,128)(2,1)S(1)}, u32[]{:S(2)}, u32[]{:S(2)}) async-start(bf16[16,32,256]{2,1,0:T(8,128)(2,1)} %get-tuple-element.48.refs_6_.refs_1_), calls=%async_computation | async-start | bytes 524288 | tf_op jit(solution)/shard_map/all_to_all | solution.py:552
  13.5 12.2 %collective-permute-start.7 = (f32[4,8,2432]{2,1,0:T(8,128)S(1)}, f32[4,8,2432]{2,1,0:T(8,128)S(1)}, u32[]{:S(2)}, u32[]{:S(2)}) collective-permute-start(f32[4,8,2432]{2,1,0:T(8,128)S(1)} %shard_map.161.refs_4_.refs_0_), channel_id=1, source_target_pairs={{0,32},{16,48},{32,0},{48,16},{64,96},{80,112},{96,64},{112,80},{1... | collective-permute-start | bytes 933896 | tf_op jit(solution)/shard_map/ppermute | solution.py:44
  15.4 7.9 %copy-start.3 = (bf16[256,2432]{1,0:T(8,128)(2,1)S(1)}, bf16[256,2432]{1,0:T(8,128)(2,1)}, u32[]{:S(2)}) copy-start(bf16[256,2432]{1,0:T(8,128)(2,1)} %refs_2_.5) | copy-start | bytes 3735556
  23.3 1.0 copy-start.13
  25.7 22.6 %copy-start.18 = (s32[20]{0:T(128)S(1)}, s32[20]{0:T(128)}, u32[]{:S(2)}) copy-start(s32[20]{0:T(128)} %fusion.3.refs_7_.refs_0_) | copy-start | bytes 244
  25.8 22.5 %collective-permute-start.8 = (f32[8,8,2432]{2,1,0:T(8,128)S(1)}, f32[8,8,2432]{2,1,0:T(8,128)S(1)}, u32[]{:S(2)}, u32[]{:S(2)}) collective-permute-start(f32[8,8,2432]{2,1,0:T(8,128)S(1)} %shard_map.164.refs_1_), channel_id=1, source_target_pairs={{0,96},{16,112},{32,64},{48,80},{64,32},{80,48},{96,0},{112,16},{1... | collective-permute-start | bytes 1867784 | tf_op jit(solution)/shard_map/ppermute | solution.py:44
  27.7 13.2 %collective-permute-start.1 = (bf16[80,2944]{1,0:T(8,128)(2,1)S(1)}, bf16[80,2944]{1,0:T(8,128)(2,1)S(1)}, u32[]{:S(2)}, u32[]{:S(2)}) collective-permute-start(bf16[80,2944]{1,0:T(8,128)(2,1)S(1)} %get-tuple-element.52), channel_id=1, source_target_pairs={{0,12},{1,13},{2,14},{3,15},{4,0},{5,1},{6,2},{7,3},{8,4},{9,5},{1... | collective-permute-start | bytes 1413128 | tf_op jit(solution)/shard_map/ppermute | solution.py:32
  30.2 10.6 %collective-permute-start.2 = (bf16[80,2944]{1,0:T(8,128)(2,1)S(1)}, bf16[80,2944]{1,0:T(8,128)(2,1)S(1)}, u32[]{:S(2)}, u32[]{:S(2)}) collective-permute-start(bf16[80,2944]{1,0:T(8,128)(2,1)S(1)} %get-tuple-element.53), channel_id=1, source_target_pairs={{0,8},{1,9},{2,10},{3,11},{4,12},{5,13},{6,14},{7,15},{8,0},{9,1},... | collective-permute-start | bytes 1413128 | tf_op jit(solution)/shard_map/ppermute | solution.py:32
  30.8 13.7 %collective-permute-start.3 = (bf16[80,2944]{1,0:T(8,128)(2,1)S(1)}, bf16[80,2944]{1,0:T(8,128)(2,1)S(1)}, u32[]{:S(2)}, u32[]{:S(2)}) collective-permute-start(bf16[80,2944]{1,0:T(8,128)(2,1)S(1)} %get-tuple-element.54), channel_id=1, source_target_pairs={{0,4},{1,5},{2,6},{3,7},{4,8},{5,9},{6,10},{7,11},{8,12},{9,13},{1... | collective-permute-start | bytes 1413128 | tf_op jit(solution)/shard_map/ppermute | solution.py:32
  45.0 5.7 %collective-permute-start.4 = (bf16[20,2944]{1,0:T(8,128)(2,1)S(1)}, bf16[20,2944]{1,0:T(8,128)(2,1)S(1)}, u32[]{:S(2)}, u32[]{:S(2)}) collective-permute-start(bf16[20,2944]{1,0:T(8,128)(2,1)S(1)} %get-tuple-element.56), channel_id=1, source_target_pairs={{0,3},{1,0},{2,1},{3,2},{4,7},{5,4},{6,5},{7,6},{8,11},{9,8},{10,9... | collective-permute-start | bytes 353288 | tf_op jit(solution)/shard_map/ppermute | solution.py:32
  47.2 5.5 %collective-permute-start.5 = (bf16[20,2944]{1,0:T(8,128)(2,1)S(1)}, bf16[20,2944]{1,0:T(8,128)(2,1)S(1)}, u32[]{:S(2)}, u32[]{:S(2)}) collective-permute-start(bf16[20,2944]{1,0:T(8,128)(2,1)S(1)} %get-tuple-element.57), channel_id=1, source_target_pairs={{0,2},{1,3},{2,0},{3,1},{4,6},{5,7},{6,4},{7,5},{8,10},{9,11},{10,... | collective-permute-start | bytes 353288 | tf_op jit(solution)/shard_map/ppermute | solution.py:32
  47.8 6.4 %collective-permute-start.6 = (bf16[20,2944]{1,0:T(8,128)(2,1)S(1)}, bf16[20,2944]{1,0:T(8,128)(2,1)S(1)}, u32[]{:S(2)}, u32[]{:S(2)}) collective-permute-start(bf16[20,2944]{1,0:T(8,128)(2,1)S(1)} %get-tuple-element.58), channel_id=1, source_target_pairs={{0,1},{1,2},{2,3},{3,0},{4,5},{5,6},{6,7},{7,4},{8,9},{9,10},{10,1... | collective-permute-start | bytes 353288 | tf_op jit(solution)/shard_map/ppermute | solution.py:32
  49.3 15.9 %copy-start.23 = (f32[2,2,64]{2,1,0:T(2,128)S(1)}, f32[2,2,64]{2,1,0:T(2,128)}, u32[]{:S(2)}) copy-start(f32[2,2,64]{2,1,0:T(2,128)} %param.20) | copy-start | bytes 3076
  49.3 27.6 %copy-start.1 = (bf16[2432,3,128]{2,0,1:T(8,128)(2,1)S(1)}, bf16[2432,3,128]{2,0,1:T(8,128)(2,1)}, u32[]{:S(2)}) copy-start(bf16[2432,3,128]{2,0,1:T(8,128)(2,1)} %param.23) | copy-start | bytes 5603332
  54.4 7.6 %copy-start.16 = (bf16[20,2432]{1,0:T(8,128)(2,1)}, bf16[20,2432]{1,0:T(8,128)(2,1)S(1)}, u32[]{:S(2)}) copy-start(bf16[20,2432]{1,0:T(8,128)(2,1)S(1)} %get-tuple-element.59.refs_1_) | copy-start | bytes 291844
  54.5 6.7 %collective-permute-start.11 = (bf16[20,2944]{1,0:T(8,128)(2,1)S(1)}, bf16[20,2944]{1,0:T(8,128)(2,1)S(1)}, u32[]{:S(2)}, u32[]{:S(2)}) collective-permute-start(bf16[20,2944]{1,0:T(8,128)(2,1)S(1)} %get-tuple-element.60.refs_0_), channel_id=1, source_target_pairs={{0,1},{1,2},{2,3},{3,0},{4,5},{5,6},{6,7},{7,4},{8,9},{9,10},{10,1... | collective-permute-start | bytes 353288 | tf_op jit(solution)/shard_map/ppermute | solution.py:32
  54.5 6.6 %collective-permute-start.10 = (bf16[20,2944]{1,0:T(8,128)(2,1)S(1)}, bf16[20,2944]{1,0:T(8,128)(2,1)S(1)}, u32[]{:S(2)}, u32[]{:S(2)}) collective-permute-start(bf16[20,2944]{1,0:T(8,128)(2,1)S(1)} %get-tuple-element.60.refs_0_), channel_id=1, source_target_pairs={{0,2},{1,3},{2,0},{3,1},{4,6},{5,7},{6,4},{7,5},{8,10},{9,11},{10,... | collective-permute-start | bytes 353288 | tf_op jit(solution)/shard_map/ppermute | solution.py:32
  56.0 5.8 %collective-permute-start.9 = (bf16[20,2944]{1,0:T(8,128)(2,1)S(1)}, bf16[20,2944]{1,0:T(8,128)(2,1)S(1)}, u32[]{:S(2)}, u32[]{:S(2)}) collective-permute-start(bf16[20,2944]{1,0:T(8,128)(2,1)S(1)} %get-tuple-element.60.refs_0_), channel_id=1, source_target_pairs={{0,3},{1,0},{2,1},{3,2},{4,7},{5,4},{6,5},{7,6},{8,11},{9,8},{10,9... | collective-permute-start | bytes 353288 | tf_op jit(solution)/shard_map/ppermute | solution.py:32
  61.9 14.1 %collective-permute-start.14 = (bf16[80,2944]{1,0:T(8,128)(2,1)S(1)}, bf16[80,2944]{1,0:T(8,128)(2,1)S(1)}, u32[]{:S(2)}, u32[]{:S(2)}) collective-permute-start(bf16[80,2944]{1,0:T(8,128)(2,1)S(1)} %shard_map.167.refs_1_), channel_id=1, source_target_pairs={{0,4},{1,5},{2,6},{3,7},{4,8},{5,9},{6,10},{7,11},{8,12},{9,13},{1... | collective-permute-start | bytes 1413128 | tf_op jit(solution)/shard_map/ppermute | solution.py:32
  62.0 14.0 %collective-permute-start.13 = (bf16[80,2944]{1,0:T(8,128)(2,1)S(1)}, bf16[80,2944]{1,0:T(8,128)(2,1)S(1)}, u32[]{:S(2)}, u32[]{:S(2)}) collective-permute-start(bf16[80,2944]{1,0:T(8,128)(2,1)S(1)} %shard_map.167.refs_1_), channel_id=1, source_target_pairs={{0,8},{1,9},{2,10},{3,11},{4,12},{5,13},{6,14},{7,15},{8,0},{9,1},... | collective-permute-start | bytes 1413128 | tf_op jit(solution)/shard_map/ppermute | solution.py:32
  64.4 12.6 %collective-permute-start.12 = (bf16[80,2944]{1,0:T(8,128)(2,1)S(1)}, bf16[80,2944]{1,0:T(8,128)(2,1)S(1)}, u32[]{:S(2)}, u32[]{:S(2)}) collective-permute-start(bf16[80,2944]{1,0:T(8,128)(2,1)S(1)} %shard_map.167.refs_1_), channel_id=1, source_target_pairs={{0,12},{1,13},{2,14},{3,15},{4,0},{5,1},{6,2},{7,3},{8,4},{9,5},{1... | collective-permute-start | bytes 1413128 | tf_op jit(solution)/shard_map/ppermute | solution.py:32
  77.0 13.7 %copy-start.2 = (bf16[32,3,64,128]{3,2,1,0:T(8,128)(2,1)S(1)}, bf16[32,3,64,128]{3,2,1,0:T(8,128)(2,1)}, u32[]{:S(2)}) copy-start(bf16[32,3,64,128]{3,2,1,0:T(8,128)(2,1)} %refs_3_.2) | copy-start | bytes 4718596
  77.0 13.7 %copy-start.21 = (s32[2]{0:T(128)S(1)}, s32[2]{0:T(128)}, u32[]{:S(2)}) copy-start(s32[2]{0:T(128)} %refs_0_.5) | copy-start | bytes 28
  80.8 19.4 %all-to-all-start.1 = ((bf16[8,64,512]{2,1,0:T(8,128)(2,1)}), bf16[8,64,512]{2,1,0:T(8,128)(2,1)S(1)}, u32[]{:S(2)}, u32[]{:S(2)}) async-start(bf16[8,64,512]{2,1,0:T(8,128)(2,1)} %bitcast.36), calls=%async_computation.1 | async-start | bytes 1048576 | tf_op jit(solution)/shard_map/all_to_all | solution.py:649
  90.7 1.1 copy-start.5
  91.8 1.0 copy-start.9
  100.2 1.0 copy-start.11
  101.2 1.1 copy-start.22
  104.8 16.2 %copy-start.6 = (bf16[128,2432]{1,0:T(8,128)(2,1)S(1)}, bf16[128,2432]{1,0:T(8,128)(2,1)}, u32[]{:S(2)}) copy-start(bf16[128,2432]{1,0:T(8,128)(2,1)} %refs_2_.6) | copy-start | bytes 1867780
  104.8 16.2 %collective-permute-start.15 = (bf16[128,2432]{1,0:T(8,128)(2,1)S(1)}, bf16[128,2432]{1,0:T(8,128)(2,1)S(1)}, u32[]{:S(2)}, u32[]{:S(2)}) collective-permute-start(bf16[128,2432]{1,0:T(8,128)(2,1)S(1)} %get-tuple-element.66), channel_id=1, source_target_pairs={{0,12},{1,13},{2,14},{3,15},{4,0},{5,1},{6,2},{7,3},{8,4},{9,5},{1... | collective-permute-start | bytes 1867784 | tf_op jit(solution)/shard_map/ppermute | solution.py:32
  107.2 18.9 %collective-permute-start.16 = (bf16[128,2432]{1,0:T(8,128)(2,1)S(1)}, bf16[128,2432]{1,0:T(8,128)(2,1)S(1)}, u32[]{:S(2)}, u32[]{:S(2)}) collective-permute-start(bf16[128,2432]{1,0:T(8,128)(2,1)S(1)} %get-tuple-element.67), channel_id=1, source_target_pairs={{0,8},{1,9},{2,10},{3,11},{4,12},{5,13},{6,14},{7,15},{8,0},{9,1},... | collective-permute-start | bytes 1867784 | tf_op jit(solution)/shard_map/ppermute | solution.py:32
  107.2 18.9 %collective-permute-start.17 = (bf16[128,2432]{1,0:T(8,128)(2,1)S(1)}, bf16[128,2432]{1,0:T(8,128)(2,1)S(1)}, u32[]{:S(2)}, u32[]{:S(2)}) collective-permute-start(bf16[128,2432]{1,0:T(8,128)(2,1)S(1)} %get-tuple-element.68), channel_id=1, source_target_pairs={{0,4},{1,5},{2,6},{3,7},{4,8},{5,9},{6,10},{7,11},{8,12},{9,13},{1... | collective-permute-start | bytes 1867784 | tf_op jit(solution)/shard_map/ppermute | solution.py:32
  107.9 56.6 %slice-start = ((s8[5914624]{0:T(1024)(128)(4,1)}), s8[4194304]{0:T(1024)(128)(4,1)S(1)}, s32[]{:S(2)}) async-start(s8[5914624]{0:T(1024)(128)(4,1)} %bitcast.28), calls=%async_computation.4 | async-start | bytes 8388608
  121.9 12.3 %collective-permute-start.18 = (bf16[80,2432]{1,0:T(8,128)(2,1)S(1)}, bf16[80,2432]{1,0:T(8,128)(2,1)S(1)}, u32[]{:S(2)}, u32[]{:S(2)}) collective-permute-start(bf16[80,2432]{1,0:T(8,128)(2,1)S(1)} %get-tuple-element.71), channel_id=1, source_target_pairs={{0,12},{1,13},{2,14},{3,15},{4,0},{5,1},{6,2},{7,3},{8,4},{9,5},{1... | collective-permute-start | bytes 1167368 | tf_op jit(solution)/shard_map/ppermute | solution.py:32
  125.4 8.8 %collective-permute-start.19 = (bf16[80,2432]{1,0:T(8,128)(2,1)S(1)}, bf16[80,2432]{1,0:T(8,128)(2,1)S(1)}, u32[]{:S(2)}, u32[]{:S(2)}) collective-permute-start(bf16[80,2432]{1,0:T(8,128)(2,1)S(1)} %get-tuple-element.72), channel_id=1, source_target_pairs={{0,8},{1,9},{2,10},{3,11},{4,12},{5,13},{6,14},{7,15},{8,0},{9,1},... | collective-permute-start | bytes 1167368 | tf_op jit(solution)/shard_map/ppermute | solution.py:32
  125.4 12.3 %collective-permute-start.20 = (bf16[80,2432]{1,0:T(8,128)(2,1)S(1)}, bf16[80,2432]{1,0:T(8,128)(2,1)S(1)}, u32[]{:S(2)}, u32[]{:S(2)}) collective-permute-start(bf16[80,2432]{1,0:T(8,128)(2,1)S(1)} %get-tuple-element.73), channel_id=1, source_target_pairs={{0,4},{1,5},{2,6},{3,7},{4,8},{5,9},{6,10},{7,11},{8,12},{9,13},{1... | collective-permute-start | bytes 1167368 | tf_op jit(solution)/shard_map/ppermute | solution.py:32
  137.7 12.9 %copy-start.12 = (f32[6,2432]{1,0:T(8,128)S(1)}, f32[6,2432]{1,0:T(8,128)}, u32[]{:S(2)}) copy-start(f32[6,2432]{1,0:T(8,128)} %get-tuple-element.78.refs_6_.refs_5_) | copy-start | bytes 175108
  137.7 12.9 %copy-start.15 = (bf16[32,2432]{1,0:T(8,128)(2,1)S(1)}, bf16[32,2432]{1,0:T(8,128)(2,1)}, u32[]{:S(2)}) copy-start(bf16[32,2432]{1,0:T(8,128)(2,1)} %get-tuple-element.49.refs_0_) | copy-start | bytes 466948
  137.7 12.9 %copy-start.17 = (bf16[20,2432]{1,0:T(8,128)(2,1)S(1)}, bf16[20,2432]{1,0:T(8,128)(2,1)}, u32[]{:S(2)}) copy-start(bf16[20,2432]{1,0:T(8,128)(2,1)} %copy-done.16) | copy-start | bytes 291844
  137.7 26.8 %slice-start.1 = ((s8[5914624]{0:T(1024)(128)(4,1)}), s8[1720320]{0:T(1024)(128)(4,1)S(1)}, s32[]{:S(2)}) async-start(s8[5914624]{0:T(1024)(128)(4,1)} %bitcast.28), calls=%async_computation.5 | async-start | bytes 3440640
  138.6 8.6 %collective-permute-start.21 = (bf16[52,2432]{1,0:T(8,128)(2,1)S(1)}, bf16[52,2432]{1,0:T(8,128)(2,1)S(1)}, u32[]{:S(2)}, u32[]{:S(2)}) collective-permute-start(bf16[52,2432]{1,0:T(8,128)(2,1)S(1)} %get-tuple-element.75), channel_id=1, source_target_pairs={{0,3},{1,0},{2,1},{3,2},{4,7},{5,4},{6,5},{7,6},{8,11},{9,8},{10,9... | collective-permute-start | bytes 758792 | tf_op jit(solution)/shard_map/ppermute | solution.py:32
  140.8 6.9 %collective-permute-start.22 = (bf16[52,2432]{1,0:T(8,128)(2,1)S(1)}, bf16[52,2432]{1,0:T(8,128)(2,1)S(1)}, u32[]{:S(2)}, u32[]{:S(2)}) collective-permute-start(bf16[52,2432]{1,0:T(8,128)(2,1)S(1)} %get-tuple-element.76), channel_id=1, source_target_pairs={{0,2},{1,3},{2,0},{3,1},{4,6},{5,7},{6,4},{7,5},{8,10},{9,11},{10,... | collective-permute-start | bytes 758792 | tf_op jit(solution)/shard_map/ppermute | solution.py:32
  140.8 9.8 %collective-permute-start.23 = (bf16[52,2432]{1,0:T(8,128)(2,1)S(1)}, bf16[52,2432]{1,0:T(8,128)(2,1)S(1)}, u32[]{:S(2)}, u32[]{:S(2)}) collective-permute-start(bf16[52,2432]{1,0:T(8,128)(2,1)S(1)} %get-tuple-element.77), channel_id=1, source_target_pairs={{0,1},{1,2},{2,3},{3,0},{4,5},{5,6},{6,7},{7,4},{8,9},{9,10},{10,1... | collective-permute-start | bytes 758792 | tf_op jit(solution)/shard_map/ppermute | solution.py:32
  151.1 9.8 %collective-permute-start.26 = (bf16[52,2432]{1,0:T(8,128)(2,1)S(1)}, bf16[52,2432]{1,0:T(8,128)(2,1)S(1)}, u32[]{:S(2)}, u32[]{:S(2)}) collective-permute-start(bf16[52,2432]{1,0:T(8,128)(2,1)S(1)} %get-tuple-element.80.refs_0_), channel_id=1, source_target_pairs={{0,1},{1,2},{2,3},{3,0},{4,5},{5,6},{6,7},{7,4},{8,9},{9,10},{10,1... | collective-permute-start | bytes 758792 | tf_op jit(solution)/shard_map/ppermute | solution.py:32
  151.2 9.7 %collective-permute-start.25 = (bf16[52,2432]{1,0:T(8,128)(2,1)S(1)}, bf16[52,2432]{1,0:T(8,128)(2,1)S(1)}, u32[]{:S(2)}, u32[]{:S(2)}) collective-permute-start(bf16[52,2432]{1,0:T(8,128)(2,1)S(1)} %get-tuple-element.80.refs_0_), channel_id=1, source_target_pairs={{0,2},{1,3},{2,0},{3,1},{4,6},{5,7},{6,4},{7,5},{8,10},{9,11},{10,... | collective-permute-start | bytes 758792 | tf_op jit(solution)/shard_map/ppermute | solution.py:32
  153.0 8.6 %collective-permute-start.24 = (bf16[52,2432]{1,0:T(8,128)(2,1)S(1)}, bf16[52,2432]{1,0:T(8,128)(2,1)S(1)}, u32[]{:S(2)}, u32[]{:S(2)}) collective-permute-start(bf16[52,2432]{1,0:T(8,128)(2,1)S(1)} %get-tuple-element.80.refs_0_), channel_id=1, source_target_pairs={{0,3},{1,0},{2,1},{3,2},{4,7},{5,4},{6,5},{7,6},{8,11},{9,8},{10,9... | collective-permute-start | bytes 758792 | tf_op jit(solution)/shard_map/ppermute | solution.py:32
  161.7 25.7 %collective-permute-start.29 = (bf16[208,2432]{1,0:T(8,128)(2,1)S(1)}, bf16[208,2432]{1,0:T(8,128)(2,1)S(1)}, u32[]{:S(2)}, u32[]{:S(2)}) collective-permute-start(bf16[208,2432]{1,0:T(8,128)(2,1)S(1)} %shard_map.175.refs_0_), channel_id=1, source_target_pairs={{0,4},{1,5},{2,6},{3,7},{4,8},{5,9},{6,10},{7,11},{8,12},{9,13},{1... | collective-permute-start | bytes 3035144 | tf_op jit(solution)/shard_map/ppermute | solution.py:32
  161.8 25.6 %collective-permute-start.28 = (bf16[208,2432]{1,0:T(8,128)(2,1)S(1)}, bf16[208,2432]{1,0:T(8,128)(2,1)S(1)}, u32[]{:S(2)}, u32[]{:S(2)}) collective-permute-start(bf16[208,2432]{1,0:T(8,128)(2,1)S(1)} %shard_map.175.refs_0_), channel_id=1, source_target_pairs={{0,8},{1,9},{2,10},{3,11},{4,12},{5,13},{6,14},{7,15},{8,0},{9,1},... | collective-permute-start | bytes 3035144 | tf_op jit(solution)/shard_map/ppermute | solution.py:32
  163.3 24.8 %collective-permute-start.27 = (bf16[208,2432]{1,0:T(8,128)(2,1)S(1)}, bf16[208,2432]{1,0:T(8,128)(2,1)S(1)}, u32[]{:S(2)}, u32[]{:S(2)}) collective-permute-start(bf16[208,2432]{1,0:T(8,128)(2,1)S(1)} %shard_map.175.refs_0_), channel_id=1, source_target_pairs={{0,12},{1,13},{2,14},{3,15},{4,0},{5,1},{6,2},{7,3},{8,4},{9,5},{1... | collective-permute-start | bytes 3035144 | tf_op jit(solution)/shard_map/ppermute | solution.py:32
  164.5 2.7 %copy-start = (bf16[2,608,2432]{2,1,0:T(8,128)(2,1)S(1)}, bf16[2,608,2432]{2,1,0:T(8,128)(2,1)}, u32[]{:S(2)}) copy-start(bf16[2,608,2432]{2,1,0:T(8,128)(2,1)} %refs_4_.1) | copy-start | bytes 17743876
  194.5 24.3 %collective-permute-start.30 = (bf16[208,2432]{1,0:T(8,128)(2,1)S(1)}, bf16[208,2432]{1,0:T(8,128)(2,1)S(1)}, u32[]{:S(2)}, u32[]{:S(2)}) collective-permute-start(bf16[208,2432]{1,0:T(8,128)(2,1)S(1)} %get-tuple-element.81), channel_id=1, source_target_pairs={{0,12},{1,13},{2,14},{3,15},{4,0},{5,1},{6,2},{7,3},{8,4},{9,5},{1... | collective-permute-start | bytes 3035144 | tf_op jit(solution)/shard_map/ppermute | solution.py:32
  196.6 22.2 %collective-permute-start.31 = (bf16[208,2432]{1,0:T(8,128)(2,1)S(1)}, bf16[208,2432]{1,0:T(8,128)(2,1)S(1)}, u32[]{:S(2)}, u32[]{:S(2)}) collective-permute-start(bf16[208,2432]{1,0:T(8,128)(2,1)S(1)} %get-tuple-element.82), channel_id=1, source_target_pairs={{0,8},{1,9},{2,10},{3,11},{4,12},{5,13},{6,14},{7,15},{8,0},{9,1},... | collective-permute-start | bytes 3035144 | tf_op jit(solution)/shard_map/ppermute | solution.py:32
  196.6 25.6 %collective-permute-start.32 = (bf16[208,2432]{1,0:T(8,128)(2,1)S(1)}, bf16[208,2432]{1,0:T(8,128)(2,1)S(1)}, u32[]{:S(2)}, u32[]{:S(2)}) collective-permute-start(bf16[208,2432]{1,0:T(8,128)(2,1)S(1)} %get-tuple-element.83), channel_id=1, source_target_pairs={{0,4},{1,5},{2,6},{3,7},{4,8},{5,9},{6,10},{7,11},{8,12},{9,13},{1... | collective-permute-start | bytes 3035144 | tf_op jit(solution)/shard_map/ppermute | solution.py:32
  223.1 6.5 %collective-permute-start.36 = (bf16[20,2432]{1,0:T(8,128)(2,1)S(1)}, bf16[20,2432]{1,0:T(8,128)(2,1)S(1)}, u32[]{:S(2)}, u32[]{:S(2)}) collective-permute-start(bf16[20,2432]{1,0:T(8,128)(2,1)S(1)} %get-tuple-element.90), channel_id=1, source_target_pairs={{0,3},{1,0},{2,1},{3,2},{4,7},{5,4},{6,5},{7,6},{8,11},{9,8},{10,9... | collective-permute-start | bytes 291848 | tf_op jit(solution)/shard_map/ppermute | solution.py:32
  225.2 5.4 %collective-permute-start.37 = (bf16[20,2432]{1,0:T(8,128)(2,1)S(1)}, bf16[20,2432]{1,0:T(8,128)(2,1)S(1)}, u32[]{:S(2)}, u32[]{:S(2)}) collective-permute-start(bf16[20,2432]{1,0:T(8,128)(2,1)S(1)} %get-tuple-element.91), channel_id=1, source_target_pairs={{0,2},{1,3},{2,0},{3,1},{4,6},{5,7},{6,4},{7,5},{8,10},{9,11},{10,... | collective-permute-start | bytes 291848 | tf_op jit(solution)/shard_map/ppermute | solution.py:32
  225.2 6.2 %collective-permute-start.38 = (bf16[20,2432]{1,0:T(8,128)(2,1)S(1)}, bf16[20,2432]{1,0:T(8,128)(2,1)S(1)}, u32[]{:S(2)}, u32[]{:S(2)}) collective-permute-start(bf16[20,2432]{1,0:T(8,128)(2,1)S(1)} %get-tuple-element.92), channel_id=1, source_target_pairs={{0,1},{1,2},{2,3},{3,0},{4,5},{5,6},{6,7},{7,4},{8,9},{9,10},{10,1... | collective-permute-start | bytes 291848 | tf_op jit(solution)/shard_map/ppermute | solution.py:32
  225.9 21.0 %collective-permute-start.33 = (bf16[32,2432]{1,0:T(8,128)(2,1)S(1)}, bf16[32,2432]{1,0:T(8,128)(2,1)S(1)}, u32[]{:S(2)}, u32[]{:S(2)}) collective-permute-start(bf16[32,2432]{1,0:T(8,128)(2,1)S(1)} %get-tuple-element.85), channel_id=1, source_target_pairs={{0,3},{1,0},{2,1},{3,2},{4,7},{5,4},{6,5},{7,6},{8,11},{9,8},{10,9... | collective-permute-start | bytes 466952 | tf_op jit(solution)/shard_map/ppermute | solution.py:32
  227.9 19.0 %collective-permute-start.34 = (bf16[32,2432]{1,0:T(8,128)(2,1)S(1)}, bf16[32,2432]{1,0:T(8,128)(2,1)S(1)}, u32[]{:S(2)}, u32[]{:S(2)}) collective-permute-start(bf16[32,2432]{1,0:T(8,128)(2,1)S(1)} %get-tuple-element.86), channel_id=1, source_target_pairs={{0,2},{1,3},{2,0},{3,1},{4,6},{5,7},{6,4},{7,5},{8,10},{9,11},{10,... | collective-permute-start | bytes 466952 | tf_op jit(solution)/shard_map/ppermute | solution.py:32
  229.6 17.3 %collective-permute-start.35 = (bf16[32,2432]{1,0:T(8,128)(2,1)S(1)}, bf16[32,2432]{1,0:T(8,128)(2,1)S(1)}, u32[]{:S(2)}, u32[]{:S(2)}) collective-permute-start(bf16[32,2432]{1,0:T(8,128)(2,1)S(1)} %get-tuple-element.87), channel_id=1, source_target_pairs={{0,1},{1,2},{2,3},{3,0},{4,5},{5,6},{6,7},{7,4},{8,9},{9,10},{10,1... | collective-permute-start | bytes 466952 | tf_op jit(solution)/shard_map/ppermute | solution.py:32
  232.4 20.1 %all-to-all-start.3 = ((bf16[8,4,2432]{2,1,0:T(4,128)(2,1)}), bf16[8,4,2432]{2,1,0:T(4,128)(2,1)S(1)}, u32[]{:S(2)}, u32[]{:S(2)}) async-start(bf16[8,4,2432]{2,1,0:T(4,128)(2,1)} %shard_map.180), calls=%async_computation.3 | async-start | bytes 311296 | tf_op jit(solution)/shard_map/all_to_all | solution.py:702
  (4 other events, 3.0 us)
